TPU v7x, 128 devices: a whole 4x4x4 slice. The times are simulated.
128 devices in a mesh: seq: 32 (over x, y, core), head: 4 (over z).
Axes of the slice: x: 4, y: 4, z: 4, core: 2. Of those that a mesh axis runs over, the one named last changes fastest.
Arguments:
- normed: bfloat16 [8192, 2560], P('seq'), may hold values from -6 to 6
- w_x: bfloat16 [2560, 5120], P(None, 'head'), may hold values from -0.125 to 0.125
- w_bc: bfloat16 [2560, 256], replicated, may hold values from -0.125 to 0.125
- conv_w: float32 [4, 5120], P(None, 'head'), may hold values from -3 to 3
- decay_code: int32 [80], P('head'), may hold values from 0 to 255, as said below
- step: float32 [80, 8192], P('head', 'seq'), may hold values from 0.0001 to 10000
- d_skip: float32 [80], P('head'), may hold values from 0.5 to 2
- grad_y: bfloat16 [8192, 5120], P('seq', 'head'), may hold values from -6 to 6
Outputs:
- grad_u: bfloat16 [2560, 8192], P('head', 'seq')
- grad_wx: float32 [2560, 5120], P('seq', 'head')
- grad_wbc: float32 [2560, 256], P('seq')
- grad_log_step: float32 [80, 8192], P('head', 'seq')
Inputs may be any that keep to these rules, and one draw needn't show every extreme that they name: `decay_code`: the same codes are used for every token.
All inputs are finite; a program needn't handle non-finite values.
Results may differ from a plain program's by a relative error of at most 0.0056.
Values may be sent and summed in bfloat16 or wider, within the bound.
No kernel may reach another device: no remote copies, remote signals or barrier semaphores. Data moves between devices by JAX's collectives and lax.ppermute only.
A program may use at most 128 MiB of HBM per device.

v0:
```python
import math

import jax
import jax.numpy as jnp
from jax import lax
from jax.sharding import PartitionSpec as P

D = 2560
HEAD_DIM = 64
STATE = 128
GROUP = 256
CONV = 4
LEVELS = 256


HIGH = lax.Precision.HIGHEST


def from_behind(value, axis, by):
    count = lax.axis_size(axis)
    pairs = [(i, i + by) for i in range(count) if 0 <= i + by < count]
    return lax.ppermute(value, axis, pairs)


def head_rates(codes):
    low = math.log(0.995)
    high = math.log(0.9999)
    return low + codes.astype(jnp.float32) / (LEVELS - 1) * (high - low)


def group_pass(state, pieces):
    xs, bq, cq, lq, gq = pieces
    scale = STATE ** (-0.5)
    cum = jnp.cumsum(lq, axis=1)
    size = lq.shape[1]
    mask = jnp.arange(size)[:, None] >= jnp.arange(size)[None, :]
    diff = cum[:, :, None] - cum[:, None, :]
    lmat = jnp.where(mask, jnp.exp(jnp.where(mask, diff, 0.0)), 0.0)
    gram = jnp.dot(cq, bq.T, precision=HIGH) * scale
    xg = xs * gq.T[:, :, None]
    y_intra = jnp.einsum("hij,jhp->ihp", lmat * gram[None], xg, precision=HIGH)
    y_inter = (
        jnp.einsum("hpn,in->ihp", state, cq, precision=HIGH) * (jnp.exp(cum).T * scale)[:, :, None]
    )
    tail = jnp.exp(cum[:, -1:] - cum)
    carried = jnp.exp(cum[:, -1])[:, None, None] * state
    fresh = jnp.einsum("jhp,jn->hpn", xg * tail.T[:, :, None], bq, precision=HIGH)
    return (carried + fresh, y_intra + y_inter)


def state_space(x3, bmat, cmat, logd, gain, state):
    length, heads, width = x3.shape
    count = length // GROUP
    xs = x3.reshape(count, GROUP, heads, width)
    bs = bmat.reshape(count, GROUP, STATE)
    cs = cmat.reshape(count, GROUP, STATE)
    ls = logd.reshape(heads, count, GROUP).transpose(1, 0, 2)
    gs = gain.reshape(heads, count, GROUP).transpose(1, 0, 2)
    final, ys = lax.scan(jax.checkpoint(group_pass), state, (xs, bs, cs, ls, gs))
    return (final, ys.reshape(length, heads, width))


def mixer(x_act, shared, step, rates, d_skip, state):
    length = x_act.shape[0]
    heads = step.shape[0]
    x3 = x_act.reshape(length, heads, HEAD_DIM)
    logd = rates[:, None] * step
    gain = jnp.sqrt(-2.0 * logd)
    final, y3 = state_space(x3, shared[:, :STATE], shared[:, STATE:], logd, gain, state)
    y3 = y3 + d_skip[None, :, None] * x3
    return (y3.reshape(length, heads * HEAD_DIM), final)


def conv_forward(x_pre, conv_w, before):
    length = x_pre.shape[0]
    ext = jnp.concatenate([before, x_pre], axis=0).astype(jnp.float32)
    total = conv_w[0] * ext[CONV - 1 : CONV - 1 + length]
    for tap in range(1, CONV):
        total = total + conv_w[tap] * ext[CONV - 1 - tap : CONV - 1 - tap + length]
    return total


def conv_backward(dxc, conv_w, after):
    length = dxc.shape[0]
    ext = jnp.concatenate([dxc, after], axis=0)
    total = conv_w[0] * ext[0:length]
    for tap in range(1, CONV):
        total = total + conv_w[tap] * ext[tap : tap + length]
    return total


def silu_grad(xc):
    sig = jax.nn.sigmoid(xc)
    return sig * (1.0 + xc * (1.0 - sig))


def body(normed, w_x, w_bc, conv_w, decay_code, step, d_skip, grad_y):
    length = normed.shape[0]
    heads = step.shape[0]
    scale = STATE ** (-0.5)
    x_pre = jnp.dot(normed, w_x, preferred_element_type=jnp.float32).astype(jnp.bfloat16)
    before = from_behind(x_pre[length - (CONV - 1) :], "seq", 1)
    xc = conv_forward(x_pre, conv_w, before)
    x_act = jax.nn.silu(xc)
    shared = jnp.dot(normed, w_bc, preferred_element_type=jnp.float32)
    rates = head_rates(decay_code)
    logd = rates[:, None] * step
    gain = jnp.sqrt(-2.0 * logd)
    cumd = jnp.cumsum(logd, axis=1)
    through = jnp.exp(cumd[:, -1])
    x3 = x_act.reshape(length, heads, HEAD_DIM)
    cotangent = grad_y.astype(jnp.float32)
    dy3 = cotangent.reshape(length, heads, HEAD_DIM)
    weights_in = (gain * jnp.exp(cumd[:, -1:] - cumd)).T
    own_state = jnp.einsum(
        "thp,tn->hpn", x3 * weights_in[:, :, None], shared[:, :STATE], precision=HIGH
    )
    weights_out = (jnp.exp(cumd) * scale).T
    own_pull = jnp.einsum(
        "thp,tn->hpn", dy3 * weights_out[:, :, None], shared[:, STATE:], precision=HIGH
    )
    blank = jnp.zeros((heads, HEAD_DIM, STATE), jnp.float32)

    def forward_turn(index, carry):
        return from_behind(through[:, None, None] * carry + own_state, "seq", 1)

    def backward_turn(index, carry):
        return from_behind(through[:, None, None] * carry + own_pull, "seq", -1)

    turns = lax.axis_size("seq") - 1
    incoming = lax.fori_loop(0, turns, forward_turn, blank)
    leaving_grad = lax.fori_loop(0, turns, backward_turn, blank)

    def forward(x_act, shared, step):
        return mixer(x_act, shared, step, rates, d_skip, incoming)

    outputs, pull = jax.vjp(forward, x_act, shared, step)
    d_x, d_bc, d_step = pull((cotangent, leaving_grad))
    d_shared = lax.psum(d_bc, "head").astype(jnp.bfloat16)
    dxc = d_x * silu_grad(xc)
    after = from_behind(dxc[: CONV - 1], "seq", -1)
    d_pre = conv_backward(dxc, conv_w, after).astype(jnp.bfloat16)
    contract = (((1,), (1,)), ((), ()))
    rows_head = D // lax.axis_size("head")
    part_u = lax.psum_scatter(
        lax.dot_general(w_x, d_pre, contract, preferred_element_type=jnp.float32),
        "head",
        scatter_dimension=0,
        tiled=True,
    )
    own_rows = lax.dynamic_slice_in_dim(w_bc, lax.axis_index("head") * rows_head, rows_head, 0)
    grad_u = (
        part_u + lax.dot_general(own_rows, d_shared, contract, preferred_element_type=jnp.float32)
    ).astype(jnp.bfloat16)
    norm = (length * lax.axis_size("seq")) ** (-0.5)
    over_tokens = (((0,), (0,)), ((), ()))
    columns = normed
    grad_wx = (
        lax.psum_scatter(
            lax.dot_general(columns, d_pre, over_tokens, preferred_element_type=jnp.float32),
            "seq",
            scatter_dimension=0,
            tiled=True,
        )
        * norm
    )
    columns = normed
    grad_wbc = (
        lax.psum_scatter(
            lax.dot_general(columns, d_shared, over_tokens, preferred_element_type=jnp.float32),
            "seq",
            scatter_dimension=0,
            tiled=True,
        )
        * norm
    )
    grad_log_step = step * d_step
    return (grad_u, grad_wx, grad_wbc, grad_log_step)


def solution(mesh):
    return jax.shard_map(
        body,
        mesh=mesh,
        in_specs=(
            P("seq", None),
            P(None, "head"),
            P(),
            P(None, "head"),
            P("head"),
            P("head", "seq"),
            P("head"),
            P("seq", "head"),
        ),
        out_specs=(P("head", "seq"), P("seq", "head"), P("seq", None), P("head", "seq")),
        check_vma=False,
    )
```

profile of v0, /device:TPU:0, one launch (start us, length us, event | category | flops | bytes accessed | tf_op | source)
XLA Modules:
  0.0 1298.0 jit_solution(1835519115022338194)
XLA Ops:
  34.6 442.6 %while.5 = (s32[]{:T(128)}, f32[20,64,128]{2,1,0:T(8,128)S(1)}, f32[20]{0:T(128)}, f32[20,64,128]{2,1,0:T(8,128)S(1)}, s32[]{:T(128)}) while((s32[]{:T(128)}, f32[20,64,128]{2,1,0:T(8,128)S(1)}, f32[20]{0:T(128)}, f32[20,64,128]{2,1,0:T(8,128)S(1)}, s32[]{:T(128)}) %tuple.64), condition=%wide.region_5.6_spmd, body=%wide.region_4.5_spmd.sunk | while | flops 327682 | bytes 4587701 | solution.py:132
  291.2 12.2 collective-permute-done.1
  306.2 12.9 collective-permute-done.1
  322.0 12.9 collective-permute-done.1
  337.8 12.9 collective-permute-done.1
  353.7 12.9 collective-permute-done.1
  369.5 12.9 collective-permute-done.1
  385.3 12.9 collective-permute-done.1
  401.1 12.9 collective-permute-done.1
  416.9 12.9 collective-permute-done.1
  432.7 12.9 collective-permute-done.1
  448.5 12.9 collective-permute-done.1
  464.3 12.9 collective-permute-done.1
  477.3 484.1 %while.4 = (s32[]{:T(128)}, f32[20,64,128]{2,1,0:T(8,128)S(1)}, f32[20]{0:T(128)}, f32[20,64,128]{2,1,0:T(8,128)S(1)}, s32[]{:T(128)}) while((s32[]{:T(128)}, f32[20,64,128]{2,1,0:T(8,128)S(1)}, f32[20]{0:T(128)}, f32[20,64,128]{2,1,0:T(8,128)S(1)}, s32[]{:T(128)}) %tuple.73), condition=%wide.region_3.4_spmd, body=%wide.region_2.3_spmd.sunk | while | flops 327682 | bytes 4587701 | solution.py:131
  478.9 12.5 collective-permute-start
  494.8 11.7 collective-permute-start
  510.0 12.7 collective-permute-start
  526.2 11.4 collective-permute-start
  541.1 12.7 collective-permute-start
  557.3 11.4 collective-permute-start
  572.2 12.5 collective-permute-start
  615.5 12.1 collective-permute-start
  631.1 12.3 collective-permute-start
  646.9 12.3 collective-permute-start
  662.7 12.3 collective-permute-start
  678.5 12.3 collective-permute-start
  694.3 12.3 collective-permute-start
  710.1 12.3 collective-permute-start
  725.9 12.3 collective-permute-start
  741.7 12.3 collective-permute-start
  757.5 12.3 collective-permute-start
  773.3 12.3 collective-permute-start
  789.1 12.3 collective-permute-start
  804.9 12.3 collective-permute-start
  820.8 12.3 collective-permute-start
  836.6 12.3 collective-permute-start
  852.4 12.3 collective-permute-start
  868.2 12.3 collective-permute-start
  884.0 12.3 collective-permute-start
  899.8 12.3 collective-permute-start
  915.6 12.3 collective-permute-start
  931.4 12.3 collective-permute-start
  947.2 12.3 collective-permute-start
  986.9 21.1 %all-reduce.5 = bf16[256,256]{1,0:T(8,128)(2,1)S(1)} all-reduce(f32[256,256]{1,0:T(8,128)S(1)} %pad_add_fusion), channel_id=1, replica_groups=mesh['seq'=32,'head'=4] {'head'}, use_global_device_ids=true, to_apply=%region_10.11 | all-reduce | flops 65536 | bytes 393216 | tf_op jit(solution)/shard_map/psum | solution.py:139
  1041.3 14.0 %copy.83 = f32[2560,1280]{1,0:T(8,128)} copy(f32[2560,1280]{0,1:T(8,128)} %convolution_bitcast_fusion) | data formatting | bytes 26214400
  1060.1 83.2 %reduce-scatter.12.cloned.1.call-done = f32[80,256]{1,0:T(8,128)} async-done(((f32[2560,256]{1,0:T(8,128)}), f32[80,256]{1,0:T(8,128)}) %reduce-scatter.12.cloned.1.call-update) | async-done | bytes 81936
  1145.1 34.4 %reduce-scatter.8.cloned.1.call-done = f32[640,256]{0,1:T(8,128)} async-done(((f32[2560,256]{0,1:T(8,128)}), f32[640,256]{0,1:T(8,128)}) %reduce-scatter.8.cloned.1.call-update) | async-done | bytes 655376 | tf_op jit(solution)/shard_map/reduce_scatter | solution.py:145
  1181.6 107.6 %reduce-scatter.10.cloned.1.call-done = f32[80,1280]{1,0:T(8,128)} async-done(((f32[2560,1280]{1,0:T(8,128)}), f32[80,1280]{1,0:T(8,128)}) %reduce-scatter.10.cloned.1.call-update) | async-done | bytes 409616
  (299 shorter events, 512.4 us)
Async XLA Ops:
  7.2 1136.1 %reduce-scatter.12.cloned.1.call-start = ((), (), s32[]{:S(2)}) async-start(), calls=%async_computation.5 | async-start | bytes 2703360
  43.3 12.1 collective-permute-start.1
  70.7 12.1 collective-permute-start.1
  289.9 13.4 %collective-permute-start.1 = (f32[20,64,128]{2,1,0:T(8,128)}, f32[20,64,128]{2,1,0:T(8,128)S(1)}, u32[]{:S(2)}, u32[]{:S(2)}) collective-permute-start(f32[20,64,128]{2,1,0:T(8,128)} %multiply_add_fusion.6), channel_id=1, source_target_pairs={{4,0},{8,4},{12,8},{16,12},{20,16},{24,20},{28,24},{32,28},{36,32}... | collective-permute-start | bytes 1966088 | tf_op jit(solution)/shard_map/while/body/eval_jaxpr/ppermute | solution.py:22
  304.9 14.2 %collective-permute-start.1 = (f32[20,64,128]{2,1,0:T(8,128)}, f32[20,64,128]{2,1,0:T(8,128)S(1)}, u32[]{:S(2)}, u32[]{:S(2)}) collective-permute-start(f32[20,64,128]{2,1,0:T(8,128)} %multiply_add_fusion.6), channel_id=1, source_target_pairs={{4,0},{8,4},{12,8},{16,12},{20,16},{24,20},{28,24},{32,28},{36,32}... | collective-permute-start | bytes 1966088 | tf_op jit(solution)/shard_map/while/body/eval_jaxpr/ppermute | solution.py:22
  320.7 14.2 %collective-permute-start.1 = (f32[20,64,128]{2,1,0:T(8,128)}, f32[20,64,128]{2,1,0:T(8,128)S(1)}, u32[]{:S(2)}, u32[]{:S(2)}) collective-permute-start(f32[20,64,128]{2,1,0:T(8,128)} %multiply_add_fusion.6), channel_id=1, source_target_pairs={{4,0},{8,4},{12,8},{16,12},{20,16},{24,20},{28,24},{32,28},{36,32}... | collective-permute-start | bytes 1966088 | tf_op jit(solution)/shard_map/while/body/eval_jaxpr/ppermute | solution.py:22
  336.6 14.2 %collective-permute-start.1 = (f32[20,64,128]{2,1,0:T(8,128)}, f32[20,64,128]{2,1,0:T(8,128)S(1)}, u32[]{:S(2)}, u32[]{:S(2)}) collective-permute-start(f32[20,64,128]{2,1,0:T(8,128)} %multiply_add_fusion.6), channel_id=1, source_target_pairs={{4,0},{8,4},{12,8},{16,12},{20,16},{24,20},{28,24},{32,28},{36,32}... | collective-permute-start | bytes 1966088 | tf_op jit(solution)/shard_map/while/body/eval_jaxpr/ppermute | solution.py:22
  352.4 14.2 %collective-permute-start.1 = (f32[20,64,128]{2,1,0:T(8,128)}, f32[20,64,128]{2,1,0:T(8,128)S(1)}, u32[]{:S(2)}, u32[]{:S(2)}) collective-permute-start(f32[20,64,128]{2,1,0:T(8,128)} %multiply_add_fusion.6), channel_id=1, source_target_pairs={{4,0},{8,4},{12,8},{16,12},{20,16},{24,20},{28,24},{32,28},{36,32}... | collective-permute-start | bytes 1966088 | tf_op jit(solution)/shard_map/while/body/eval_jaxpr/ppermute | solution.py:22
  368.2 14.2 %collective-permute-start.1 = (f32[20,64,128]{2,1,0:T(8,128)}, f32[20,64,128]{2,1,0:T(8,128)S(1)}, u32[]{:S(2)}, u32[]{:S(2)}) collective-permute-start(f32[20,64,128]{2,1,0:T(8,128)} %multiply_add_fusion.6), channel_id=1, source_target_pairs={{4,0},{8,4},{12,8},{16,12},{20,16},{24,20},{28,24},{32,28},{36,32}... | collective-permute-start | bytes 1966088 | tf_op jit(solution)/shard_map/while/body/eval_jaxpr/ppermute | solution.py:22
  384.0 14.2 %collective-permute-start.1 = (f32[20,64,128]{2,1,0:T(8,128)}, f32[20,64,128]{2,1,0:T(8,128)S(1)}, u32[]{:S(2)}, u32[]{:S(2)}) collective-permute-start(f32[20,64,128]{2,1,0:T(8,128)} %multiply_add_fusion.6), channel_id=1, source_target_pairs={{4,0},{8,4},{12,8},{16,12},{20,16},{24,20},{28,24},{32,28},{36,32}... | collective-permute-start | bytes 1966088 | tf_op jit(solution)/shard_map/while/body/eval_jaxpr/ppermute | solution.py:22
  399.8 14.2 %collective-permute-start.1 = (f32[20,64,128]{2,1,0:T(8,128)}, f32[20,64,128]{2,1,0:T(8,128)S(1)}, u32[]{:S(2)}, u32[]{:S(2)}) collective-permute-start(f32[20,64,128]{2,1,0:T(8,128)} %multiply_add_fusion.6), channel_id=1, source_target_pairs={{4,0},{8,4},{12,8},{16,12},{20,16},{24,20},{28,24},{32,28},{36,32}... | collective-permute-start | bytes 1966088 | tf_op jit(solution)/shard_map/while/body/eval_jaxpr/ppermute | solution.py:22
  415.6 14.2 %collective-permute-start.1 = (f32[20,64,128]{2,1,0:T(8,128)}, f32[20,64,128]{2,1,0:T(8,128)S(1)}, u32[]{:S(2)}, u32[]{:S(2)}) collective-permute-start(f32[20,64,128]{2,1,0:T(8,128)} %multiply_add_fusion.6), channel_id=1, source_target_pairs={{4,0},{8,4},{12,8},{16,12},{20,16},{24,20},{28,24},{32,28},{36,32}... | collective-permute-start | bytes 1966088 | tf_op jit(solution)/shard_map/while/body/eval_jaxpr/ppermute | solution.py:22
  431.4 14.2 %collective-permute-start.1 = (f32[20,64,128]{2,1,0:T(8,128)}, f32[20,64,128]{2,1,0:T(8,128)S(1)}, u32[]{:S(2)}, u32[]{:S(2)}) collective-permute-start(f32[20,64,128]{2,1,0:T(8,128)} %multiply_add_fusion.6), channel_id=1, source_target_pairs={{4,0},{8,4},{12,8},{16,12},{20,16},{24,20},{28,24},{32,28},{36,32}... | collective-permute-start | bytes 1966088 | tf_op jit(solution)/shard_map/while/body/eval_jaxpr/ppermute | solution.py:22
  447.2 14.2 %collective-permute-start.1 = (f32[20,64,128]{2,1,0:T(8,128)}, f32[20,64,128]{2,1,0:T(8,128)S(1)}, u32[]{:S(2)}, u32[]{:S(2)}) collective-permute-start(f32[20,64,128]{2,1,0:T(8,128)} %multiply_add_fusion.6), channel_id=1, source_target_pairs={{4,0},{8,4},{12,8},{16,12},{20,16},{24,20},{28,24},{32,28},{36,32}... | collective-permute-start | bytes 1966088 | tf_op jit(solution)/shard_map/while/body/eval_jaxpr/ppermute | solution.py:22
  463.0 14.2 %collective-permute-start.1 = (f32[20,64,128]{2,1,0:T(8,128)}, f32[20,64,128]{2,1,0:T(8,128)S(1)}, u32[]{:S(2)}, u32[]{:S(2)}) collective-permute-start(f32[20,64,128]{2,1,0:T(8,128)} %multiply_add_fusion.6), channel_id=1, source_target_pairs={{4,0},{8,4},{12,8},{16,12},{20,16},{24,20},{28,24},{32,28},{36,32}... | collective-permute-start | bytes 1966088 | tf_op jit(solution)/shard_map/while/body/eval_jaxpr/ppermute | solution.py:22
  478.9 14.3 %collective-permute-start = (f32[20,64,128]{2,1,0:T(8,128)}, f32[20,64,128]{2,1,0:T(8,128)S(1)}, u32[]{:S(2)}, u32[]{:S(2)}) collective-permute-start(f32[20,64,128]{2,1,0:T(8,128)} %multiply_add_fusion.5), channel_id=1, source_target_pairs={{0,4},{4,8},{8,12},{12,16},{16,20},{20,24},{24,28},{28,32},{32,36}... | collective-permute-start | bytes 1966088 | tf_op jit(solution)/shard_map/while/body/eval_jaxpr/ppermute | solution.py:22
  494.8 13.6 %collective-permute-start = (f32[20,64,128]{2,1,0:T(8,128)}, f32[20,64,128]{2,1,0:T(8,128)S(1)}, u32[]{:S(2)}, u32[]{:S(2)}) collective-permute-start(f32[20,64,128]{2,1,0:T(8,128)} %multiply_add_fusion.5), channel_id=1, source_target_pairs={{0,4},{4,8},{8,12},{12,16},{16,20},{20,24},{24,28},{28,32},{32,36}... | collective-permute-start | bytes 1966088 | tf_op jit(solution)/shard_map/while/body/eval_jaxpr/ppermute | solution.py:22
  510.0 14.6 %collective-permute-start = (f32[20,64,128]{2,1,0:T(8,128)}, f32[20,64,128]{2,1,0:T(8,128)S(1)}, u32[]{:S(2)}, u32[]{:S(2)}) collective-permute-start(f32[20,64,128]{2,1,0:T(8,128)} %multiply_add_fusion.5), channel_id=1, source_target_pairs={{0,4},{4,8},{8,12},{12,16},{16,20},{20,24},{24,28},{28,32},{32,36}... | collective-permute-start | bytes 1966088 | tf_op jit(solution)/shard_map/while/body/eval_jaxpr/ppermute | solution.py:22
  526.2 13.3 %collective-permute-start = (f32[20,64,128]{2,1,0:T(8,128)}, f32[20,64,128]{2,1,0:T(8,128)S(1)}, u32[]{:S(2)}, u32[]{:S(2)}) collective-permute-start(f32[20,64,128]{2,1,0:T(8,128)} %multiply_add_fusion.5), channel_id=1, source_target_pairs={{0,4},{4,8},{8,12},{12,16},{16,20},{20,24},{24,28},{28,32},{32,36}... | collective-permute-start | bytes 1966088 | tf_op jit(solution)/shard_map/while/body/eval_jaxpr/ppermute | solution.py:22
  541.1 14.6 %collective-permute-start = (f32[20,64,128]{2,1,0:T(8,128)}, f32[20,64,128]{2,1,0:T(8,128)S(1)}, u32[]{:S(2)}, u32[]{:S(2)}) collective-permute-start(f32[20,64,128]{2,1,0:T(8,128)} %multiply_add_fusion.5), channel_id=1, source_target_pairs={{0,4},{4,8},{8,12},{12,16},{16,20},{20,24},{24,28},{28,32},{32,36}... | collective-permute-start | bytes 1966088 | tf_op jit(solution)/shard_map/while/body/eval_jaxpr/ppermute | solution.py:22
  557.3 13.3 %collective-permute-start = (f32[20,64,128]{2,1,0:T(8,128)}, f32[20,64,128]{2,1,0:T(8,128)S(1)}, u32[]{:S(2)}, u32[]{:S(2)}) collective-permute-start(f32[20,64,128]{2,1,0:T(8,128)} %multiply_add_fusion.5), channel_id=1, source_target_pairs={{0,4},{4,8},{8,12},{12,16},{16,20},{20,24},{24,28},{28,32},{32,36}... | collective-permute-start | bytes 1966088 | tf_op jit(solution)/shard_map/while/body/eval_jaxpr/ppermute | solution.py:22
  572.2 14.3 %collective-permute-start = (f32[20,64,128]{2,1,0:T(8,128)}, f32[20,64,128]{2,1,0:T(8,128)S(1)}, u32[]{:S(2)}, u32[]{:S(2)}) collective-permute-start(f32[20,64,128]{2,1,0:T(8,128)} %multiply_add_fusion.5), channel_id=1, source_target_pairs={{0,4},{4,8},{8,12},{12,16},{16,20},{20,24},{24,28},{28,32},{32,36}... | collective-permute-start | bytes 1966088 | tf_op jit(solution)/shard_map/while/body/eval_jaxpr/ppermute | solution.py:22
  588.1 12.1 collective-permute-start
  601.8 12.1 collective-permute-start
  615.5 14.0 %collective-permute-start = (f32[20,64,128]{2,1,0:T(8,128)}, f32[20,64,128]{2,1,0:T(8,128)S(1)}, u32[]{:S(2)}, u32[]{:S(2)}) collective-permute-start(f32[20,64,128]{2,1,0:T(8,128)} %multiply_add_fusion.5), channel_id=1, source_target_pairs={{0,4},{4,8},{8,12},{12,16},{16,20},{20,24},{24,28},{28,32},{32,36}... | collective-permute-start | bytes 1966088 | tf_op jit(solution)/shard_map/while/body/eval_jaxpr/ppermute | solution.py:22
  631.1 14.2 %collective-permute-start = (f32[20,64,128]{2,1,0:T(8,128)}, f32[20,64,128]{2,1,0:T(8,128)S(1)}, u32[]{:S(2)}, u32[]{:S(2)}) collective-permute-start(f32[20,64,128]{2,1,0:T(8,128)} %multiply_add_fusion.5), channel_id=1, source_target_pairs={{0,4},{4,8},{8,12},{12,16},{16,20},{20,24},{24,28},{28,32},{32,36}... | collective-permute-start | bytes 1966088 | tf_op jit(solution)/shard_map/while/body/eval_jaxpr/ppermute | solution.py:22
  646.9 14.2 %collective-permute-start = (f32[20,64,128]{2,1,0:T(8,128)}, f32[20,64,128]{2,1,0:T(8,128)S(1)}, u32[]{:S(2)}, u32[]{:S(2)}) collective-permute-start(f32[20,64,128]{2,1,0:T(8,128)} %multiply_add_fusion.5), channel_id=1, source_target_pairs={{0,4},{4,8},{8,12},{12,16},{16,20},{20,24},{24,28},{28,32},{32,36}... | collective-permute-start | bytes 1966088 | tf_op jit(solution)/shard_map/while/body/eval_jaxpr/ppermute | solution.py:22
  662.7 14.2 %collective-permute-start = (f32[20,64,128]{2,1,0:T(8,128)}, f32[20,64,128]{2,1,0:T(8,128)S(1)}, u32[]{:S(2)}, u32[]{:S(2)}) collective-permute-start(f32[20,64,128]{2,1,0:T(8,128)} %multiply_add_fusion.5), channel_id=1, source_target_pairs={{0,4},{4,8},{8,12},{12,16},{16,20},{20,24},{24,28},{28,32},{32,36}... | collective-permute-start | bytes 1966088 | tf_op jit(solution)/shard_map/while/body/eval_jaxpr/ppermute | solution.py:22
  678.5 14.2 %collective-permute-start = (f32[20,64,128]{2,1,0:T(8,128)}, f32[20,64,128]{2,1,0:T(8,128)S(1)}, u32[]{:S(2)}, u32[]{:S(2)}) collective-permute-start(f32[20,64,128]{2,1,0:T(8,128)} %multiply_add_fusion.5), channel_id=1, source_target_pairs={{0,4},{4,8},{8,12},{12,16},{16,20},{20,24},{24,28},{28,32},{32,36}... | collective-permute-start | bytes 1966088 | tf_op jit(solution)/shard_map/while/body/eval_jaxpr/ppermute | solution.py:22
  694.3 14.2 %collective-permute-start = (f32[20,64,128]{2,1,0:T(8,128)}, f32[20,64,128]{2,1,0:T(8,128)S(1)}, u32[]{:S(2)}, u32[]{:S(2)}) collective-permute-start(f32[20,64,128]{2,1,0:T(8,128)} %multiply_add_fusion.5), channel_id=1, source_target_pairs={{0,4},{4,8},{8,12},{12,16},{16,20},{20,24},{24,28},{28,32},{32,36}... | collective-permute-start | bytes 1966088 | tf_op jit(solution)/shard_map/while/body/eval_jaxpr/ppermute | solution.py:22
  710.1 14.2 %collective-permute-start = (f32[20,64,128]{2,1,0:T(8,128)}, f32[20,64,128]{2,1,0:T(8,128)S(1)}, u32[]{:S(2)}, u32[]{:S(2)}) collective-permute-start(f32[20,64,128]{2,1,0:T(8,128)} %multiply_add_fusion.5), channel_id=1, source_target_pairs={{0,4},{4,8},{8,12},{12,16},{16,20},{20,24},{24,28},{28,32},{32,36}... | collective-permute-start | bytes 1966088 | tf_op jit(solution)/shard_map/while/body/eval_jaxpr/ppermute | solution.py:22
  725.9 14.2 %collective-permute-start = (f32[20,64,128]{2,1,0:T(8,128)}, f32[20,64,128]{2,1,0:T(8,128)S(1)}, u32[]{:S(2)}, u32[]{:S(2)}) collective-permute-start(f32[20,64,128]{2,1,0:T(8,128)} %multiply_add_fusion.5), channel_id=1, source_target_pairs={{0,4},{4,8},{8,12},{12,16},{16,20},{20,24},{24,28},{28,32},{32,36}... | collective-permute-start | bytes 1966088 | tf_op jit(solution)/shard_map/while/body/eval_jaxpr/ppermute | solution.py:22
  741.7 14.2 %collective-permute-start = (f32[20,64,128]{2,1,0:T(8,128)}, f32[20,64,128]{2,1,0:T(8,128)S(1)}, u32[]{:S(2)}, u32[]{:S(2)}) collective-permute-start(f32[20,64,128]{2,1,0:T(8,128)} %multiply_add_fusion.5), channel_id=1, source_target_pairs={{0,4},{4,8},{8,12},{12,16},{16,20},{20,24},{24,28},{28,32},{32,36}... | collective-permute-start | bytes 1966088 | tf_op jit(solution)/shard_map/while/body/eval_jaxpr/ppermute | solution.py:22
  757.5 14.2 %collective-permute-start = (f32[20,64,128]{2,1,0:T(8,128)}, f32[20,64,128]{2,1,0:T(8,128)S(1)}, u32[]{:S(2)}, u32[]{:S(2)}) collective-permute-start(f32[20,64,128]{2,1,0:T(8,128)} %multiply_add_fusion.5), channel_id=1, source_target_pairs={{0,4},{4,8},{8,12},{12,16},{16,20},{20,24},{24,28},{28,32},{32,36}... | collective-permute-start | bytes 1966088 | tf_op jit(solution)/shard_map/while/body/eval_jaxpr/ppermute | solution.py:22
  773.3 14.2 %collective-permute-start = (f32[20,64,128]{2,1,0:T(8,128)}, f32[20,64,128]{2,1,0:T(8,128)S(1)}, u32[]{:S(2)}, u32[]{:S(2)}) collective-permute-start(f32[20,64,128]{2,1,0:T(8,128)} %multiply_add_fusion.5), channel_id=1, source_target_pairs={{0,4},{4,8},{8,12},{12,16},{16,20},{20,24},{24,28},{28,32},{32,36}... | collective-permute-start | bytes 1966088 | tf_op jit(solution)/shard_map/while/body/eval_jaxpr/ppermute | solution.py:22
  789.1 14.2 %collective-permute-start = (f32[20,64,128]{2,1,0:T(8,128)}, f32[20,64,128]{2,1,0:T(8,128)S(1)}, u32[]{:S(2)}, u32[]{:S(2)}) collective-permute-start(f32[20,64,128]{2,1,0:T(8,128)} %multiply_add_fusion.5), channel_id=1, source_target_pairs={{0,4},{4,8},{8,12},{12,16},{16,20},{20,24},{24,28},{28,32},{32,36}... | collective-permute-start | bytes 1966088 | tf_op jit(solution)/shard_map/while/body/eval_jaxpr/ppermute | solution.py:22
  804.9 14.2 %collective-permute-start = (f32[20,64,128]{2,1,0:T(8,128)}, f32[20,64,128]{2,1,0:T(8,128)S(1)}, u32[]{:S(2)}, u32[]{:S(2)}) collective-permute-start(f32[20,64,128]{2,1,0:T(8,128)} %multiply_add_fusion.5), channel_id=1, source_target_pairs={{0,4},{4,8},{8,12},{12,16},{16,20},{20,24},{24,28},{28,32},{32,36}... | collective-permute-start | bytes 1966088 | tf_op jit(solution)/shard_map/while/body/eval_jaxpr/ppermute | solution.py:22
  820.8 14.2 %collective-permute-start = (f32[20,64,128]{2,1,0:T(8,128)}, f32[20,64,128]{2,1,0:T(8,128)S(1)}, u32[]{:S(2)}, u32[]{:S(2)}) collective-permute-start(f32[20,64,128]{2,1,0:T(8,128)} %multiply_add_fusion.5), channel_id=1, source_target_pairs={{0,4},{4,8},{8,12},{12,16},{16,20},{20,24},{24,28},{28,32},{32,36}... | collective-permute-start | bytes 1966088 | tf_op jit(solution)/shard_map/while/body/eval_jaxpr/ppermute | solution.py:22
  836.6 14.2 %collective-permute-start = (f32[20,64,128]{2,1,0:T(8,128)}, f32[20,64,128]{2,1,0:T(8,128)S(1)}, u32[]{:S(2)}, u32[]{:S(2)}) collective-permute-start(f32[20,64,128]{2,1,0:T(8,128)} %multiply_add_fusion.5), channel_id=1, source_target_pairs={{0,4},{4,8},{8,12},{12,16},{16,20},{20,24},{24,28},{28,32},{32,36}... | collective-permute-start | bytes 1966088 | tf_op jit(solution)/shard_map/while/body/eval_jaxpr/ppermute | solution.py:22
  852.4 14.2 %collective-permute-start = (f32[20,64,128]{2,1,0:T(8,128)}, f32[20,64,128]{2,1,0:T(8,128)S(1)}, u32[]{:S(2)}, u32[]{:S(2)}) collective-permute-start(f32[20,64,128]{2,1,0:T(8,128)} %multiply_add_fusion.5), channel_id=1, source_target_pairs={{0,4},{4,8},{8,12},{12,16},{16,20},{20,24},{24,28},{28,32},{32,36}... | collective-permute-start | bytes 1966088 | tf_op jit(solution)/shard_map/while/body/eval_jaxpr/ppermute | solution.py:22
  868.2 14.2 %collective-permute-start = (f32[20,64,128]{2,1,0:T(8,128)}, f32[20,64,128]{2,1,0:T(8,128)S(1)}, u32[]{:S(2)}, u32[]{:S(2)}) collective-permute-start(f32[20,64,128]{2,1,0:T(8,128)} %multiply_add_fusion.5), channel_id=1, source_target_pairs={{0,4},{4,8},{8,12},{12,16},{16,20},{20,24},{24,28},{28,32},{32,36}... | collective-permute-start | bytes 1966088 | tf_op jit(solution)/shard_map/while/body/eval_jaxpr/ppermute | solution.py:22
  884.0 14.2 %collective-permute-start = (f32[20,64,128]{2,1,0:T(8,128)}, f32[20,64,128]{2,1,0:T(8,128)S(1)}, u32[]{:S(2)}, u32[]{:S(2)}) collective-permute-start(f32[20,64,128]{2,1,0:T(8,128)} %multiply_add_fusion.5), channel_id=1, source_target_pairs={{0,4},{4,8},{8,12},{12,16},{16,20},{20,24},{24,28},{28,32},{32,36}... | collective-permute-start | bytes 1966088 | tf_op jit(solution)/shard_map/while/body/eval_jaxpr/ppermute | solution.py:22
  899.8 14.2 %collective-permute-start = (f32[20,64,128]{2,1,0:T(8,128)}, f32[20,64,128]{2,1,0:T(8,128)S(1)}, u32[]{:S(2)}, u32[]{:S(2)}) collective-permute-start(f32[20,64,128]{2,1,0:T(8,128)} %multiply_add_fusion.5), channel_id=1, source_target_pairs={{0,4},{4,8},{8,12},{12,16},{16,20},{20,24},{24,28},{28,32},{32,36}... | collective-permute-start | bytes 1966088 | tf_op jit(solution)/shard_map/while/body/eval_jaxpr/ppermute | solution.py:22
  915.6 14.2 %collective-permute-start = (f32[20,64,128]{2,1,0:T(8,128)}, f32[20,64,128]{2,1,0:T(8,128)S(1)}, u32[]{:S(2)}, u32[]{:S(2)}) collective-permute-start(f32[20,64,128]{2,1,0:T(8,128)} %multiply_add_fusion.5), channel_id=1, source_target_pairs={{0,4},{4,8},{8,12},{12,16},{16,20},{20,24},{24,28},{28,32},{32,36}... | collective-permute-start | bytes 1966088 | tf_op jit(solution)/shard_map/while/body/eval_jaxpr/ppermute | solution.py:22
  931.4 14.2 %collective-permute-start = (f32[20,64,128]{2,1,0:T(8,128)}, f32[20,64,128]{2,1,0:T(8,128)S(1)}, u32[]{:S(2)}, u32[]{:S(2)}) collective-permute-start(f32[20,64,128]{2,1,0:T(8,128)} %multiply_add_fusion.5), channel_id=1, source_target_pairs={{0,4},{4,8},{8,12},{12,16},{16,20},{20,24},{24,28},{28,32},{32,36}... | collective-permute-start | bytes 1966088 | tf_op jit(solution)/shard_map/while/body/eval_jaxpr/ppermute | solution.py:22
  947.2 14.2 %collective-permute-start = (f32[20,64,128]{2,1,0:T(8,128)}, f32[20,64,128]{2,1,0:T(8,128)S(1)}, u32[]{:S(2)}, u32[]{:S(2)}) collective-permute-start(f32[20,64,128]{2,1,0:T(8,128)} %multiply_add_fusion.5), channel_id=1, source_target_pairs={{0,4},{4,8},{8,12},{12,16},{16,20},{20,24},{24,28},{28,32},{32,36}... | collective-permute-start | bytes 1966088 | tf_op jit(solution)/shard_map/while/body/eval_jaxpr/ppermute | solution.py:22
  1013.3 166.2 %reduce-scatter.8.cloned.1.call-start = ((), (), s32[]{:S(2)}) async-start(), calls=%async_computation.3 | async-start | bytes 3276800 | tf_op jit(solution)/shard_map/reduce_scatter | solution.py:145
  1034.5 254.7 %reduce-scatter.10.cloned.1.call-start = ((), (), s32[]{:S(2)}) async-start(), calls=%async_computation.4 | async-start | bytes 13516800
  (48 other events, 811.9 us)
Sparse Core Ops, SparseCore 0:
  1013.4 129.8 reduce-scatter.11
  1145.9 33.5 reduce-scatter.7
  1183.9 105.2 reduce-scatter.9
where the time goes:
time: 1300 us
  waiting for transfers between devices  645 us (50%)
  starting transfers between devices  419 us (32%)
  other arithmetic  113 us (9%)
  matrix products  49.9 us (4%)
  local copies, waits for them, and re-layouts  35 us (3%)
  blocking collectives  21.1 us (2%)
  between operations  14.3 us (1%)
    ppermute x64, waiting for transfers between devices, from_behind(): return lax.ppermute(value, axis, pairs)  420 us
    ppermute x64, starting transfers between devices, from_behind(): return lax.ppermute(value, axis, pairs)  419 us
    unnamed x5, waiting for transfers between devices  191 us
    add x31, other arithmetic, backward_turn(): return from_behind(through[:, None, None] * carry + own_pull, 'seq', -1)  49.4 us
    add x31, other arithmetic, forward_turn(): return from_behind(through[:, None, None] * carry + own_state, 'seq', 1)  49.4 us
    reduce_scatter x1, waiting for transfers between devices, body(): lax.psum_scatter(lax.dot_general(w_x, d_pre, contract, preferred_element_...  34.4 us
  transfers between devices with their start and end apart: 67, of which 66 were waited for; matrix products, arithmetic and copies ran while one was open for 4% of the time, Pallas kernels for 0%

commit v1 on v0

v1 whole, which is shorter than its diff:
```python
import functools
import math

import jax
import jax.numpy as jnp
import numpy as np
from jax import lax
from jax.experimental import pallas as pl
from jax.experimental.pallas import tpu as pltpu
from jax.sharding import PartitionSpec as P

D = 2560
HEAD_DIM = 64
STATE = 128
CONV = 4
LEVELS = 256
T = 256
CH = 1280
HEADS = 20
SEQ = 32
ZS = 4
ROWS = 80
SLICE = 40
MSG = 48
BLK = 256
NBLK = CH // BLK
SCALE = STATE ** (-0.5)
F32 = jnp.float32
BF16 = jnp.bfloat16
HIGH = lax.Precision.HIGHEST
NT = (((1,), (1,)), ((), ()))
VMEM = 56 * 2**20


def nt(a, b):
    return lax.dot_general(a, b, NT, preferred_element_type=F32)


def nn(a, b):
    return jnp.dot(a, b, preferred_element_type=F32)


def split(value):
    high = value.astype(BF16)
    return high, (value - high.astype(F32)).astype(BF16)


def wide(dot, a, b):
    a_high, a_low = split(a)
    b_high, b_low = split(b)
    return dot(a_high, b_high) + (dot(a_low, b_high) + dot(a_high, b_low))


def params():
    return pltpu.CompilerParams(vmem_limit_bytes=VMEM)


def cost(flops, nbytes, trans=0):
    return pl.CostEstimate(flops=flops, bytes_accessed=nbytes, transcendentals=trans)


def whole(*shape):
    return pl.BlockSpec(shape, lambda i: (0,) * len(shape))


def triangle(upper):
    row = lax.broadcasted_iota(jnp.int32, (T, T), 0)
    col = lax.broadcasted_iota(jnp.int32, (T, T), 1)
    return jnp.where(row <= col if upper else row >= col, 1.0, 0.0).astype(F32)


def front_kernel(normed, w_bc, rates, step, grad_y, bmat, cmat, cum, logd, dyt, dywt, msg, pulled, turn):
    shared = nn(normed[...], w_bc[...])
    bmat[...] = shared[:, :STATE]
    cmat[...] = shared[:, STATE:]
    c_high, c_low = split(shared[:, STATE:])
    logs = rates[...] * step[...]
    logd[...] = logs
    cums = jnp.dot(logs, triangle(True), precision=HIGH, preferred_element_type=F32)
    cum[...] = cums
    grown = jnp.exp(cums)
    weight = grown * SCALE
    for pair in range(HEADS // 2):
        rows = slice(128 * pair, 128 * pair + 128)
        tile = grad_y[:, rows].astype(F32).T
        dyt[rows, :] = tile.astype(BF16)
        tile = jnp.concatenate(
            [
                tile[:64] * weight[2 * pair : 2 * pair + 1],
                tile[64:] * weight[2 * pair + 1 : 2 * pair + 2],
            ],
            axis=0,
        )
        high, low = split(tile)
        dywt[rows, :] = high
        pulled[rows, :] = nn(high, c_high) + (nn(low, c_high) + nn(high, c_low))
    turn[...] = jnp.zeros((128, 128), F32)
    turn[:HEADS, :] = grown[:, 128:]
    through = jnp.broadcast_to(turn[...].T[127:, :], (MSG - SLICE, STATE))
    for k in range(SEQ):
        msg[k, :SLICE, :] = pulled[SLICE * k : SLICE * (k + 1), :]
        msg[k, SLICE:, :] = through


def front(normed, w_bc, rates, step, grad_y):
    return pl.pallas_call(
        front_kernel,
        out_shape=(
            jax.ShapeDtypeStruct((T, STATE), F32),
            jax.ShapeDtypeStruct((T, STATE), F32),
            jax.ShapeDtypeStruct((HEADS, T), F32),
            jax.ShapeDtypeStruct((HEADS, T), F32),
            jax.ShapeDtypeStruct((CH, T), BF16),
            jax.ShapeDtypeStruct((CH, T), BF16),
            jax.ShapeDtypeStruct((SEQ, MSG, STATE), F32),
        ),
        scratch_shapes=[pltpu.VMEM((CH, STATE), F32), pltpu.VMEM((128, 128), F32)],
        compiler_params=params(),
        cost_estimate=cost(2 * T * D * 256 + 6 * CH * T * 128, 6 * 2**20),
    )(normed, w_bc, rates, step, grad_y)


def chain_kernel(reverse, table, recv, decays, tie, out, turn):
    del tie
    lanes = jnp.concatenate([decays[:, 0, :], jnp.zeros((128 - SEQ, 128), F32)], axis=0)
    turn[...] = lanes.T
    head = table[32]
    row = lax.broadcasted_iota(jnp.int32, (SLICE, 128), 0)
    cols = jnp.where(row < table[33], turn[pl.ds(head, 1), :], turn[pl.ds(head + 1, 1), :])
    state = jnp.zeros((SLICE, STATE), F32)
    for k in range(SEQ - 1, -1, -1) if reverse else range(SEQ):
        out[k] = state
        state = cols[:, k : k + 1] * state + recv[k]


def chain(table, recv, pulls, tie, reverse):
    return pl.pallas_call(
        functools.partial(chain_kernel, reverse),
        grid=(1,),
        in_specs=[
            pl.BlockSpec(memory_space=pltpu.SMEM),
            whole(SEQ, SLICE, STATE),
            pl.BlockSpec((SEQ, MSG - SLICE, STATE), lambda i: (0, SLICE // 8, 0)),
            pl.BlockSpec(memory_space=pl.ANY),
        ],
        out_specs=whole(SEQ, SLICE, STATE),
        out_shape=jax.ShapeDtypeStruct((SEQ, SLICE, STATE), F32),
        scratch_shapes=[pltpu.VMEM((128, 128), F32)],
        compiler_params=params(),
        cost_estimate=cost(10**6, 2 * 2**20),
    )(table, recv, pulls, tie)


def channel_kernel(before, normed, w_x, conv_w, cum, logd, bmat, xgt, sgt, xwt, own, ext, pre):
    step = pl.program_id(0)

    @pl.when(step == 0)
    def _():
        ext[:16, :] = before[...]
        ext[16:, :] = normed[...]

    now = lax.rem(step, 2)
    past = pre.at[1 - now]
    total = conv_w[0:1, :] * past[16 : 16 + T, :]
    for tap in range(1, CONV):
        total = total + conv_w[tap : tap + 1, :] * past[16 - tap : 16 - tap + T, :]
    sig = 1.0 / (1.0 + jnp.exp(-total))
    xt = (total * sig).T
    sgt[...] = (sig * (1.0 + total * (1.0 - sig))).T
    parts = []
    block = jnp.maximum(step - 1, 0)
    for q in range(BLK // HEAD_DIM):
        head = pl.ds(block * (BLK // HEAD_DIM) + q, 1)
        rows = slice(64 * q, 64 * q + 64)
        gain = jnp.sqrt(-2.0 * logd[head, :])
        cums = cum[head, :]
        tail = jnp.exp(cums[:, T - 1 :] - cums)
        xg = xt[rows] * gain
        xgt[rows, :] = xg.astype(BF16)
        parts.append(xg * tail)
    weighted = jnp.concatenate(parts, axis=0)
    xwt[...] = weighted.astype(BF16)
    own[...] = wide(nn, weighted, bmat[...])
    pre[now] = nn(ext[...], w_x[...]).astype(BF16).astype(F32)


def channels(before, normed, w_x, conv_w, cum, logd, bmat):
    def late(i):
        return jnp.maximum(i - 1, 0)

    rows = pl.BlockSpec((BLK, T), lambda i: (late(i), 0))
    return pl.pallas_call(
        channel_kernel,
        grid=(NBLK + 1,),
        in_specs=[
            whole(16, D),
            whole(T, D),
            pl.BlockSpec((D, BLK), lambda i: (0, jnp.minimum(i, NBLK - 1))),
            pl.BlockSpec((CONV, BLK), lambda i: (0, late(i))),
            whole(HEADS, T),
            whole(HEADS, T),
            whole(T, STATE),
        ],
        out_specs=(rows, rows, rows, pl.BlockSpec((BLK, STATE), lambda i: (late(i), 0))),
        out_shape=(
            jax.ShapeDtypeStruct((CH, T), BF16),
            jax.ShapeDtypeStruct((CH, T), F32),
            jax.ShapeDtypeStruct((CH, T), BF16),
            jax.ShapeDtypeStruct((CH, STATE), F32),
        ),
        scratch_shapes=[pltpu.VMEM((T + 16, D), BF16), pltpu.VMEM((2, T + 16, BLK), F32)],
        compiler_params=params(),
        cost_estimate=cost(2 * T * D * CH, 10 * 2**20, T * CH),
    )(before, normed, w_x, conv_w, cum, logd, bmat)


def intra_kernel(grad_y, dyt, xgt, cum, bmat, cmat, tie, dxg, rc, dbc, gram, dgram):
    del tie
    step = pl.program_id(0)

    @pl.when(step == 0)
    def _():
        gram[...] = wide(nt, cmat[...], bmat[...]) * SCALE
        dgram[...] = jnp.zeros((T, T), F32)

    half = T // 2
    row = lax.broadcasted_iota(jnp.int32, (half, half), 0)
    col = lax.broadcasted_iota(jnp.int32, (half, half), 1)
    keep = row >= col
    blank = jnp.zeros((HEAD_DIM, T), BF16)
    corner = jnp.zeros((half, half), BF16)
    for q in range(BLK // HEAD_DIM):
        head = pl.ds(step * (BLK // HEAD_DIM) + q, 1)
        rows = slice(64 * q, 64 * q + 64)
        cums = cum[head, :]
        column = jnp.broadcast_to(cums, (half, T)).T
        l00 = jnp.exp(jnp.where(keep, column[:half] - cums[:, :half], -1e30))
        l10 = jnp.exp(column[half:] - cums[:, :half])
        l11 = jnp.exp(jnp.where(keep, column[half:] - cums[:, half:], -1e30))
        m00 = (l00 * gram[:half, :half]).astype(BF16)
        m10 = (l10 * gram[half:, :half]).astype(BF16)
        m11 = (l11 * gram[half:, half:]).astype(BF16)
        mat = jnp.concatenate(
            [jnp.concatenate([m00, corner], axis=1), jnp.concatenate([m10, m11], axis=1)], axis=0
        )
        dy = dyt[rows, :]
        xg = xgt[rows, :]
        pair = slice(128 * (q // 2), 128 * (q // 2) + 128)
        right = jnp.concatenate([xg, blank] if q % 2 == 0 else [blank, xg], axis=0)
        dm0 = nn(grad_y[:, pair], right[:, :half])
        dm1 = nn(grad_y[half:, pair], right[:, half:])
        dgram[:half, :half] += l00 * dm0[:half]
        dgram[half:, :half] += l10 * dm0[half:]
        dgram[half:, half:] += l11 * dm1
        back = nn(dy, mat)
        yin = nt(xg, mat)
        dxg[rows, :] = back
        rc[head, :] = jnp.sum(dy.astype(F32) * yin - xg.astype(F32) * back, axis=0, keepdims=True)

    @pl.when(step == NBLK - 1)
    def _():
        dg = (dgram[...] * SCALE).astype(BF16)
        dbc[:STATE, :] = nn(cmat[...].T.astype(BF16), dg)
        dbc[STATE:, :] = nn(dg, bmat[...].astype(BF16)).T


def intra(grad_y, dyt, xgt, cum, bmat, cmat, tie):
    rows = pl.BlockSpec((BLK, T), lambda i: (i, 0))
    return pl.pallas_call(
        intra_kernel,
        grid=(NBLK,),
        in_specs=[
            pl.BlockSpec((T, BLK), lambda i: (0, i)),
            rows,
            rows,
            whole(HEADS, T),
            whole(T, STATE),
            whole(T, STATE),
            pl.BlockSpec(memory_space=pl.ANY),
        ],
        out_specs=(rows, whole(HEADS, T), whole(2 * STATE, T)),
        out_shape=(
            jax.ShapeDtypeStruct((CH, T), F32),
            jax.ShapeDtypeStruct((HEADS, T), F32),
            jax.ShapeDtypeStruct((2 * STATE, T), F32),
        ),
        scratch_shapes=[pltpu.VMEM((T, T), F32), pltpu.VMEM((T, T), F32)],
        compiler_params=params(),
        cost_estimate=cost(HEADS * 2 * T * T * 64 * 8, 4 * 2**20, HEADS * T * T),
    )(grad_y, dyt, xgt, cum, bmat, cmat, tie)


def grad_kernel(
    skip, back, bmat, dxg, dyt, xgt, xwt, sgt, taps, cum, logd, tie, dpre, halo, halves, cross, dbt, ext
):
    del tie
    step = pl.program_id(0)

    @pl.when(step == 0)
    def _():
        dbt[...] = jnp.zeros((STATE, T), F32)

    own = back[...]
    later = wide(nt, own, bmat[...])
    dbt[...] += nn(own.T.astype(BF16), xwt[...])
    parts = []
    for q in range(BLK // HEAD_DIM):
        index = step * (BLK // HEAD_DIM) + q
        head = pl.ds(index, 1)
        rows = slice(64 * q, 64 * q + 64)
        gain = jnp.sqrt(-2.0 * logd[head, :])
        cums = cum[head, :]
        tail = jnp.exp(cums[:, T - 1 :] - cums)
        inter = later[rows] * tail
        whole_dxg = dxg[rows, :] + inter
        xg = xgt[rows, :].astype(F32)
        cross[head, :] = jnp.sum(xg * inter, axis=0, keepdims=True)
        halves[head, :] = 0.5 * jnp.sum(xg * whole_dxg, axis=0, keepdims=True)
        d_x = gain * whole_dxg + skip[index] * dyt[rows, :].astype(F32)
        parts.append(d_x * sgt[rows, :])
    ext[:8, :] = jnp.zeros((8, BLK), F32)
    ext[8 : T + 8, :] = jnp.concatenate(parts, axis=0).T
    ext[T + 8 :, :] = jnp.zeros((8, BLK), F32)
    total = taps[0:1, :] * ext[8 : T + 8, :]
    edge = taps[0:1, :] * ext[:8, :]
    for tap in range(1, CONV):
        weight = taps[tap : tap + 1, :]
        total = total + weight * ext[8 + tap : T + 8 + tap, :]
        edge = edge + weight * ext[tap : 8 + tap, :]
    dpre[...] = total.astype(BF16)
    halo[...] = edge


def gradients(skip, back, bmat, dxg, dyt, xgt, xwt, sgt, taps, cum, logd, tie):
    rows = pl.BlockSpec((BLK, T), lambda i: (i, 0))
    return pl.pallas_call(
        grad_kernel,
        grid=(NBLK,),
        in_specs=[
            pl.BlockSpec(memory_space=pltpu.SMEM),
            pl.BlockSpec((BLK, STATE), lambda i: (i, 0)),
            whole(T, STATE),
            rows,
            rows,
            rows,
            rows,
            rows,
            pl.BlockSpec((CONV, BLK), lambda i: (0, i)),
            whole(HEADS, T),
            whole(HEADS, T),
            pl.BlockSpec(memory_space=pl.ANY),
        ],
        out_specs=(
            pl.BlockSpec((T, BLK), lambda i: (0, i)),
            pl.BlockSpec((8, BLK), lambda i: (0, i)),
            whole(HEADS, T),
            whole(HEADS, T),
            whole(STATE, T),
        ),
        out_shape=(
            jax.ShapeDtypeStruct((T, CH), BF16),
            jax.ShapeDtypeStruct((8, CH), F32),
            jax.ShapeDtypeStruct((HEADS, T), F32),
            jax.ShapeDtypeStruct((HEADS, T), F32),
            jax.ShapeDtypeStruct((STATE, T), F32),
        ),
        scratch_shapes=[pltpu.VMEM((T + 16, BLK), F32)],
        compiler_params=params(),
        cost_estimate=cost(4 * CH * T * 128, 6 * 2**20, T * HEADS),
    )(skip, back, bmat, dxg, dyt, xgt, xwt, sgt, taps, cum, logd, tie)


def state_kernel(
    fore, back, cmat, dyt, dywt, cum, logd, rc, halves, cross, dbt, dbc, gls, shared
):
    state = fore[...]
    before = wide(nt, state, cmat[...])
    dct = nn(state.T.astype(BF16), dywt[...])
    cums = cum[...]
    inner = []
    through = []
    for h in range(HEADS):
        rows = slice(64 * h, 64 * h + 64)
        inner.append(jnp.sum(dyt[rows, :].astype(F32) * before[rows], axis=0, keepdims=True))
        both = jnp.sum(fore[rows, :] * back[rows, :], axis=0, keepdims=True)
        through.append(jnp.sum(both, axis=1, keepdims=True))
    arriving = rc[...] + jnp.exp(cums) * SCALE * jnp.concatenate(inner, axis=0)
    later = jnp.dot(arriving, triangle(False), precision=HIGH, preferred_element_type=F32)
    crossing = cross[...]
    earlier = (
        jnp.dot(crossing, triangle(True), precision=HIGH, preferred_element_type=F32) - crossing
    )
    kept = jnp.exp(cums[:, T - 1 :]) * jnp.concatenate(through, axis=0)
    gls[...] = logd[...] * (later + earlier + kept) + halves[...]
    total = dbc[...] + jnp.concatenate([dbt[...], dct], axis=0)
    shared[...] = total.T.astype(BF16)


def states(fore, back, cmat, dyt, dywt, cum, logd, rc, halves, cross, dbt, dbc):
    vm = pl.BlockSpec(memory_space=pltpu.VMEM)
    return pl.pallas_call(
        state_kernel,
        in_specs=[vm] * 12,
        out_shape=(
            jax.ShapeDtypeStruct((HEADS, T), F32),
            jax.ShapeDtypeStruct((T, 2 * STATE), BF16),
        ),
        compiler_params=params(),
        cost_estimate=cost(4 * CH * T * 128, 4 * 2**20),
    )(fore, back, cmat, dyt, dywt, cum, logd, rc, halves, cross, dbt, dbc)


def select_kernel(order, normed, tie, mine, other, flip):
    del tie
    for k in range(D // 128):
        cols = slice(128 * k, 128 * k + 128)
        flip[cols, :] = normed[:, cols].astype(F32).T.astype(BF16)
    for k in range(16):
        rows = slice(ROWS * k, ROWS * (k + 1))
        mine[rows, :] = flip[pl.ds(pl.multiple_of(order[k] * ROWS, 16), ROWS), :]
        other[rows, :] = flip[pl.ds(pl.multiple_of(order[16 + k] * ROWS, 16), ROWS), :]


def select(order, normed, tie):
    vm = pl.BlockSpec(memory_space=pltpu.VMEM)
    return pl.pallas_call(
        select_kernel,
        in_specs=[pl.BlockSpec(memory_space=pltpu.SMEM), vm, pl.BlockSpec(memory_space=pl.ANY)],
        out_shape=(jax.ShapeDtypeStruct((CH, T), BF16), jax.ShapeDtypeStruct((CH, T), BF16)),
        scratch_shapes=[pltpu.VMEM((D, T), BF16)],
        compiler_params=params(),
        cost_estimate=cost(10**6, 3 * 2**20),
    )(order, normed, tie)


PART = [slice(320 * r, 320 * (r + 1)) for r in range(4)]
WIDE = 640
FULL = WIDE + STATE
MAIN = [slice(0, WIDE), slice(WIDE, 2 * WIDE)]
EXTRA = [slice(0, STATE), slice(STATE, 2 * STATE)]


def mended(grad, halo, cols):
    edge = jnp.concatenate([jnp.zeros((8, WIDE), F32), halo[:, cols]], axis=0)
    return grad[: T - 16, cols], (grad[T - 16 :, cols].astype(F32) + edge).astype(BF16)


def product(refs, side):
    mine, other, grad, grad_other, halo, halo_other, shared, shared_other = refs
    cols = MAIN[side]
    right = jnp.concatenate(
        mended(grad, halo, cols) + mended(grad_other, halo_other, cols), axis=0
    )
    extra = jnp.concatenate([shared[:, EXTRA[side]], shared_other[:, EXTRA[side]]], axis=0)

    def rows(part):
        left = jnp.concatenate([mine[PART[part], :], other[PART[part], :]], axis=1)
        return nn(left, right), nn(left, extra)

    return rows


def up_kernel(*refs):
    up = refs[8]
    for at, (part, side) in enumerate(((2, 0), (1, 1))):
        main, extra = product(refs[:8], side)(part)
        up[PART[at], :WIDE] = main.astype(BF16)
        up[PART[at], WIDE:] = extra.astype(BF16)


def down_kernel(*refs):
    down = refs[9]
    for at, (part, side) in enumerate(((2, 1), (3, 0))):
        main, extra = product(refs[:8], side)(part)
        down[PART[at], :WIDE] = main.astype(BF16)
        down[PART[at], WIDE:] = extra.astype(BF16)


def keep_kernel(*refs):
    for out, (part, side) in zip(refs[9:], ((1, 0), (3, 1), (0, 0), (0, 1))):
        main, extra = product(refs[:8], side)(part)
        out[:, :WIDE] = main
        out[:, WIDE:] = extra


def up_part(args):
    return pl.pallas_call(
        up_kernel,
        out_shape=jax.ShapeDtypeStruct((640, FULL), BF16),
        compiler_params=params(),
        cost_estimate=cost(2 * 512 * FULL * 640, 4 * 2**20),
    )(*args)


def down_part(args, tie):
    vm = pl.BlockSpec(memory_space=pltpu.VMEM)
    return pl.pallas_call(
        down_kernel,
        in_specs=[vm] * 8 + [pl.BlockSpec(memory_space=pl.ANY)],
        out_shape=jax.ShapeDtypeStruct((640, FULL), BF16),
        compiler_params=params(),
        cost_estimate=cost(2 * 512 * FULL * 640, 4 * 2**20),
    )(*args, tie)


def keep_part(args, tie):
    vm = pl.BlockSpec(memory_space=pltpu.VMEM)
    one = jax.ShapeDtypeStruct((320, FULL), F32)
    return pl.pallas_call(
        keep_kernel,
        in_specs=[vm] * 8 + [pl.BlockSpec(memory_space=pl.ANY)],
        out_shape=(one,) * 4,
        compiler_params=params(),
        cost_estimate=cost(2 * 512 * FULL * 1280, 8 * 2**20),
    )(*args, tie)


def input_kernel(w_x, w_bc, grad, halo, shared, tie, out):
    del tie
    edge = jnp.concatenate([jnp.zeros((8, CH), F32), halo[...]], axis=0)
    last = (grad[T - 16 :, :].astype(F32) + edge).astype(BF16)
    right = jnp.concatenate([grad[: T - 16, :], last], axis=0)
    out[...] = (nt(w_x[...], right) + nt(w_bc[...], shared[...])).astype(BF16)


def input_part(w_x, w_bc, grad, halo, shared, tie):
    rows = D // ZS
    return pl.pallas_call(
        input_kernel,
        grid=(ZS,),
        in_specs=[
            pl.BlockSpec((rows, CH), lambda i: (i, 0)),
            pl.BlockSpec((rows, 2 * STATE), lambda i: (i, 0)),
            whole(T, CH),
            whole(8, CH),
            whole(T, 2 * STATE),
            pl.BlockSpec(memory_space=pl.ANY),
        ],
        out_specs=pl.BlockSpec((rows, T), lambda i: (i, 0)),
        out_shape=jax.ShapeDtypeStruct((D, T), BF16),
        compiler_params=params(),
        cost_estimate=cost(2 * D * (CH + 256) * T, 10 * 2**20),
    )(w_x, w_bc, grad, halo, shared, tie)


def device(x, y, core):
    return ((x % 4) * 4 + y % 4) * 2 + core


def ring(first, by):
    pairs = []
    for x in range(4):
        for y in range(4):
            for core in range(2):
                along_x = (core == 0) == first
                goal = device(x + by, y, core) if along_x else device(x, y + by, core)
                pairs.append((device(x, y, core), goal))
    return pairs


def along(first, by):
    return lambda value: lax.ppermute(value, "seq", ring(first, by))


def ring_sum(move, up1, down1, near_up, near_down, here_a, here_b, size):
    from_up = move(1)(up1)
    from_down = move(-1)(down1)
    up2 = (near_up + from_up[:size].astype(F32)).astype(BF16)
    down2 = (near_down + from_down[:size].astype(F32)).astype(BF16)
    last_up = move(1)(up2)
    last_down = move(-1)(down2)
    total_a = here_a + from_down[size:].astype(F32) + last_up.astype(F32)
    total_b = here_b + from_up[size:].astype(F32) + last_down.astype(F32)
    return total_a, total_b


def place_table():
    rows = []
    for place in range(SEQ):
        core, y, x = place % 2, place // 2 % 4, place // 8
        blocks = [
            [device(x + a, y + b, 0) for a in range(4) for b in range(4)],
            [device(x + b, y + a, 1) for a in range(4) for b in range(4)],
        ]
        head = SLICE * place // HEAD_DIM
        bound = HEAD_DIM * (head + 1) - SLICE * place
        rows.append(blocks[core] + blocks[1 - core] + [head, bound])
    return np.array(rows, np.int32)


def body(normed, w_x, w_bc, conv_w, decay_code, step, d_skip, grad_y):
    place = lax.axis_index("seq")
    core = place % 2
    table = lax.dynamic_index_in_dim(jnp.asarray(place_table()), place, 0, keepdims=False)
    swap = [(i, i ^ 1) for i in range(SEQ)]

    low = math.log(0.995)
    high = math.log(0.9999)
    rates = low + decay_code.astype(F32)[:, None] / (LEVELS - 1) * (high - low)
    before = lax.ppermute(normed[T - 16 :], "seq", [(i, i + 1) for i in range(SEQ - 1)])

    bmat, cmat, cum, logd, dyt, dywt, msg = front(normed, w_bc, rates, step, grad_y)
    pulls = lax.all_to_all(msg, "seq", 0, 0)
    xgt, sgt, xwt, own = channels(before, normed, w_x, conv_w, cum, logd, bmat)
    ahead = lax.all_to_all(own.reshape(SEQ, SLICE, STATE), "seq", 0, 0)
    back_parts = chain(table, pulls, pulls, own, True)
    back = lax.all_to_all(back_parts, "seq", 0, 0).reshape(CH, STATE)
    dxg, rc, dbc = intra(grad_y, dyt, xgt, cum, bmat, cmat, back_parts)
    fore_parts = chain(table, ahead, pulls, rc, False)
    fore = lax.all_to_all(fore_parts, "seq", 0, 0).reshape(CH, STATE)

    dpre, halo, halves, cross, dbt = gradients(
        d_skip, back, bmat, dxg, dyt, xgt, xwt, sgt, conv_w, cum, logd, fore_parts
    )
    dpre_other = lax.ppermute(dpre, "seq", swap)
    halo_mine = lax.ppermute(halo, "seq", [(i, i - 1) for i in range(1, SEQ)])
    halo_pair = lax.ppermute(halo, "seq", [(i, i - 2) for i in range(2, SEQ, 2)])
    halo_other = jnp.where(core == 0, halo_pair, halo)
    mine, other = select(table, normed, dpre)
    other = lax.ppermute(other, "seq", swap)
    gls, shared = states(fore, back, cmat, dyt, dywt, cum, logd, rc, halves, cross, dbt, dbc)
    shared_other = lax.ppermute(shared, "seq", swap)

    args = (mine, other, dpre, dpre_other, halo_mine, halo_other, shared, shared_other)
    up1 = up_part(args)
    down1 = down_part(args, up1)
    near_up, near_down, here_a, here_b = keep_part(args, down1)
    part = input_part(w_x, w_bc, dpre, halo_mine, shared, here_a)
    grad_u = lax.psum_scatter(part, "head", scatter_dimension=0, tiled=True)
    sum_a, sum_b = ring_sum(
        lambda by: along(True, by), up1, down1, near_up, near_down, here_a, here_b, 320
    )
    a4 = sum_a.reshape(4, ROWS, FULL)
    b4 = sum_b.reshape(4, ROWS, FULL)
    up1 = jnp.concatenate([a4[2], b4[1]], axis=0).astype(BF16)
    down1 = jnp.concatenate([b4[2], a4[3]], axis=0).astype(BF16)
    sum_a, sum_b = ring_sum(
        lambda by: along(False, by), up1, down1, a4[1], b4[3], a4[0], b4[0], ROWS
    )
    norm = (T * SEQ) ** (-0.5)
    grad_wx = jnp.concatenate([sum_a[:, :WIDE], sum_b[:, :WIDE]], axis=1) * norm
    grad_wbc = jnp.concatenate([sum_a[:, WIDE:], sum_b[:, WIDE:]], axis=1) * norm
    for bit in (1, 2):
        pairs = [(i, i ^ bit) for i in range(ZS)]
        grad_wbc = grad_wbc + lax.ppermute(grad_wbc, "head", pairs)
    return (grad_u, grad_wx, grad_wbc, gls)


def solution(mesh):
    return jax.shard_map(
        body,
        mesh=mesh,
        in_specs=(
            P("seq", None),
            P(None, "head"),
            P(),
            P(None, "head"),
            P("head"),
            P("head", "seq"),
            P("head"),
            P("seq", "head"),
        ),
        out_specs=(P("head", "seq"), P("seq", "head"), P("seq", None), P("head", "seq")),
        check_vma=False,
    )
```

time: 1300 us -> 187 us (0.14)
  waiting for transfers between devices: 645 us -> 49.5 us
  starting transfers between devices: 419 us -> 53.4 us
  other arithmetic: 113 us -> 6.52 us
  Pallas kernels: 0 us -> 55.6 us
  matrix products: 49.9 us -> 0 us
  local copies, waits for them, and re-layouts: 35 us -> 5.52 us
  blocking collectives: 21.1 us -> 0 us
    ppermute x64 -> x16, starting transfers between devices: 419 us -> 23.6 us  [the longest x8 11.5 us: along(): return lambda value: lax.ppermute(value, 'seq', ring(first, by))]
    ppermute x64 -> x16, waiting for transfers between devices: 420 us -> 36.7 us  [the longest x8 30.9 us: along(): return lambda value: lax.ppermute(value, 'seq', ring(first, by))]
    unnamed x5 -> x1, waiting for transfers between devices: 191 us -> 0.02 us
    add x63 -> x5, other arithmetic: 98.8 us -> 1.43 us  [the longest x1 0.66 us: body(): rates = low + decay_code.astype(F32)[:, None] / (LEVELS - 1) * (high - low)]
    pallas_call x0 -> x12, Pallas kernels: none -> 55.6 us  [the longest x1 8.95 us: channels(): pl.pallas_call(channel_kernel, grid=(NBLK + 1,), in_specs=[whole(16, D),...]
    dot_general x17 -> x0, matrix products: 49.9 us -> none  [the longest x2 13.8 us: group_pass(): y_intra = jnp.einsum('hij,jhp->ihp', lmat * gram[None], xg, precision=HIGH)]
    reduce_scatter x1, waiting for transfers between devices: 34.4 us -> 0.01 us  [body(): grad_u = lax.psum_scatter(part, 'head', scatter_dimension=0, tiled=True)]
    all_to_all x0 -> x4, starting transfers between devices: none -> 29.8 us  [the longest x1 14.1 us: body(): ahead = lax.all_to_all(own.reshape(SEQ, SLICE, STATE), 'seq', 0, 0)]
  transfers between devices with their start and end apart: 67 -> 21, of which waited for: 66 -> 14; matrix products, arithmetic and copies ran while one was open for 4% -> 4% of each run, Pallas kernels for 0% -> 26%
where the time goes in v1:
time: 187 us; the launch traced here: 185 us
  Pallas kernels  55.6 us (30%)
  starting transfers between devices  53.4 us (29%)
  waiting for transfers between devices  49.5 us (26%)
  between operations  14.3 us (8%)
  other arithmetic  6.52 us (3%)
  local copies, waits for them, and re-layouts  5.52 us (3%)
    ppermute x8, waiting for transfers between devices, along(): return lambda value: lax.ppermute(value, 'seq', ring(first, by))  30.9 us
    all_to_all x1, starting transfers between devices, body(): ahead = lax.all_to_all(own.reshape(SEQ, SLICE, STATE), 'seq', 0, 0)  14.1 us
    ppermute x8, starting transfers between devices, along(): return lambda value: lax.ppermute(value, 'seq', ring(first, by))  11.5 us
    all_to_all x1, waiting for transfers between devices, body(): ahead = lax.all_to_all(own.reshape(SEQ, SLICE, STATE), 'seq', 0, 0)  8.95 us
    pallas_call x1, Pallas kernels, channels(): pl.pallas_call(channel_kernel, grid=(NBLK + 1,), in_specs=[whole(16, D),...  8.95 us
    all_to_all x1, starting transfers between devices, body(): pulls = lax.all_to_all(msg, 'seq', 0, 0)  7.41 us
    pallas_call x1, Pallas kernels, intra(): pl.pallas_call(intra_kernel, grid=(NBLK,), in_specs=[pl.BlockSpec((T, BLK...  6.58 us
    pallas_call x1, Pallas kernels, input_part(): pl.pallas_call(input_kernel, grid=(ZS,), in_specs=[pl.BlockSpec((rows, CH...  6.34 us
  transfers between devices with their start and end apart: 21, of which 14 were waited for; matrix products, arithmetic and copies ran while one was open for 4% of the time, Pallas kernels for 26%

profile of v1, /device:TPU:0, one launch (start us, length us, event | category | flops | bytes accessed | tf_op | source)
XLA Modules:
  0.0 184.9 jit_solution(10636044117925489328)
XLA Ops:
  7.2 0.7 add_bitcast_fusion
  7.8 0.7 copy.13.rates
  8.5 4.5 %shard_map.120 = (f32[256,128]{1,0:T(8,128)}, f32[256,128]{1,0:T(8,128)}, f32[20,256]{1,0:T(8,128)}, f32[20,256]{1,0:T(8,128)}, bf16[1280,256]{1,0:T(8,128)(2,1)...) custom-call(bf16[256,2560]{1,0:T(8,128)(2,1)} %normed.5, bf16[2560,256]{1,0:T(8,128)(2,1)} %w_bc.3, ...), custom_call_target="tpu_custom_call" | custom-call | flops 587202560 | bytes 6291456 | tf_op jit(solution)/shard_map/pallas_call | solution.py:106
  13.1 7.4 %all-to-all-start = ((f32[32,48,128]{2,1,0:T(8,128)}), f32[32,48,128]{2,1,0:T(8,128)S(1)}, u32[]{:S(2)}, u32[]{:S(2)}) async-start(f32[32,48,128]{2,1,0:T(8,128)} %get-tuple-element.31), calls=%async_computation | async-start | bytes 1572864 | tf_op jit(solution)/shard_map/all_to_all | solution.py:603
  20.5 0.9 slice.75
  21.4 2.2 %collective-permute-start = (bf16[16,2560]{1,0:T(8,128)(2,1)S(1)}, bf16[16,2560]{1,0:T(8,128)(2,1)S(1)}, u32[]{:S(2)}, u32[]{:S(2)}) collective-permute-start(bf16[16,2560]{1,0:T(8,128)(2,1)S(1)} %slice.75), channel_id=1, source_target_pairs={{0,4},{4,8},{8,12},{12,16},{16,20},{20,24},{24,28},{28,32},{32,36}... | collective-permute-start | bytes 245768 | tf_op jit(solution)/shard_map/ppermute | solution.py:600
  23.6 0.9 collective-permute-done.before
  25.1 8.9 %shard_map.121 = (bf16[1280,256]{1,0:T(8,128)(2,1)}, f32[1280,256]{1,0:T(8,128)}, bf16[1280,256]{1,0:T(8,128)(2,1)}, f32[1280,128]{1,0:T(8,128)}) custom-call(bf16[16,2560]{1,0:T(8,128)(2,1)} %copy-done.12, bf16[256,2560]{1,0:T(8,128)(2,1)} %normed.5, bf16[2560,1280]{1,0:T(8,128)(2,1)} %w_x.3, f32[4,1280]{1,0:T(4,128)} %taps.1, ...), custom_call_target="tpu_custom_call" | custom-call | flops 1677721600 | bytes 10485760 | tf_op jit(solution)/shard_map/pallas_call | solution.py:192
  34.3 14.1 %all-to-all-start.2 = ((f32[32,40,128]{2,1,0:T(8,128)}), f32[32,40,128]{2,1,0:T(8,128)S(1)}, u32[]{:S(2)}, u32[]{:S(2)}) async-start(f32[32,40,128]{2,1,0:T(8,128)} %bitcast.10), calls=%async_computation.2 | async-start | bytes 1310720 | tf_op jit(solution)/shard_map/all_to_all | solution.py:605
  48.5 1.2 dynamic-slice_bitcast_fusion.table.order
  49.7 2.4 %shard_map.122.tie = f32[32,40,128]{2,1,0:T(8,128)} custom-call(s32[34]{0:T(128)} %dynamic-slice_bitcast_fusion.table.order, f32[32,48,128]{2,1,0:T(8,128)} %copy-done.1, f32[32,48,128]{2,1,0:T(8,128)} %copy-done.1, f32[1280,128]{1,0:T(8,128)} %get-tuple-element.35.tie), custom_call_target="tpu_custom_call" | custom-call | flops 1000000 | bytes 2097152 | tf_op jit(solution)/shard_map/pallas_call | solution.py:137
  52.0 8.9 %all-to-all-done.2.recv = f32[32,40,128]{2,1,0:T(8,128)S(1)} async-done(((f32[32,40,128]{2,1,0:T(8,128)}), f32[32,40,128]{2,1,0:T(8,128)S(1)}, u32[]{:S(2)}, u32[]{:S(2)}) %all-to-all-start.2) | async-done | bytes 655392 | tf_op jit(solution)/shard_map/all_to_all | solution.py:605
  61.0 4.1 %all-to-all-start.1 = ((f32[32,40,128]{2,1,0:T(8,128)}), f32[32,40,128]{2,1,0:T(8,128)S(1)}, u32[]{:S(2)}, u32[]{:S(2)}) async-start(f32[32,40,128]{2,1,0:T(8,128)} %shard_map.122.tie), calls=%async_computation.1 | async-start | bytes 1310720 | tf_op jit(solution)/shard_map/all_to_all | solution.py:607
  65.1 6.6 %shard_map.123 = (f32[1280,256]{1,0:T(8,128)}, f32[20,256]{1,0:T(8,128)}, f32[256,256]{1,0:T(8,128)}) custom-call(bf16[256,1280]{1,0:T(8,128)(2,1)} %grad_y.3, bf16[1280,256]{1,0:T(8,128)(2,1)} %get-tuple-element.36.dyt, bf16[1280,256]{1,0:T(8,128)(2,1)} %get-tuple-element.37.xgt, f32[20,256]{1,0:T(8,128)} %get-tuple-element.32.cum, ...), custom_call_target="tpu_custom_call" | custom-call | flops 1342177280 | bytes 4194304 | tf_op jit(solution)/shard_map/pallas_call | solution.py:269
  71.7 2.4 %shard_map.124.tie = f32[32,40,128]{2,1,0:T(8,128)} custom-call(s32[34]{0:T(128)} %dynamic-slice_bitcast_fusion.table.order, f32[32,40,128]{2,1,0:T(8,128)} %copy-done.6, f32[32,48,128]{2,1,0:T(8,128)} %copy-done.1, f32[20,256]{1,0:T(8,128)} %get-tuple-element.42.tie.rc), custom_call_target="tpu_custom_call" | custom-call | flops 1000000 | bytes 2097152 | tf_op jit(solution)/shard_map/pallas_call | solution.py:137
  74.1 3.5 %all-to-all-done.1 = f32[32,40,128]{2,1,0:T(8,128)S(1)} async-done(((f32[32,40,128]{2,1,0:T(8,128)}), f32[32,40,128]{2,1,0:T(8,128)S(1)}, u32[]{:S(2)}, u32[]{:S(2)}) %all-to-all-start.1) | async-done | bytes 655392 | tf_op jit(solution)/shard_map/all_to_all | solution.py:607
  77.6 4.1 %all-to-all-start.3 = ((f32[32,40,128]{2,1,0:T(8,128)}), f32[32,40,128]{2,1,0:T(8,128)S(1)}, u32[]{:S(2)}, u32[]{:S(2)}) async-start(f32[32,40,128]{2,1,0:T(8,128)} %shard_map.124.tie), calls=%async_computation.3 | async-start | bytes 1310720 | tf_op jit(solution)/shard_map/all_to_all | solution.py:610
  81.8 6.3 %shard_map.125 = (bf16[256,1280]{1,0:T(8,128)(2,1)}, f32[8,1280]{1,0:T(8,128)}, f32[20,256]{1,0:T(8,128)}, f32[20,256]{1,0:T(8,128)}, f32[128,256]{1,0:T(8,128)}) custom-call(f32[20]{0:T(128)} %skip.1, f32[1280,128]{1,0:T(8,128)} %bitcast.7, f32[256,128]{1,0:T(8,128)} %get-tuple-element.34.bmat, f32[1280,256]{1,0:T(8,128)} %get-tuple-element.39.dxg, ...), custom_call_target="tpu_custom_call" | custom-call | flops 167772160 | bytes 6291456 | tf_op jit(solution)/shard_map/pallas_call | solution.py:336
  88.2 3.0 %shard_map.127 = (bf16[1280,256]{1,0:T(8,128)(2,1)}, bf16[1280,256]{1,0:T(8,128)(2,1)}) custom-call(s32[34]{0:T(128)} %dynamic-slice_bitcast_fusion.table.order, bf16[256,2560]{1,0:T(8,128)(2,1)} %normed.5, bf16[256,1280]{1,0:T(8,128)(2,1)} %get-tuple-element.43.tie.refs_2_.grad), custom_call_target="tpu_custom_call" | custom-call | flops 1000000 | bytes 3145728 | tf_op jit(solution)/shard_map/pallas_call | solution.py:426
  91.7 1.3 collective-permute-start.4
  93.0 1.3 collective-permute-start.1
  94.3 0.8 copy-done.7
  95.1 3.7 %shard_map.126 = (f32[20,256]{1,0:T(8,128)}, bf16[256,256]{1,0:T(8,128)(2,1)}) custom-call(f32[1280,128]{1,0:T(8,128)} %bitcast.9, f32[1280,128]{1,0:T(8,128)} %bitcast.8, f32[256,128]{1,0:T(8,128)} %get-tuple-element.38.cmat, bf16[1280,256]{1,0:T(8,128)(2,1)} %get-tuple-element.36.dyt, bf16[1280,256]{1,0:T(8,128)(2,1)} %get-tuple-element.45.dywt, ...), custom_call_target="tpu_custom_call" | custom-call | flops 167772160 | bytes 4194304 | tf_op jit(solution)/shard_map/pallas_call | solution.py:401
  98.9 1.1 collective-permute-start.5
  102.3 3.6 %shard_map.128.refs_8_ = bf16[640,768]{1,0:T(8,128)(2,1)} custom-call(bf16[1280,256]{1,0:T(8,128)(2,1)} %get-tuple-element.51.refs_0_, bf16[1280,256]{1,0:T(8,128)(2,1)} %copy-done.3, bf16[256,1280]{1,0:T(8,128)(2,1)} %get-tuple-element.43.tie.refs_2_.grad, bf16[256,1280]{1,0:T(8,128)(2,1)} %copy-done.4, f32[8,1280]{1,0:T(8,128)} %copy-done.11, ...), custom_call_target="tpu_custom_call" | custom-call | flops 503316480 | bytes 4194304 | tf_op jit(solution)/shard_map/pallas_call | solution.py:487
  105.9 5.1 %collective-permute-start.7 = (bf16[640,768]{1,0:T(8,128)(2,1)}, bf16[640,768]{1,0:T(8,128)(2,1)S(1)}, u32[]{:S(2)}, u32[]{:S(2)}) collective-permute-start(bf16[640,768]{1,0:T(8,128)(2,1)} %shard_map.128.refs_8_), channel_id=1, source_target_pairs={{0,32},{4,12},{8,40},{12,20},{16,48},{20,28},{24,56},{28,4},{32,64... | collective-permute-start | bytes 2949128 | tf_op jit(solution)/shard_map/ppermute | solution.py:562
  111.0 3.6 %shard_map.129.refs_8_ = bf16[640,768]{1,0:T(8,128)(2,1)} custom-call(bf16[1280,256]{1,0:T(8,128)(2,1)} %get-tuple-element.51.refs_0_, bf16[1280,256]{1,0:T(8,128)(2,1)} %copy-done.3, bf16[256,1280]{1,0:T(8,128)(2,1)} %get-tuple-element.43.tie.refs_2_.grad, bf16[256,1280]{1,0:T(8,128)(2,1)} %copy-done.4, f32[8,1280]{1,0:T(8,128)} %copy-done.11, ...), custom_call_target="tpu_custom_call" | custom-call | flops 503316480 | bytes 4194304 | tf_op jit(solution)/shard_map/pallas_call | solution.py:497
  114.6 1.5 collective-permute-start.6
  116.1 4.3 %shard_map.130 = (f32[320,768]{1,0:T(8,128)}, f32[320,768]{1,0:T(8,128)}, f32[320,768]{1,0:T(8,128)}, f32[320,768]{1,0:T(8,128)}) custom-call(bf16[1280,256]{1,0:T(8,128)(2,1)} %get-tuple-element.51.refs_0_, bf16[1280,256]{1,0:T(8,128)(2,1)} %copy-done.3, bf16[256,1280]{1,0:T(8,128)(2,1)} %get-tuple-element.43.tie.refs_2_.grad, bf16[256,1280]{1,0:T(8,128)(2,1)} %copy-done.4, ...), custom_call_target="tpu_custom_call" | custom-call | flops 1006632960 | bytes 8388608 | tf_op jit(solution)/shard_map/pallas_call | solution.py:509
  120.4 4.4 %collective-permute-done.7 = bf16[640,768]{1,0:T(8,128)(2,1)S(1)} collective-permute-done((bf16[640,768]{1,0:T(8,128)(2,1)}, bf16[640,768]{1,0:T(8,128)(2,1)S(1)}, u32[]{:S(2)}, u32[]{:S(2)}) %collective-permute-start.7) | collective-permute-done | bytes 983072 | tf_op jit(solution)/shard_map/ppermute | solution.py:562
  124.8 1.3 add_convert_fusion.1
  126.7 2.2 %collective-permute-done.6 = bf16[640,768]{1,0:T(8,128)(2,1)S(1)} collective-permute-done((bf16[640,768]{1,0:T(8,128)(2,1)}, bf16[640,768]{1,0:T(8,128)(2,1)S(1)}, u32[]{:S(2)}, u32[]{:S(2)}) %collective-permute-start.6) | collective-permute-done | bytes 983072 | tf_op jit(solution)/shard_map/ppermute | solution.py:562
  128.9 7.3 %collective-permute-done.8 = bf16[320,768]{1,0:T(8,128)(2,1)S(1)} collective-permute-done((bf16[320,768]{1,0:T(8,128)(2,1)S(1)}, bf16[320,768]{1,0:T(8,128)(2,1)S(1)}, u32[]{:S(2)}, u32[]{:S(2)}) %collective-permute-start.8) | collective-permute-done | bytes 491552 | tf_op jit(solution)/shard_map/ppermute | solution.py:562
  136.2 1.1 fusion.6
  137.3 0.8 collective-permute-start.9
  138.2 6.3 %shard_map.131 = bf16[2560,256]{1,0:T(8,128)(2,1)} custom-call(bf16[2560,1280]{1,0:T(8,128)(2,1)} %w_x.3, bf16[2560,256]{1,0:T(8,128)(2,1)} %w_bc.3, bf16[256,1280]{1,0:T(8,128)(2,1)} %get-tuple-element.43.tie.refs_2_.grad, f32[8,1280]{1,0:T(8,128)} %copy-done.11, bf16[256,256]{1,0:T(8,128)(2,1)} %get-tuple-element.50.refs_6_.shared, ...), custom_call_target="tpu_custom_call" | custom-call | flops 2013265920 | bytes 10485760 | tf_op jit(solution)/shard_map/pallas_call | solution.py:528
  144.6 1.9 %collective-permute-done.9 = bf16[320,768]{1,0:T(8,128)(2,1)} collective-permute-done((bf16[320,768]{1,0:T(8,128)(2,1)}, bf16[320,768]{1,0:T(8,128)(2,1)}, u32[]{:S(2)}, u32[]{:S(2)}) %collective-permute-start.9) | collective-permute-done | bytes 491552 | tf_op jit(solution)/shard_map/ppermute | solution.py:562
  146.5 1.2 fusion.5
  147.8 3.3 %collective-permute-start.10 = (bf16[160,768]{1,0:T(8,128)(2,1)S(1)}, bf16[160,768]{1,0:T(8,128)(2,1)S(1)}, u32[]{:S(2)}, u32[]{:S(2)}) collective-permute-start(bf16[160,768]{1,0:T(8,128)(2,1)S(1)} %pad_maximum_fusion), channel_id=1, source_target_pairs={{0,24},{4,100},{8,0},{12,108},{16,8},{20,116},{24,16},{28,124},{32... | collective-permute-start | bytes 737288 | tf_op jit(solution)/shard_map/ppermute | solution.py:562
  151.1 4.1 %collective-permute-done.11 = bf16[160,768]{1,0:T(8,128)(2,1)S(1)} collective-permute-done((bf16[160,768]{1,0:T(8,128)(2,1)S(1)}, bf16[160,768]{1,0:T(8,128)(2,1)S(1)}, u32[]{:S(2)}, u32[]{:S(2)}) %collective-permute-start.11) | collective-permute-done | bytes 245792 | tf_op jit(solution)/shard_map/ppermute | solution.py:562
  155.3 6.1 %collective-permute-done.12 = bf16[80,768]{1,0:T(8,128)(2,1)S(1)} collective-permute-done((bf16[80,768]{1,0:T(8,128)(2,1)S(1)}, bf16[80,768]{1,0:T(8,128)(2,1)S(1)}, u32[]{:S(2)}, u32[]{:S(2)}) %collective-permute-start.12) | collective-permute-done | bytes 122912 | tf_op jit(solution)/shard_map/ppermute | solution.py:562
  161.6 4.9 %collective-permute-done.13 = bf16[80,768]{1,0:T(8,128)(2,1)S(1)} collective-permute-done((bf16[80,768]{1,0:T(8,128)(2,1)S(1)}, bf16[80,768]{1,0:T(8,128)(2,1)S(1)}, u32[]{:S(2)}, u32[]{:S(2)}) %collective-permute-start.13) | collective-permute-done | bytes 122912 | tf_op jit(solution)/shard_map/ppermute | solution.py:562
  166.5 2.0 %collective-permute-start.14 = (f32[80,256]{1,0:T(8,128)S(1)}, f32[80,256]{1,0:T(8,128)S(1)}, u32[]{:S(2)}, u32[]{:S(2)}) collective-permute-start(f32[80,256]{1,0:T(8,128)S(1)} %maximum_multiply_fusion.1), channel_id=1, source_target_pairs={{0,1},{1,0},{2,3},{3,2},{4,5},{5,4},{6,7},{7,6},{8,9},{9,8},{10,11... | collective-permute-start | bytes 245768 | tf_op jit(solution)/shard_map/ppermute | solution.py:645
  168.5 2.7 %collective-permute-done.14 = f32[80,256]{1,0:T(8,128)S(1)} collective-permute-done((f32[80,256]{1,0:T(8,128)S(1)}, f32[80,256]{1,0:T(8,128)S(1)}, u32[]{:S(2)}, u32[]{:S(2)}) %collective-permute-start.14) | collective-permute-done | bytes 81952 | tf_op jit(solution)/shard_map/ppermute | solution.py:645
  171.2 3.8 %collective-permute-start.15 = (f32[80,256]{1,0:T(8,128)S(1)}, f32[80,256]{1,0:T(8,128)S(1)}, u32[]{:S(2)}, u32[]{:S(2)}) collective-permute-start(f32[80,256]{1,0:T(8,128)S(1)} %fusion.4), channel_id=1, source_target_pairs={{0,2},{1,3},{2,0},{3,1},{4,6},{5,7},{6,4},{7,5},{8,10},{9,11},{10,... | collective-permute-start | bytes 245768 | tf_op jit(solution)/shard_map/ppermute | solution.py:645
  175.0 0.8 maximum_multiply_fusion
  175.8 1.6 collective-permute-done.15
  177.4 0.6 add.74
  (58 shorter events, 4.9 us)
Async XLA Ops:
  13.1 21.3 %all-to-all-start = ((f32[32,48,128]{2,1,0:T(8,128)}), f32[32,48,128]{2,1,0:T(8,128)S(1)}, u32[]{:S(2)}, u32[]{:S(2)}) async-start(f32[32,48,128]{2,1,0:T(8,128)} %get-tuple-element.31), calls=%async_computation | async-start | bytes 1572864 | tf_op jit(solution)/shard_map/all_to_all | solution.py:603
  21.4 3.1 %collective-permute-start = (bf16[16,2560]{1,0:T(8,128)(2,1)S(1)}, bf16[16,2560]{1,0:T(8,128)(2,1)S(1)}, u32[]{:S(2)}, u32[]{:S(2)}) collective-permute-start(bf16[16,2560]{1,0:T(8,128)(2,1)S(1)} %slice.75), channel_id=1, source_target_pairs={{0,4},{4,8},{8,12},{12,16},{16,20},{20,24},{24,28},{28,32},{32,36}... | collective-permute-start | bytes 245768 | tf_op jit(solution)/shard_map/ppermute | solution.py:600
  24.5 0.6 copy-start.12
  34.3 15.3 %copy-start.1 = (f32[32,48,128]{2,1,0:T(8,128)}, f32[32,48,128]{2,1,0:T(8,128)S(1)}, u32[]{:S(2)}) copy-start(f32[32,48,128]{2,1,0:T(8,128)S(1)} %all-to-all-done.recv.decays) | copy-start | bytes 2359300
  34.3 26.7 %all-to-all-start.2 = ((f32[32,40,128]{2,1,0:T(8,128)}), f32[32,40,128]{2,1,0:T(8,128)S(1)}, u32[]{:S(2)}, u32[]{:S(2)}) async-start(f32[32,40,128]{2,1,0:T(8,128)} %bitcast.10), calls=%async_computation.2 | async-start | bytes 1310720 | tf_op jit(solution)/shard_map/all_to_all | solution.py:605
  61.0 10.7 %copy-start.6 = (f32[32,40,128]{2,1,0:T(8,128)}, f32[32,40,128]{2,1,0:T(8,128)S(1)}, u32[]{:S(2)}) copy-start(f32[32,40,128]{2,1,0:T(8,128)S(1)} %all-to-all-done.2.recv) | copy-start | bytes 1966084
  61.0 16.7 %all-to-all-start.1 = ((f32[32,40,128]{2,1,0:T(8,128)}), f32[32,40,128]{2,1,0:T(8,128)S(1)}, u32[]{:S(2)}, u32[]{:S(2)}) async-start(f32[32,40,128]{2,1,0:T(8,128)} %shard_map.122.tie), calls=%async_computation.1 | async-start | bytes 1310720 | tf_op jit(solution)/shard_map/all_to_all | solution.py:607
  77.6 4.2 %copy-start.2 = (f32[32,40,128]{2,1,0:T(8,128)}, f32[32,40,128]{2,1,0:T(8,128)S(1)}, u32[]{:S(2)}) copy-start(f32[32,40,128]{2,1,0:T(8,128)S(1)} %all-to-all-done.1) | copy-start | bytes 1966084
  77.6 16.7 %all-to-all-start.3 = ((f32[32,40,128]{2,1,0:T(8,128)}), f32[32,40,128]{2,1,0:T(8,128)S(1)}, u32[]{:S(2)}, u32[]{:S(2)}) async-start(f32[32,40,128]{2,1,0:T(8,128)} %shard_map.124.tie), calls=%async_computation.3 | async-start | bytes 1310720 | tf_op jit(solution)/shard_map/all_to_all | solution.py:610
  81.8 96.3 %reduce-scatter.2.cloned.1.call-start = ((), (), s32[]{:S(2)}) async-start(), calls=%async_computation.5 | async-start | bytes 1638400 | tf_op jit(solution)/shard_map/reduce_scatter | solution.py:629
  88.2 3.3 %copy-start = (bf16[256,1280]{1,0:T(8,128)(2,1)S(1)}, bf16[256,1280]{1,0:T(8,128)(2,1)}, u32[]{:S(2)}) copy-start(bf16[256,1280]{1,0:T(8,128)(2,1)} %get-tuple-element.43.tie.refs_2_.grad) | copy-start | bytes 1966084
  88.2 3.5 %copy-start.13 = (f32[8,1280]{1,0:T(8,128)S(1)}, f32[8,1280]{1,0:T(8,128)}, u32[]{:S(2)}) copy-start(f32[8,1280]{1,0:T(8,128)} %get-tuple-element.44) | copy-start | bytes 122884
  91.2 10.0 %collective-permute-start.2 = (bf16[1280,256]{1,0:T(8,128)(2,1)}, bf16[1280,256]{1,0:T(8,128)(2,1)S(1)}, u32[]{:S(2)}, u32[]{:S(2)}) collective-permute-start(bf16[1280,256]{1,0:T(8,128)(2,1)} %get-tuple-element.52), channel_id=1, source_target_pairs={{0,4},{4,0},{8,12},{12,8},{16,20},{20,16},{24,28},{28,24},{32,36},... | collective-permute-start | bytes 1966088 | tf_op jit(solution)/shard_map/ppermute | solution.py:620
  91.4 9.8 %collective-permute-start.3 = (bf16[256,1280]{1,0:T(8,128)(2,1)S(1)}, bf16[256,1280]{1,0:T(8,128)(2,1)S(1)}, u32[]{:S(2)}, u32[]{:S(2)}) collective-permute-start(bf16[256,1280]{1,0:T(8,128)(2,1)S(1)} %copy-done), channel_id=1, source_target_pairs={{0,4},{4,0},{8,12},{12,8},{16,20},{20,16},{24,28},{28,24},{32,36},... | collective-permute-start | bytes 1966088 | tf_op jit(solution)/shard_map/ppermute | solution.py:615
  91.7 8.3 %collective-permute-start.4 = (f32[8,1280]{1,0:T(8,128)S(1)}, f32[8,1280]{1,0:T(8,128)S(1)}, u32[]{:S(2)}, u32[]{:S(2)}) collective-permute-start(f32[8,1280]{1,0:T(8,128)S(1)} %copy-done.13), channel_id=1, source_target_pairs={{8,0},{16,8},{24,16},{32,24},{40,32},{48,40},{56,48},{64,56},{72,6... | collective-permute-start | bytes 122888 | tf_op jit(solution)/shard_map/ppermute | solution.py:617
  93.0 7.6 %collective-permute-start.1 = (f32[8,1280]{1,0:T(8,128)S(1)}, f32[8,1280]{1,0:T(8,128)S(1)}, u32[]{:S(2)}, u32[]{:S(2)}) collective-permute-start(f32[8,1280]{1,0:T(8,128)S(1)} %copy-done.13), channel_id=1, source_target_pairs={{4,0},{8,4},{12,8},{16,12},{20,16},{24,20},{28,24},{32,28},{36,32}... | collective-permute-start | bytes 122888 | tf_op jit(solution)/shard_map/ppermute | solution.py:616
  94.3 0.8 copy-start.7
  98.9 2.3 %collective-permute-start.5 = (bf16[256,256]{1,0:T(8,128)(2,1)}, bf16[256,256]{1,0:T(8,128)(2,1)S(1)}, u32[]{:S(2)}, u32[]{:S(2)}) collective-permute-start(bf16[256,256]{1,0:T(8,128)(2,1)} %get-tuple-element.50.refs_6_.shared), channel_id=1, source_target_pairs={{0,4},{4,0},{8,12},{12,8},{16,20},{20,16},{24,28},{28,24},{32,36},... | collective-permute-start | bytes 393224 | tf_op jit(solution)/shard_map/ppermute | solution.py:622
  100.6 0.6 copy-start.11
  101.2 0.7 copy-start.8
  101.2 0.9 copy-start.3
  101.2 1.1 copy-start.4
  105.9 18.9 %collective-permute-start.7 = (bf16[640,768]{1,0:T(8,128)(2,1)}, bf16[640,768]{1,0:T(8,128)(2,1)S(1)}, u32[]{:S(2)}, u32[]{:S(2)}) collective-permute-start(bf16[640,768]{1,0:T(8,128)(2,1)} %shard_map.128.refs_8_), channel_id=1, source_target_pairs={{0,32},{4,12},{8,40},{12,20},{16,48},{20,28},{24,56},{28,4},{32,64... | collective-permute-start | bytes 2949128 | tf_op jit(solution)/shard_map/ppermute | solution.py:562
  114.6 14.3 %collective-permute-start.6 = (bf16[640,768]{1,0:T(8,128)(2,1)}, bf16[640,768]{1,0:T(8,128)(2,1)S(1)}, u32[]{:S(2)}, u32[]{:S(2)}) collective-permute-start(bf16[640,768]{1,0:T(8,128)(2,1)} %shard_map.129.refs_8_), channel_id=1, source_target_pairs={{0,96},{4,28},{8,104},{12,4},{16,112},{20,12},{24,120},{28,20},{32... | collective-permute-start | bytes 2949128 | tf_op jit(solution)/shard_map/ppermute | solution.py:562
  120.4 15.8 %copy-start.5 = (f32[320,768]{1,0:T(8,128)S(1)}, f32[320,768]{1,0:T(8,128)}, u32[]{:S(2)}) copy-start(f32[320,768]{1,0:T(8,128)} %get-tuple-element.53.tie) | copy-start | bytes 2949124
  120.4 15.8 %copy-start.9 = (f32[320,768]{1,0:T(8,128)S(1)}, f32[320,768]{1,0:T(8,128)}, u32[]{:S(2)}) copy-start(f32[320,768]{1,0:T(8,128)} %get-tuple-element.56) | copy-start | bytes 2949124
  126.1 10.1 %collective-permute-start.8 = (bf16[320,768]{1,0:T(8,128)(2,1)S(1)}, bf16[320,768]{1,0:T(8,128)(2,1)S(1)}, u32[]{:S(2)}, u32[]{:S(2)}) collective-permute-start(bf16[320,768]{1,0:T(8,128)(2,1)S(1)} %add_convert_fusion.1), channel_id=1, source_target_pairs={{0,32},{4,12},{8,40},{12,20},{16,48},{20,28},{24,56},{28,4},{32,64... | collective-permute-start | bytes 1474568 | tf_op jit(solution)/shard_map/ppermute | solution.py:562
  137.3 9.1 %collective-permute-start.9 = (bf16[320,768]{1,0:T(8,128)(2,1)}, bf16[320,768]{1,0:T(8,128)(2,1)}, u32[]{:S(2)}, u32[]{:S(2)}) collective-permute-start(bf16[320,768]{1,0:T(8,128)(2,1)} %get-tuple-element.62), channel_id=1, source_target_pairs={{0,96},{4,28},{8,104},{12,4},{16,112},{20,12},{24,120},{28,20},{32... | collective-permute-start | bytes 1474568 | tf_op jit(solution)/shard_map/ppermute | solution.py:562
  144.5 2.0 %copy-start.10 = (f32[320,768]{1,0:T(8,128)S(1)}, f32[320,768]{1,0:T(8,128)}, u32[]{:S(2)}) copy-start(f32[320,768]{1,0:T(8,128)} %get-tuple-element.55) | copy-start | bytes 2949124
  147.7 7.5 %collective-permute-start.11 = (bf16[160,768]{1,0:T(8,128)(2,1)S(1)}, bf16[160,768]{1,0:T(8,128)(2,1)S(1)}, u32[]{:S(2)}, u32[]{:S(2)}) collective-permute-start(bf16[160,768]{1,0:T(8,128)(2,1)S(1)} %pad_maximum_fusion.1), channel_id=1, source_target_pairs={{0,8},{4,36},{8,16},{12,44},{16,24},{20,52},{24,0},{28,60},{32,40}... | collective-permute-start | bytes 737288 | tf_op jit(solution)/shard_map/ppermute | solution.py:562
  147.8 7.5 %collective-permute-start.10 = (bf16[160,768]{1,0:T(8,128)(2,1)S(1)}, bf16[160,768]{1,0:T(8,128)(2,1)S(1)}, u32[]{:S(2)}, u32[]{:S(2)}) collective-permute-start(bf16[160,768]{1,0:T(8,128)(2,1)S(1)} %pad_maximum_fusion), channel_id=1, source_target_pairs={{0,24},{4,100},{8,0},{12,108},{16,8},{20,116},{24,16},{28,124},{32... | collective-permute-start | bytes 737288 | tf_op jit(solution)/shard_map/ppermute | solution.py:562
  155.2 6.2 %collective-permute-start.12 = (bf16[80,768]{1,0:T(8,128)(2,1)S(1)}, bf16[80,768]{1,0:T(8,128)(2,1)S(1)}, u32[]{:S(2)}, u32[]{:S(2)}) collective-permute-start(bf16[80,768]{1,0:T(8,128)(2,1)S(1)} %fusion.2), channel_id=1, source_target_pairs={{0,8},{4,36},{8,16},{12,44},{16,24},{20,52},{24,0},{28,60},{32,40}... | collective-permute-start | bytes 368648 | tf_op jit(solution)/shard_map/ppermute | solution.py:562
  161.5 4.9 %collective-permute-start.13 = (bf16[80,768]{1,0:T(8,128)(2,1)S(1)}, bf16[80,768]{1,0:T(8,128)(2,1)S(1)}, u32[]{:S(2)}, u32[]{:S(2)}) collective-permute-start(bf16[80,768]{1,0:T(8,128)(2,1)S(1)} %get-tuple-element.68), channel_id=1, source_target_pairs={{0,24},{4,100},{8,0},{12,108},{16,8},{20,116},{24,16},{28,124},{32... | collective-permute-start | bytes 368648 | tf_op jit(solution)/shard_map/ppermute | solution.py:562
  166.5 4.7 %collective-permute-start.14 = (f32[80,256]{1,0:T(8,128)S(1)}, f32[80,256]{1,0:T(8,128)S(1)}, u32[]{:S(2)}, u32[]{:S(2)}) collective-permute-start(f32[80,256]{1,0:T(8,128)S(1)} %maximum_multiply_fusion.1), channel_id=1, source_target_pairs={{0,1},{1,0},{2,3},{3,2},{4,5},{5,4},{6,7},{7,6},{8,9},{9,8},{10,11... | collective-permute-start | bytes 245768 | tf_op jit(solution)/shard_map/ppermute | solution.py:645
  171.2 6.2 %collective-permute-start.15 = (f32[80,256]{1,0:T(8,128)S(1)}, f32[80,256]{1,0:T(8,128)S(1)}, u32[]{:S(2)}, u32[]{:S(2)}) collective-permute-start(f32[80,256]{1,0:T(8,128)S(1)} %fusion.4), channel_id=1, source_target_pairs={{0,2},{1,3},{2,0},{3,1},{4,6},{5,7},{6,4},{7,5},{8,10},{9,11},{10,... | collective-permute-start | bytes 245768 | tf_op jit(solution)/shard_map/ppermute | solution.py:645
Sparse Core Ops, SparseCore 0:
  144.7 23.1 reduce-scatter.1

commit v2 on v1

--- a/solution.py
+++ b/solution.py
@@ -21,7 +21,7 @@
 ZS = 4
 ROWS = 80
 SLICE = 40
-MSG = 48
+MSG = 88
 BLK = 256
 NBLK = CH // BLK
 SCALE = STATE ** (-0.5)
@@ -29,7 +29,7 @@
 BF16 = jnp.bfloat16
 HIGH = lax.Precision.HIGHEST
 NT = (((1,), (1,)), ((), ()))
-VMEM = 56 * 2**20
+VMEM = 20 * 2**20
 
 
 def nt(a, b):
@@ -69,7 +69,7 @@
     return jnp.where(row <= col if upper else row >= col, 1.0, 0.0).astype(F32)
 
 
-def front_kernel(normed, w_bc, rates, step, grad_y, bmat, cmat, cum, logd, dyt, dywt, msg, pulled, turn):
+def front_kernel(normed, w_bc, rates, step, grad_y, bmat, cmat, cum, logd, dyt, dywt, pulled, through, turn):
     shared = nn(normed[...], w_bc[...])
     bmat[...] = shared[:, :STATE]
     cmat[...] = shared[:, STATE:]
@@ -96,10 +96,7 @@
         pulled[rows, :] = nn(high, c_high) + (nn(low, c_high) + nn(high, c_low))
     turn[...] = jnp.zeros((128, 128), F32)
     turn[:HEADS, :] = grown[:, 128:]
-    through = jnp.broadcast_to(turn[...].T[127:, :], (MSG - SLICE, STATE))
-    for k in range(SEQ):
-        msg[k, :SLICE, :] = pulled[SLICE * k : SLICE * (k + 1), :]
-        msg[k, SLICE:, :] = through
+    through[...] = jnp.broadcast_to(turn[...].T[127:, :], (8, STATE))
 
 
 def front(normed, w_bc, rates, step, grad_y):
@@ -112,46 +109,53 @@
             jax.ShapeDtypeStruct((HEADS, T), F32),
             jax.ShapeDtypeStruct((CH, T), BF16),
             jax.ShapeDtypeStruct((CH, T), BF16),
-            jax.ShapeDtypeStruct((SEQ, MSG, STATE), F32),
-        ),
-        scratch_shapes=[pltpu.VMEM((CH, STATE), F32), pltpu.VMEM((128, 128), F32)],
+            jax.ShapeDtypeStruct((CH, STATE), F32),
+            jax.ShapeDtypeStruct((8, STATE), F32),
+        ),
+        scratch_shapes=[pltpu.VMEM((128, 128), F32)],
         compiler_params=params(),
         cost_estimate=cost(2 * T * D * 256 + 6 * CH * T * 128, 6 * 2**20),
     )(normed, w_bc, rates, step, grad_y)
 
 
-def chain_kernel(reverse, table, recv, decays, tie, out, turn):
+def chain_kernel(table, recv, tie, out, turn):
     del tie
-    lanes = jnp.concatenate([decays[:, 0, :], jnp.zeros((128 - SEQ, 128), F32)], axis=0)
+    lanes = jnp.concatenate([recv[:, 2 * SLICE, :], jnp.zeros((128 - SEQ, 128), F32)], axis=0)
     turn[...] = lanes.T
     head = table[32]
     row = lax.broadcasted_iota(jnp.int32, (SLICE, 128), 0)
     cols = jnp.where(row < table[33], turn[pl.ds(head, 1), :], turn[pl.ds(head + 1, 1), :])
+    pulled = jnp.zeros((SLICE, STATE), F32)
+    pulls = [None] * SEQ
+    for k in range(SEQ - 1, -1, -1):
+        pulls[k] = pulled
+        pulled = cols[:, k : k + 1] * pulled + recv[k, :SLICE, :]
     state = jnp.zeros((SLICE, STATE), F32)
-    for k in range(SEQ - 1, -1, -1) if reverse else range(SEQ):
-        out[k] = state
-        state = cols[:, k : k + 1] * state + recv[k]
-
-
-def chain(table, recv, pulls, tie, reverse):
-    return pl.pallas_call(
-        functools.partial(chain_kernel, reverse),
+    for k in range(SEQ):
+        out[k] = jnp.concatenate([pulls[k], state], axis=0).astype(BF16)
+        state = cols[:, k : k + 1] * state + recv[k, SLICE : 2 * SLICE, :]
+
+
+def chain(table, recv, tie):
+    return pl.pallas_call(
+        chain_kernel,
         grid=(1,),
         in_specs=[
             pl.BlockSpec(memory_space=pltpu.SMEM),
-            whole(SEQ, SLICE, STATE),
-            pl.BlockSpec((SEQ, MSG - SLICE, STATE), lambda i: (0, SLICE // 8, 0)),
+            whole(SEQ, MSG, STATE),
             pl.BlockSpec(memory_space=pl.ANY),
         ],
-        out_specs=whole(SEQ, SLICE, STATE),
-        out_shape=jax.ShapeDtypeStruct((SEQ, SLICE, STATE), F32),
+        out_specs=whole(SEQ, 2 * SLICE, STATE),
+        out_shape=jax.ShapeDtypeStruct((SEQ, 2 * SLICE, STATE), BF16),
         scratch_shapes=[pltpu.VMEM((128, 128), F32)],
         compiler_params=params(),
-        cost_estimate=cost(10**6, 2 * 2**20),
-    )(table, recv, pulls, tie)
-
-
-def channel_kernel(before, normed, w_x, conv_w, cum, logd, bmat, xgt, sgt, xwt, own, ext, pre):
+        cost_estimate=cost(10**6, 3 * 2**20),
+    )(table, recv, tie)
+
+
+def channel_kernel(
+    before, normed, w_x, conv_w, cum, logd, bmat, pulled, through, xgt, slope, xwt, msg, ext, pre, own
+):
     step = pl.program_id(0)
 
     @pl.when(step == 0)
@@ -164,9 +168,9 @@
     total = conv_w[0:1, :] * past[16 : 16 + T, :]
     for tap in range(1, CONV):
         total = total + conv_w[tap : tap + 1, :] * past[16 - tap : 16 - tap + T, :]
-    sig = 1.0 / (1.0 + jnp.exp(-total))
+    sig = 0.5 * jnp.tanh(0.5 * total) + 0.5
     xt = (total * sig).T
-    sgt[...] = (sig * (1.0 + total * (1.0 - sig))).T
+    slope[...] = sig * (1.0 + total * (1.0 - sig))
     parts = []
     block = jnp.maximum(step - 1, 0)
     for q in range(BLK // HEAD_DIM):
@@ -180,11 +184,19 @@
         parts.append(xg * tail)
     weighted = jnp.concatenate(parts, axis=0)
     xwt[...] = weighted.astype(BF16)
-    own[...] = wide(nn, weighted, bmat[...])
+    own[pl.ds(pl.multiple_of(block * BLK, BLK), BLK), :] = wide(nn, weighted, bmat[...])
     pre[now] = nn(ext[...], w_x[...]).astype(BF16).astype(F32)
 
-
-def channels(before, normed, w_x, conv_w, cum, logd, bmat):
+    @pl.when(step == NBLK)
+    def _():
+        for k in range(SEQ):
+            rows = slice(SLICE * k, SLICE * (k + 1))
+            msg[k, :SLICE, :] = pulled[rows, :]
+            msg[k, SLICE : 2 * SLICE, :] = own[rows, :]
+            msg[k, 2 * SLICE :, :] = through[...]
+
+
+def channels(before, normed, w_x, conv_w, cum, logd, bmat, pulled, through):
     def late(i):
         return jnp.maximum(i - 1, 0)
 
@@ -200,18 +212,29 @@
             whole(HEADS, T),
             whole(HEADS, T),
             whole(T, STATE),
+            whole(CH, STATE),
+            whole(8, STATE),
         ],
-        out_specs=(rows, rows, rows, pl.BlockSpec((BLK, STATE), lambda i: (late(i), 0))),
+        out_specs=(
+            rows,
+            pl.BlockSpec((T, BLK), lambda i: (0, late(i))),
+            rows,
+            whole(SEQ, MSG, STATE),
+        ),
         out_shape=(
             jax.ShapeDtypeStruct((CH, T), BF16),
-            jax.ShapeDtypeStruct((CH, T), F32),
+            jax.ShapeDtypeStruct((T, CH), F32),
             jax.ShapeDtypeStruct((CH, T), BF16),
-            jax.ShapeDtypeStruct((CH, STATE), F32),
-        ),
-        scratch_shapes=[pltpu.VMEM((T + 16, D), BF16), pltpu.VMEM((2, T + 16, BLK), F32)],
+            jax.ShapeDtypeStruct((SEQ, MSG, STATE), F32),
+        ),
+        scratch_shapes=[
+            pltpu.VMEM((T + 16, D), BF16),
+            pltpu.VMEM((2, T + 16, BLK), F32),
+            pltpu.VMEM((CH, STATE), F32),
+        ],
         compiler_params=params(),
         cost_estimate=cost(2 * T * D * CH, 10 * 2**20, T * CH),
-    )(before, normed, w_x, conv_w, cum, logd, bmat)
+    )(before, normed, w_x, conv_w, cum, logd, bmat, pulled, through)
 
 
 def intra_kernel(grad_y, dyt, xgt, cum, bmat, cmat, tie, dxg, rc, dbc, gram, dgram):
@@ -290,19 +313,37 @@
     )(grad_y, dyt, xgt, cum, bmat, cmat, tie)
 
 
+def shared_kernel(back, xwt, dywt, dbc, ds, st, shared):
+    for k in range(SEQ):
+        rows = slice(SLICE * k, SLICE * (k + 1))
+        both = back[k].astype(F32)
+        ds[rows, :] = both[:SLICE]
+        st[rows, :] = both[SLICE:]
+    for at, (state, tokens) in enumerate(((ds, xwt), (st, dywt))):
+        turned = state[...].T.astype(BF16)
+        part = nn(turned, tokens[...]) + dbc[STATE * at : STATE * (at + 1), :]
+        shared[:, STATE * at : STATE * (at + 1)] = part.T
+
+
+def shared_part(back, xwt, dywt, dbc):
+    return pl.pallas_call(
+        shared_kernel,
+        out_shape=(
+            jax.ShapeDtypeStruct((CH, STATE), F32),
+            jax.ShapeDtypeStruct((CH, STATE), F32),
+            jax.ShapeDtypeStruct((T, 2 * STATE), F32),
+        ),
+        compiler_params=params(),
+        cost_estimate=cost(4 * CH * T * 128, 4 * 2**20),
+    )(back, xwt, dywt, dbc)
+
+
 def grad_kernel(
-    skip, back, bmat, dxg, dyt, xgt, xwt, sgt, taps, cum, logd, tie, dpre, halo, halves, cross, dbt, ext
+    skip, back, bmat, dxg, dyt, xgt, slope, taps, cum, logd, tie, dpre, halo, halves, cross, ext
 ):
     del tie
     step = pl.program_id(0)
-
-    @pl.when(step == 0)
-    def _():
-        dbt[...] = jnp.zeros((STATE, T), F32)
-
-    own = back[...]
-    later = wide(nt, own, bmat[...])
-    dbt[...] += nn(own.T.astype(BF16), xwt[...])
+    later = wide(nt, back[...], bmat[...])
     parts = []
     for q in range(BLK // HEAD_DIM):
         index = step * (BLK // HEAD_DIM) + q
@@ -316,10 +357,9 @@
         xg = xgt[rows, :].astype(F32)
         cross[head, :] = jnp.sum(xg * inter, axis=0, keepdims=True)
         halves[head, :] = 0.5 * jnp.sum(xg * whole_dxg, axis=0, keepdims=True)
-        d_x = gain * whole_dxg + skip[index] * dyt[rows, :].astype(F32)
-        parts.append(d_x * sgt[rows, :])
+        parts.append(gain * whole_dxg + skip[index] * dyt[rows, :].astype(F32))
     ext[:8, :] = jnp.zeros((8, BLK), F32)
-    ext[8 : T + 8, :] = jnp.concatenate(parts, axis=0).T
+    ext[8 : T + 8, :] = jnp.concatenate(parts, axis=0).T * slope[...]
     ext[T + 8 :, :] = jnp.zeros((8, BLK), F32)
     total = taps[0:1, :] * ext[8 : T + 8, :]
     edge = taps[0:1, :] * ext[:8, :]
@@ -331,8 +371,9 @@
     halo[...] = edge
 
 
-def gradients(skip, back, bmat, dxg, dyt, xgt, xwt, sgt, taps, cum, logd, tie):
+def gradients(skip, back, bmat, dxg, dyt, xgt, slope, taps, cum, logd, tie):
     rows = pl.BlockSpec((BLK, T), lambda i: (i, 0))
+    cols = pl.BlockSpec((T, BLK), lambda i: (0, i))
     return pl.pallas_call(
         grad_kernel,
         grid=(NBLK,),
@@ -343,39 +384,33 @@
             rows,
             rows,
             rows,
-            rows,
-            rows,
+            cols,
             pl.BlockSpec((CONV, BLK), lambda i: (0, i)),
             whole(HEADS, T),
             whole(HEADS, T),
             pl.BlockSpec(memory_space=pl.ANY),
         ],
         out_specs=(
-            pl.BlockSpec((T, BLK), lambda i: (0, i)),
+            cols,
             pl.BlockSpec((8, BLK), lambda i: (0, i)),
             whole(HEADS, T),
             whole(HEADS, T),
-            whole(STATE, T),
         ),
         out_shape=(
             jax.ShapeDtypeStruct((T, CH), BF16),
             jax.ShapeDtypeStruct((8, CH), F32),
             jax.ShapeDtypeStruct((HEADS, T), F32),
             jax.ShapeDtypeStruct((HEADS, T), F32),
-            jax.ShapeDtypeStruct((STATE, T), F32),
         ),
         scratch_shapes=[pltpu.VMEM((T + 16, BLK), F32)],
         compiler_params=params(),
         cost_estimate=cost(4 * CH * T * 128, 6 * 2**20, T * HEADS),
-    )(skip, back, bmat, dxg, dyt, xgt, xwt, sgt, taps, cum, logd, tie)
-
-
-def state_kernel(
-    fore, back, cmat, dyt, dywt, cum, logd, rc, halves, cross, dbt, dbc, gls, shared
-):
-    state = fore[...]
-    before = wide(nt, state, cmat[...])
-    dct = nn(state.T.astype(BF16), dywt[...])
+    )(skip, back, bmat, dxg, dyt, xgt, slope, taps, cum, logd, tie)
+
+
+def step_kernel(fore, back, cmat, dyt, cum, logd, rc, halves, cross, tie, gls):
+    del tie
+    before = wide(nt, fore[...], cmat[...])
     cums = cum[...]
     inner = []
     through = []
@@ -392,22 +427,17 @@
     )
     kept = jnp.exp(cums[:, T - 1 :]) * jnp.concatenate(through, axis=0)
     gls[...] = logd[...] * (later + earlier + kept) + halves[...]
-    total = dbc[...] + jnp.concatenate([dbt[...], dct], axis=0)
-    shared[...] = total.T.astype(BF16)
-
-
-def states(fore, back, cmat, dyt, dywt, cum, logd, rc, halves, cross, dbt, dbc):
+
+
+def step_part(fore, back, cmat, dyt, cum, logd, rc, halves, cross, tie):
     vm = pl.BlockSpec(memory_space=pltpu.VMEM)
     return pl.pallas_call(
-        state_kernel,
-        in_specs=[vm] * 12,
-        out_shape=(
-            jax.ShapeDtypeStruct((HEADS, T), F32),
-            jax.ShapeDtypeStruct((T, 2 * STATE), BF16),
-        ),
+        step_kernel,
+        in_specs=[vm] * 9 + [pl.BlockSpec(memory_space=pl.ANY)],
+        out_shape=jax.ShapeDtypeStruct((HEADS, T), F32),
         compiler_params=params(),
         cost_estimate=cost(4 * CH * T * 128, 4 * 2**20),
-    )(fore, back, cmat, dyt, dywt, cum, logd, rc, halves, cross, dbt, dbc)
+    )(fore, back, cmat, dyt, cum, logd, rc, halves, cross, tie)
 
 
 def select_kernel(order, normed, tie, mine, other, flip):
@@ -460,87 +490,176 @@
     return rows
 
 
-def up_kernel(*refs):
-    up = refs[8]
-    for at, (part, side) in enumerate(((2, 0), (1, 1))):
+def far_kernel(*refs):
+    for out, (part, side) in zip(refs[8:], ((2, 0), (2, 1))):
         main, extra = product(refs[:8], side)(part)
-        up[PART[at], :WIDE] = main.astype(BF16)
-        up[PART[at], WIDE:] = extra.astype(BF16)
-
-
-def down_kernel(*refs):
-    down = refs[9]
-    for at, (part, side) in enumerate(((2, 1), (3, 0))):
+        out[:, :WIDE] = main.astype(BF16)
+        out[:, WIDE:] = extra.astype(BF16)
+
+
+def near_kernel(*refs):
+    for out, (part, side) in zip(refs[9:], ((1, 0), (3, 1), (1, 1), (3, 0))):
         main, extra = product(refs[:8], side)(part)
-        down[PART[at], :WIDE] = main.astype(BF16)
-        down[PART[at], WIDE:] = extra.astype(BF16)
-
-
-def keep_kernel(*refs):
-    for out, (part, side) in zip(refs[9:], ((1, 0), (3, 1), (0, 0), (0, 1))):
+        out[:, :WIDE] = main.astype(out.dtype)
+        out[:, WIDE:] = extra.astype(out.dtype)
+
+
+def here_kernel(*refs):
+    for out, (part, side) in zip(refs[9:], ((0, 0), (0, 1))):
         main, extra = product(refs[:8], side)(part)
         out[:, :WIDE] = main
         out[:, WIDE:] = extra
 
 
-def up_part(args):
-    return pl.pallas_call(
-        up_kernel,
-        out_shape=jax.ShapeDtypeStruct((640, FULL), BF16),
-        compiler_params=params(),
-        cost_estimate=cost(2 * 512 * FULL * 640, 4 * 2**20),
+def product_part(kernel, args, ties, types):
+    vm = pl.BlockSpec(memory_space=pltpu.VMEM)
+    return pl.pallas_call(
+        kernel,
+        in_specs=[vm] * 8 + [pl.BlockSpec(memory_space=pl.ANY)] * len(ties),
+        out_shape=tuple(jax.ShapeDtypeStruct((320, FULL), one) for one in types),
+        compiler_params=params(),
+        cost_estimate=cost(2 * 512 * FULL * 320 * len(types), (3 + len(types)) * 2**20),
+    )(*args, *ties)
+
+
+def join_kernel(count, *refs):
+    ins, outs = refs[: 3 * count], refs[3 * count :]
+    for i, out in enumerate(outs):
+        near, arrived, direct = ins[3 * i : 3 * i + 3]
+        size = near.shape[0]
+        out[:size, :] = (near[...] + arrived[...].astype(F32)).astype(BF16)
+        out[size:, :] = direct[...]
+
+
+def join(*triples):
+    count = len(triples)
+    return pl.pallas_call(
+        functools.partial(join_kernel, count),
+        out_shape=tuple(
+            jax.ShapeDtypeStruct((2 * near.shape[0], near.shape[1]), BF16)
+            for near, _, _ in triples
+        ),
+        compiler_params=params(),
+        cost_estimate=cost(10**6, 4 * 2**20),
+    )(*[one for triple in triples for one in triple])
+
+
+def turn_kernel(here_a, here_b, up, down, far_up, far_down, near_up, near_down, dir_up, dir_down, a, b):
+    size = 4 * ROWS
+
+    def one(r, side):
+        rows = slice(ROWS * r, ROWS * (r + 1))
+        direct = slice(size + ROWS * r, size + ROWS * (r + 1))
+        if side == 0:
+            arrived = up[rows, :].astype(F32) + down[direct, :].astype(F32)
+            return here_a[rows, :] + arrived
+        arrived = down[rows, :].astype(F32) + up[direct, :].astype(F32)
+        return here_b[rows, :] + arrived
+
+    far_up[...] = one(2, 0).astype(BF16)
+    far_down[...] = one(2, 1).astype(BF16)
+    near_up[...] = one(1, 0)
+    near_down[...] = one(3, 1)
+    dir_up[...] = one(1, 1).astype(BF16)
+    dir_down[...] = one(3, 0).astype(BF16)
+    a[...] = one(0, 0)
+    b[...] = one(0, 1)
+
+
+def turn_part(here_a, here_b, up, down):
+    return pl.pallas_call(
+        turn_kernel,
+        out_shape=tuple(
+            jax.ShapeDtypeStruct((ROWS, FULL), one)
+            for one in (BF16, BF16, F32, F32, BF16, BF16, F32, F32)
+        ),
+        compiler_params=params(),
+        cost_estimate=cost(10**6, 4 * 2**20),
+    )(here_a, here_b, up, down)
+
+
+def last_kernel(a, b, up, down, here_u, up_u, down_u, grad_wx, grad_wbc, grad_u):
+    norm = (T * SEQ) ** (-0.5)
+    first = a[...] + (up[:ROWS, :].astype(F32) + down[ROWS:, :].astype(F32))
+    second = b[...] + (down[:ROWS, :].astype(F32) + up[ROWS:, :].astype(F32))
+    grad_wx[:, :WIDE] = first[:, :WIDE] * norm
+    grad_wx[:, WIDE:] = second[:, :WIDE] * norm
+    grad_wbc[:, :STATE] = first[:, WIDE:] * norm
+    grad_wbc[:, STATE:] = second[:, WIDE:] * norm
+    size = here_u.shape[0] // 2
+    low = here_u[:size, :] + (up_u[:size, :].astype(F32) + down_u[size:, :].astype(F32))
+    high = here_u[size:, :] + (down_u[:size, :].astype(F32) + up_u[size:, :].astype(F32))
+    grad_u[:size, :] = low.astype(BF16)
+    grad_u[size:, :] = high.astype(BF16)
+
+
+def last_part(*args):
+    return pl.pallas_call(
+        last_kernel,
+        out_shape=(
+            jax.ShapeDtypeStruct((ROWS, CH), F32),
+            jax.ShapeDtypeStruct((ROWS, 2 * STATE), F32),
+            jax.ShapeDtypeStruct((D // ZS, T), BF16),
+        ),
+        compiler_params=params(),
+        cost_estimate=cost(10**6, 3 * 2**20),
     )(*args)
 
 
-def down_part(args, tie):
-    vm = pl.BlockSpec(memory_space=pltpu.VMEM)
-    return pl.pallas_call(
-        down_kernel,
-        in_specs=[vm] * 8 + [pl.BlockSpec(memory_space=pl.ANY)],
-        out_shape=jax.ShapeDtypeStruct((640, FULL), BF16),
-        compiler_params=params(),
-        cost_estimate=cost(2 * 512 * FULL * 640, 4 * 2**20),
-    )(*args, tie)
-
-
-def keep_part(args, tie):
-    vm = pl.BlockSpec(memory_space=pltpu.VMEM)
-    one = jax.ShapeDtypeStruct((320, FULL), F32)
-    return pl.pallas_call(
-        keep_kernel,
-        in_specs=[vm] * 8 + [pl.BlockSpec(memory_space=pl.ANY)],
-        out_shape=(one,) * 4,
-        compiler_params=params(),
-        cost_estimate=cost(2 * 512 * FULL * 1280, 8 * 2**20),
-    )(*args, tie)
-
-
-def input_kernel(w_x, w_bc, grad, halo, shared, tie, out):
-    del tie
+def input_kernel(order, w_x, w_bc, grad, halo, shared, tie, *outs):
+    del order, tie
+    far_up, far_down, near_up, near_down, dir_up, dir_down, here = outs
+    step = pl.program_id(0)
+    rows = w_x.shape[0] // 2
+    low, high = slice(0, rows), slice(rows, 2 * rows)
     edge = jnp.concatenate([jnp.zeros((8, CH), F32), halo[...]], axis=0)
     last = (grad[T - 16 :, :].astype(F32) + edge).astype(BF16)
     right = jnp.concatenate([grad[: T - 16, :], last], axis=0)
-    out[...] = (nt(w_x[...], right) + nt(w_bc[...], shared[...])).astype(BF16)
-
-
-def input_part(w_x, w_bc, grad, halo, shared, tie):
+    part = nt(w_x[...], right)
+
+    @pl.when(step == 0)
+    def _():
+        far_up[...] = part[low].astype(BF16)
+        far_down[...] = part[high].astype(BF16)
+
+    @pl.when(step == 1)
+    def _():
+        near_up[...] = part[low]
+        dir_up[...] = part[high].astype(BF16)
+
+    @pl.when(step == 2)
+    def _():
+        dir_down[...] = part[low].astype(BF16)
+        near_down[...] = part[high]
+
+    @pl.when(step == 3)
+    def _():
+        here[...] = part + nt(w_bc[...], shared[...])
+
+
+def input_part(order, w_x, w_bc, grad, halo, shared, tie):
     rows = D // ZS
+    sizes = (rows // 2,) * 6 + (rows,)
+    types = (BF16, BF16, F32, F32, BF16, BF16, F32)
     return pl.pallas_call(
         input_kernel,
-        grid=(ZS,),
-        in_specs=[
-            pl.BlockSpec((rows, CH), lambda i: (i, 0)),
-            pl.BlockSpec((rows, 2 * STATE), lambda i: (i, 0)),
-            whole(T, CH),
-            whole(8, CH),
-            whole(T, 2 * STATE),
-            pl.BlockSpec(memory_space=pl.ANY),
-        ],
-        out_specs=pl.BlockSpec((rows, T), lambda i: (i, 0)),
-        out_shape=jax.ShapeDtypeStruct((D, T), BF16),
-        compiler_params=params(),
-        cost_estimate=cost(2 * D * (CH + 256) * T, 10 * 2**20),
-    )(w_x, w_bc, grad, halo, shared, tie)
+        grid_spec=pltpu.PrefetchScalarGridSpec(
+            num_scalar_prefetch=1,
+            grid=(ZS,),
+            in_specs=[
+                pl.BlockSpec((rows, CH), lambda i, order: (order[i], 0)),
+                pl.BlockSpec((rows, 2 * STATE), lambda i, order: (order[3], 0)),
+                pl.BlockSpec((T, CH), lambda i, order: (0, 0)),
+                pl.BlockSpec((8, CH), lambda i, order: (0, 0)),
+                pl.BlockSpec((T, 2 * STATE), lambda i, order: (0, 0)),
+                pl.BlockSpec(memory_space=pl.ANY),
+            ],
+            out_specs=[pl.BlockSpec((size, T), lambda i, order: (0, 0)) for size in sizes],
+        ),
+        out_shape=tuple(jax.ShapeDtypeStruct((size, T), one) for size, one in zip(sizes, types)),
+        compiler_params=params(),
+        cost_estimate=cost(2 * D * (CH + 64) * T, 10 * 2**20),
+    )(order, w_x, w_bc, grad, halo, shared, tie)
 
 
 def device(x, y, core):
@@ -562,16 +681,8 @@
     return lambda value: lax.ppermute(value, "seq", ring(first, by))
 
 
-def ring_sum(move, up1, down1, near_up, near_down, here_a, here_b, size):
-    from_up = move(1)(up1)
-    from_down = move(-1)(down1)
-    up2 = (near_up + from_up[:size].astype(F32)).astype(BF16)
-    down2 = (near_down + from_down[:size].astype(F32)).astype(BF16)
-    last_up = move(1)(up2)
-    last_down = move(-1)(down2)
-    total_a = here_a + from_down[size:].astype(F32) + last_up.astype(F32)
-    total_b = here_b + from_up[size:].astype(F32) + last_down.astype(F32)
-    return total_a, total_b
+def along_head(by):
+    return lambda value: lax.ppermute(value, "head", [(i, (i + by) % ZS) for i in range(ZS)])
 
 
 def place_table():
@@ -588,9 +699,15 @@
     return np.array(rows, np.int32)
 
 
+def head_table():
+    return np.array([[(z + r) % ZS for r in (2, 1, 3, 0)] for z in range(ZS)], np.int32)
+
+
 def body(normed, w_x, w_bc, conv_w, decay_code, step, d_skip, grad_y):
     place = lax.axis_index("seq")
     core = place % 2
+    z = lax.axis_index("head")
+    order_z = jnp.asarray(head_table())[z]
     table = lax.dynamic_index_in_dim(jnp.asarray(place_table()), place, 0, keepdims=False)
     swap = [(i, i ^ 1) for i in range(SEQ)]
 
@@ -599,50 +716,60 @@
     rates = low + decay_code.astype(F32)[:, None] / (LEVELS - 1) * (high - low)
     before = lax.ppermute(normed[T - 16 :], "seq", [(i, i + 1) for i in range(SEQ - 1)])
 
-    bmat, cmat, cum, logd, dyt, dywt, msg = front(normed, w_bc, rates, step, grad_y)
-    pulls = lax.all_to_all(msg, "seq", 0, 0)
-    xgt, sgt, xwt, own = channels(before, normed, w_x, conv_w, cum, logd, bmat)
-    ahead = lax.all_to_all(own.reshape(SEQ, SLICE, STATE), "seq", 0, 0)
-    back_parts = chain(table, pulls, pulls, own, True)
-    back = lax.all_to_all(back_parts, "seq", 0, 0).reshape(CH, STATE)
-    dxg, rc, dbc = intra(grad_y, dyt, xgt, cum, bmat, cmat, back_parts)
-    fore_parts = chain(table, ahead, pulls, rc, False)
-    fore = lax.all_to_all(fore_parts, "seq", 0, 0).reshape(CH, STATE)
-
-    dpre, halo, halves, cross, dbt = gradients(
-        d_skip, back, bmat, dxg, dyt, xgt, xwt, sgt, conv_w, cum, logd, fore_parts
+    bmat, cmat, cum, logd, dyt, dywt, pulled, through = front(normed, w_bc, rates, step, grad_y)
+    xgt, slope, xwt, msg = channels(
+        before, normed, w_x, conv_w, cum, logd, bmat, pulled, through
+    )
+    recv = lax.all_to_all(msg, "seq", 0, 0)
+    mine, other = select(table, normed, msg)
+    other = lax.ppermute(other, "seq", swap)
+    dxg, rc, dbc = intra(grad_y, dyt, xgt, cum, bmat, cmat, mine)
+    back = lax.all_to_all(chain(table, recv, rc), "seq", 0, 0)
+
+    ds, st, shared = shared_part(back, xwt, dywt, dbc)
+    for bit in (1, 2):
+        pairs = [(i, i ^ bit) for i in range(ZS)]
+        shared = shared + lax.ppermute(shared, "head", pairs)
+    shared = shared.astype(BF16)
+    dpre, halo, halves, cross = gradients(
+        d_skip, ds, bmat, dxg, dyt, xgt, slope, conv_w, cum, logd, st
     )
     dpre_other = lax.ppermute(dpre, "seq", swap)
     halo_mine = lax.ppermute(halo, "seq", [(i, i - 1) for i in range(1, SEQ)])
     halo_pair = lax.ppermute(halo, "seq", [(i, i - 2) for i in range(2, SEQ, 2)])
     halo_other = jnp.where(core == 0, halo_pair, halo)
-    mine, other = select(table, normed, dpre)
-    other = lax.ppermute(other, "seq", swap)
-    gls, shared = states(fore, back, cmat, dyt, dywt, cum, logd, rc, halves, cross, dbt, dbc)
     shared_other = lax.ppermute(shared, "seq", swap)
 
     args = (mine, other, dpre, dpre_other, halo_mine, halo_other, shared, shared_other)
-    up1 = up_part(args)
-    down1 = down_part(args, up1)
-    near_up, near_down, here_a, here_b = keep_part(args, down1)
-    part = input_part(w_x, w_bc, dpre, halo_mine, shared, here_a)
-    grad_u = lax.psum_scatter(part, "head", scatter_dimension=0, tiled=True)
-    sum_a, sum_b = ring_sum(
-        lambda by: along(True, by), up1, down1, near_up, near_down, here_a, here_b, 320
-    )
-    a4 = sum_a.reshape(4, ROWS, FULL)
-    b4 = sum_b.reshape(4, ROWS, FULL)
-    up1 = jnp.concatenate([a4[2], b4[1]], axis=0).astype(BF16)
-    down1 = jnp.concatenate([b4[2], a4[3]], axis=0).astype(BF16)
-    sum_a, sum_b = ring_sum(
-        lambda by: along(False, by), up1, down1, a4[1], b4[3], a4[0], b4[0], ROWS
-    )
-    norm = (T * SEQ) ** (-0.5)
-    grad_wx = jnp.concatenate([sum_a[:, :WIDE], sum_b[:, :WIDE]], axis=1) * norm
-    grad_wbc = jnp.concatenate([sum_a[:, WIDE:], sum_b[:, WIDE:]], axis=1) * norm
-    for bit in (1, 2):
-        pairs = [(i, i ^ bit) for i in range(ZS)]
-        grad_wbc = grad_wbc + lax.ppermute(grad_wbc, "head", pairs)
+    move = {by: along(True, by) for by in (1, -1)}
+    turn = {by: along(False, by) for by in (1, -1)}
+    head = {by: along_head(by) for by in (1, -1)}
+    far_up, far_down = product_part(far_kernel, args, (), (BF16, BF16))
+    ru, rd = move[1](far_up), move[-1](far_down)
+    near_up, near_down, dir_up, dir_down = product_part(
+        near_kernel, args, (far_up,), (F32, F32, BF16, BF16)
+    )
+    up, down = join((near_up, ru, dir_up), (near_down, rd, dir_down))
+    ru, rd = move[1](up), move[-1](down)
+    here_a, here_b = product_part(here_kernel, args, (up,), (F32, F32))
+    z_far_up, z_far_down, z_up, z_down, z_dir_up, z_dir_down, z_here = input_part(
+        order_z, w_x, w_bc, dpre, halo_mine, shared, here_a
+    )
+    gls = step_part(st, ds, cmat, dyt, cum, logd, rc, halves, cross, z_here)
+    far_up, far_down, near_up, near_down, dir_up, dir_down, here_a, here_b = turn_part(
+        here_a, here_b, ru, rd
+    )
+    ru, rd = turn[1](far_up), turn[-1](far_down)
+    zu, zd = head[1](z_far_up), head[-1](z_far_down)
+    up, down, z_up, z_down = join(
+        (near_up, ru, dir_up),
+        (near_down, rd, dir_down),
+        (z_up, zu, z_dir_up),
+        (z_down, zd, z_dir_down),
+    )
+    ru, rd = turn[1](up), turn[-1](down)
+    zu, zd = head[1](z_up), head[-1](z_down)
+    grad_wx, grad_wbc, grad_u = last_part(here_a, here_b, ru, rd, z_here, zu, zd)
     return (grad_u, grad_wx, grad_wbc, gls)
 
 

time: 187 us -> 153 us (0.82)
  Pallas kernels: 55.6 us -> 31 us
  local copies, waits for them, and re-layouts: 5.52 us -> 27.7 us
  blocking collectives: 0 us -> 15.9 us
  waiting for transfers between devices: 49.5 us -> 34.7 us
  starting transfers between devices: 53.4 us -> 38.8 us
  between operations: 14.3 us -> 1.07 us
  other arithmetic: 6.52 us -> 2.46 us
    unnamed x28 -> x102, local copies, waits for them, and re-layouts: 2.65 us -> 25.3 us
    all_to_all x4 -> x1, starting transfers between devices: 29.8 us -> 9.15 us  [body(): recv = lax.all_to_all(msg, 'seq', 0, 0)]
    ppermute x8, waiting for transfers between devices: 30.9 us -> 12.8 us  [along(): return lambda value: lax.ppermute(value, 'seq', ring(first, by))]
    all_to_all x0 -> x1, blocking collectives: none -> 15.9 us  [body(): back = lax.all_to_all(chain(table, recv, rc), 'seq', 0, 0)]
    pallas_call x7 -> x11, Pallas kernels: 26.3 us -> 14.4 us  [the longest x1 3.49 us: input_part(): pl.pallas_call(input_kernel, grid_spec=pltpu.PrefetchScalarGridSpec(num_s...]
    ppermute x2 -> x6, starting transfers between devices: 5.75 us -> 12.3 us  [the longest x4 6.61 us: along_head(): lax.ppermute(value, 'head', [(i, (i + by) % ZS) for i in range(ZS)])]
    pallas_call x1, Pallas kernels: 6.33 us -> 3.06 us  [gradients(): pl.pallas_call(grad_kernel, grid=(NBLK,), in_specs=[pl.BlockSpec(memory_s...]
    pallas_call x1, Pallas kernels: 6.58 us -> 3.45 us  [intra(): pl.pallas_call(intra_kernel, grid=(NBLK,), in_specs=[pl.BlockSpec((T, BLK...]
  transfers between devices with their start and end apart: 21 -> 21, of which waited for: 14 -> 8; matrix products, arithmetic and copies ran while one was open for 4% -> 2% of each run, Pallas kernels for 26% -> 12%
where the time goes in v2:
time: 153 us; the launch traced here: 152 us
  starting transfers between devices  38.8 us (25%)
  waiting for transfers between devices  34.7 us (23%)
  Pallas kernels  31 us (20%)
  local copies, waits for them, and re-layouts  27.7 us (18%)
  blocking collectives  15.9 us (10%)
  other arithmetic  2.46 us (2%)
    unnamed x102, local copies, waits for them, and re-layouts  25.3 us
    all_to_all x1, blocking collectives, body(): back = lax.all_to_all(chain(table, recv, rc), 'seq', 0, 0)  15.9 us
    all_to_all x1, waiting for transfers between devices, body(): recv = lax.all_to_all(msg, 'seq', 0, 0)  13.5 us
    ppermute x8, waiting for transfers between devices, along(): return lambda value: lax.ppermute(value, 'seq', ring(first, by))  12.8 us
    ppermute x8, starting transfers between devices, along(): return lambda value: lax.ppermute(value, 'seq', ring(first, by))  12.2 us
    all_to_all x1, starting transfers between devices, body(): recv = lax.all_to_all(msg, 'seq', 0, 0)  9.15 us
    pallas_call x1, Pallas kernels, channels(): pl.pallas_call(channel_kernel, grid=(NBLK + 1,), in_specs=[whole(16, D),...  7.23 us
    ppermute x2, waiting for transfers between devices, body(): shared = shared + lax.ppermute(shared, 'head', pairs)  7.15 us
  transfers between devices with their start and end apart: 21, of which 8 were waited for; matrix products, arithmetic and copies ran while one was open for 2% of the time, Pallas kernels for 12%

profile of v2, /device:TPU:0, one launch (start us, length us, event | category | flops | bytes accessed | tf_op | source)
XLA Modules:
  0.0 151.5 jit_solution(2658281847880244467)
XLA Ops:
  0.6 0.9 slice.3
  1.5 1.3 collective-permute-start
  3.6 1.3 copy-done.2
  4.9 1.3 copy-done.4
  6.2 1.1 copy-done.16
  8.0 1.8 %shard_map.129 = (f32[256,128]{1,0:T(8,128)S(1)}, f32[256,128]{1,0:T(8,128)S(1)}, f32[20,256]{1,0:T(8,128)S(1)}, f32[20,256]{1,0:T(8,128)S(1)}, bf16[1280,256]{1...) custom-call(bf16[256,2560]{1,0:T(8,128)(2,1)S(1)} %copy-done.2, ...), custom_call_target="tpu_custom_call" | custom-call | flops 587202560 | bytes 6291456 | tf_op jit(solution)/shard_map/pallas_call | solution.py:103
  11.3 2.9 %copy-done = bf16[2560,1280]{1,0:T(8,128)(2,1)S(1)} copy-done((bf16[2560,1280]{1,0:T(8,128)(2,1)S(1)}, bf16[2560,1280]{1,0:T(8,128)(2,1)}, u32[]{:S(2)}) %copy-start) | copy-done | bytes 6553624
  14.2 7.2 %shard_map.130 = (bf16[1280,256]{1,0:T(8,128)(2,1)S(1)}, f32[256,1280]{1,0:T(8,128)S(1)}, bf16[1280,256]{1,0:T(8,128)(2,1)S(1)}, f32[32,88,128]{2,1,0:T(8,128)}) custom-call(bf16[16,2560]{1,0:T(8,128)(2,1)S(1)} %collective-permute-done.before, bf16[256,2560]{1,0:T(8,128)(2,1)S(1)} %copy-done.2, bf16[2560,1280]{1,0:T(8,128)(2,1)S(1)} %copy-done, ...), custom_call_target="tpu_custom_call" | custom-call | flops 1677721600 | bytes 10485760 | tf_op jit(solution)/shard_map/pallas_call | solution.py:204
  21.4 1.1 copy-done.12
  24.2 9.1 %all-to-all-start = ((f32[32,88,128]{2,1,0:T(8,128)}), f32[32,88,128]{2,1,0:T(8,128)S(1)}, u32[]{:S(2)}, u32[]{:S(2)}) async-start(f32[32,88,128]{2,1,0:T(8,128)} %get-tuple-element.65.tie), calls=%async_computation | async-start | bytes 2883584 | tf_op jit(solution)/shard_map/all_to_all | solution.py:723
  34.1 1.0 shard_map.131
  36.0 3.5 %shard_map.132 = (f32[1280,256]{1,0:T(8,128)S(1)}, f32[20,256]{1,0:T(8,128)S(1)}, f32[256,256]{1,0:T(8,128)S(1)}) custom-call(bf16[256,1280]{1,0:T(8,128)(2,1)S(1)} %copy-done.17, bf16[1280,256]{1,0:T(8,128)(2,1)S(1)} %get-tuple-element.68.dyt, bf16[1280,256]{1,0:T(8,128)(2,1)S(1)} %copy-done.19, f32[20,256]{1,0:T(8,128)S(1)} %copy-done.31, ...), custom_call_target="tpu_custom_call" | custom-call | flops 1342177280 | bytes 4194304 | tf_op jit(solution)/shard_map/pallas_call | solution.py:292
  40.4 1.0 copy-done.14
  41.4 13.5 %all-to-all-done.recv = f32[32,88,128]{2,1,0:T(8,128)S(1)} async-done(((f32[32,88,128]{2,1,0:T(8,128)}), f32[32,88,128]{2,1,0:T(8,128)S(1)}, u32[]{:S(2)}, u32[]{:S(2)}) %all-to-all-start) | async-done | bytes 1441824 | tf_op jit(solution)/shard_map/all_to_all | solution.py:723
  54.9 1.0 shard_map.133
  55.9 15.9 %all_to_all.10.back = bf16[32,80,128]{2,1,0:T(8,128)(2,1)S(1)} all-to-all(bf16[32,80,128]{2,1,0:T(8,128)(2,1)S(1)} %shard_map.133), channel_id=1, replica_groups=mesh['seq'=32,'head'=4] {'seq'}, dimensions={0} | all-to-all | bytes 1310720 | tf_op jit(solution)/shard_map/all_to_all | solution.py:727
  72.4 2.0 %collective-permute-start.5 = (f32[256,256]{1,0:T(8,128)S(1)}, f32[256,256]{1,0:T(8,128)S(1)}, u32[]{:S(2)}, u32[]{:S(2)}) collective-permute-start(f32[256,256]{1,0:T(8,128)S(1)} %get-tuple-element.81), channel_id=1, source_target_pairs={{0,1},{1,0},{2,3},{3,2},{4,5},{5,4},{6,7},{7,6},{8,9},{9,8},{10,11... | collective-permute-start | bytes 786440 | tf_op jit(solution)/shard_map/ppermute | solution.py:732
  74.4 7.1 %collective-permute-done.5 = f32[256,256]{1,0:T(8,128)S(1)} collective-permute-done((f32[256,256]{1,0:T(8,128)S(1)}, f32[256,256]{1,0:T(8,128)S(1)}, u32[]{:S(2)}, u32[]{:S(2)}) %collective-permute-start.5) | collective-permute-done | bytes 262176 | tf_op jit(solution)/shard_map/ppermute | solution.py:732
  82.2 3.7 %collective-permute-start.6 = (f32[256,256]{1,0:T(8,128)}, f32[256,256]{1,0:T(8,128)}, u32[]{:S(2)}, u32[]{:S(2)}) collective-permute-start(f32[256,256]{1,0:T(8,128)} %add.26), channel_id=1, source_target_pairs={{0,2},{1,3},{2,0},{3,1},{4,6},{5,7},{6,4},{7,5},{8,10},{9,11},{10,... | collective-permute-start | bytes 786440 | tf_op jit(solution)/shard_map/ppermute | solution.py:732
  86.0 1.3 copy-done.13
  87.3 1.3 copy-done.15
  88.6 1.1 copy-done.20
  89.7 3.1 %shard_map.135 = (bf16[256,1280]{1,0:T(8,128)(2,1)S(1)}, f32[8,1280]{1,0:T(8,128)S(1)}, f32[20,256]{1,0:T(8,128)S(1)}, f32[20,256]{1,0:T(8,128)S(1)}) custom-call(f32[20]{0:T(128)S(1)} %copy-done.49, f32[1280,128]{1,0:T(8,128)S(1)} %get-tuple-element.75.back, f32[256,128]{1,0:T(8,128)S(1)} %get-tuple-element.62.bmat, f32[1280,256]{1,0:T(8,128)S(1)} %copy-done.15, ...), custom_call_target="tpu_custom_call" | custom-call | flops 167772160 | bytes 6291456 | tf_op jit(solution)/shard_map/pallas_call | solution.py:377
  92.8 1.3 collective-permute-start.4
  94.1 1.3 collective-permute-start.3
  95.4 1.2 collective-permute-start.2
  96.6 1.1 add_convert_fusion.refs_6_.shared
  97.8 0.9 collective-permute-done.4
  100.0 2.7 %collective-permute-start.9 = (bf16[320,768]{1,0:T(8,128)(2,1)S(1)}, bf16[320,768]{1,0:T(8,128)(2,1)S(1)}, u32[]{:S(2)}, u32[]{:S(2)}) collective-permute-start(bf16[320,768]{1,0:T(8,128)(2,1)S(1)} %get-tuple-element.86), channel_id=1, source_target_pairs={{0,96},{4,28},{8,104},{12,4},{16,112},{20,12},{24,120},{28,20},{32... | collective-permute-start | bytes 1474568 | tf_op jit(solution)/shard_map/ppermute | solution.py:681
  103.6 1.5 %shard_map.137 = (f32[320,768]{1,0:T(8,128)S(1)}, f32[320,768]{1,0:T(8,128)S(1)}, bf16[320,768]{1,0:T(8,128)(2,1)S(1)}, bf16[320,768]{1,0:T(8,128)(2,1)S(1)}) custom-call(bf16[1280,256]{1,0:T(8,128)(2,1)S(1)} %copy-done.7, bf16[1280,256]{1,0:T(8,128)(2,1)S(1)} %collective-permute-done.1.refs_1_, bf16[256,1280]{1,0:T(8,128)(2,1)S(1)} %get-tuple-element.79.refs_2_.grad, ...), custom_call_target="tpu_custom_call" | custom-call | flops 1006632960 | bytes 7340032 | tf_op jit(solution)/shard_map/pallas_call | solution.py:516
  105.1 5.2 %collective-permute-done.9.refs_4_ = bf16[320,768]{1,0:T(8,128)(2,1)S(1)} collective-permute-done((bf16[320,768]{1,0:T(8,128)(2,1)S(1)}, bf16[320,768]{1,0:T(8,128)(2,1)S(1)}, u32[]{:S(2)}, u32[]{:S(2)}) %collective-permute-start.9) | collective-permute-done | bytes 491552 | tf_op jit(solution)/shard_map/ppermute | solution.py:681
  110.3 2.4 %collective-permute-done.8.refs_1_ = bf16[320,768]{1,0:T(8,128)(2,1)S(1)} collective-permute-done((bf16[320,768]{1,0:T(8,128)(2,1)S(1)}, bf16[320,768]{1,0:T(8,128)(2,1)S(1)}, u32[]{:S(2)}, u32[]{:S(2)}) %collective-permute-start.8) | collective-permute-done | bytes 491552 | tf_op jit(solution)/shard_map/ppermute | solution.py:681
  112.7 1.5 shard_map.138
  115.0 1.2 collective-permute-start.10
  116.9 1.1 copy-done.9
  118.0 1.1 copy-done.11
  122.0 2.9 %copy-done.1 = bf16[2560,1280]{1,0:T(8,128)(2,1)S(1)} copy-done((bf16[2560,1280]{1,0:T(8,128)(2,1)S(1)}, bf16[2560,1280]{1,0:T(8,128)(2,1)}, u32[]{:S(2)}) %copy-start.1) | copy-done | bytes 6553624
  124.8 3.5 %shard_map.141 = (bf16[320,256]{1,0:T(8,128)(2,1)S(1)}, bf16[320,256]{1,0:T(8,128)(2,1)S(1)}, f32[320,256]{1,0:T(8,128)S(1)}, f32[320,256]{1,0:T(8,128)S(1)}, bf...) custom-call(s32[4]{0:T(128)S(1)} %dynamic-slice_bitcast_fusion.order, ...), custom_call_target="tpu_custom_call" | custom-call | flops 1761607680 | bytes 10485760 | tf_op jit(solution)/shard_map/pallas_call | solution.py:644
  128.3 1.1 collective-permute-start.14
  129.4 2.2 %collective-permute-start.15 = (bf16[320,256]{1,0:T(8,128)(2,1)S(1)}, bf16[320,256]{1,0:T(8,128)(2,1)S(1)}, u32[]{:S(2)}, u32[]{:S(2)}) collective-permute-start(bf16[320,256]{1,0:T(8,128)(2,1)S(1)} %get-tuple-element.104), channel_id=1, source_target_pairs={{0,3},{1,0},{2,1},{3,2},{4,7},{5,4},{6,5},{7,6},{8,11},{9,8},{10,9... | collective-permute-start | bytes 491528 | tf_op jit(solution)/shard_map/ppermute | solution.py:685
  131.6 1.8 %shard_map.140 = (bf16[80,768]{1,0:T(8,128)(2,1)S(1)}, bf16[80,768]{1,0:T(8,128)(2,1)S(1)}, f32[80,768]{1,0:T(8,128)S(1)}, f32[80,768]{1,0:T(8,128)S(1)}, bf16[8...) custom-call(f32[320,768]{1,0:T(8,128)S(1)} %get-tuple-element.89.here_a.tie,, ...), custom_call_target="tpu_custom_call" | custom-call | flops 1000000 | bytes 4194304 | tf_op jit(solution)/shard_map/pallas_call | solution.py:570
  134.3 2.5 %collective-permute-start.13 = (bf16[80,768]{1,0:T(8,128)(2,1)S(1)}, bf16[80,768]{1,0:T(8,128)(2,1)S(1)}, u32[]{:S(2)}, u32[]{:S(2)}) collective-permute-start(bf16[80,768]{1,0:T(8,128)(2,1)S(1)} %get-tuple-element.98), channel_id=1, source_target_pairs={{0,24},{4,100},{8,0},{12,108},{16,8},{20,116},{24,16},{28,124},{32... | collective-permute-start | bytes 368648 | tf_op jit(solution)/shard_map/ppermute | solution.py:681
  136.8 2.8 %collective-permute-done.12.refs_1_ = bf16[80,768]{1,0:T(8,128)(2,1)S(1)} collective-permute-done((bf16[80,768]{1,0:T(8,128)(2,1)S(1)}, bf16[80,768]{1,0:T(8,128)(2,1)S(1)}, u32[]{:S(2)}, u32[]{:S(2)}) %collective-permute-start.12) | collective-permute-done | bytes 122912 | tf_op jit(solution)/shard_map/ppermute | solution.py:681
  139.9 3.2 %collective-permute-start.19 = (bf16[640,256]{1,0:T(8,128)(2,1)S(1)}, bf16[640,256]{1,0:T(8,128)(2,1)S(1)}, u32[]{:S(2)}, u32[]{:S(2)}) collective-permute-start(bf16[640,256]{1,0:T(8,128)(2,1)S(1)} %get-tuple-element.110), channel_id=1, source_target_pairs={{0,3},{1,0},{2,1},{3,2},{4,7},{5,4},{6,5},{7,6},{8,11},{9,8},{10,9... | collective-permute-start | bytes 983048 | tf_op jit(solution)/shard_map/ppermute | solution.py:685
  143.6 2.7 %collective-permute-start.17 = (bf16[160,768]{1,0:T(8,128)(2,1)S(1)}, bf16[160,768]{1,0:T(8,128)(2,1)S(1)}, u32[]{:S(2)}, u32[]{:S(2)}) collective-permute-start(bf16[160,768]{1,0:T(8,128)(2,1)S(1)} %get-tuple-element.107), channel_id=1, source_target_pairs={{0,24},{4,100},{8,0},{12,108},{16,8},{20,116},{24,16},{28,124},{32... | collective-permute-start | bytes 737288 | tf_op jit(solution)/shard_map/ppermute | solution.py:681
  146.4 1.8 %shard_map.144 = f32[20,256]{1,0:T(8,128)} custom-call(f32[1280,128]{1,0:T(8,128)S(1)} %get-tuple-element.78.tie.fore, f32[1280,128]{1,0:T(8,128)S(1)} %get-tuple-element.75.back, f32[256,128]{1,0:T(8,128)S(1)} %copy-done.39, bf16[1280,256]{1,0:T(8,128)(2,1)S(1)} %get-tuple-element.68.dyt, f32[20,256]{1,0:T(8,128)S(1)} %copy-done.33, ...), custom_call_target="tpu_custom_call" | custom-call | flops 167772160 | bytes 4194304 | tf_op jit(solution)/shard_map/pallas_call | solution.py:434
  148.2 2.3 %collective-permute-done.16.up = bf16[160,768]{1,0:T(8,128)(2,1)S(1)} collective-permute-done((bf16[160,768]{1,0:T(8,128)(2,1)S(1)}, bf16[160,768]{1,0:T(8,128)(2,1)S(1)}, u32[]{:S(2)}, u32[]{:S(2)}) %collective-permute-start.16) | collective-permute-done | bytes 245792 | tf_op jit(solution)/shard_map/ppermute | solution.py:681
  150.5 1.0 shard_map.143
  (121 shorter events, 16.7 us)
Async XLA Ops:
  1.5 9.8 %collective-permute-start = (bf16[16,2560]{1,0:T(8,128)(2,1)S(1)}, bf16[16,2560]{1,0:T(8,128)(2,1)S(1)}, u32[]{:S(2)}, u32[]{:S(2)}) collective-permute-start(bf16[16,2560]{1,0:T(8,128)(2,1)S(1)} %slice.3), channel_id=1, source_target_pairs={{0,4},{4,8},{8,12},{12,16},{16,20},{20,24},{24,28},{28,32},{32,36}... | collective-permute-start | bytes 245768 | tf_op jit(solution)/shard_map/ppermute | solution.py:717
  8.0 3.3 %copy-start.42 = (f32[4,1280]{1,0:T(4,128)S(1)}, f32[4,1280]{1,0:T(4,128)}, u32[]{:S(2)}) copy-start(f32[4,1280]{1,0:T(4,128)} %taps.1) | copy-start | bytes 61444
  11.3 10.1 %copy-start.30 = (f32[20,256]{1,0:T(8,128)}, f32[20,256]{1,0:T(8,128)S(1)}, u32[]{:S(2)}) copy-start(f32[20,256]{1,0:T(8,128)S(1)} %get-tuple-element.60.cum) | copy-start | bytes 61444
  11.3 10.1 %copy-start.34 = (f32[20,256]{1,0:T(8,128)}, f32[20,256]{1,0:T(8,128)S(1)}, u32[]{:S(2)}) copy-start(f32[20,256]{1,0:T(8,128)S(1)} %get-tuple-element.61.logd) | copy-start | bytes 61444
  11.3 2.9 %copy-start = (bf16[2560,1280]{1,0:T(8,128)(2,1)S(1)}, bf16[2560,1280]{1,0:T(8,128)(2,1)}, u32[]{:S(2)}) copy-start(bf16[2560,1280]{1,0:T(8,128)(2,1)} %w_x.3) | copy-start | bytes 19660804
  24.2 9.9 %copy-start.3 = (bf16[256,2560]{1,0:T(8,128)(2,1)S(1)}, bf16[256,2560]{1,0:T(8,128)(2,1)}, u32[]{:S(2)}) copy-start(bf16[256,2560]{1,0:T(8,128)(2,1)} %normed.5) | copy-start | bytes 3932164
  24.2 30.7 %all-to-all-start = ((f32[32,88,128]{2,1,0:T(8,128)}), f32[32,88,128]{2,1,0:T(8,128)S(1)}, u32[]{:S(2)}, u32[]{:S(2)}) async-start(f32[32,88,128]{2,1,0:T(8,128)} %get-tuple-element.65.tie), calls=%async_computation | async-start | bytes 2883584 | tf_op jit(solution)/shard_map/all_to_all | solution.py:723
  34.1 1.9 %copy-start.19 = (bf16[1280,256]{1,0:T(8,128)(2,1)S(1)}, bf16[1280,256]{1,0:T(8,128)(2,1)}, u32[]{:S(2)}) copy-start(bf16[1280,256]{1,0:T(8,128)(2,1)} %copy-done.18) | copy-start | bytes 1966084
  41.4 30.4 %copy-start.40 = (f32[20,256]{1,0:T(8,128)}, f32[20,256]{1,0:T(8,128)S(1)}, u32[]{:S(2)}) copy-start(f32[20,256]{1,0:T(8,128)S(1)} %get-tuple-element.71.tie.rc) | copy-start | bytes 61444
  54.9 16.9 %copy-start.22 = (bf16[1280,256]{1,0:T(8,128)(2,1)S(1)}, bf16[1280,256]{1,0:T(8,128)(2,1)}, u32[]{:S(2)}) copy-start(bf16[1280,256]{1,0:T(8,128)(2,1)} %copy-done.21) | copy-start | bytes 1966084
  54.9 16.9 %copy-start.24 = (bf16[1280,256]{1,0:T(8,128)(2,1)S(1)}, bf16[1280,256]{1,0:T(8,128)(2,1)}, u32[]{:S(2)}) copy-start(bf16[1280,256]{1,0:T(8,128)(2,1)} %copy-done.23) | copy-start | bytes 1966084
  71.8 14.1 %copy-start.32 = (f32[20,256]{1,0:T(8,128)S(1)}, f32[20,256]{1,0:T(8,128)}, u32[]{:S(2)}) copy-start(f32[20,256]{1,0:T(8,128)} %copy-done.30) | copy-start | bytes 61444
  71.8 14.1 %copy-start.35 = (f32[20,256]{1,0:T(8,128)S(1)}, f32[20,256]{1,0:T(8,128)}, u32[]{:S(2)}) copy-start(f32[20,256]{1,0:T(8,128)} %copy-done.34) | copy-start | bytes 61444
  71.8 14.1 %copy-start.43 = (f32[4,1280]{1,0:T(4,128)S(1)}, f32[4,1280]{1,0:T(4,128)}, u32[]{:S(2)}) copy-start(f32[4,1280]{1,0:T(4,128)} %taps.1) | copy-start | bytes 61444
  71.8 14.1 %copy-start.49 = (f32[20]{0:T(128)S(1)}, f32[20]{0:T(128)}, u32[]{:S(2)}) copy-start(f32[20]{0:T(128)} %skip.1) | copy-start | bytes 244
  72.4 9.2 %collective-permute-start.5 = (f32[256,256]{1,0:T(8,128)S(1)}, f32[256,256]{1,0:T(8,128)S(1)}, u32[]{:S(2)}, u32[]{:S(2)}) collective-permute-start(f32[256,256]{1,0:T(8,128)S(1)} %get-tuple-element.81), channel_id=1, source_target_pairs={{0,1},{1,0},{2,3},{3,2},{4,5},{5,4},{6,7},{7,6},{8,9},{9,8},{10,11... | collective-permute-start | bytes 786440 | tf_op jit(solution)/shard_map/ppermute | solution.py:732
  82.2 14.4 %collective-permute-start.6 = (f32[256,256]{1,0:T(8,128)}, f32[256,256]{1,0:T(8,128)}, u32[]{:S(2)}, u32[]{:S(2)}) collective-permute-start(f32[256,256]{1,0:T(8,128)} %add.26), channel_id=1, source_target_pairs={{0,2},{1,3},{2,0},{3,1},{4,6},{5,7},{6,4},{7,5},{8,10},{9,11},{10,... | collective-permute-start | bytes 786440 | tf_op jit(solution)/shard_map/ppermute | solution.py:732
  85.9 12.8 %collective-permute-start.1 = (bf16[1280,256]{1,0:T(8,128)(2,1)}, bf16[1280,256]{1,0:T(8,128)(2,1)S(1)}, u32[]{:S(2)}, u32[]{:S(2)}) collective-permute-start(bf16[1280,256]{1,0:T(8,128)(2,1)} %copy-done.50), channel_id=1, source_target_pairs={{0,4},{4,0},{8,12},{12,8},{16,20},{20,16},{24,28},{28,24},{32,36},... | collective-permute-start | bytes 1966088 | tf_op jit(solution)/shard_map/ppermute | solution.py:725
  89.7 9.4 %copy-start.7 = (bf16[1280,256]{1,0:T(8,128)(2,1)S(1)}, bf16[1280,256]{1,0:T(8,128)(2,1)}, u32[]{:S(2)}) copy-start(bf16[1280,256]{1,0:T(8,128)(2,1)} %copy-done.6) | copy-start | bytes 1966084
  92.8 7.2 %copy-start.45 = (f32[20,256]{1,0:T(8,128)}, f32[20,256]{1,0:T(8,128)S(1)}, u32[]{:S(2)}) copy-start(f32[20,256]{1,0:T(8,128)S(1)} %get-tuple-element.114.halves) | copy-start | bytes 61444
  92.8 7.2 %copy-start.47 = (f32[20,256]{1,0:T(8,128)}, f32[20,256]{1,0:T(8,128)S(1)}, u32[]{:S(2)}) copy-start(f32[20,256]{1,0:T(8,128)S(1)} %get-tuple-element.115.cross) | copy-start | bytes 61444
  92.8 5.9 %collective-permute-start.4 = (f32[8,1280]{1,0:T(8,128)S(1)}, f32[8,1280]{1,0:T(8,128)S(1)}, u32[]{:S(2)}, u32[]{:S(2)}) collective-permute-start(f32[8,1280]{1,0:T(8,128)S(1)} %get-tuple-element.80), channel_id=1, source_target_pairs={{8,0},{16,8},{24,16},{32,24},{40,32},{48,40},{56,48},{64,56},{72,6... | collective-permute-start | bytes 122888 | tf_op jit(solution)/shard_map/ppermute | solution.py:739
  94.1 4.6 %collective-permute-start.3 = (f32[8,1280]{1,0:T(8,128)S(1)}, f32[8,1280]{1,0:T(8,128)S(1)}, u32[]{:S(2)}, u32[]{:S(2)}) collective-permute-start(f32[8,1280]{1,0:T(8,128)S(1)} %get-tuple-element.80), channel_id=1, source_target_pairs={{4,0},{8,4},{12,8},{16,12},{20,16},{24,20},{28,24},{32,28},{36,32}... | collective-permute-start | bytes 122888 | tf_op jit(solution)/shard_map/ppermute | solution.py:738
  95.4 3.7 %collective-permute-start.2 = (bf16[256,1280]{1,0:T(8,128)(2,1)S(1)}, bf16[256,1280]{1,0:T(8,128)(2,1)S(1)}, u32[]{:S(2)}, u32[]{:S(2)}) collective-permute-start(bf16[256,1280]{1,0:T(8,128)(2,1)S(1)} %get-tuple-element.79.refs_2_.grad), channel_id=1, source_target_pairs={{0,4},{4,0},{8,12},{12,8},{16,20},{20,16},{24,28},{28,24},{32,36},... | collective-permute-start | bytes 1966088 | tf_op jit(solution)/shard_map/ppermute | solution.py:737
  97.7 1.4 collective-permute-start.7
  98.7 4.9 %copy-start.25 = (f32[8,1280]{1,0:T(8,128)}, f32[8,1280]{1,0:T(8,128)S(1)}, u32[]{:S(2)}) copy-start(f32[8,1280]{1,0:T(8,128)S(1)} %broadcast_select_fusion.refs_5_) | copy-start | bytes 122884
  98.7 4.9 %copy-start.8 = (bf16[1280,256]{1,0:T(8,128)(2,1)}, bf16[1280,256]{1,0:T(8,128)(2,1)S(1)}, u32[]{:S(2)}) copy-start(bf16[1280,256]{1,0:T(8,128)(2,1)S(1)} %collective-permute-done.1.refs_1_) | copy-start | bytes 1966084
  98.7 4.9 %copy-start.27 = (f32[8,1280]{1,0:T(8,128)}, f32[8,1280]{1,0:T(8,128)S(1)}, u32[]{:S(2)}) copy-start(f32[8,1280]{1,0:T(8,128)S(1)} %collective-permute-done.3.refs_4_.halo) | copy-start | bytes 122884
  99.1 4.5 %copy-start.10 = (bf16[256,1280]{1,0:T(8,128)(2,1)}, bf16[256,1280]{1,0:T(8,128)(2,1)S(1)}, u32[]{:S(2)}) copy-start(bf16[256,1280]{1,0:T(8,128)(2,1)S(1)} %collective-permute-done.2.refs_3_) | copy-start | bytes 1966084
  100.0 10.3 %collective-permute-start.9 = (bf16[320,768]{1,0:T(8,128)(2,1)S(1)}, bf16[320,768]{1,0:T(8,128)(2,1)S(1)}, u32[]{:S(2)}, u32[]{:S(2)}) collective-permute-start(bf16[320,768]{1,0:T(8,128)(2,1)S(1)} %get-tuple-element.86), channel_id=1, source_target_pairs={{0,96},{4,28},{8,104},{12,4},{16,112},{20,12},{24,120},{28,20},{32... | collective-permute-start | bytes 1474568 | tf_op jit(solution)/shard_map/ppermute | solution.py:681
  102.7 10.0 %collective-permute-start.8 = (bf16[320,768]{1,0:T(8,128)(2,1)S(1)}, bf16[320,768]{1,0:T(8,128)(2,1)S(1)}, u32[]{:S(2)}, u32[]{:S(2)}) collective-permute-start(bf16[320,768]{1,0:T(8,128)(2,1)S(1)} %get-tuple-element.82.refs_8_), channel_id=1, source_target_pairs={{0,32},{4,12},{8,40},{12,20},{16,48},{20,28},{24,56},{28,4},{32,64... | collective-permute-start | bytes 1474568 | tf_op jit(solution)/shard_map/ppermute | solution.py:681
  114.2 17.4 %collective-permute-start.11 = (bf16[640,768]{1,0:T(8,128)(2,1)}, bf16[640,768]{1,0:T(8,128)(2,1)}, u32[]{:S(2)}, u32[]{:S(2)}) collective-permute-start(bf16[640,768]{1,0:T(8,128)(2,1)} %get-tuple-element.91), channel_id=1, source_target_pairs={{0,96},{4,28},{8,104},{12,4},{16,112},{20,12},{24,120},{28,20},{32... | collective-permute-start | bytes 2949128 | tf_op jit(solution)/shard_map/ppermute | solution.py:681
  115.0 16.6 %collective-permute-start.10 = (bf16[640,768]{1,0:T(8,128)(2,1)}, bf16[640,768]{1,0:T(8,128)(2,1)}, u32[]{:S(2)}, u32[]{:S(2)}) collective-permute-start(bf16[640,768]{1,0:T(8,128)(2,1)} %get-tuple-element.88.refs_8_), channel_id=1, source_target_pairs={{0,32},{4,12},{8,40},{12,20},{16,48},{20,28},{24,56},{28,4},{32,64... | collective-permute-start | bytes 2949128 | tf_op jit(solution)/shard_map/ppermute | solution.py:681
  122.0 2.9 %copy-start.1 = (bf16[2560,1280]{1,0:T(8,128)(2,1)S(1)}, bf16[2560,1280]{1,0:T(8,128)(2,1)}, u32[]{:S(2)}) copy-start(bf16[2560,1280]{1,0:T(8,128)(2,1)} %w_x.3) | copy-start | bytes 19660804
  128.3 8.5 %collective-permute-start.14 = (bf16[320,256]{1,0:T(8,128)(2,1)S(1)}, bf16[320,256]{1,0:T(8,128)(2,1)S(1)}, u32[]{:S(2)}, u32[]{:S(2)}) collective-permute-start(bf16[320,256]{1,0:T(8,128)(2,1)S(1)} %get-tuple-element.101), channel_id=1, source_target_pairs={{0,1},{1,2},{2,3},{3,0},{4,5},{5,6},{6,7},{7,4},{8,9},{9,10},{10,1... | collective-permute-start | bytes 491528 | tf_op jit(solution)/shard_map/ppermute | solution.py:685
  129.4 7.4 %collective-permute-start.15 = (bf16[320,256]{1,0:T(8,128)(2,1)S(1)}, bf16[320,256]{1,0:T(8,128)(2,1)S(1)}, u32[]{:S(2)}, u32[]{:S(2)}) collective-permute-start(bf16[320,256]{1,0:T(8,128)(2,1)S(1)} %get-tuple-element.104), channel_id=1, source_target_pairs={{0,3},{1,0},{2,1},{3,2},{4,7},{5,4},{6,5},{7,6},{8,11},{9,8},{10,9... | collective-permute-start | bytes 491528 | tf_op jit(solution)/shard_map/ppermute | solution.py:685
  133.4 12.9 %copy-start.33 = (f32[20,256]{1,0:T(8,128)S(1)}, f32[20,256]{1,0:T(8,128)}, u32[]{:S(2)}) copy-start(f32[20,256]{1,0:T(8,128)} %copy-done.30) | copy-start | bytes 61444
  133.4 12.9 %copy-start.36 = (f32[20,256]{1,0:T(8,128)S(1)}, f32[20,256]{1,0:T(8,128)}, u32[]{:S(2)}) copy-start(f32[20,256]{1,0:T(8,128)} %copy-done.34) | copy-start | bytes 61444
  133.5 12.9 %copy-start.39 = (f32[256,128]{1,0:T(8,128)S(1)}, f32[256,128]{1,0:T(8,128)}, u32[]{:S(2)}) copy-start(f32[256,128]{1,0:T(8,128)} %copy-done.37) | copy-start | bytes 393220
  133.5 12.9 %copy-start.41 = (f32[20,256]{1,0:T(8,128)S(1)}, f32[20,256]{1,0:T(8,128)}, u32[]{:S(2)}) copy-start(f32[20,256]{1,0:T(8,128)} %copy-done.40) | copy-start | bytes 61444
  133.5 12.9 %copy-start.46 = (f32[20,256]{1,0:T(8,128)S(1)}, f32[20,256]{1,0:T(8,128)}, u32[]{:S(2)}) copy-start(f32[20,256]{1,0:T(8,128)} %copy-done.45) | copy-start | bytes 61444
  133.5 12.9 %copy-start.48 = (f32[20,256]{1,0:T(8,128)S(1)}, f32[20,256]{1,0:T(8,128)}, u32[]{:S(2)}) copy-start(f32[20,256]{1,0:T(8,128)} %copy-done.47) | copy-start | bytes 61444
  133.5 6.2 %collective-permute-start.12 = (bf16[80,768]{1,0:T(8,128)(2,1)S(1)}, bf16[80,768]{1,0:T(8,128)(2,1)S(1)}, u32[]{:S(2)}, u32[]{:S(2)}) collective-permute-start(bf16[80,768]{1,0:T(8,128)(2,1)S(1)} %get-tuple-element.95), channel_id=1, source_target_pairs={{0,8},{4,36},{8,16},{12,44},{16,24},{20,52},{24,0},{28,60},{32,40}... | collective-permute-start | bytes 368648 | tf_op jit(solution)/shard_map/ppermute | solution.py:681
  134.3 5.3 %collective-permute-start.13 = (bf16[80,768]{1,0:T(8,128)(2,1)S(1)}, bf16[80,768]{1,0:T(8,128)(2,1)S(1)}, u32[]{:S(2)}, u32[]{:S(2)}) collective-permute-start(bf16[80,768]{1,0:T(8,128)(2,1)S(1)} %get-tuple-element.98), channel_id=1, source_target_pairs={{0,24},{4,100},{8,0},{12,108},{16,8},{20,116},{24,16},{28,124},{32... | collective-permute-start | bytes 368648 | tf_op jit(solution)/shard_map/ppermute | solution.py:681
  139.8 10.7 %collective-permute-start.18 = (bf16[640,256]{1,0:T(8,128)(2,1)S(1)}, bf16[640,256]{1,0:T(8,128)(2,1)S(1)}, u32[]{:S(2)}, u32[]{:S(2)}) collective-permute-start(bf16[640,256]{1,0:T(8,128)(2,1)S(1)} %get-tuple-element.109), channel_id=1, source_target_pairs={{0,1},{1,2},{2,3},{3,0},{4,5},{5,6},{6,7},{7,4},{8,9},{9,10},{10,1... | collective-permute-start | bytes 983048 | tf_op jit(solution)/shard_map/ppermute | solution.py:685
  139.9 10.6 %collective-permute-start.19 = (bf16[640,256]{1,0:T(8,128)(2,1)S(1)}, bf16[640,256]{1,0:T(8,128)(2,1)S(1)}, u32[]{:S(2)}, u32[]{:S(2)}) collective-permute-start(bf16[640,256]{1,0:T(8,128)(2,1)S(1)} %get-tuple-element.110), channel_id=1, source_target_pairs={{0,3},{1,0},{2,1},{3,2},{4,7},{5,4},{6,5},{7,6},{8,11},{9,8},{10,9... | collective-permute-start | bytes 983048 | tf_op jit(solution)/shard_map/ppermute | solution.py:685
  143.1 7.4 %collective-permute-start.16 = (bf16[160,768]{1,0:T(8,128)(2,1)S(1)}, bf16[160,768]{1,0:T(8,128)(2,1)S(1)}, u32[]{:S(2)}, u32[]{:S(2)}) collective-permute-start(bf16[160,768]{1,0:T(8,128)(2,1)S(1)} %get-tuple-element.106), channel_id=1, source_target_pairs={{0,8},{4,36},{8,16},{12,44},{16,24},{20,52},{24,0},{28,60},{32,40}... | collective-permute-start | bytes 737288 | tf_op jit(solution)/shard_map/ppermute | solution.py:681
  143.6 6.9 %collective-permute-start.17 = (bf16[160,768]{1,0:T(8,128)(2,1)S(1)}, bf16[160,768]{1,0:T(8,128)(2,1)S(1)}, u32[]{:S(2)}, u32[]{:S(2)}) collective-permute-start(bf16[160,768]{1,0:T(8,128)(2,1)S(1)} %get-tuple-element.107), channel_id=1, source_target_pairs={{0,24},{4,100},{8,0},{12,108},{16,8},{20,116},{24,16},{28,124},{32... | collective-permute-start | bytes 737288 | tf_op jit(solution)/shard_map/ppermute | solution.py:681
  (24 other events, 27.4 us)

commit v3 on v2

--- a/solution.py
+++ b/solution.py
@@ -21,7 +21,7 @@
 ZS = 4
 ROWS = 80
 SLICE = 40
-MSG = 88
+MSG = 48
 BLK = 256
 NBLK = CH // BLK
 SCALE = STATE ** (-0.5)
@@ -29,7 +29,6 @@
 BF16 = jnp.bfloat16
 HIGH = lax.Precision.HIGHEST
 NT = (((1,), (1,)), ((), ()))
-VMEM = 20 * 2**20
 
 
 def nt(a, b):
@@ -51,8 +50,8 @@
     return dot(a_high, b_high) + (dot(a_low, b_high) + dot(a_high, b_low))
 
 
-def params():
-    return pltpu.CompilerParams(vmem_limit_bytes=VMEM)
+def params(mib=14):
+    return pltpu.CompilerParams(vmem_limit_bytes=mib * 2**20)
 
 
 def cost(flops, nbytes, trans=0):
@@ -69,7 +68,7 @@
     return jnp.where(row <= col if upper else row >= col, 1.0, 0.0).astype(F32)
 
 
-def front_kernel(normed, w_bc, rates, step, grad_y, bmat, cmat, cum, logd, dyt, dywt, pulled, through, turn):
+def front_kernel(normed, w_bc, rates, step, grad_y, bmat, cmat, cum, logd, dyt, dywt, msg, pulled, turn):
     shared = nn(normed[...], w_bc[...])
     bmat[...] = shared[:, :STATE]
     cmat[...] = shared[:, STATE:]
@@ -96,7 +95,10 @@
         pulled[rows, :] = nn(high, c_high) + (nn(low, c_high) + nn(high, c_low))
     turn[...] = jnp.zeros((128, 128), F32)
     turn[:HEADS, :] = grown[:, 128:]
-    through[...] = jnp.broadcast_to(turn[...].T[127:, :], (8, STATE))
+    through = jnp.broadcast_to(turn[...].T[127:, :], (MSG - SLICE, STATE))
+    for k in range(SEQ):
+        msg[k, :SLICE, :] = pulled[SLICE * k : SLICE * (k + 1), :]
+        msg[k, SLICE:, :] = through
 
 
 def front(normed, w_bc, rates, step, grad_y):
@@ -109,135 +111,109 @@
             jax.ShapeDtypeStruct((HEADS, T), F32),
             jax.ShapeDtypeStruct((CH, T), BF16),
             jax.ShapeDtypeStruct((CH, T), BF16),
-            jax.ShapeDtypeStruct((CH, STATE), F32),
-            jax.ShapeDtypeStruct((8, STATE), F32),
-        ),
-        scratch_shapes=[pltpu.VMEM((128, 128), F32)],
+            jax.ShapeDtypeStruct((SEQ, MSG, STATE), F32),
+        ),
+        scratch_shapes=[pltpu.VMEM((CH, STATE), F32), pltpu.VMEM((128, 128), F32)],
         compiler_params=params(),
         cost_estimate=cost(2 * T * D * 256 + 6 * CH * T * 128, 6 * 2**20),
     )(normed, w_bc, rates, step, grad_y)
 
 
-def chain_kernel(table, recv, tie, out, turn):
+def chain_kernel(reverse, table, recv, decays, tie, out, turn):
     del tie
-    lanes = jnp.concatenate([recv[:, 2 * SLICE, :], jnp.zeros((128 - SEQ, 128), F32)], axis=0)
+    lanes = jnp.concatenate([decays[:, 0, :], jnp.zeros((128 - SEQ, 128), F32)], axis=0)
     turn[...] = lanes.T
     head = table[32]
     row = lax.broadcasted_iota(jnp.int32, (SLICE, 128), 0)
     cols = jnp.where(row < table[33], turn[pl.ds(head, 1), :], turn[pl.ds(head + 1, 1), :])
-    pulled = jnp.zeros((SLICE, STATE), F32)
-    pulls = [None] * SEQ
-    for k in range(SEQ - 1, -1, -1):
-        pulls[k] = pulled
-        pulled = cols[:, k : k + 1] * pulled + recv[k, :SLICE, :]
     state = jnp.zeros((SLICE, STATE), F32)
-    for k in range(SEQ):
-        out[k] = jnp.concatenate([pulls[k], state], axis=0).astype(BF16)
-        state = cols[:, k : k + 1] * state + recv[k, SLICE : 2 * SLICE, :]
-
-
-def chain(table, recv, tie):
-    return pl.pallas_call(
-        chain_kernel,
+    for k in range(SEQ - 1, -1, -1) if reverse else range(SEQ):
+        out[k] = state.astype(out.dtype)
+        state = cols[:, k : k + 1] * state + recv[k]
+
+
+def chain(table, recv, pulls, tie, reverse):
+    return pl.pallas_call(
+        functools.partial(chain_kernel, reverse),
         grid=(1,),
         in_specs=[
             pl.BlockSpec(memory_space=pltpu.SMEM),
-            whole(SEQ, MSG, STATE),
+            whole(SEQ, SLICE, STATE),
+            pl.BlockSpec((SEQ, MSG - SLICE, STATE), lambda i: (0, SLICE // 8, 0)),
             pl.BlockSpec(memory_space=pl.ANY),
         ],
-        out_specs=whole(SEQ, 2 * SLICE, STATE),
-        out_shape=jax.ShapeDtypeStruct((SEQ, 2 * SLICE, STATE), BF16),
+        out_specs=whole(SEQ, SLICE, STATE),
+        out_shape=jax.ShapeDtypeStruct((SEQ, SLICE, STATE), F32),
         scratch_shapes=[pltpu.VMEM((128, 128), F32)],
         compiler_params=params(),
-        cost_estimate=cost(10**6, 3 * 2**20),
-    )(table, recv, tie)
+        cost_estimate=cost(10**6, 2 * 2**20),
+    )(table, recv, pulls, tie)
 
 
 def channel_kernel(
-    before, normed, w_x, conv_w, cum, logd, bmat, pulled, through, xgt, slope, xwt, msg, ext, pre, own
+    before, normed, conv_w, cum, logd, w_x, xgt, slope, xwt, xlt, ext, pre, held, sems
 ):
-    step = pl.program_id(0)
-
-    @pl.when(step == 0)
-    def _():
-        ext[:16, :] = before[...]
-        ext[16:, :] = normed[...]
-
-    now = lax.rem(step, 2)
-    past = pre.at[1 - now]
-    total = conv_w[0:1, :] * past[16 : 16 + T, :]
-    for tap in range(1, CONV):
-        total = total + conv_w[tap : tap + 1, :] * past[16 - tap : 16 - tap + T, :]
-    sig = 0.5 * jnp.tanh(0.5 * total) + 0.5
-    xt = (total * sig).T
-    slope[...] = sig * (1.0 + total * (1.0 - sig))
-    parts = []
-    block = jnp.maximum(step - 1, 0)
-    for q in range(BLK // HEAD_DIM):
-        head = pl.ds(block * (BLK // HEAD_DIM) + q, 1)
-        rows = slice(64 * q, 64 * q + 64)
-        gain = jnp.sqrt(-2.0 * logd[head, :])
-        cums = cum[head, :]
-        tail = jnp.exp(cums[:, T - 1 :] - cums)
-        xg = xt[rows] * gain
-        xgt[rows, :] = xg.astype(BF16)
-        parts.append(xg * tail)
-    weighted = jnp.concatenate(parts, axis=0)
-    xwt[...] = weighted.astype(BF16)
-    own[pl.ds(pl.multiple_of(block * BLK, BLK), BLK), :] = wide(nn, weighted, bmat[...])
-    pre[now] = nn(ext[...], w_x[...]).astype(BF16).astype(F32)
-
-    @pl.when(step == NBLK)
-    def _():
-        for k in range(SEQ):
-            rows = slice(SLICE * k, SLICE * (k + 1))
-            msg[k, :SLICE, :] = pulled[rows, :]
-            msg[k, SLICE : 2 * SLICE, :] = own[rows, :]
-            msg[k, 2 * SLICE :, :] = through[...]
-
-
-def channels(before, normed, w_x, conv_w, cum, logd, bmat, pulled, through):
-    def late(i):
-        return jnp.maximum(i - 1, 0)
-
-    rows = pl.BlockSpec((BLK, T), lambda i: (late(i), 0))
+    copies = [
+        pltpu.make_async_copy(w_x.at[:, pl.ds(BLK * i, BLK)], held.at[i], sems.at[i])
+        for i in range(NBLK)
+    ]
+    for one in copies:
+        one.start()
+    ext[:16, :] = before[...]
+    ext[16:, :] = normed[...]
+    for i in range(NBLK + 1):
+        if i < NBLK:
+            copies[i].wait()
+            pre[i % 2] = nn(ext[...], held[i]).astype(BF16).astype(F32)
+        if i == 0:
+            continue
+        block = i - 1
+        past = pre.at[block % 2]
+        cols = slice(BLK * block, BLK * (block + 1))
+        total = conv_w[0:1, cols] * past[16 : 16 + T, :]
+        for tap in range(1, CONV):
+            total = total + conv_w[tap : tap + 1, cols] * past[16 - tap : 16 - tap + T, :]
+        sig = 0.5 * jnp.tanh(0.5 * total) + 0.5
+        xt = (total * sig).T
+        slope[:, cols] = sig * (1.0 + total * (1.0 - sig))
+        for q in range(BLK // HEAD_DIM):
+            h = block * (BLK // HEAD_DIM) + q
+            rows = slice(64 * h, 64 * h + 64)
+            gain = jnp.sqrt(-2.0 * logd[h : h + 1, :])
+            cums = cum[h : h + 1, :]
+            tail = jnp.exp(cums[:, T - 1 :] - cums)
+            xg = xt[64 * q : 64 * q + 64] * gain
+            xgt[rows, :] = xg.astype(BF16)
+            high, low = split(xg * tail)
+            xwt[rows, :] = high
+            xlt[rows, :] = low
+
+
+def channels(before, normed, conv_w, cum, logd, w_x):
+    vm = pl.BlockSpec(memory_space=pltpu.VMEM)
     return pl.pallas_call(
         channel_kernel,
-        grid=(NBLK + 1,),
-        in_specs=[
-            whole(16, D),
-            whole(T, D),
-            pl.BlockSpec((D, BLK), lambda i: (0, jnp.minimum(i, NBLK - 1))),
-            pl.BlockSpec((CONV, BLK), lambda i: (0, late(i))),
-            whole(HEADS, T),
-            whole(HEADS, T),
-            whole(T, STATE),
-            whole(CH, STATE),
-            whole(8, STATE),
-        ],
-        out_specs=(
-            rows,
-            pl.BlockSpec((T, BLK), lambda i: (0, late(i))),
-            rows,
-            whole(SEQ, MSG, STATE),
-        ),
+        in_specs=[vm] * 5 + [pl.BlockSpec(memory_space=pltpu.HBM)],
         out_shape=(
             jax.ShapeDtypeStruct((CH, T), BF16),
             jax.ShapeDtypeStruct((T, CH), F32),
             jax.ShapeDtypeStruct((CH, T), BF16),
-            jax.ShapeDtypeStruct((SEQ, MSG, STATE), F32),
+            jax.ShapeDtypeStruct((CH, T), BF16),
         ),
         scratch_shapes=[
             pltpu.VMEM((T + 16, D), BF16),
             pltpu.VMEM((2, T + 16, BLK), F32),
-            pltpu.VMEM((CH, STATE), F32),
+            pltpu.VMEM((NBLK, D, BLK), BF16),
+            pltpu.SemaphoreType.DMA((NBLK,)),
         ],
-        compiler_params=params(),
+        compiler_params=params(24),
         cost_estimate=cost(2 * T * D * CH, 10 * 2**20, T * CH),
-    )(before, normed, w_x, conv_w, cum, logd, bmat, pulled, through)
-
-
-def intra_kernel(grad_y, dyt, xgt, cum, bmat, cmat, tie, dxg, rc, dbc, gram, dgram):
+    )(before, normed, conv_w, cum, logd, w_x)
+
+
+def intra_kernel(
+    grad_y, dyt, xgt, xwt, xlt, cum, bmat, cmat, tie, dxg, rc, dbc, own, gram, dgram
+):
     del tie
     step = pl.program_id(0)
 
@@ -246,6 +222,8 @@
         gram[...] = wide(nt, cmat[...], bmat[...]) * SCALE
         dgram[...] = jnp.zeros((T, T), F32)
 
+    b_high, b_low = split(bmat[...])
+    own[...] = nn(xwt[...], b_high) + (nn(xlt[...], b_high) + nn(xwt[...], b_low))
     half = T // 2
     row = lax.broadcasted_iota(jnp.int32, (half, half), 0)
     col = lax.broadcasted_iota(jnp.int32, (half, half), 1)
@@ -287,13 +265,15 @@
         dbc[STATE:, :] = nn(dg, bmat[...].astype(BF16)).T
 
 
-def intra(grad_y, dyt, xgt, cum, bmat, cmat, tie):
+def intra(grad_y, dyt, xgt, xwt, xlt, cum, bmat, cmat, tie):
     rows = pl.BlockSpec((BLK, T), lambda i: (i, 0))
     return pl.pallas_call(
         intra_kernel,
         grid=(NBLK,),
         in_specs=[
             pl.BlockSpec((T, BLK), lambda i: (0, i)),
+            rows,
+            rows,
             rows,
             rows,
             whole(HEADS, T),
@@ -301,41 +281,67 @@
             whole(T, STATE),
             pl.BlockSpec(memory_space=pl.ANY),
         ],
-        out_specs=(rows, whole(HEADS, T), whole(2 * STATE, T)),
+        out_specs=(
+            rows,
+            whole(HEADS, T),
+            whole(2 * STATE, T),
+            pl.BlockSpec((BLK, STATE), lambda i: (i, 0)),
+        ),
         out_shape=(
             jax.ShapeDtypeStruct((CH, T), F32),
             jax.ShapeDtypeStruct((HEADS, T), F32),
             jax.ShapeDtypeStruct((2 * STATE, T), F32),
+            jax.ShapeDtypeStruct((CH, STATE), F32),
         ),
         scratch_shapes=[pltpu.VMEM((T, T), F32), pltpu.VMEM((T, T), F32)],
         compiler_params=params(),
         cost_estimate=cost(HEADS * 2 * T * T * 64 * 8, 4 * 2**20, HEADS * T * T),
-    )(grad_y, dyt, xgt, cum, bmat, cmat, tie)
-
-
-def shared_kernel(back, xwt, dywt, dbc, ds, st, shared):
-    for k in range(SEQ):
-        rows = slice(SLICE * k, SLICE * (k + 1))
-        both = back[k].astype(F32)
-        ds[rows, :] = both[:SLICE]
-        st[rows, :] = both[SLICE:]
+    )(grad_y, dyt, xgt, xwt, xlt, cum, bmat, cmat, tie)
+
+
+def shared_kernel(order, ds, st, xwt, dywt, dbc, tie, shared, *outs):
+    del tie
+    chunks, total = outs[:ZS], outs[ZS]
     for at, (state, tokens) in enumerate(((ds, xwt), (st, dywt))):
-        turned = state[...].T.astype(BF16)
-        part = nn(turned, tokens[...]) + dbc[STATE * at : STATE * (at + 1), :]
-        shared[:, STATE * at : STATE * (at + 1)] = part.T
-
-
-def shared_part(back, xwt, dywt, dbc):
+        rows = slice(STATE * at, STATE * (at + 1))
+        total[rows, :] = nn(state[...].T.astype(BF16), tokens[...]) + dbc[rows, :]
+    shared[...] = total[...].astype(BF16)
+    for r in range(ZS):
+        chunks[r][...] = total[pl.ds(pl.multiple_of(order[r] * 64, 64), 64), :]
+
+
+def shared_part(order, ds, st, xwt, dywt, dbc, tie):
+    vm = pl.BlockSpec(memory_space=pltpu.VMEM)
     return pl.pallas_call(
         shared_kernel,
-        out_shape=(
-            jax.ShapeDtypeStruct((CH, STATE), F32),
-            jax.ShapeDtypeStruct((CH, STATE), F32),
-            jax.ShapeDtypeStruct((T, 2 * STATE), F32),
-        ),
+        in_specs=[pl.BlockSpec(memory_space=pltpu.SMEM)]
+        + [vm] * 5
+        + [pl.BlockSpec(memory_space=pl.ANY)],
+        out_shape=(jax.ShapeDtypeStruct((2 * STATE, T), BF16),)
+        + (jax.ShapeDtypeStruct((64, T), F32),) * ZS,
+        scratch_shapes=[pltpu.VMEM((2 * STATE, T), F32)],
         compiler_params=params(),
         cost_estimate=cost(4 * CH * T * 128, 4 * 2**20),
-    )(back, xwt, dywt, dbc)
+    )(order, ds, st, xwt, dywt, dbc, tie)
+
+
+def small_kernel(table, mine, other, chunk, chunk_other, out):
+    part = nt(mine[...], chunk[...]) + nt(other[...], chunk_other[...])
+    for k in range(16):
+        low = part[ROWS * k : ROWS * k + 40]
+        high = part[ROWS * k + 40 : ROWS * (k + 1)]
+        out[table[k] // 2] = jnp.concatenate([low, high], axis=1)
+
+
+def small_part(table, mine, other, chunk, chunk_other):
+    vm = pl.BlockSpec(memory_space=pltpu.VMEM)
+    return pl.pallas_call(
+        small_kernel,
+        in_specs=[pl.BlockSpec(memory_space=pltpu.SMEM)] + [vm] * 4,
+        out_shape=jax.ShapeDtypeStruct((16, 40, 128), F32),
+        compiler_params=params(),
+        cost_estimate=cost(2 * CH * 512 * 64, 2 * 2**20),
+    )(table, mine, other, chunk, chunk_other)
 
 
 def grad_kernel(
@@ -465,9 +471,7 @@
 
 PART = [slice(320 * r, 320 * (r + 1)) for r in range(4)]
 WIDE = 640
-FULL = WIDE + STATE
 MAIN = [slice(0, WIDE), slice(WIDE, 2 * WIDE)]
-EXTRA = [slice(0, STATE), slice(STATE, 2 * STATE)]
 
 
 def mended(grad, halo, cols):
@@ -476,49 +480,41 @@
 
 
 def product(refs, side):
-    mine, other, grad, grad_other, halo, halo_other, shared, shared_other = refs
+    mine, other, grad, grad_other, halo, halo_other = refs
     cols = MAIN[side]
     right = jnp.concatenate(
         mended(grad, halo, cols) + mended(grad_other, halo_other, cols), axis=0
     )
-    extra = jnp.concatenate([shared[:, EXTRA[side]], shared_other[:, EXTRA[side]]], axis=0)
 
     def rows(part):
-        left = jnp.concatenate([mine[PART[part], :], other[PART[part], :]], axis=1)
-        return nn(left, right), nn(left, extra)
+        return nn(jnp.concatenate([mine[PART[part], :], other[PART[part], :]], axis=1), right)
 
     return rows
 
 
 def far_kernel(*refs):
-    for out, (part, side) in zip(refs[8:], ((2, 0), (2, 1))):
-        main, extra = product(refs[:8], side)(part)
-        out[:, :WIDE] = main.astype(BF16)
-        out[:, WIDE:] = extra.astype(BF16)
+    for out, (part, side) in zip(refs[6:], ((2, 0), (2, 1))):
+        out[...] = product(refs[:6], side)(part).astype(BF16)
 
 
 def near_kernel(*refs):
-    for out, (part, side) in zip(refs[9:], ((1, 0), (3, 1), (1, 1), (3, 0))):
-        main, extra = product(refs[:8], side)(part)
-        out[:, :WIDE] = main.astype(out.dtype)
-        out[:, WIDE:] = extra.astype(out.dtype)
+    for out, (part, side) in zip(refs[7:], ((1, 0), (3, 1), (1, 1), (3, 0))):
+        out[...] = product(refs[:6], side)(part).astype(out.dtype)
 
 
 def here_kernel(*refs):
-    for out, (part, side) in zip(refs[9:], ((0, 0), (0, 1))):
-        main, extra = product(refs[:8], side)(part)
-        out[:, :WIDE] = main
-        out[:, WIDE:] = extra
+    for out, (part, side) in zip(refs[7:], ((0, 0), (0, 1))):
+        out[...] = product(refs[:6], side)(part)
 
 
 def product_part(kernel, args, ties, types):
     vm = pl.BlockSpec(memory_space=pltpu.VMEM)
     return pl.pallas_call(
         kernel,
-        in_specs=[vm] * 8 + [pl.BlockSpec(memory_space=pl.ANY)] * len(ties),
-        out_shape=tuple(jax.ShapeDtypeStruct((320, FULL), one) for one in types),
-        compiler_params=params(),
-        cost_estimate=cost(2 * 512 * FULL * 320 * len(types), (3 + len(types)) * 2**20),
+        in_specs=[vm] * 6 + [pl.BlockSpec(memory_space=pl.ANY)] * len(ties),
+        out_shape=tuple(jax.ShapeDtypeStruct((320, WIDE), one) for one in types),
+        compiler_params=params(),
+        cost_estimate=cost(2 * 512 * WIDE * 320 * len(types), (3 + len(types)) * 2**20),
     )(*args, *ties)
 
 
@@ -570,7 +566,7 @@
     return pl.pallas_call(
         turn_kernel,
         out_shape=tuple(
-            jax.ShapeDtypeStruct((ROWS, FULL), one)
+            jax.ShapeDtypeStruct((ROWS, WIDE), one)
             for one in (BF16, BF16, F32, F32, BF16, BF16, F32, F32)
         ),
         compiler_params=params(),
@@ -578,14 +574,21 @@
     )(here_a, here_b, up, down)
 
 
-def last_kernel(a, b, up, down, here_u, up_u, down_u, grad_wx, grad_wbc, grad_u):
+def last_kernel(
+    order, a, b, up, down, here_u, up_u, down_u, c0, c1, c2, c3, grad_wx, grad_wbc, grad_u
+):
     norm = (T * SEQ) ** (-0.5)
     first = a[...] + (up[:ROWS, :].astype(F32) + down[ROWS:, :].astype(F32))
     second = b[...] + (down[:ROWS, :].astype(F32) + up[ROWS:, :].astype(F32))
-    grad_wx[:, :WIDE] = first[:, :WIDE] * norm
-    grad_wx[:, WIDE:] = second[:, :WIDE] * norm
-    grad_wbc[:, :STATE] = first[:, WIDE:] * norm
-    grad_wbc[:, STATE:] = second[:, WIDE:] * norm
+    grad_wx[:, :WIDE] = first * norm
+    grad_wx[:, WIDE:] = second * norm
+    pieces = []
+    for z in range(ZS):
+        piece = c0[...]
+        for r, one in enumerate((c1, c2, c3)):
+            piece = jnp.where(order[r + 1] == z, one[...], piece)
+        pieces.append(jnp.concatenate([piece[:, :64], piece[:, 64:]], axis=0) * norm)
+    grad_wbc[...] = jnp.concatenate(pieces, axis=1)
     size = here_u.shape[0] // 2
     low = here_u[:size, :] + (up_u[:size, :].astype(F32) + down_u[size:, :].astype(F32))
     high = here_u[size:, :] + (down_u[:size, :].astype(F32) + up_u[size:, :].astype(F32))
@@ -594,8 +597,10 @@
 
 
 def last_part(*args):
+    vm = pl.BlockSpec(memory_space=pltpu.VMEM)
     return pl.pallas_call(
         last_kernel,
+        in_specs=[pl.BlockSpec(memory_space=pltpu.SMEM)] + [vm] * 11,
         out_shape=(
             jax.ShapeDtypeStruct((ROWS, CH), F32),
             jax.ShapeDtypeStruct((ROWS, 2 * STATE), F32),
@@ -606,59 +611,47 @@
     )(*args)
 
 
-def input_kernel(order, w_x, w_bc, grad, halo, shared, tie, *outs):
-    del order, tie
-    far_up, far_down, near_up, near_down, dir_up, dir_down, here = outs
-    step = pl.program_id(0)
-    rows = w_x.shape[0] // 2
-    low, high = slice(0, rows), slice(rows, 2 * rows)
+def input_kernel(order, w_x, w_bc, grad, halo, shared, tie, *refs):
+    del tie
+    far_up, far_down, near_up, near_down, dir_up, dir_down, here, held, sems = refs
+    size = D // ZS
+    half = size // 2
+    copies = []
+    turn = (2, 1, 3, 0)
+    for at, r in enumerate(turn):
+        rows = pl.ds(pl.multiple_of(order[r] * size, size), size)
+        copies.append(pltpu.make_async_copy(w_x.at[rows, :], held.at[at], sems.at[at]))
+        copies[at].start()
     edge = jnp.concatenate([jnp.zeros((8, CH), F32), halo[...]], axis=0)
     last = (grad[T - 16 :, :].astype(F32) + edge).astype(BF16)
     right = jnp.concatenate([grad[: T - 16, :], last], axis=0)
-    part = nt(w_x[...], right)
-
-    @pl.when(step == 0)
-    def _():
-        far_up[...] = part[low].astype(BF16)
-        far_down[...] = part[high].astype(BF16)
-
-    @pl.when(step == 1)
-    def _():
-        near_up[...] = part[low]
-        dir_up[...] = part[high].astype(BF16)
-
-    @pl.when(step == 2)
-    def _():
-        dir_down[...] = part[low].astype(BF16)
-        near_down[...] = part[high]
-
-    @pl.when(step == 3)
-    def _():
-        here[...] = part + nt(w_bc[...], shared[...])
+    outs = ((far_up, far_down), (near_up, dir_up), (dir_down, near_down))
+    for at, r in enumerate(turn):
+        copies[at].wait()
+        rows = pl.ds(pl.multiple_of(order[r] * size, size), size)
+        part = nt(held[at], right) + nn(w_bc[rows, :], shared[...])
+        if r == 0:
+            here[...] = part
+        else:
+            low, high = outs[at]
+            low[...] = part[:half].astype(low.dtype)
+            high[...] = part[half:].astype(high.dtype)
 
 
 def input_part(order, w_x, w_bc, grad, halo, shared, tie):
     rows = D // ZS
+    vm = pl.BlockSpec(memory_space=pltpu.VMEM)
     sizes = (rows // 2,) * 6 + (rows,)
     types = (BF16, BF16, F32, F32, BF16, BF16, F32)
     return pl.pallas_call(
         input_kernel,
-        grid_spec=pltpu.PrefetchScalarGridSpec(
-            num_scalar_prefetch=1,
-            grid=(ZS,),
-            in_specs=[
-                pl.BlockSpec((rows, CH), lambda i, order: (order[i], 0)),
-                pl.BlockSpec((rows, 2 * STATE), lambda i, order: (order[3], 0)),
-                pl.BlockSpec((T, CH), lambda i, order: (0, 0)),
-                pl.BlockSpec((8, CH), lambda i, order: (0, 0)),
-                pl.BlockSpec((T, 2 * STATE), lambda i, order: (0, 0)),
-                pl.BlockSpec(memory_space=pl.ANY),
-            ],
-            out_specs=[pl.BlockSpec((size, T), lambda i, order: (0, 0)) for size in sizes],
-        ),
+        in_specs=[pl.BlockSpec(memory_space=pltpu.SMEM), pl.BlockSpec(memory_space=pltpu.HBM)]
+        + [vm] * 4
+        + [pl.BlockSpec(memory_space=pl.ANY)],
         out_shape=tuple(jax.ShapeDtypeStruct((size, T), one) for size, one in zip(sizes, types)),
-        compiler_params=params(),
-        cost_estimate=cost(2 * D * (CH + 64) * T, 10 * 2**20),
+        scratch_shapes=[pltpu.VMEM((ZS, rows, CH), BF16), pltpu.SemaphoreType.DMA((ZS,))],
+        compiler_params=params(20),
+        cost_estimate=cost(2 * D * (CH + 256) * T, 10 * 2**20),
     )(order, w_x, w_bc, grad, halo, shared, tie)
 
 
@@ -700,7 +693,7 @@
 
 
 def head_table():
-    return np.array([[(z + r) % ZS for r in (2, 1, 3, 0)] for z in range(ZS)], np.int32)
+    return np.array([[(z + r) % ZS for r in range(ZS)] for z in range(ZS)], np.int32)
 
 
 def body(normed, w_x, w_bc, conv_w, decay_code, step, d_skip, grad_y):
@@ -716,31 +709,25 @@
     rates = low + decay_code.astype(F32)[:, None] / (LEVELS - 1) * (high - low)
     before = lax.ppermute(normed[T - 16 :], "seq", [(i, i + 1) for i in range(SEQ - 1)])
 
-    bmat, cmat, cum, logd, dyt, dywt, pulled, through = front(normed, w_bc, rates, step, grad_y)
-    xgt, slope, xwt, msg = channels(
-        before, normed, w_x, conv_w, cum, logd, bmat, pulled, through
-    )
-    recv = lax.all_to_all(msg, "seq", 0, 0)
-    mine, other = select(table, normed, msg)
+    bmat, cmat, cum, logd, dyt, dywt, msg = front(normed, w_bc, rates, step, grad_y)
+    pulls = lax.all_to_all(msg, "seq", 0, 0)
+    xgt, slope, xwt, xlt = channels(before, normed, conv_w, cum, logd, w_x)
+    back_parts = chain(table, pulls, pulls, xgt, True)
+    ds = lax.all_to_all(back_parts, "seq", 0, 0).reshape(CH, STATE)
+    dxg, rc, dbc, own = intra(grad_y, dyt, xgt, xwt, xlt, cum, bmat, cmat, back_parts)
+    mine, other = select(table, normed, rc)
     other = lax.ppermute(other, "seq", swap)
-    dxg, rc, dbc = intra(grad_y, dyt, xgt, cum, bmat, cmat, mine)
-    back = lax.all_to_all(chain(table, recv, rc), "seq", 0, 0)
-
-    ds, st, shared = shared_part(back, xwt, dywt, dbc)
-    for bit in (1, 2):
-        pairs = [(i, i ^ bit) for i in range(ZS)]
-        shared = shared + lax.ppermute(shared, "head", pairs)
-    shared = shared.astype(BF16)
+    ahead = lax.all_to_all(own.reshape(SEQ, SLICE, STATE), "seq", 0, 0)
+
     dpre, halo, halves, cross = gradients(
-        d_skip, ds, bmat, dxg, dyt, xgt, slope, conv_w, cum, logd, st
+        d_skip, ds, bmat, dxg, dyt, xgt, slope, conv_w, cum, logd, mine
     )
     dpre_other = lax.ppermute(dpre, "seq", swap)
     halo_mine = lax.ppermute(halo, "seq", [(i, i - 1) for i in range(1, SEQ)])
     halo_pair = lax.ppermute(halo, "seq", [(i, i - 2) for i in range(2, SEQ, 2)])
     halo_other = jnp.where(core == 0, halo_pair, halo)
-    shared_other = lax.ppermute(shared, "seq", swap)
-
-    args = (mine, other, dpre, dpre_other, halo_mine, halo_other, shared, shared_other)
+
+    args = (mine, other, dpre, dpre_other, halo_mine, halo_other)
     move = {by: along(True, by) for by in (1, -1)}
     turn = {by: along(False, by) for by in (1, -1)}
     head = {by: along_head(by) for by in (1, -1)}
@@ -749,13 +736,24 @@
     near_up, near_down, dir_up, dir_down = product_part(
         near_kernel, args, (far_up,), (F32, F32, BF16, BF16)
     )
+    fore_parts = chain(table, ahead, pulls, near_up, False)
+    st = lax.all_to_all(fore_parts, "seq", 0, 0).reshape(CH, STATE)
     up, down = join((near_up, ru, dir_up), (near_down, rd, dir_down))
     ru, rd = move[1](up), move[-1](down)
     here_a, here_b = product_part(here_kernel, args, (up,), (F32, F32))
+    shared, *chunks = shared_part(order_z, ds, st, xwt, dywt, dbc, here_a)
+    arrived = [along_head(by)(chunks[by]) for by in (1, 2, 3)]
     z_far_up, z_far_down, z_up, z_down, z_dir_up, z_dir_down, z_here = input_part(
         order_z, w_x, w_bc, dpre, halo_mine, shared, here_a
     )
+    chunk = (chunks[0] + arrived[0] + arrived[1] + arrived[2]).astype(BF16)
+    chunk_other = lax.ppermute(chunk, "seq", swap)
     gls = step_part(st, ds, cmat, dyt, cum, logd, rc, halves, cross, z_here)
+    small = small_part(table, mine, other, chunk, chunk_other)
+    groups = [[2 * i + c for i in range(16)] for c in range(2)]
+    small = lax.all_to_all(small, "seq", 0, 0, axis_index_groups=groups)
+    small = jnp.sum(small, axis=0)
+    ring = [small] + [along_head(-by)(small) for by in (1, 2, 3)]
     far_up, far_down, near_up, near_down, dir_up, dir_down, here_a, here_b = turn_part(
         here_a, here_b, ru, rd
     )
@@ -769,7 +767,9 @@
     )
     ru, rd = turn[1](up), turn[-1](down)
     zu, zd = head[1](z_up), head[-1](z_down)
-    grad_wx, grad_wbc, grad_u = last_part(here_a, here_b, ru, rd, z_here, zu, zd)
+    grad_wx, grad_wbc, grad_u = last_part(
+        order_z, here_a, here_b, ru, rd, z_here, zu, zd, *ring
+    )
     return (grad_u, grad_wx, grad_wbc, gls)
 
 

time: 153 us -> 209 us (1.37)
  starting transfers between devices: 38.8 us -> 81.6 us
  local copies, waits for them, and re-layouts: 27.7 us -> 61 us
  waiting for transfers between devices: 34.7 us -> 14.1 us
  blocking collectives: 15.9 us -> 0 us
  Pallas kernels: 31 us -> 45.6 us
    all_to_all x1 -> x5, starting transfers between devices: 9.15 us -> 45.6 us  [the longest x1 15.2 us: body(): ds = lax.all_to_all(back_parts, 'seq', 0, 0).reshape(CH, STATE)]
    unnamed x102 -> x164, local copies, waits for them, and re-layouts: 25.3 us -> 59.5 us
    all_to_all x1 -> x0, blocking collectives: 15.9 us -> none  [body(): back = lax.all_to_all(chain(table, recv, rc), 'seq', 0, 0)]
    all_to_all x1 -> x5, waiting for transfers between devices: 13.5 us -> 0.01 us  [the longest x1 0.01 us: body(): pulls = lax.all_to_all(msg, 'seq', 0, 0)]
    ppermute x8, waiting for transfers between devices: 12.8 us -> 0.02 us  [along(): return lambda value: lax.ppermute(value, 'seq', ring(first, by))]
    ppermute x4 -> x10, waiting for transfers between devices: 0.01 us -> 11.5 us  [along_head(): lax.ppermute(value, 'head', [(i, (i + by) % ZS) for i in range(ZS)])]
    pallas_call x8 -> x10, Pallas kernels: 16.4 us -> 24.9 us  [the longest x3 6.56 us: product_part(): pl.pallas_call(kernel, in_specs=[vm] * 6 + [pl.BlockSpec(memory_space=pl....]
    ppermute x4 -> x10, starting transfers between devices: 6.61 us -> 13.2 us  [along_head(): lax.ppermute(value, 'head', [(i, (i + by) % ZS) for i in range(ZS)])]
  transfers between devices with their start and end apart: 21 -> 29, of which waited for: 8 -> 6; matrix products, arithmetic and copies ran while one was open for 2% -> 2% of each run, Pallas kernels for 12% -> 19%
where the time goes in v3:
time: 209 us; the launch traced here: 206 us
  starting transfers between devices  81.6 us (39%)
  local copies, waits for them, and re-layouts  61 us (29%)
  Pallas kernels  45.6 us (22%)
  waiting for transfers between devices  14.1 us (7%)
  other arithmetic  2.48 us (1%)
    unnamed x164, local copies, waits for them, and re-layouts  59.5 us
    ppermute x8, starting transfers between devices, along(): return lambda value: lax.ppermute(value, 'seq', ring(first, by))  17.3 us
    all_to_all x1, starting transfers between devices, body(): ds = lax.all_to_all(back_parts, 'seq', 0, 0).reshape(CH, STATE)  15.2 us
    ppermute x10, starting transfers between devices, along_head(): lax.ppermute(value, 'head', [(i, (i + by) % ZS) for i in range(ZS)])  13.2 us
    ppermute x10, waiting for transfers between devices, along_head(): lax.ppermute(value, 'head', [(i, (i + by) % ZS) for i in range(ZS)])  11.5 us
    all_to_all x1, starting transfers between devices, body(): ahead = lax.all_to_all(own.reshape(SEQ, SLICE, STATE), 'seq', 0, 0)  9.03 us
    all_to_all x1, starting transfers between devices, body(): st = lax.all_to_all(fore_parts, 'seq', 0, 0).reshape(CH, STATE)  7.8 us
    all_to_all x1, starting transfers between devices, body(): pulls = lax.all_to_all(msg, 'seq', 0, 0)  7.54 us
  transfers between devices with their start and end apart: 29, of which 6 were waited for; matrix products, arithmetic and copies ran while one was open for 2% of the time, Pallas kernels for 19%

profile of v3, /device:TPU:0, one launch (start us, length us, event | category | flops | bytes accessed | tf_op | source)
XLA Modules:
  0.0 205.9 jit_solution(3105684316284592729)
XLA Ops:
  1.4 1.3 copy-done.2
  2.7 1.3 copy-done.7
  5.9 2.6 %shard_map.129 = (f32[256,128]{1,0:T(8,128)S(1)}, f32[256,128]{1,0:T(8,128)S(1)}, f32[20,256]{1,0:T(8,128)S(1)}, f32[20,256]{1,0:T(8,128)S(1)}, bf16[1280,256]{1...) custom-call(bf16[256,2560]{1,0:T(8,128)(2,1)S(1)} %copy-done.2, ...), custom_call_target="tpu_custom_call" | custom-call | flops 587202560 | bytes 6291456 | tf_op jit(solution)/shard_map/pallas_call | solution.py:105
  10.6 7.5 %all-to-all-start = ((f32[32,48,128]{2,1,0:T(8,128)}), f32[32,48,128]{2,1,0:T(8,128)S(1)}, u32[]{:S(2)}, u32[]{:S(2)}) async-start(f32[32,48,128]{2,1,0:T(8,128)} %get-tuple-element.70), calls=%async_computation | async-start | bytes 1572864 | tf_op jit(solution)/shard_map/all_to_all | solution.py:713
  18.2 2.2 %collective-permute-start = (bf16[16,2560]{1,0:T(8,128)(2,1)S(1)}, bf16[16,2560]{1,0:T(8,128)(2,1)S(1)}, u32[]{:S(2)}, u32[]{:S(2)}) collective-permute-start(bf16[16,2560]{1,0:T(8,128)(2,1)S(1)} %slice.3), channel_id=1, source_target_pairs={{0,4},{4,8},{8,12},{12,16},{16,20},{20,24},{24,28},{28,32},{32,36}... | collective-permute-start | bytes 245768 | tf_op jit(solution)/shard_map/ppermute | solution.py:710
  21.9 2.9 %copy-done = bf16[2560,1280]{1,0:T(8,128)(2,1)S(1)} copy-done((bf16[2560,1280]{1,0:T(8,128)(2,1)S(1)}, bf16[2560,1280]{1,0:T(8,128)(2,1)}, u32[]{:S(2)}) %copy-start) | copy-done | bytes 6553624
  25.7 4.9 %shard_map.130 = (bf16[1280,256]{1,0:T(8,128)(2,1)S(1)}, f32[256,1280]{1,0:T(8,128)S(1)}, bf16[1280,256]{1,0:T(8,128)(2,1)S(1)}, bf16[1280,256]{1,0:T(8,128)(2,1)S(1)}) custom-call(bf16[16,2560]{1,0:T(8,128)(2,1)S(1)} %copy-done.73, bf16[256,2560]{1,0:T(8,128)(2,1)S(1)} %copy-done.3, f32[4,1280]{1,0:T(4,128)S(1)} %copy-done.71, ...), custom_call_target="tpu_custom_call" | custom-call | flops 1677721600 | bytes 10485760 | tf_op jit(solution)/shard_map/pallas_call | solution.py:194
  35.2 15.2 %all-to-all-start.1 = ((f32[32,40,128]{2,1,0:T(8,128)}), f32[32,40,128]{2,1,0:T(8,128)S(1)}, u32[]{:S(2)}, u32[]{:S(2)}) async-start(f32[32,40,128]{2,1,0:T(8,128)} %copy-done.21), calls=%async_computation.1 | async-start | bytes 1310720 | tf_op jit(solution)/shard_map/all_to_all | solution.py:716
  57.7 3.7 %shard_map.132 = (f32[1280,256]{1,0:T(8,128)S(1)}, f32[20,256]{1,0:T(8,128)S(1)}, f32[256,256]{1,0:T(8,128)S(1)}, f32[1280,128]{1,0:T(8,128)S(1)}) custom-call(bf16[256,1280]{1,0:T(8,128)(2,1)S(1)} %copy-done.32, bf16[1280,256]{1,0:T(8,128)(2,1)S(1)} %get-tuple-element.62.dyt, bf16[1280,256]{1,0:T(8,128)(2,1)S(1)} %copy-done.18, ...), custom_call_target="tpu_custom_call" | custom-call | flops 1342177280 | bytes 4194304 | tf_op jit(solution)/shard_map/pallas_call | solution.py:270
  62.1 1.9 shard_map.133
  66.5 1.3 copy-done.24
  67.8 1.3 copy-done.26
  70.1 3.8 %shard_map.134 = (bf16[256,1280]{1,0:T(8,128)(2,1)S(1)}, f32[8,1280]{1,0:T(8,128)}, f32[20,256]{1,0:T(8,128)S(1)}, f32[20,256]{1,0:T(8,128)S(1)}) custom-call(f32[20]{0:T(128)S(1)} %copy-done.79, f32[1280,128]{1,0:T(8,128)S(1)} %bitcast.9, f32[256,128]{1,0:T(8,128)S(1)} %copy-done.66, f32[1280,256]{1,0:T(8,128)S(1)} %copy-done.26, ...), custom_call_target="tpu_custom_call" | custom-call | flops 167772160 | bytes 6291456 | tf_op jit(solution)/shard_map/pallas_call | solution.py:383
  75.3 1.3 collective-permute-start.4
  76.6 9.0 %all-to-all-start.2 = ((f32[32,40,128]{2,1,0:T(8,128)}), f32[32,40,128]{2,1,0:T(8,128)}, u32[]{:S(2)}, u32[]{:S(2)}) async-start(f32[32,40,128]{2,1,0:T(8,128)} %bitcast.14), calls=%async_computation.2 | async-start | bytes 1310720 | tf_op jit(solution)/shard_map/all_to_all | solution.py:720
  85.7 1.3 collective-permute-start.3
  87.8 1.2 collective-permute-done.3.refs_4_.halo
  89.0 2.5 %shard_map.135 = (bf16[320,640]{1,0:T(8,128)(2,1)}, bf16[320,640]{1,0:T(8,128)(2,1)}) custom-call(bf16[1280,256]{1,0:T(8,128)(2,1)S(1)} %get-tuple-element.72.tie.refs_0_.mine, bf16[1280,256]{1,0:T(8,128)(2,1)S(1)} %collective-permute-done.1.refs_1_.other, bf16[256,1280]{1,0:T(8,128)(2,1)S(1)} %get-tuple-element.76.refs_2_.grad, ...), custom_call_target="tpu_custom_call" | custom-call | flops 419430400 | bytes 5242880 | tf_op jit(solution)/shard_map/pallas_call | solution.py:512
  91.5 7.8 %collective-permute-start.6 = (bf16[320,640]{1,0:T(8,128)(2,1)}, bf16[320,640]{1,0:T(8,128)(2,1)}, u32[]{:S(2)}, u32[]{:S(2)}) collective-permute-start(bf16[320,640]{1,0:T(8,128)(2,1)} %get-tuple-element.82), channel_id=1, source_target_pairs={{0,96},{4,28},{8,104},{12,4},{16,112},{20,12},{24,120},{28,20},{32... | collective-permute-start | bytes 1228808 | tf_op jit(solution)/shard_map/ppermute | solution.py:674
  99.3 2.3 %shard_map.136 = (f32[320,640]{1,0:T(8,128)S(1)}, f32[320,640]{1,0:T(8,128)S(1)}, bf16[320,640]{1,0:T(8,128)(2,1)S(1)}, bf16[320,640]{1,0:T(8,128)(2,1)S(1)}) custom-call(bf16[1280,256]{1,0:T(8,128)(2,1)S(1)} %get-tuple-element.72.tie.refs_0_.mine, bf16[1280,256]{1,0:T(8,128)(2,1)S(1)} %collective-permute-done.1.refs_1_.other, ...), custom_call_target="tpu_custom_call" | custom-call | flops 838860800 | bytes 7340032 | tf_op jit(solution)/shard_map/pallas_call | solution.py:512
  105.0 1.1 copy-done.10
  106.1 1.5 shard_map.140
  108.6 7.8 %all-to-all-start.3 = ((f32[32,40,128]{2,1,0:T(8,128)}), f32[32,40,128]{2,1,0:T(8,128)S(1)}, u32[]{:S(2)}, u32[]{:S(2)}) async-start(f32[32,40,128]{2,1,0:T(8,128)} %copy-done.20), calls=%async_computation.3 | async-start | bytes 1310720 | tf_op jit(solution)/shard_map/all_to_all | solution.py:740
  117.5 1.1 copy-done.30
  120.7 2.4 %shard_map.137 = (bf16[640,640]{1,0:T(8,128)(2,1)}, bf16[640,640]{1,0:T(8,128)(2,1)}) custom-call(f32[320,640]{1,0:T(8,128)S(1)} %copy-done.11, bf16[320,640]{1,0:T(8,128)(2,1)} %collective-permute-done.5.refs_1_, bf16[320,640]{1,0:T(8,128)(2,1)S(1)} %copy-done.40, f32[320,640]{1,0:T(8,128)S(1)} %copy-done.30, ...), custom_call_target="tpu_custom_call" | custom-call | flops 1000000 | bytes 4194304 | tf_op jit(solution)/shard_map/pallas_call | solution.py:532
  123.1 3.0 %collective-permute-start.8 = (bf16[640,640]{1,0:T(8,128)(2,1)}, bf16[640,640]{1,0:T(8,128)(2,1)}, u32[]{:S(2)}, u32[]{:S(2)}) collective-permute-start(bf16[640,640]{1,0:T(8,128)(2,1)} %get-tuple-element.87), channel_id=1, source_target_pairs={{0,96},{4,28},{8,104},{12,4},{16,112},{20,12},{24,120},{28,20},{32... | collective-permute-start | bytes 2457608 | tf_op jit(solution)/shard_map/ppermute | solution.py:674
  126.8 1.8 shard_map.138
  130.4 1.1 copy-done.5
  135.7 2.0 collective-permute-start.17
  137.7 3.6 %collective-permute-start.18 = (f32[64,256]{1,0:T(8,128)S(1)}, f32[64,256]{1,0:T(8,128)S(1)}, u32[]{:S(2)}, u32[]{:S(2)}) collective-permute-start(f32[64,256]{1,0:T(8,128)S(1)} %get-tuple-element.113), channel_id=1, source_target_pairs={{0,2},{1,3},{2,0},{3,1},{4,6},{5,7},{6,4},{7,5},{8,10},{9,11},{10,... | collective-permute-start | bytes 196616 | tf_op jit(solution)/shard_map/ppermute | solution.py:678
  142.3 2.9 %copy-done.1 = bf16[2560,1280]{1,0:T(8,128)(2,1)S(1)} copy-done((bf16[2560,1280]{1,0:T(8,128)(2,1)S(1)}, bf16[2560,1280]{1,0:T(8,128)(2,1)}, u32[]{:S(2)}) %copy-start.1) | copy-done | bytes 6553624
  145.1 6.1 %shard_map.142 = (bf16[320,256]{1,0:T(8,128)(2,1)}, bf16[320,256]{1,0:T(8,128)(2,1)}, f32[320,256]{1,0:T(8,128)S(1)}, f32[320,256]{1,0:T(8,128)S(1)}, bf16[320,2...) custom-call(s32[4]{0:T(128)S(1)} %dynamic-slice_bitcast_fusion.1.order, ...), custom_call_target="tpu_custom_call" | custom-call | flops 2013265920 | bytes 10485760 | tf_op jit(solution)/shard_map/pallas_call | solution.py:646
  153.6 2.2 %collective-permute-start.12 = (bf16[320,256]{1,0:T(8,128)(2,1)}, bf16[320,256]{1,0:T(8,128)(2,1)}, u32[]{:S(2)}, u32[]{:S(2)}) collective-permute-start(bf16[320,256]{1,0:T(8,128)(2,1)} %get-tuple-element.104), channel_id=1, source_target_pairs={{0,3},{1,0},{2,1},{3,2},{4,7},{5,4},{6,5},{7,6},{8,11},{9,8},{10,9... | collective-permute-start | bytes 491528 | tf_op jit(solution)/shard_map/ppermute | solution.py:678
  155.9 2.2 %shard_map.139 = (bf16[80,640]{1,0:T(8,128)(2,1)}, bf16[80,640]{1,0:T(8,128)(2,1)}, f32[80,640]{1,0:T(8,128)S(1)}, f32[80,640]{1,0:T(8,128)S(1)}, bf16[80,640]{1...) custom-call(f32[320,640]{1,0:T(8,128)S(1)} %copy-done.6, ...), custom_call_target="tpu_custom_call" | custom-call | flops 1000000 | bytes 4194304 | tf_op jit(solution)/shard_map/pallas_call | solution.py:566
  160.8 1.5 collective-permute-start.9
  162.3 1.8 collective-permute-start.10
  164.2 1.2 collective-permute-done.20.chunk_other
  165.4 1.8 shard_map.144
  167.2 6.0 %all-to-all-start.4 = ((f32[16,40,128]{2,1,0:T(8,128)}), f32[16,40,128]{2,1,0:T(8,128)}, u32[]{:S(2)}, u32[]{:S(2)}) async-start(f32[16,40,128]{2,1,0:T(8,128)} %shard_map.144), calls=%async_computation.4 | async-start | bytes 655360 | tf_op jit(solution)/shard_map/all_to_all | solution.py:754
  179.9 2.2 %shard_map.143 = (bf16[160,640]{1,0:T(8,128)(2,1)}, bf16[160,640]{1,0:T(8,128)(2,1)}, bf16[640,256]{1,0:T(8,128)(2,1)}, bf16[640,256]{1,0:T(8,128)(2,1)}) custom-call(f32[80,640]{1,0:T(8,128)S(1)} %copy-done.54, bf16[80,640]{1,0:T(8,128)(2,1)} %collective-permute-done.9.refs_1_, bf16[80,640]{1,0:T(8,128)(2,1)S(1)} %get-tuple-element.92.refs_2_, ...), custom_call_target="tpu_custom_call" | custom-call | flops 1000000 | bytes 4194304 | tf_op jit(solution)/shard_map/pallas_call | solution.py:532
  182.1 3.2 %collective-permute-start.16 = (bf16[640,256]{1,0:T(8,128)(2,1)}, bf16[640,256]{1,0:T(8,128)(2,1)S(1)}, u32[]{:S(2)}, u32[]{:S(2)}) collective-permute-start(bf16[640,256]{1,0:T(8,128)(2,1)} %get-tuple-element.110), channel_id=1, source_target_pairs={{0,3},{1,0},{2,1},{3,2},{4,7},{5,4},{6,5},{7,6},{8,11},{9,8},{10,9... | collective-permute-start | bytes 983048 | tf_op jit(solution)/shard_map/ppermute | solution.py:678
  185.3 1.9 collective-permute-start.13
  187.2 1.4 collective-permute-start.14
  189.7 5.0 %collective-permute-done.23.c3 = f32[40,128]{1,0:T(8,128)S(1)} collective-permute-done((f32[40,128]{1,0:T(8,128)S(1)}, f32[40,128]{1,0:T(8,128)S(1)}, u32[]{:S(2)}, u32[]{:S(2)}) %collective-permute-start.23) | collective-permute-done | bytes 20512 | tf_op jit(solution)/shard_map/ppermute | solution.py:678
  194.6 5.3 %collective-permute-done.22.c2 = f32[40,128]{1,0:T(8,128)S(1)} collective-permute-done((f32[40,128]{1,0:T(8,128)S(1)}, f32[40,128]{1,0:T(8,128)S(1)}, u32[]{:S(2)}, u32[]{:S(2)}) %collective-permute-start.22) | collective-permute-done | bytes 20512 | tf_op jit(solution)/shard_map/ppermute | solution.py:678
  200.7 1.8 shard_map.146
  202.5 1.2 collective-permute-done.21.c1
  203.8 2.2 %shard_map.145 = (f32[80,1280]{1,0:T(8,128)}, f32[80,256]{1,0:T(8,128)}, bf16[640,256]{1,0:T(8,128)(2,1)}) custom-call(s32[4]{0:T(128)S(1)} %dynamic-slice_bitcast_fusion.1.order, f32[80,640]{1,0:T(8,128)S(1)} %copy-done.50, f32[80,640]{1,0:T(8,128)S(1)} %copy-done.52, bf16[160,640]{1,0:T(8,128)(2,1)} %collective-permute-done.13.up, ...), custom_call_target="tpu_custom_call" | custom-call | flops 1000000 | bytes 3145728 | tf_op jit(solution)/shard_map/pallas_call | solution.py:601
  (200 shorter events, 54.1 us)
Async XLA Ops:
  10.6 39.8 %copy-start.12 = (bf16[1280,256]{1,0:T(8,128)(2,1)}, bf16[1280,256]{1,0:T(8,128)(2,1)S(1)}, u32[]{:S(2)}) copy-start(bf16[1280,256]{1,0:T(8,128)(2,1)S(1)} %get-tuple-element.62.dyt) | copy-start | bytes 1966084
  10.6 7.6 %copy-start.3 = (bf16[256,2560]{1,0:T(8,128)(2,1)S(1)}, bf16[256,2560]{1,0:T(8,128)(2,1)}, u32[]{:S(2)}) copy-start(bf16[256,2560]{1,0:T(8,128)(2,1)} %normed.5) | copy-start | bytes 3932164
  10.6 11.3 %copy-start.71 = (f32[4,1280]{1,0:T(4,128)S(1)}, f32[4,1280]{1,0:T(4,128)}, u32[]{:S(2)}) copy-start(f32[4,1280]{1,0:T(4,128)} %taps.1) | copy-start | bytes 61444
  10.6 22.7 %all-to-all-start = ((f32[32,48,128]{2,1,0:T(8,128)}), f32[32,48,128]{2,1,0:T(8,128)S(1)}, u32[]{:S(2)}, u32[]{:S(2)}) async-start(f32[32,48,128]{2,1,0:T(8,128)} %get-tuple-element.70), calls=%async_computation | async-start | bytes 1572864 | tf_op jit(solution)/shard_map/all_to_all | solution.py:713
  18.2 3.1 %collective-permute-start = (bf16[16,2560]{1,0:T(8,128)(2,1)S(1)}, bf16[16,2560]{1,0:T(8,128)(2,1)S(1)}, u32[]{:S(2)}, u32[]{:S(2)}) collective-permute-start(bf16[16,2560]{1,0:T(8,128)(2,1)S(1)} %slice.3), channel_id=1, source_target_pairs={{0,4},{4,8},{8,12},{12,16},{16,20},{20,24},{24,28},{28,32},{32,36}... | collective-permute-start | bytes 245768 | tf_op jit(solution)/shard_map/ppermute | solution.py:710
  21.9 2.9 %copy-start = (bf16[2560,1280]{1,0:T(8,128)(2,1)S(1)}, bf16[2560,1280]{1,0:T(8,128)(2,1)}, u32[]{:S(2)}) copy-start(bf16[2560,1280]{1,0:T(8,128)(2,1)} %w_x.3) | copy-start | bytes 19660804
  35.2 29.2 %all-to-all-start.1 = ((f32[32,40,128]{2,1,0:T(8,128)}), f32[32,40,128]{2,1,0:T(8,128)S(1)}, u32[]{:S(2)}, u32[]{:S(2)}) async-start(f32[32,40,128]{2,1,0:T(8,128)} %copy-done.21), calls=%async_computation.1 | async-start | bytes 1310720 | tf_op jit(solution)/shard_map/all_to_all | solution.py:716
  64.0 23.8 %collective-permute-start.1 = (bf16[1280,256]{1,0:T(8,128)(2,1)}, bf16[1280,256]{1,0:T(8,128)(2,1)S(1)}, u32[]{:S(2)}, u32[]{:S(2)}) collective-permute-start(bf16[1280,256]{1,0:T(8,128)(2,1)} %get-tuple-element.73), channel_id=1, source_target_pairs={{0,4},{4,0},{8,12},{12,8},{16,20},{20,16},{24,28},{28,24},{32,36},... | collective-permute-start | bytes 1966088 | tf_op jit(solution)/shard_map/ppermute | solution.py:719
  75.1 13.9 %collective-permute-start.2 = (bf16[256,1280]{1,0:T(8,128)(2,1)S(1)}, bf16[256,1280]{1,0:T(8,128)(2,1)}, u32[]{:S(2)}, u32[]{:S(2)}) collective-permute-start(bf16[256,1280]{1,0:T(8,128)(2,1)S(1)} %get-tuple-element.76.refs_2_.grad), channel_id=1, source_target_pairs={{0,4},{4,0},{8,12},{12,8},{16,20},{20,16},{24,28},{28,24},{32,36},... | collective-permute-start | bytes 1966088 | tf_op jit(solution)/shard_map/ppermute | solution.py:725
  75.3 11.6 %collective-permute-start.4 = (f32[8,1280]{1,0:T(8,128)}, f32[8,1280]{1,0:T(8,128)}, u32[]{:S(2)}, u32[]{:S(2)}) collective-permute-start(f32[8,1280]{1,0:T(8,128)} %get-tuple-element.77), channel_id=1, source_target_pairs={{8,0},{16,8},{24,16},{32,24},{40,32},{48,40},{56,48},{64,56},{72,6... | collective-permute-start | bytes 122888 | tf_op jit(solution)/shard_map/ppermute | solution.py:727
  76.6 28.4 %all-to-all-start.2 = ((f32[32,40,128]{2,1,0:T(8,128)}), f32[32,40,128]{2,1,0:T(8,128)}, u32[]{:S(2)}, u32[]{:S(2)}) async-start(f32[32,40,128]{2,1,0:T(8,128)} %bitcast.14), calls=%async_computation.2 | async-start | bytes 1310720 | tf_op jit(solution)/shard_map/all_to_all | solution.py:720
  85.7 3.3 %collective-permute-start.3 = (f32[8,1280]{1,0:T(8,128)}, f32[8,1280]{1,0:T(8,128)S(1)}, u32[]{:S(2)}, u32[]{:S(2)}) collective-permute-start(f32[8,1280]{1,0:T(8,128)} %get-tuple-element.77), channel_id=1, source_target_pairs={{4,0},{8,4},{12,8},{16,12},{20,16},{24,20},{28,24},{32,28},{36,32}... | collective-permute-start | bytes 122888 | tf_op jit(solution)/shard_map/ppermute | solution.py:726
  91.5 24.8 %collective-permute-start.6 = (bf16[320,640]{1,0:T(8,128)(2,1)}, bf16[320,640]{1,0:T(8,128)(2,1)}, u32[]{:S(2)}, u32[]{:S(2)}) collective-permute-start(bf16[320,640]{1,0:T(8,128)(2,1)} %get-tuple-element.82), channel_id=1, source_target_pairs={{0,96},{4,28},{8,104},{12,4},{16,112},{20,12},{24,120},{28,20},{32... | collective-permute-start | bytes 1228808 | tf_op jit(solution)/shard_map/ppermute | solution.py:674
  99.3 17.0 %collective-permute-start.5 = (bf16[320,640]{1,0:T(8,128)(2,1)}, bf16[320,640]{1,0:T(8,128)(2,1)}, u32[]{:S(2)}, u32[]{:S(2)}) collective-permute-start(bf16[320,640]{1,0:T(8,128)(2,1)} %get-tuple-element.78.refs_6_), channel_id=1, source_target_pairs={{0,32},{4,12},{8,40},{12,20},{16,48},{20,28},{24,56},{28,4},{32,64... | collective-permute-start | bytes 1228808 | tf_op jit(solution)/shard_map/ppermute | solution.py:674
  108.6 21.9 %all-to-all-start.3 = ((f32[32,40,128]{2,1,0:T(8,128)}), f32[32,40,128]{2,1,0:T(8,128)S(1)}, u32[]{:S(2)}, u32[]{:S(2)}) async-start(f32[32,40,128]{2,1,0:T(8,128)} %copy-done.20), calls=%async_computation.3 | async-start | bytes 1310720 | tf_op jit(solution)/shard_map/all_to_all | solution.py:740
  123.1 29.4 %collective-permute-start.8 = (bf16[640,640]{1,0:T(8,128)(2,1)}, bf16[640,640]{1,0:T(8,128)(2,1)}, u32[]{:S(2)}, u32[]{:S(2)}) collective-permute-start(bf16[640,640]{1,0:T(8,128)(2,1)} %get-tuple-element.87), channel_id=1, source_target_pairs={{0,96},{4,28},{8,104},{12,4},{16,112},{20,12},{24,120},{28,20},{32... | collective-permute-start | bytes 2457608 | tf_op jit(solution)/shard_map/ppermute | solution.py:674
  126.1 27.5 %collective-permute-start.7 = (bf16[640,640]{1,0:T(8,128)(2,1)}, bf16[640,640]{1,0:T(8,128)(2,1)}, u32[]{:S(2)}, u32[]{:S(2)}) collective-permute-start(bf16[640,640]{1,0:T(8,128)(2,1)} %get-tuple-element.84.refs_6_), channel_id=1, source_target_pairs={{0,32},{4,12},{8,40},{12,20},{16,48},{20,28},{24,56},{28,4},{32,64... | collective-permute-start | bytes 2457608 | tf_op jit(solution)/shard_map/ppermute | solution.py:674
  134.7 7.6 %copy-start.6 = (f32[320,640]{1,0:T(8,128)S(1)}, f32[320,640]{1,0:T(8,128)}, u32[]{:S(2)}) copy-start(f32[320,640]{1,0:T(8,128)} %copy-done.4) | copy-start | bytes 2457604
  134.7 7.6 %copy-start.8 = (bf16[2560,256]{1,0:T(8,128)(2,1)S(1)}, bf16[2560,256]{1,0:T(8,128)(2,1)}, u32[]{:S(2)}) copy-start(bf16[2560,256]{1,0:T(8,128)(2,1)} %w_bc.3) | copy-start | bytes 3932164
  135.7 25.1 %collective-permute-start.17 = (f32[64,256]{1,0:T(8,128)S(1)}, f32[64,256]{1,0:T(8,128)S(1)}, u32[]{:S(2)}, u32[]{:S(2)}) collective-permute-start(f32[64,256]{1,0:T(8,128)S(1)} %get-tuple-element.112), channel_id=1, source_target_pairs={{0,1},{1,2},{2,3},{3,0},{4,5},{5,6},{6,7},{7,4},{8,9},{9,10},{10,1... | collective-permute-start | bytes 196616 | tf_op jit(solution)/shard_map/ppermute | solution.py:678
  137.7 24.6 %collective-permute-start.18 = (f32[64,256]{1,0:T(8,128)S(1)}, f32[64,256]{1,0:T(8,128)S(1)}, u32[]{:S(2)}, u32[]{:S(2)}) collective-permute-start(f32[64,256]{1,0:T(8,128)S(1)} %get-tuple-element.113), channel_id=1, source_target_pairs={{0,2},{1,3},{2,0},{3,1},{4,6},{5,7},{6,4},{7,5},{8,10},{9,11},{10,... | collective-permute-start | bytes 196616 | tf_op jit(solution)/shard_map/ppermute | solution.py:678
  141.3 22.8 %collective-permute-start.19 = (f32[64,256]{1,0:T(8,128)S(1)}, f32[64,256]{1,0:T(8,128)S(1)}, u32[]{:S(2)}, u32[]{:S(2)}) collective-permute-start(f32[64,256]{1,0:T(8,128)S(1)} %get-tuple-element.114), channel_id=1, source_target_pairs={{0,3},{1,0},{2,1},{3,2},{4,7},{5,4},{6,5},{7,6},{8,11},{9,8},{10,9... | collective-permute-start | bytes 196616 | tf_op jit(solution)/shard_map/ppermute | solution.py:678
  142.3 2.9 %copy-start.1 = (bf16[2560,1280]{1,0:T(8,128)(2,1)S(1)}, bf16[2560,1280]{1,0:T(8,128)(2,1)}, u32[]{:S(2)}) copy-start(bf16[2560,1280]{1,0:T(8,128)(2,1)} %w_x.3) | copy-start | bytes 19660804
  145.1 10.7 %copy-start.28 = (f32[320,640]{1,0:T(8,128)S(1)}, f32[320,640]{1,0:T(8,128)}, u32[]{:S(2)}) copy-start(f32[320,640]{1,0:T(8,128)} %copy-done.27) | copy-start | bytes 2457604
  152.5 5.6 %copy-start.15 = (f32[640,256]{1,0:T(8,128)}, f32[640,256]{1,0:T(8,128)S(1)}, u32[]{:S(2)}) copy-start(f32[640,256]{1,0:T(8,128)S(1)} %get-tuple-element.108.here_u.tie) | copy-start | bytes 1966084
  152.5 5.6 %copy-start.43 = (f32[320,256]{1,0:T(8,128)}, f32[320,256]{1,0:T(8,128)S(1)}, u32[]{:S(2)}) copy-start(f32[320,256]{1,0:T(8,128)S(1)} %get-tuple-element.100.refs_6_) | copy-start | bytes 983044
  152.5 5.6 %copy-start.45 = (f32[320,256]{1,0:T(8,128)}, f32[320,256]{1,0:T(8,128)S(1)}, u32[]{:S(2)}) copy-start(f32[320,256]{1,0:T(8,128)S(1)} %get-tuple-element.103.refs_9_) | copy-start | bytes 983044
  152.5 20.7 %collective-permute-start.11 = (bf16[320,256]{1,0:T(8,128)(2,1)}, bf16[320,256]{1,0:T(8,128)(2,1)}, u32[]{:S(2)}, u32[]{:S(2)}) collective-permute-start(bf16[320,256]{1,0:T(8,128)(2,1)} %get-tuple-element.101), channel_id=1, source_target_pairs={{0,1},{1,2},{2,3},{3,0},{4,5},{5,6},{6,7},{7,4},{8,9},{9,10},{10,1... | collective-permute-start | bytes 491528 | tf_op jit(solution)/shard_map/ppermute | solution.py:678
  153.6 19.6 %collective-permute-start.12 = (bf16[320,256]{1,0:T(8,128)(2,1)}, bf16[320,256]{1,0:T(8,128)(2,1)}, u32[]{:S(2)}, u32[]{:S(2)}) collective-permute-start(bf16[320,256]{1,0:T(8,128)(2,1)} %get-tuple-element.104), channel_id=1, source_target_pairs={{0,3},{1,0},{2,1},{3,2},{4,7},{5,4},{6,5},{7,6},{8,11},{9,8},{10,9... | collective-permute-start | bytes 491528 | tf_op jit(solution)/shard_map/ppermute | solution.py:678
  160.8 4.6 %copy-start.67 = (bf16[80,640]{1,0:T(8,128)(2,1)}, bf16[80,640]{1,0:T(8,128)(2,1)S(1)}, u32[]{:S(2)}) copy-start(bf16[80,640]{1,0:T(8,128)(2,1)S(1)} %get-tuple-element.95.refs_5_) | copy-start | bytes 307204
  160.8 12.4 %collective-permute-start.9 = (bf16[80,640]{1,0:T(8,128)(2,1)}, bf16[80,640]{1,0:T(8,128)(2,1)}, u32[]{:S(2)}, u32[]{:S(2)}) collective-permute-start(bf16[80,640]{1,0:T(8,128)(2,1)} %get-tuple-element.91), channel_id=1, source_target_pairs={{0,8},{4,36},{8,16},{12,44},{16,24},{20,52},{24,0},{28,60},{32,40}... | collective-permute-start | bytes 307208 | tf_op jit(solution)/shard_map/ppermute | solution.py:674
  162.3 11.0 %collective-permute-start.10 = (bf16[80,640]{1,0:T(8,128)(2,1)}, bf16[80,640]{1,0:T(8,128)(2,1)}, u32[]{:S(2)}, u32[]{:S(2)}) collective-permute-start(bf16[80,640]{1,0:T(8,128)(2,1)} %get-tuple-element.94), channel_id=1, source_target_pairs={{0,24},{4,100},{8,0},{12,108},{16,8},{20,116},{24,16},{28,124},{32... | collective-permute-start | bytes 307208 | tf_op jit(solution)/shard_map/ppermute | solution.py:674
  164.1 1.3 collective-permute-start.20
  167.2 32.7 %copy-start.63 = (f32[256,128]{1,0:T(8,128)S(1)}, f32[256,128]{1,0:T(8,128)}, u32[]{:S(2)}) copy-start(f32[256,128]{1,0:T(8,128)} %copy-done.61) | copy-start | bytes 393220
  167.2 32.7 %copy-start.70 = (f32[20,256]{1,0:T(8,128)S(1)}, f32[20,256]{1,0:T(8,128)}, u32[]{:S(2)}) copy-start(f32[20,256]{1,0:T(8,128)} %copy-done.69) | copy-start | bytes 61444
  167.2 32.7 %copy-start.76 = (f32[20,256]{1,0:T(8,128)S(1)}, f32[20,256]{1,0:T(8,128)}, u32[]{:S(2)}) copy-start(f32[20,256]{1,0:T(8,128)} %copy-done.75) | copy-start | bytes 61444
  167.2 21.4 %all-to-all-start.4 = ((f32[16,40,128]{2,1,0:T(8,128)}), f32[16,40,128]{2,1,0:T(8,128)}, u32[]{:S(2)}, u32[]{:S(2)}) async-start(f32[16,40,128]{2,1,0:T(8,128)} %shard_map.144), calls=%async_computation.4 | async-start | bytes 655360 | tf_op jit(solution)/shard_map/all_to_all | solution.py:754
  173.2 26.7 %copy-start.14 = (bf16[1280,256]{1,0:T(8,128)(2,1)S(1)}, bf16[1280,256]{1,0:T(8,128)(2,1)}, u32[]{:S(2)}) copy-start(bf16[1280,256]{1,0:T(8,128)(2,1)} %copy-done.12) | copy-start | bytes 1966084
  173.2 26.7 %copy-start.16 = (f32[640,256]{1,0:T(8,128)S(1)}, f32[640,256]{1,0:T(8,128)}, u32[]{:S(2)}) copy-start(f32[640,256]{1,0:T(8,128)} %copy-done.15) | copy-start | bytes 1966084
  182.1 21.6 %collective-permute-start.15 = (bf16[640,256]{1,0:T(8,128)(2,1)}, bf16[640,256]{1,0:T(8,128)(2,1)S(1)}, u32[]{:S(2)}, u32[]{:S(2)}) collective-permute-start(bf16[640,256]{1,0:T(8,128)(2,1)} %get-tuple-element.109), channel_id=1, source_target_pairs={{0,1},{1,2},{2,3},{3,0},{4,5},{5,6},{6,7},{7,4},{8,9},{9,10},{10,1... | collective-permute-start | bytes 983048 | tf_op jit(solution)/shard_map/ppermute | solution.py:678
  182.1 21.6 %collective-permute-start.16 = (bf16[640,256]{1,0:T(8,128)(2,1)}, bf16[640,256]{1,0:T(8,128)(2,1)S(1)}, u32[]{:S(2)}, u32[]{:S(2)}) collective-permute-start(bf16[640,256]{1,0:T(8,128)(2,1)} %get-tuple-element.110), channel_id=1, source_target_pairs={{0,3},{1,0},{2,1},{3,2},{4,7},{5,4},{6,5},{7,6},{8,11},{9,8},{10,9... | collective-permute-start | bytes 983048 | tf_op jit(solution)/shard_map/ppermute | solution.py:678
  185.3 18.4 %collective-permute-start.13 = (bf16[160,640]{1,0:T(8,128)(2,1)}, bf16[160,640]{1,0:T(8,128)(2,1)}, u32[]{:S(2)}, u32[]{:S(2)}) collective-permute-start(bf16[160,640]{1,0:T(8,128)(2,1)} %get-tuple-element.106), channel_id=1, source_target_pairs={{0,8},{4,36},{8,16},{12,44},{16,24},{20,52},{24,0},{28,60},{32,40}... | collective-permute-start | bytes 614408 | tf_op jit(solution)/shard_map/ppermute | solution.py:674
  187.2 16.5 %collective-permute-start.14 = (bf16[160,640]{1,0:T(8,128)(2,1)}, bf16[160,640]{1,0:T(8,128)(2,1)}, u32[]{:S(2)}, u32[]{:S(2)}) collective-permute-start(bf16[160,640]{1,0:T(8,128)(2,1)} %get-tuple-element.107), channel_id=1, source_target_pairs={{0,24},{4,100},{8,0},{12,108},{16,8},{20,116},{24,16},{28,124},{32... | collective-permute-start | bytes 614408 | tf_op jit(solution)/shard_map/ppermute | solution.py:674
  189.6 5.1 %collective-permute-start.23 = (f32[40,128]{1,0:T(8,128)S(1)}, f32[40,128]{1,0:T(8,128)S(1)}, u32[]{:S(2)}, u32[]{:S(2)}) collective-permute-start(f32[40,128]{1,0:T(8,128)S(1)} %reduce_sum.9.c0), channel_id=1, source_target_pairs={{0,1},{1,2},{2,3},{3,0},{4,5},{5,6},{6,7},{7,4},{8,9},{9,10},{10,1... | collective-permute-start | bytes 61448 | tf_op jit(solution)/shard_map/ppermute | solution.py:678
  194.6 5.3 %collective-permute-start.22 = (f32[40,128]{1,0:T(8,128)S(1)}, f32[40,128]{1,0:T(8,128)S(1)}, u32[]{:S(2)}, u32[]{:S(2)}) collective-permute-start(f32[40,128]{1,0:T(8,128)S(1)} %reduce_sum.9.c0), channel_id=1, source_target_pairs={{0,2},{1,3},{2,0},{3,1},{4,6},{5,7},{6,4},{7,5},{8,10},{9,11},{10,... | collective-permute-start | bytes 61448 | tf_op jit(solution)/shard_map/ppermute | solution.py:678
  199.9 3.8 %collective-permute-start.21 = (f32[40,128]{1,0:T(8,128)S(1)}, f32[40,128]{1,0:T(8,128)S(1)}, u32[]{:S(2)}, u32[]{:S(2)}) collective-permute-start(f32[40,128]{1,0:T(8,128)S(1)} %reduce_sum.9.c0), channel_id=1, source_target_pairs={{0,3},{1,0},{2,1},{3,2},{4,7},{5,4},{6,5},{7,6},{8,11},{9,8},{10,9... | collective-permute-start | bytes 61448 | tf_op jit(solution)/shard_map/ppermute | solution.py:678
  200.7 3.0 %copy-start.50 = (f32[80,640]{1,0:T(8,128)S(1)}, f32[80,640]{1,0:T(8,128)}, u32[]{:S(2)}) copy-start(f32[80,640]{1,0:T(8,128)} %copy-done.49) | copy-start | bytes 614404
  200.7 3.0 %copy-start.52 = (f32[80,640]{1,0:T(8,128)S(1)}, f32[80,640]{1,0:T(8,128)}, u32[]{:S(2)}) copy-start(f32[80,640]{1,0:T(8,128)} %copy-done.51) | copy-start | bytes 614404
  (63 other events, 62.7 us)

commit v4 on v2

--- a/solution.py
+++ b/solution.py
@@ -21,7 +21,7 @@
 ZS = 4
 ROWS = 80
 SLICE = 40
-MSG = 88
+MSG = 96
 BLK = 256
 NBLK = CH // BLK
 SCALE = STATE ** (-0.5)
@@ -29,7 +29,6 @@
 BF16 = jnp.bfloat16
 HIGH = lax.Precision.HIGHEST
 NT = (((1,), (1,)), ((), ()))
-VMEM = 20 * 2**20
 
 
 def nt(a, b):
@@ -51,8 +50,8 @@
     return dot(a_high, b_high) + (dot(a_low, b_high) + dot(a_high, b_low))
 
 
-def params():
-    return pltpu.CompilerParams(vmem_limit_bytes=VMEM)
+def params(mib=20):
+    return pltpu.CompilerParams(vmem_limit_bytes=mib * 2**20)
 
 
 def cost(flops, nbytes, trans=0):
@@ -69,12 +68,17 @@
     return jnp.where(row <= col if upper else row >= col, 1.0, 0.0).astype(F32)
 
 
-def front_kernel(normed, w_bc, rates, step, grad_y, bmat, cmat, cum, logd, dyt, dywt, pulled, through, turn):
+def front_part(normed, w_bc, code, step, grad_y, bmat, cmat, cum, logd, dyt, dywt, pulled, turn):
     shared = nn(normed[...], w_bc[...])
     bmat[...] = shared[:, :STATE]
     cmat[...] = shared[:, STATE:]
     c_high, c_low = split(shared[:, STATE:])
-    logs = rates[...] * step[...]
+    low = math.log(0.995)
+    high = math.log(0.9999)
+    turn[...] = jnp.zeros((128, 128), F32)
+    turn[0:1, :HEADS] = code[...].astype(F32)
+    codes = turn[...].T[:HEADS, 0:1]
+    logs = (low + codes / (LEVELS - 1) * (high - low)) * step[...]
     logd[...] = logs
     cums = jnp.dot(logs, triangle(True), precision=HIGH, preferred_element_type=F32)
     cum[...] = cums
@@ -96,32 +100,23 @@
         pulled[rows, :] = nn(high, c_high) + (nn(low, c_high) + nn(high, c_low))
     turn[...] = jnp.zeros((128, 128), F32)
     turn[:HEADS, :] = grown[:, 128:]
-    through[...] = jnp.broadcast_to(turn[...].T[127:, :], (8, STATE))
-
-
-def front(normed, w_bc, rates, step, grad_y):
-    return pl.pallas_call(
-        front_kernel,
-        out_shape=(
-            jax.ShapeDtypeStruct((T, STATE), F32),
-            jax.ShapeDtypeStruct((T, STATE), F32),
-            jax.ShapeDtypeStruct((HEADS, T), F32),
-            jax.ShapeDtypeStruct((HEADS, T), F32),
-            jax.ShapeDtypeStruct((CH, T), BF16),
-            jax.ShapeDtypeStruct((CH, T), BF16),
-            jax.ShapeDtypeStruct((CH, STATE), F32),
-            jax.ShapeDtypeStruct((8, STATE), F32),
-        ),
-        scratch_shapes=[pltpu.VMEM((128, 128), F32)],
-        compiler_params=params(),
-        cost_estimate=cost(2 * T * D * 256 + 6 * CH * T * 128, 6 * 2**20),
-    )(normed, w_bc, rates, step, grad_y)
+    through = turn[...].T[127:, :]
+    high = through.astype(BF16).astype(F32)
+    middle = (through - high).astype(BF16).astype(F32)
+    row = lax.broadcasted_iota(jnp.int32, (MSG - 2 * SLICE, STATE), 0)
+    rest = jnp.where(row == 2, through - high - middle, 0.0)
+    return jnp.where(row == 0, high, jnp.where(row == 1, middle, rest))
 
 
 def chain_kernel(table, recv, tie, out, turn):
     del tie
-    lanes = jnp.concatenate([recv[:, 2 * SLICE, :], jnp.zeros((128 - SEQ, 128), F32)], axis=0)
-    turn[...] = lanes.T
+    turn[...] = jnp.zeros((128, 128), F32)
+    parts = []
+    for k in range(SEQ):
+        one = recv[k].astype(F32)
+        parts.append((one[:SLICE], one[SLICE : 2 * SLICE]))
+        turn[k : k + 1, :] = jnp.sum(one[2 * SLICE :], axis=0, keepdims=True)
+    turn[...] = turn[...].T
     head = table[32]
     row = lax.broadcasted_iota(jnp.int32, (SLICE, 128), 0)
     cols = jnp.where(row < table[33], turn[pl.ds(head, 1), :], turn[pl.ds(head + 1, 1), :])
@@ -129,11 +124,11 @@
     pulls = [None] * SEQ
     for k in range(SEQ - 1, -1, -1):
         pulls[k] = pulled
-        pulled = cols[:, k : k + 1] * pulled + recv[k, :SLICE, :]
+        pulled = cols[:, k : k + 1] * pulled + parts[k][0]
     state = jnp.zeros((SLICE, STATE), F32)
     for k in range(SEQ):
         out[k] = jnp.concatenate([pulls[k], state], axis=0).astype(BF16)
-        state = cols[:, k : k + 1] * state + recv[k, SLICE : 2 * SLICE, :]
+        state = cols[:, k : k + 1] * state + parts[k][1]
 
 
 def chain(table, recv, tie):
@@ -153,88 +148,86 @@
     )(table, recv, tie)
 
 
-def channel_kernel(
-    before, normed, w_x, conv_w, cum, logd, bmat, pulled, through, xgt, slope, xwt, msg, ext, pre, own
+def early_kernel(
+    code, before, normed, w_bc, step, grad_y, conv_w, w_x, *refs
 ):
-    step = pl.program_id(0)
-
-    @pl.when(step == 0)
-    def _():
-        ext[:16, :] = before[...]
-        ext[16:, :] = normed[...]
-
-    now = lax.rem(step, 2)
-    past = pre.at[1 - now]
-    total = conv_w[0:1, :] * past[16 : 16 + T, :]
-    for tap in range(1, CONV):
-        total = total + conv_w[tap : tap + 1, :] * past[16 - tap : 16 - tap + T, :]
-    sig = 0.5 * jnp.tanh(0.5 * total) + 0.5
-    xt = (total * sig).T
-    slope[...] = sig * (1.0 + total * (1.0 - sig))
-    parts = []
-    block = jnp.maximum(step - 1, 0)
-    for q in range(BLK // HEAD_DIM):
-        head = pl.ds(block * (BLK // HEAD_DIM) + q, 1)
-        rows = slice(64 * q, 64 * q + 64)
-        gain = jnp.sqrt(-2.0 * logd[head, :])
-        cums = cum[head, :]
-        tail = jnp.exp(cums[:, T - 1 :] - cums)
-        xg = xt[rows] * gain
-        xgt[rows, :] = xg.astype(BF16)
-        parts.append(xg * tail)
-    weighted = jnp.concatenate(parts, axis=0)
-    xwt[...] = weighted.astype(BF16)
-    own[pl.ds(pl.multiple_of(block * BLK, BLK), BLK), :] = wide(nn, weighted, bmat[...])
-    pre[now] = nn(ext[...], w_x[...]).astype(BF16).astype(F32)
-
-    @pl.when(step == NBLK)
-    def _():
-        for k in range(SEQ):
-            rows = slice(SLICE * k, SLICE * (k + 1))
-            msg[k, :SLICE, :] = pulled[rows, :]
-            msg[k, SLICE : 2 * SLICE, :] = own[rows, :]
-            msg[k, 2 * SLICE :, :] = through[...]
-
-
-def channels(before, normed, w_x, conv_w, cum, logd, bmat, pulled, through):
-    def late(i):
-        return jnp.maximum(i - 1, 0)
-
-    rows = pl.BlockSpec((BLK, T), lambda i: (late(i), 0))
-    return pl.pallas_call(
-        channel_kernel,
-        grid=(NBLK + 1,),
-        in_specs=[
-            whole(16, D),
-            whole(T, D),
-            pl.BlockSpec((D, BLK), lambda i: (0, jnp.minimum(i, NBLK - 1))),
-            pl.BlockSpec((CONV, BLK), lambda i: (0, late(i))),
-            whole(HEADS, T),
-            whole(HEADS, T),
-            whole(T, STATE),
-            whole(CH, STATE),
-            whole(8, STATE),
-        ],
-        out_specs=(
-            rows,
-            pl.BlockSpec((T, BLK), lambda i: (0, late(i))),
-            rows,
-            whole(SEQ, MSG, STATE),
-        ),
+    bmat, cmat, cum, logd, dyt, dywt, xgt, xlt, slope, xwt, msg = refs[:11]
+    pulled, turn, ext, pre, own, held, sems = refs[11:]
+    copies = [
+        pltpu.make_async_copy(w_x.at[:, pl.ds(BLK * i, BLK)], held.at[i], sems.at[i])
+        for i in range(NBLK)
+    ]
+    for one in copies:
+        one.start()
+    ext[:16, :] = before[...]
+    ext[16:, :] = normed[...]
+    through = front_part(
+        normed, w_bc, code, step, grad_y, bmat, cmat, cum, logd, dyt, dywt, pulled, turn
+    )
+    b_high, b_low = split(bmat[...])
+    for i in range(NBLK + 1):
+        if i < NBLK:
+            copies[i].wait()
+            pre[i % 2] = nn(ext[...], held[i]).astype(BF16).astype(F32)
+        if i == 0:
+            continue
+        block = i - 1
+        past = pre.at[block % 2]
+        cols = slice(BLK * block, BLK * (block + 1))
+        total = conv_w[0:1, cols] * past[16 : 16 + T, :]
+        for tap in range(1, CONV):
+            total = total + conv_w[tap : tap + 1, cols] * past[16 - tap : 16 - tap + T, :]
+        sig = 0.5 * jnp.tanh(0.5 * total) + 0.5
+        xt = (total * sig).T
+        slope[:, cols] = sig * (1.0 + total * (1.0 - sig))
+        parts = []
+        for q in range(BLK // HEAD_DIM):
+            h = block * (BLK // HEAD_DIM) + q
+            rows = slice(64 * h, 64 * h + 64)
+            gain = jnp.sqrt(-2.0 * logd[h : h + 1, :])
+            cums = cum[h : h + 1, :]
+            tail = jnp.exp(cums[:, T - 1 :] - cums)
+            xg = xt[64 * q : 64 * q + 64] * gain
+            xgt[rows, :], xlt[rows, :] = split(xg)
+            parts.append(xg * tail)
+        high, low = split(jnp.concatenate(parts, axis=0))
+        xwt[cols, :] = high
+        own[cols, :] = nn(high, b_high) + (nn(low, b_high) + nn(high, b_low))
+    for k in range(SEQ):
+        rows = slice(SLICE * k, SLICE * (k + 1))
+        msg[k] = jnp.concatenate([pulled[rows, :], own[rows, :], through], axis=0).astype(BF16)
+
+
+def early(code, before, normed, w_bc, step, grad_y, conv_w, w_x):
+    vm = pl.BlockSpec(memory_space=pltpu.VMEM)
+    return pl.pallas_call(
+        early_kernel,
+        in_specs=[vm] * 7 + [pl.BlockSpec(memory_space=pl.ANY)],
         out_shape=(
+            jax.ShapeDtypeStruct((T, STATE), F32),
+            jax.ShapeDtypeStruct((T, STATE), F32),
+            jax.ShapeDtypeStruct((HEADS, T), F32),
+            jax.ShapeDtypeStruct((HEADS, T), F32),
+            jax.ShapeDtypeStruct((CH, T), BF16),
+            jax.ShapeDtypeStruct((CH, T), BF16),
+            jax.ShapeDtypeStruct((CH, T), BF16),
             jax.ShapeDtypeStruct((CH, T), BF16),
             jax.ShapeDtypeStruct((T, CH), F32),
             jax.ShapeDtypeStruct((CH, T), BF16),
-            jax.ShapeDtypeStruct((SEQ, MSG, STATE), F32),
+            jax.ShapeDtypeStruct((SEQ, MSG, STATE), BF16),
         ),
         scratch_shapes=[
+            pltpu.VMEM((CH, STATE), F32),
+            pltpu.VMEM((128, 128), F32),
             pltpu.VMEM((T + 16, D), BF16),
             pltpu.VMEM((2, T + 16, BLK), F32),
             pltpu.VMEM((CH, STATE), F32),
+            pltpu.VMEM((NBLK, D, BLK), BF16),
+            pltpu.SemaphoreType.DMA((NBLK,)),
         ],
-        compiler_params=params(),
-        cost_estimate=cost(2 * T * D * CH, 10 * 2**20, T * CH),
-    )(before, normed, w_x, conv_w, cum, logd, bmat, pulled, through)
+        compiler_params=params(56),
+        cost_estimate=cost(2 * T * D * (CH + 256), 16 * 2**20, T * CH),
+    )(code, before, normed, w_bc, step, grad_y, conv_w, w_x)
 
 
 def intra_kernel(grad_y, dyt, xgt, cum, bmat, cmat, tie, dxg, rc, dbc, gram, dgram):
@@ -282,9 +275,9 @@
 
     @pl.when(step == NBLK - 1)
     def _():
-        dg = (dgram[...] * SCALE).astype(BF16)
-        dbc[:STATE, :] = nn(cmat[...].T.astype(BF16), dg)
-        dbc[STATE:, :] = nn(dg, bmat[...].astype(BF16)).T
+        dg = dgram[...] * SCALE
+        dbc[:STATE, :] = wide(nn, cmat[...].T, dg)
+        dbc[STATE:, :] = wide(nn, dg, bmat[...]).T
 
 
 def intra(grad_y, dyt, xgt, cum, bmat, cmat, tie):
@@ -322,7 +315,7 @@
     for at, (state, tokens) in enumerate(((ds, xwt), (st, dywt))):
         turned = state[...].T.astype(BF16)
         part = nn(turned, tokens[...]) + dbc[STATE * at : STATE * (at + 1), :]
-        shared[:, STATE * at : STATE * (at + 1)] = part.T
+        shared[:, STATE * at : STATE * (at + 1)] = part.T.astype(BF16)
 
 
 def shared_part(back, xwt, dywt, dbc):
@@ -331,7 +324,7 @@
         out_shape=(
             jax.ShapeDtypeStruct((CH, STATE), F32),
             jax.ShapeDtypeStruct((CH, STATE), F32),
-            jax.ShapeDtypeStruct((T, 2 * STATE), F32),
+            jax.ShapeDtypeStruct((T, 2 * STATE), BF16),
         ),
         compiler_params=params(),
         cost_estimate=cost(4 * CH * T * 128, 4 * 2**20),
@@ -339,73 +332,83 @@
 
 
 def grad_kernel(
-    skip, back, bmat, dxg, dyt, xgt, slope, taps, cum, logd, tie, dpre, halo, halves, cross, ext
+    skip, bmat, taps, cum, logd, tie, back, dxg, dyt, xgt, xlt, slope, dpre, halo, halves, cross, *refs
 ):
     del tie
-    step = pl.program_id(0)
-    later = wide(nt, back[...], bmat[...])
-    parts = []
-    for q in range(BLK // HEAD_DIM):
-        index = step * (BLK // HEAD_DIM) + q
-        head = pl.ds(index, 1)
-        rows = slice(64 * q, 64 * q + 64)
-        gain = jnp.sqrt(-2.0 * logd[head, :])
-        cums = cum[head, :]
-        tail = jnp.exp(cums[:, T - 1 :] - cums)
-        inter = later[rows] * tail
-        whole_dxg = dxg[rows, :] + inter
-        xg = xgt[rows, :].astype(F32)
-        cross[head, :] = jnp.sum(xg * inter, axis=0, keepdims=True)
-        halves[head, :] = 0.5 * jnp.sum(xg * whole_dxg, axis=0, keepdims=True)
-        parts.append(gain * whole_dxg + skip[index] * dyt[rows, :].astype(F32))
-    ext[:8, :] = jnp.zeros((8, BLK), F32)
-    ext[8 : T + 8, :] = jnp.concatenate(parts, axis=0).T * slope[...]
-    ext[T + 8 :, :] = jnp.zeros((8, BLK), F32)
-    total = taps[0:1, :] * ext[8 : T + 8, :]
-    edge = taps[0:1, :] * ext[:8, :]
-    for tap in range(1, CONV):
-        weight = taps[tap : tap + 1, :]
-        total = total + weight * ext[8 + tap : T + 8 + tap, :]
-        edge = edge + weight * ext[tap : 8 + tap, :]
-    dpre[...] = total.astype(BF16)
-    halo[...] = edge
-
-
-def gradients(skip, back, bmat, dxg, dyt, xgt, slope, taps, cum, logd, tie):
-    rows = pl.BlockSpec((BLK, T), lambda i: (i, 0))
-    cols = pl.BlockSpec((T, BLK), lambda i: (0, i))
+    ext, sems, *held = refs
+    copies = []
+    for i in range(NBLK):
+        rows = pl.ds(BLK * i, BLK)
+        parts = [one.at[rows, :] for one in (back, dxg, dyt, xgt, xlt)] + [slope.at[:, rows]]
+        copies.append(
+            [
+                pltpu.make_async_copy(part, buffer.at[i], sems.at[i, at])
+                for at, (part, buffer) in enumerate(zip(parts, held))
+            ]
+        )
+        for one in copies[i]:
+            one.start()
+    b_high, b_low = split(bmat[...])
+    for i in range(NBLK):
+        for one in copies[i]:
+            one.wait()
+        back_i, dxg_i, dyt_i, xgt_i, xlt_i, slope_i = [buffer.at[i] for buffer in held]
+        d_high, d_low = split(back_i[...])
+        later = nt(d_high, b_high) + (nt(d_low, b_high) + nt(d_high, b_low))
+        parts = []
+        for q in range(BLK // HEAD_DIM):
+            index = i * (BLK // HEAD_DIM) + q
+            head = slice(index, index + 1)
+            rows = slice(64 * q, 64 * q + 64)
+            gain = jnp.sqrt(-2.0 * logd[head, :])
+            cums = cum[head, :]
+            tail = jnp.exp(cums[:, T - 1 :] - cums)
+            inter = later[rows] * tail
+            whole_dxg = dxg_i[rows, :] + inter
+            xg = xgt_i[rows, :].astype(F32) + xlt_i[rows, :].astype(F32)
+            cross[head, :] = jnp.sum(xg * inter, axis=0, keepdims=True)
+            halves[head, :] = 0.5 * jnp.sum(xg * whole_dxg, axis=0, keepdims=True)
+            parts.append(gain * whole_dxg + skip[index] * dyt_i[rows, :].astype(F32))
+        cols = slice(BLK * i, BLK * (i + 1))
+        wide_i = ext.at[i % 2]
+        wide_i[:8, :] = jnp.zeros((8, BLK), F32)
+        wide_i[8 : T + 8, :] = jnp.concatenate(parts, axis=0).T * slope_i[...]
+        wide_i[T + 8 :, :] = jnp.zeros((8, BLK), F32)
+        total = taps[0:1, cols] * wide_i[8 : T + 8, :]
+        edge = taps[0:1, cols] * wide_i[:8, :]
+        for tap in range(1, CONV):
+            weight = taps[tap : tap + 1, cols]
+            total = total + weight * wide_i[8 + tap : T + 8 + tap, :]
+            edge = edge + weight * wide_i[tap : 8 + tap, :]
+        dpre[:, cols] = total.astype(BF16)
+        halo[:, cols] = edge
+
+
+def gradients(skip, back, bmat, dxg, dyt, xgt, xlt, slope, taps, cum, logd, tie):
+    vm = pl.BlockSpec(memory_space=pltpu.VMEM)
+    away = pl.BlockSpec(memory_space=pl.ANY)
     return pl.pallas_call(
         grad_kernel,
-        grid=(NBLK,),
-        in_specs=[
-            pl.BlockSpec(memory_space=pltpu.SMEM),
-            pl.BlockSpec((BLK, STATE), lambda i: (i, 0)),
-            whole(T, STATE),
-            rows,
-            rows,
-            rows,
-            cols,
-            pl.BlockSpec((CONV, BLK), lambda i: (0, i)),
-            whole(HEADS, T),
-            whole(HEADS, T),
-            pl.BlockSpec(memory_space=pl.ANY),
-        ],
-        out_specs=(
-            cols,
-            pl.BlockSpec((8, BLK), lambda i: (0, i)),
-            whole(HEADS, T),
-            whole(HEADS, T),
-        ),
+        in_specs=[pl.BlockSpec(memory_space=pltpu.SMEM)] + [vm] * 4 + [away] * 7,
         out_shape=(
             jax.ShapeDtypeStruct((T, CH), BF16),
             jax.ShapeDtypeStruct((8, CH), F32),
             jax.ShapeDtypeStruct((HEADS, T), F32),
             jax.ShapeDtypeStruct((HEADS, T), F32),
         ),
-        scratch_shapes=[pltpu.VMEM((T + 16, BLK), F32)],
-        compiler_params=params(),
+        scratch_shapes=[
+            pltpu.VMEM((2, T + 16, BLK), F32),
+            pltpu.SemaphoreType.DMA((NBLK, 6)),
+            pltpu.VMEM((NBLK, BLK, STATE), F32),
+            pltpu.VMEM((NBLK, BLK, T), F32),
+            pltpu.VMEM((NBLK, BLK, T), BF16),
+            pltpu.VMEM((NBLK, BLK, T), BF16),
+            pltpu.VMEM((NBLK, BLK, T), BF16),
+            pltpu.VMEM((NBLK, T, BLK), F32),
+        ],
+        compiler_params=params(56),
         cost_estimate=cost(4 * CH * T * 128, 6 * 2**20, T * HEADS),
-    )(skip, back, bmat, dxg, dyt, xgt, slope, taps, cum, logd, tie)
+    )(skip, bmat, taps, cum, logd, tie, back, dxg, dyt, xgt, xlt, slope)
 
 
 def step_kernel(fore, back, cmat, dyt, cum, logd, rc, halves, cross, tie, gls):
@@ -498,17 +501,11 @@
 
 
 def near_kernel(*refs):
-    for out, (part, side) in zip(refs[9:], ((1, 0), (3, 1), (1, 1), (3, 0))):
+    order = ((1, 0), (3, 1), (1, 1), (3, 0), (0, 0), (0, 1))
+    for out, (part, side) in zip(refs[9:], order):
         main, extra = product(refs[:8], side)(part)
         out[:, :WIDE] = main.astype(out.dtype)
         out[:, WIDE:] = extra.astype(out.dtype)
-
-
-def here_kernel(*refs):
-    for out, (part, side) in zip(refs[9:], ((0, 0), (0, 1))):
-        main, extra = product(refs[:8], side)(part)
-        out[:, :WIDE] = main
-        out[:, WIDE:] = extra
 
 
 def product_part(kernel, args, ties, types):
@@ -606,58 +603,52 @@
     )(*args)
 
 
-def input_kernel(order, w_x, w_bc, grad, halo, shared, tie, *outs):
-    del order, tie
-    far_up, far_down, near_up, near_down, dir_up, dir_down, here = outs
-    step = pl.program_id(0)
-    rows = w_x.shape[0] // 2
-    low, high = slice(0, rows), slice(rows, 2 * rows)
+def input_kernel(order, w_x, w_bc, grad, halo, shared, tie, *refs):
+    del tie
+    far_up, far_down, near_up, near_down, dir_up, dir_down, here, held, small, sems = refs
+    size = D // ZS
+    half = size // 2
+    copies = []
+    turn = (2, 1, 3, 0)
+    for at, r in enumerate(turn):
+        rows = pl.ds(pl.multiple_of(order[r] * size, size), size)
+        copies.append(pltpu.make_async_copy(w_x.at[rows, :], held.at[at], sems.at[at]))
+        copies[at].start()
+    rows = pl.ds(pl.multiple_of(order[0] * size, size), size)
+    last_copy = pltpu.make_async_copy(w_bc.at[rows, :], small, sems.at[ZS])
+    last_copy.start()
     edge = jnp.concatenate([jnp.zeros((8, CH), F32), halo[...]], axis=0)
     last = (grad[T - 16 :, :].astype(F32) + edge).astype(BF16)
     right = jnp.concatenate([grad[: T - 16, :], last], axis=0)
-    part = nt(w_x[...], right)
-
-    @pl.when(step == 0)
-    def _():
-        far_up[...] = part[low].astype(BF16)
-        far_down[...] = part[high].astype(BF16)
-
-    @pl.when(step == 1)
-    def _():
-        near_up[...] = part[low]
-        dir_up[...] = part[high].astype(BF16)
-
-    @pl.when(step == 2)
-    def _():
-        dir_down[...] = part[low].astype(BF16)
-        near_down[...] = part[high]
-
-    @pl.when(step == 3)
-    def _():
-        here[...] = part + nt(w_bc[...], shared[...])
+    outs = ((far_up, far_down), (near_up, dir_up), (dir_down, near_down))
+    for at, r in enumerate(turn):
+        copies[at].wait()
+        part = nt(held[at], right)
+        if r == 0:
+            last_copy.wait()
+            here[...] = part + nt(small[...], shared[...])
+        else:
+            low, high = outs[at]
+            low[...] = part[:half].astype(low.dtype)
+            high[...] = part[half:].astype(high.dtype)
 
 
 def input_part(order, w_x, w_bc, grad, halo, shared, tie):
     rows = D // ZS
+    vm = pl.BlockSpec(memory_space=pltpu.VMEM)
+    away = pl.BlockSpec(memory_space=pl.ANY)
     sizes = (rows // 2,) * 6 + (rows,)
     types = (BF16, BF16, F32, F32, BF16, BF16, F32)
     return pl.pallas_call(
         input_kernel,
-        grid_spec=pltpu.PrefetchScalarGridSpec(
-            num_scalar_prefetch=1,
-            grid=(ZS,),
-            in_specs=[
-                pl.BlockSpec((rows, CH), lambda i, order: (order[i], 0)),
-                pl.BlockSpec((rows, 2 * STATE), lambda i, order: (order[3], 0)),
-                pl.BlockSpec((T, CH), lambda i, order: (0, 0)),
-                pl.BlockSpec((8, CH), lambda i, order: (0, 0)),
-                pl.BlockSpec((T, 2 * STATE), lambda i, order: (0, 0)),
-                pl.BlockSpec(memory_space=pl.ANY),
-            ],
-            out_specs=[pl.BlockSpec((size, T), lambda i, order: (0, 0)) for size in sizes],
-        ),
+        in_specs=[pl.BlockSpec(memory_space=pltpu.SMEM), away, away, vm, vm, vm, away],
         out_shape=tuple(jax.ShapeDtypeStruct((size, T), one) for size, one in zip(sizes, types)),
-        compiler_params=params(),
+        scratch_shapes=[
+            pltpu.VMEM((ZS, rows, CH), BF16),
+            pltpu.VMEM((rows, 2 * STATE), BF16),
+            pltpu.SemaphoreType.DMA((ZS + 1,)),
+        ],
+        compiler_params=params(48),
         cost_estimate=cost(2 * D * (CH + 64) * T, 10 * 2**20),
     )(order, w_x, w_bc, grad, halo, shared, tie)
 
@@ -699,26 +690,23 @@
     return np.array(rows, np.int32)
 
 
-def head_table():
-    return np.array([[(z + r) % ZS for r in (2, 1, 3, 0)] for z in range(ZS)], np.int32)
+def full_table():
+    order = [[(z + r) % ZS for r in range(ZS)] for z in range(ZS)]
+    return np.array([[list(one) + o for o in order] for one in place_table()], np.int32)
 
 
 def body(normed, w_x, w_bc, conv_w, decay_code, step, d_skip, grad_y):
     place = lax.axis_index("seq")
     core = place % 2
     z = lax.axis_index("head")
-    order_z = jnp.asarray(head_table())[z]
-    table = lax.dynamic_index_in_dim(jnp.asarray(place_table()), place, 0, keepdims=False)
+    table = jnp.asarray(full_table())[place, z]
+    order_z = table[34:]
     swap = [(i, i ^ 1) for i in range(SEQ)]
 
-    low = math.log(0.995)
-    high = math.log(0.9999)
-    rates = low + decay_code.astype(F32)[:, None] / (LEVELS - 1) * (high - low)
     before = lax.ppermute(normed[T - 16 :], "seq", [(i, i + 1) for i in range(SEQ - 1)])
 
-    bmat, cmat, cum, logd, dyt, dywt, pulled, through = front(normed, w_bc, rates, step, grad_y)
-    xgt, slope, xwt, msg = channels(
-        before, normed, w_x, conv_w, cum, logd, bmat, pulled, through
+    bmat, cmat, cum, logd, dyt, dywt, xgt, xlt, slope, xwt, msg = early(
+        decay_code[None, :], before, normed, w_bc, step, grad_y, conv_w, w_x
     )
     recv = lax.all_to_all(msg, "seq", 0, 0)
     mine, other = select(table, normed, msg)
@@ -727,17 +715,18 @@
     back = lax.all_to_all(chain(table, recv, rc), "seq", 0, 0)
 
     ds, st, shared = shared_part(back, xwt, dywt, dbc)
-    for bit in (1, 2):
-        pairs = [(i, i ^ bit) for i in range(ZS)]
-        shared = shared + lax.ppermute(shared, "head", pairs)
-    shared = shared.astype(BF16)
+    others = [along_head(by)(shared) for by in (1, 2, 3)]
     dpre, halo, halves, cross = gradients(
-        d_skip, ds, bmat, dxg, dyt, xgt, slope, conv_w, cum, logd, st
+        d_skip, ds, bmat, dxg, dyt, xgt, xlt, slope, conv_w, cum, logd, st
     )
     dpre_other = lax.ppermute(dpre, "seq", swap)
     halo_mine = lax.ppermute(halo, "seq", [(i, i - 1) for i in range(1, SEQ)])
     halo_pair = lax.ppermute(halo, "seq", [(i, i - 2) for i in range(2, SEQ, 2)])
     halo_other = jnp.where(core == 0, halo_pair, halo)
+    one, two, three, _ = lax.optimization_barrier((*others, halo))
+    near_pair = shared.astype(F32) + two.astype(F32)
+    far_pair = one.astype(F32) + three.astype(F32)
+    shared = (near_pair + far_pair).astype(BF16)
     shared_other = lax.ppermute(shared, "seq", swap)
 
     args = (mine, other, dpre, dpre_other, halo_mine, halo_other, shared, shared_other)
@@ -746,14 +735,13 @@
     head = {by: along_head(by) for by in (1, -1)}
     far_up, far_down = product_part(far_kernel, args, (), (BF16, BF16))
     ru, rd = move[1](far_up), move[-1](far_down)
-    near_up, near_down, dir_up, dir_down = product_part(
-        near_kernel, args, (far_up,), (F32, F32, BF16, BF16)
+    near_up, near_down, dir_up, dir_down, here_a, here_b = product_part(
+        near_kernel, args, (far_up,), (F32, F32, BF16, BF16, F32, F32)
     )
     up, down = join((near_up, ru, dir_up), (near_down, rd, dir_down))
     ru, rd = move[1](up), move[-1](down)
-    here_a, here_b = product_part(here_kernel, args, (up,), (F32, F32))
     z_far_up, z_far_down, z_up, z_down, z_dir_up, z_dir_down, z_here = input_part(
-        order_z, w_x, w_bc, dpre, halo_mine, shared, here_a
+        order_z, w_x, w_bc, dpre, halo_mine, shared, up
     )
     gls = step_part(st, ds, cmat, dyt, cum, logd, rc, halves, cross, z_here)
     far_up, far_down, near_up, near_down, dir_up, dir_down, here_a, here_b = turn_part(
@@ -761,14 +749,10 @@
     )
     ru, rd = turn[1](far_up), turn[-1](far_down)
     zu, zd = head[1](z_far_up), head[-1](z_far_down)
-    up, down, z_up, z_down = join(
-        (near_up, ru, dir_up),
-        (near_down, rd, dir_down),
-        (z_up, zu, z_dir_up),
-        (z_down, zd, z_dir_down),
-    )
+    z_up, z_down = join((z_up, zu, z_dir_up), (z_down, zd, z_dir_down))
+    zu, zd = head[1](z_up), head[-1](z_down)
+    up, down = join((near_up, ru, dir_up), (near_down, rd, dir_down))
     ru, rd = turn[1](up), turn[-1](down)
-    zu, zd = head[1](z_up), head[-1](z_down)
     grad_wx, grad_wbc, grad_u = last_part(here_a, here_b, ru, rd, z_here, zu, zd)
     return (grad_u, grad_wx, grad_wbc, gls)
 

time: 153 us -> 126 us (0.82)
  waiting for transfers between devices: 34.7 us -> 17.3 us
  local copies, waits for them, and re-layouts: 27.7 us -> 11.6 us
  Pallas kernels: 31 us -> 35.2 us
  starting transfers between devices: 38.8 us -> 42.7 us
  other arithmetic: 2.46 us -> 0.08 us
    unnamed x102 -> x52, local copies, waits for them, and re-layouts: 25.3 us -> 9.22 us
    all_to_all x1, waiting for transfers between devices: 13.5 us -> 2.73 us  [body(): recv = lax.all_to_all(msg, 'seq', 0, 0)]
    ppermute x2 -> x0, waiting for transfers between devices: 7.15 us -> none  [body(): shared = shared + lax.ppermute(shared, 'head', pairs)]
    pallas_call x4 -> x3, Pallas kernels: 15.5 us -> 22.5 us  [the longest x1 10.4 us: early(): pl.pallas_call(early_kernel, in_specs=[vm] * 7 + [pl.BlockSpec(memory_spa...]
    ppermute x4 -> x7, starting transfers between devices: 6.61 us -> 13.1 us  [along_head(): lax.ppermute(value, 'head', [(i, (i + by) % ZS) for i in range(ZS)])]
    ppermute x2 -> x0, starting transfers between devices: 5.71 us -> none  [body(): shared = shared + lax.ppermute(shared, 'head', pairs)]
    ppermute x8, waiting for transfers between devices: 12.8 us -> 9.78 us  [along(): return lambda value: lax.ppermute(value, 'seq', ring(first, by))]
    all_to_all x1, starting transfers between devices: 9.15 us -> 11.1 us  [body(): recv = lax.all_to_all(msg, 'seq', 0, 0)]
  transfers between devices with their start and end apart: 21 -> 22, of which waited for: 8 -> 8; matrix products, arithmetic and copies ran while one was open for 2% -> 1% of each run, Pallas kernels for 12% -> 17%
where the time goes in v4:
time: 126 us; the launch traced here: 125 us
  starting transfers between devices  42.7 us (34%)
  Pallas kernels  35.2 us (28%)
  waiting for transfers between devices  17.3 us (14%)
  blocking collectives  17 us (13%)
  local copies, waits for them, and re-layouts  11.6 us (9%)
    all_to_all x1, blocking collectives, body(): back = lax.all_to_all(chain(table, recv, rc), 'seq', 0, 0)  17 us
    ppermute x8, starting transfers between devices, along(): return lambda value: lax.ppermute(value, 'seq', ring(first, by))  13.3 us
    ppermute x7, starting transfers between devices, along_head(): lax.ppermute(value, 'head', [(i, (i + by) % ZS) for i in range(ZS)])  13.1 us
    all_to_all x1, starting transfers between devices, body(): recv = lax.all_to_all(msg, 'seq', 0, 0)  11.1 us
    pallas_call x1, Pallas kernels, early(): pl.pallas_call(early_kernel, in_specs=[vm] * 7 + [pl.BlockSpec(memory_spa...  10.4 us
    ppermute x8, waiting for transfers between devices, along(): return lambda value: lax.ppermute(value, 'seq', ring(first, by))  9.78 us
    unnamed x52, local copies, waits for them, and re-layouts  9.22 us
    pallas_call x1, Pallas kernels, input_part(): pl.pallas_call(input_kernel, in_specs=[pl.BlockSpec(memory_space=pltpu.SM...  6.31 us
  transfers between devices with their start and end apart: 22, of which 8 were waited for; matrix products, arithmetic and copies ran while one was open for 1% of the time, Pallas kernels for 17%

profile of v4, /device:TPU:0, one launch (start us, length us, event | category | flops | bytes accessed | tf_op | source)
XLA Modules:
  0.0 124.8 jit_solution(16500605290335515525)
XLA Ops:
  0.6 0.9 slice.9
  1.5 1.3 %collective-permute-start = (bf16[16,2560]{1,0:T(8,128)(2,1)S(1)}, bf16[16,2560]{1,0:T(8,128)(2,1)S(1)}, u32[]{:S(2)}, u32[]{:S(2)}) collective-permute-start(bf16[16,2560]{1,0:T(8,128)(2,1)S(1)} %slice.9), channel_id=1, source_target_pairs={{0,4},{4,8},{8,12},{12,16},{16,20},{20,24},{24,28},{28,32},{32,36}... | collective-permute-start | bytes 245768 | tf_op jit(solution)/shard_map/ppermute | solution.py:706
  2.8 0.9 collective-permute-done.before
  3.7 0.6 copy-done.25
  4.4 10.4 %shard_map.120 = (f32[256,128]{1,0:T(8,128)}, f32[256,128]{1,0:T(8,128)}, f32[20,256]{1,0:T(8,128)}, f32[20,256]{1,0:T(8,128)}, bf16[1280,256]{1,0:T(8,128)(2,1)...) custom-call(s32[1,20]{1,0:T(1,128)} %bitcast.5, ...), custom_call_target="tpu_custom_call" | custom-call | flops 2013265920 | bytes 16777216 | tf_op jit(solution)/shard_map/pallas_call | solution.py:203
  14.8 11.1 %all-to-all-start = ((bf16[32,96,128]{2,1,0:T(8,128)(2,1)}), bf16[32,96,128]{2,1,0:T(8,128)(2,1)S(1)}, u32[]{:S(2)}, u32[]{:S(2)}) async-start(bf16[32,96,128]{2,1,0:T(8,128)(2,1)} %get-tuple-element.62.tie), calls=%async_computation | async-start | bytes 1572864 | tf_op jit(solution)/shard_map/all_to_all | solution.py:711
  25.9 0.7 fusion.order.table
  26.6 1.1 copy-done.2
  27.7 1.0 shard_map.121
  28.8 0.8 copy-done.23
  29.6 1.1 copy-done.14
  30.7 0.9 copy-done.17
  31.6 0.7 copy-done.18
  32.4 3.6 %shard_map.122 = (f32[1280,256]{1,0:T(8,128)S(1)}, f32[20,256]{1,0:T(8,128)S(1)}, f32[256,256]{1,0:T(8,128)S(1)}) custom-call(bf16[256,1280]{1,0:T(8,128)(2,1)S(1)} %copy-done.14, bf16[1280,256]{1,0:T(8,128)(2,1)S(1)} %copy-done.5, bf16[1280,256]{1,0:T(8,128)(2,1)S(1)} %copy-done.15, f32[20,256]{1,0:T(8,128)S(1)} %copy-done.18, f32[256,128]{1,0:T(8,128)S(1)} %copy-done.17, ...), custom_call_target="tpu_custom_call" | custom-call | flops 1342177280 | bytes 4194304 | tf_op jit(solution)/shard_map/pallas_call | solution.py:285
  36.0 1.1 copy-done.11
  37.0 2.7 %all-to-all-done.recv = bf16[32,96,128]{2,1,0:T(8,128)(2,1)S(1)} async-done(((bf16[32,96,128]{2,1,0:T(8,128)(2,1)}), bf16[32,96,128]{2,1,0:T(8,128)(2,1)S(1)}, u32[]{:S(2)}, u32[]{:S(2)}) %all-to-all-start) | async-done | bytes 786464 | tf_op jit(solution)/shard_map/all_to_all | solution.py:711
  39.7 1.0 shard_map.123
  40.8 17.0 %all_to_all.10.back = bf16[32,80,128]{2,1,0:T(8,128)(2,1)S(1)} all-to-all(bf16[32,80,128]{2,1,0:T(8,128)(2,1)S(1)} %shard_map.123), channel_id=1, replica_groups=mesh['seq'=32,'head'=4] {'seq'}, dimensions={0} | all-to-all | bytes 1310720 | tf_op jit(solution)/shard_map/all_to_all | solution.py:715
  58.3 0.8 copy-done.7
  59.1 0.8 copy-done.9
  60.0 1.9 %collective-permute-start.5 = (bf16[256,256]{1,0:T(8,128)(2,1)S(1)}, bf16[256,256]{1,0:T(8,128)(2,1)S(1)}, u32[]{:S(2)}, u32[]{:S(2)}) collective-permute-start(bf16[256,256]{1,0:T(8,128)(2,1)S(1)} %get-tuple-element.82), channel_id=1, source_target_pairs={{0,1},{1,2},{2,3},{3,0},{4,5},{5,6},{6,7},{7,4},{8,9},{9,10},{10,1... | collective-permute-start | bytes 393224 | tf_op jit(solution)/shard_map/ppermute | solution.py:676
  61.9 3.6 %collective-permute-start.6 = (bf16[256,256]{1,0:T(8,128)(2,1)S(1)}, bf16[256,256]{1,0:T(8,128)(2,1)S(1)}, u32[]{:S(2)}, u32[]{:S(2)}) collective-permute-start(bf16[256,256]{1,0:T(8,128)(2,1)S(1)} %get-tuple-element.82), channel_id=1, source_target_pairs={{0,2},{1,3},{2,0},{3,1},{4,6},{5,7},{6,4},{7,5},{8,10},{9,11},{10,... | collective-permute-start | bytes 393224 | tf_op jit(solution)/shard_map/ppermute | solution.py:676
  65.5 1.0 collective-permute-start.7
  66.5 5.8 %shard_map.125 = (bf16[256,1280]{1,0:T(8,128)(2,1)}, f32[8,1280]{1,0:T(8,128)}, f32[20,256]{1,0:T(8,128)}, f32[20,256]{1,0:T(8,128)}) custom-call(f32[20]{0:T(128)} %skip.1, f32[256,128]{1,0:T(8,128)} %get-tuple-element.65.bmat, f32[4,1280]{1,0:T(4,128)} %taps.1, f32[20,256]{1,0:T(8,128)} %get-tuple-element.66.cum, f32[20,256]{1,0:T(8,128)} %get-tuple-element.67.logd, ...), custom_call_target="tpu_custom_call" | custom-call | flops 167772160 | bytes 6291456 | tf_op jit(solution)/shard_map/pallas_call | solution.py:390
  72.3 1.3 %collective-permute-start.4 = (f32[8,1280]{1,0:T(8,128)}, f32[8,1280]{1,0:T(8,128)S(1)}, u32[]{:S(2)}, u32[]{:S(2)}) collective-permute-start(f32[8,1280]{1,0:T(8,128)} %get-tuple-element.81), channel_id=1, source_target_pairs={{8,0},{16,8},{24,16},{32,24},{40,32},{48,40},{56,48},{64,56},{72,6... | collective-permute-start | bytes 122888 | tf_op jit(solution)/shard_map/ppermute | solution.py:724
  73.6 1.3 %collective-permute-start.3 = (f32[8,1280]{1,0:T(8,128)}, f32[8,1280]{1,0:T(8,128)S(1)}, u32[]{:S(2)}, u32[]{:S(2)}) collective-permute-start(f32[8,1280]{1,0:T(8,128)} %get-tuple-element.81), channel_id=1, source_target_pairs={{4,0},{8,4},{12,8},{16,12},{20,16},{24,20},{28,24},{32,28},{36,32}... | collective-permute-start | bytes 122888 | tf_op jit(solution)/shard_map/ppermute | solution.py:723
  74.9 1.2 collective-permute-start.2
  76.3 2.1 %collective-permute-done.4 = f32[8,1280]{1,0:T(8,128)S(1)} collective-permute-done((f32[8,1280]{1,0:T(8,128)}, f32[8,1280]{1,0:T(8,128)S(1)}, u32[]{:S(2)}, u32[]{:S(2)}) %collective-permute-start.4) | collective-permute-done | bytes 40992 | tf_op jit(solution)/shard_map/ppermute | solution.py:724
  78.5 1.1 copy-done.3
  79.5 0.8 shard_map.126
  80.4 3.2 %collective-permute-start.10 = (bf16[320,768]{1,0:T(8,128)(2,1)S(1)}, bf16[320,768]{1,0:T(8,128)(2,1)S(1)}, u32[]{:S(2)}, u32[]{:S(2)}) collective-permute-start(bf16[320,768]{1,0:T(8,128)(2,1)S(1)} %get-tuple-element.92), channel_id=1, source_target_pairs={{0,96},{4,28},{8,104},{12,4},{16,112},{20,12},{24,120},{28,20},{32... | collective-permute-start | bytes 1474568 | tf_op jit(solution)/shard_map/ppermute | solution.py:672
  83.8 2.3 %shard_map.127 = (f32[320,768]{1,0:T(8,128)S(1)}, f32[320,768]{1,0:T(8,128)S(1)}, bf16[320,768]{1,0:T(8,128)(2,1)S(1)}, bf16[320,768]{1,0:T(8,128)(2,1)S(1)}, f3...) custom-call(bf16[1280,256]{1,0:T(8,128)(2,1)S(1)} %get-tuple-element.63.tie.refs_0_, ...), custom_call_target="tpu_custom_call" | custom-call | flops 1509949440 | bytes 9437184 | tf_op jit(solution)/shard_map/pallas_call | solution.py:513
  86.1 4.5 %collective-permute-done.10.refs_4_ = bf16[320,768]{1,0:T(8,128)(2,1)S(1)} collective-permute-done((bf16[320,768]{1,0:T(8,128)(2,1)S(1)}, bf16[320,768]{1,0:T(8,128)(2,1)S(1)}, u32[]{:S(2)}, u32[]{:S(2)}) %collective-permute-start.10) | collective-permute-done | bytes 491552 | tf_op jit(solution)/shard_map/ppermute | solution.py:672
  90.5 3.1 %collective-permute-done.9.refs_1_ = bf16[320,768]{1,0:T(8,128)(2,1)S(1)} collective-permute-done((bf16[320,768]{1,0:T(8,128)(2,1)S(1)}, bf16[320,768]{1,0:T(8,128)(2,1)S(1)}, u32[]{:S(2)}, u32[]{:S(2)}) %collective-permute-start.9) | collective-permute-done | bytes 491552 | tf_op jit(solution)/shard_map/ppermute | solution.py:672
  93.9 3.2 %collective-permute-start.12 = (bf16[640,768]{1,0:T(8,128)(2,1)S(1)}, bf16[640,768]{1,0:T(8,128)(2,1)S(1)}, u32[]{:S(2)}, u32[]{:S(2)}) collective-permute-start(bf16[640,768]{1,0:T(8,128)(2,1)S(1)} %get-tuple-element.95), channel_id=1, source_target_pairs={{0,96},{4,28},{8,104},{12,4},{16,112},{20,12},{24,120},{28,20},{32... | collective-permute-start | bytes 2949128 | tf_op jit(solution)/shard_map/ppermute | solution.py:672
  97.2 0.7 constant_dynamic-slice_fusion
  97.9 6.3 %shard_map.131 = (bf16[320,256]{1,0:T(8,128)(2,1)S(1)}, bf16[320,256]{1,0:T(8,128)(2,1)S(1)}, f32[320,256]{1,0:T(8,128)S(1)}, f32[320,256]{1,0:T(8,128)S(1)}, bf...) custom-call(s32[4]{0:T(128)S(1)} %slice_bitcast_fusion.order, ...), custom_call_target="tpu_custom_call" | custom-call | flops 1761607680 | bytes 10485760 | tf_op jit(solution)/shard_map/pallas_call | solution.py:642
  104.2 1.1 collective-permute-start.17
  105.3 2.2 %collective-permute-start.18 = (bf16[320,256]{1,0:T(8,128)(2,1)S(1)}, bf16[320,256]{1,0:T(8,128)(2,1)S(1)}, u32[]{:S(2)}, u32[]{:S(2)}) collective-permute-start(bf16[320,256]{1,0:T(8,128)(2,1)S(1)} %get-tuple-element.111), channel_id=1, source_target_pairs={{0,3},{1,0},{2,1},{3,2},{4,7},{5,4},{6,5},{7,6},{8,11},{9,8},{10,9... | collective-permute-start | bytes 491528 | tf_op jit(solution)/shard_map/ppermute | solution.py:676
  107.6 1.7 %collective-permute-done.11.up = bf16[640,768]{1,0:T(8,128)(2,1)S(1)} collective-permute-done((bf16[640,768]{1,0:T(8,128)(2,1)S(1)}, bf16[640,768]{1,0:T(8,128)(2,1)S(1)}, u32[]{:S(2)}, u32[]{:S(2)}) %collective-permute-start.11) | collective-permute-done | bytes 983072 | tf_op jit(solution)/shard_map/ppermute | solution.py:672
  109.9 3.0 %collective-permute-start.14 = (bf16[80,768]{1,0:T(8,128)(2,1)S(1)}, bf16[80,768]{1,0:T(8,128)(2,1)S(1)}, u32[]{:S(2)}, u32[]{:S(2)}) collective-permute-start(bf16[80,768]{1,0:T(8,128)(2,1)S(1)} %get-tuple-element.102), channel_id=1, source_target_pairs={{0,24},{4,100},{8,0},{12,108},{16,8},{20,116},{24,16},{28,124},{32... | collective-permute-start | bytes 368648 | tf_op jit(solution)/shard_map/ppermute | solution.py:672
  113.0 1.1 collective-permute-start.19
  114.1 2.2 %collective-permute-start.20 = (bf16[640,256]{1,0:T(8,128)(2,1)S(1)}, bf16[640,256]{1,0:T(8,128)(2,1)S(1)}, u32[]{:S(2)}, u32[]{:S(2)}) collective-permute-start(bf16[640,256]{1,0:T(8,128)(2,1)S(1)} %get-tuple-element.114), channel_id=1, source_target_pairs={{0,3},{1,0},{2,1},{3,2},{4,7},{5,4},{6,5},{7,6},{8,11},{9,8},{10,9... | collective-permute-start | bytes 983048 | tf_op jit(solution)/shard_map/ppermute | solution.py:676
  116.4 3.2 %collective-permute-start.16 = (bf16[160,768]{1,0:T(8,128)(2,1)S(1)}, bf16[160,768]{1,0:T(8,128)(2,1)S(1)}, u32[]{:S(2)}, u32[]{:S(2)}) collective-permute-start(bf16[160,768]{1,0:T(8,128)(2,1)S(1)} %get-tuple-element.105), channel_id=1, source_target_pairs={{0,24},{4,100},{8,0},{12,108},{16,8},{20,116},{24,16},{28,124},{32... | collective-permute-start | bytes 737288 | tf_op jit(solution)/shard_map/ppermute | solution.py:672
  119.7 1.8 %shard_map.134 = f32[20,256]{1,0:T(8,128)} custom-call(f32[1280,128]{1,0:T(8,128)S(1)} %copy-done.10, f32[1280,128]{1,0:T(8,128)S(1)} %copy-done.8, f32[256,128]{1,0:T(8,128)S(1)} %copy-done.16, bf16[1280,256]{1,0:T(8,128)(2,1)S(1)} %copy-done.6, f32[20,256]{1,0:T(8,128)S(1)} %copy-done.19, f32[20,256]{1,0:T(8,128)S(1)} %copy-done.20, ...), custom_call_target="tpu_custom_call" | custom-call | flops 167772160 | bytes 4194304 | tf_op jit(solution)/shard_map/pallas_call | solution.py:437
  121.5 1.8 %collective-permute-done.19.up_u = bf16[640,256]{1,0:T(8,128)(2,1)S(1)} collective-permute-done((bf16[640,256]{1,0:T(8,128)(2,1)S(1)}, bf16[640,256]{1,0:T(8,128)(2,1)S(1)}, u32[]{:S(2)}, u32[]{:S(2)}) %collective-permute-start.19) | collective-permute-done | bytes 327712 | tf_op jit(solution)/shard_map/ppermute | solution.py:676
  123.3 0.5 collective-permute-done.15.up
  123.8 1.0 shard_map.133
  (70 shorter events, 2.1 us)
Async XLA Ops:
  1.5 2.2 %collective-permute-start = (bf16[16,2560]{1,0:T(8,128)(2,1)S(1)}, bf16[16,2560]{1,0:T(8,128)(2,1)S(1)}, u32[]{:S(2)}, u32[]{:S(2)}) collective-permute-start(bf16[16,2560]{1,0:T(8,128)(2,1)S(1)} %slice.9), channel_id=1, source_target_pairs={{0,4},{4,8},{8,12},{12,16},{16,20},{20,24},{24,28},{28,32},{32,36}... | collective-permute-start | bytes 245768 | tf_op jit(solution)/shard_map/ppermute | solution.py:706
  3.7 0.6 copy-start.25
  14.8 11.8 %copy-start = (bf16[256,2560]{1,0:T(8,128)(2,1)S(1)}, bf16[256,2560]{1,0:T(8,128)(2,1)}, u32[]{:S(2)}) copy-start(bf16[256,2560]{1,0:T(8,128)(2,1)} %normed.3) | copy-start | bytes 3932164
  14.8 14.9 %copy-start.16 = (f32[256,128]{1,0:T(8,128)S(1)}, f32[256,128]{1,0:T(8,128)}, u32[]{:S(2)}) copy-start(f32[256,128]{1,0:T(8,128)} %get-tuple-element.70.cmat) | copy-start | bytes 393220
  14.8 25.0 %all-to-all-start = ((bf16[32,96,128]{2,1,0:T(8,128)(2,1)}), bf16[32,96,128]{2,1,0:T(8,128)(2,1)S(1)}, u32[]{:S(2)}, u32[]{:S(2)}) async-start(bf16[32,96,128]{2,1,0:T(8,128)(2,1)} %get-tuple-element.62.tie), calls=%async_computation | async-start | bytes 1572864 | tf_op jit(solution)/shard_map/all_to_all | solution.py:711
  26.6 1.1 copy-start.2
  27.7 1.9 %copy-start.5 = (bf16[1280,256]{1,0:T(8,128)(2,1)S(1)}, bf16[1280,256]{1,0:T(8,128)(2,1)}, u32[]{:S(2)}) copy-start(bf16[1280,256]{1,0:T(8,128)(2,1)} %get-tuple-element.68.dyt) | copy-start | bytes 1966084
  27.7 1.9 %copy-start.15 = (bf16[1280,256]{1,0:T(8,128)(2,1)S(1)}, bf16[1280,256]{1,0:T(8,128)(2,1)}, u32[]{:S(2)}) copy-start(bf16[1280,256]{1,0:T(8,128)(2,1)} %get-tuple-element.69.xgt) | copy-start | bytes 1966084
  28.8 0.9 copy-start.23
  29.6 1.1 copy-start.14
  30.7 0.9 copy-start.17
  31.6 0.7 copy-start.18
  35.9 1.1 copy-start.11
  39.7 18.1 %copy-start.12 = (bf16[1280,256]{1,0:T(8,128)(2,1)S(1)}, bf16[1280,256]{1,0:T(8,128)(2,1)}, u32[]{:S(2)}) copy-start(bf16[1280,256]{1,0:T(8,128)(2,1)} %get-tuple-element.73.dywt) | copy-start | bytes 1966084
  39.7 18.1 %copy-start.13 = (bf16[1280,256]{1,0:T(8,128)(2,1)S(1)}, bf16[1280,256]{1,0:T(8,128)(2,1)}, u32[]{:S(2)}) copy-start(bf16[1280,256]{1,0:T(8,128)(2,1)} %get-tuple-element.72.xwt) | copy-start | bytes 1966084
  57.8 8.7 %copy-start.24 = (bf16[1280,256]{1,0:T(8,128)(2,1)S(1)}, bf16[1280,256]{1,0:T(8,128)(2,1)}, u32[]{:S(2)}) copy-start(bf16[1280,256]{1,0:T(8,128)(2,1)} %copy-done.23) | copy-start | bytes 1966084
  58.3 0.8 copy-start.7
  59.1 0.8 copy-start.9
  60.0 13.6 %collective-permute-start.5 = (bf16[256,256]{1,0:T(8,128)(2,1)S(1)}, bf16[256,256]{1,0:T(8,128)(2,1)S(1)}, u32[]{:S(2)}, u32[]{:S(2)}) collective-permute-start(bf16[256,256]{1,0:T(8,128)(2,1)S(1)} %get-tuple-element.82), channel_id=1, source_target_pairs={{0,1},{1,2},{2,3},{3,0},{4,5},{5,6},{6,7},{7,4},{8,9},{9,10},{10,1... | collective-permute-start | bytes 393224 | tf_op jit(solution)/shard_map/ppermute | solution.py:676
  61.9 13.0 %collective-permute-start.6 = (bf16[256,256]{1,0:T(8,128)(2,1)S(1)}, bf16[256,256]{1,0:T(8,128)(2,1)S(1)}, u32[]{:S(2)}, u32[]{:S(2)}) collective-permute-start(bf16[256,256]{1,0:T(8,128)(2,1)S(1)} %get-tuple-element.82), channel_id=1, source_target_pairs={{0,2},{1,3},{2,0},{3,1},{4,6},{5,7},{6,4},{7,5},{8,10},{9,11},{10,... | collective-permute-start | bytes 393224 | tf_op jit(solution)/shard_map/ppermute | solution.py:676
  65.5 10.6 %collective-permute-start.7 = (bf16[256,256]{1,0:T(8,128)(2,1)S(1)}, bf16[256,256]{1,0:T(8,128)(2,1)S(1)}, u32[]{:S(2)}, u32[]{:S(2)}) collective-permute-start(bf16[256,256]{1,0:T(8,128)(2,1)S(1)} %get-tuple-element.82), channel_id=1, source_target_pairs={{0,3},{1,0},{2,1},{3,2},{4,7},{5,4},{6,5},{7,6},{8,11},{9,8},{10,9... | collective-permute-start | bytes 393224 | tf_op jit(solution)/shard_map/ppermute | solution.py:676
  66.5 11.9 %collective-permute-start.1 = (bf16[1280,256]{1,0:T(8,128)(2,1)S(1)}, bf16[1280,256]{1,0:T(8,128)(2,1)S(1)}, u32[]{:S(2)}, u32[]{:S(2)}) collective-permute-start(bf16[1280,256]{1,0:T(8,128)(2,1)S(1)} %copy-done.24), channel_id=1, source_target_pairs={{0,4},{4,0},{8,12},{12,8},{16,20},{20,16},{24,28},{28,24},{32,36},... | collective-permute-start | bytes 1966088 | tf_op jit(solution)/shard_map/ppermute | solution.py:713
  72.3 6.1 %collective-permute-start.4 = (f32[8,1280]{1,0:T(8,128)}, f32[8,1280]{1,0:T(8,128)S(1)}, u32[]{:S(2)}, u32[]{:S(2)}) collective-permute-start(f32[8,1280]{1,0:T(8,128)} %get-tuple-element.81), channel_id=1, source_target_pairs={{8,0},{16,8},{24,16},{32,24},{40,32},{48,40},{56,48},{64,56},{72,6... | collective-permute-start | bytes 122888 | tf_op jit(solution)/shard_map/ppermute | solution.py:724
  73.6 4.8 %collective-permute-start.3 = (f32[8,1280]{1,0:T(8,128)}, f32[8,1280]{1,0:T(8,128)S(1)}, u32[]{:S(2)}, u32[]{:S(2)}) collective-permute-start(f32[8,1280]{1,0:T(8,128)} %get-tuple-element.81), channel_id=1, source_target_pairs={{4,0},{8,4},{12,8},{16,12},{20,16},{24,20},{28,24},{32,28},{36,32}... | collective-permute-start | bytes 122888 | tf_op jit(solution)/shard_map/ppermute | solution.py:723
  74.9 3.5 %collective-permute-start.2 = (bf16[256,1280]{1,0:T(8,128)(2,1)}, bf16[256,1280]{1,0:T(8,128)(2,1)S(1)}, u32[]{:S(2)}, u32[]{:S(2)}) collective-permute-start(bf16[256,1280]{1,0:T(8,128)(2,1)} %get-tuple-element.80.refs_2_.grad), channel_id=1, source_target_pairs={{0,4},{4,0},{8,12},{12,8},{16,20},{20,16},{24,28},{28,24},{32,36},... | collective-permute-start | bytes 1966088 | tf_op jit(solution)/shard_map/ppermute | solution.py:722
  76.2 2.2 %collective-permute-start.8 = (bf16[256,256]{1,0:T(8,128)(2,1)S(1)}, bf16[256,256]{1,0:T(8,128)(2,1)S(1)}, u32[]{:S(2)}, u32[]{:S(2)}) collective-permute-start(bf16[256,256]{1,0:T(8,128)(2,1)S(1)} %add_convert_fusion.refs_6_.shared), channel_id=1, source_target_pairs={{0,4},{4,0},{8,12},{12,8},{16,20},{20,16},{24,28},{28,24},{32,36},... | collective-permute-start | bytes 393224 | tf_op jit(solution)/shard_map/ppermute | solution.py:730
  78.4 1.1 copy-start.3
  79.5 4.3 %copy-start.4 = (bf16[256,1280]{1,0:T(8,128)(2,1)S(1)}, bf16[256,1280]{1,0:T(8,128)(2,1)}, u32[]{:S(2)}) copy-start(bf16[256,1280]{1,0:T(8,128)(2,1)} %get-tuple-element.80.refs_2_.grad) | copy-start | bytes 1966084
  80.4 10.1 %collective-permute-start.10 = (bf16[320,768]{1,0:T(8,128)(2,1)S(1)}, bf16[320,768]{1,0:T(8,128)(2,1)S(1)}, u32[]{:S(2)}, u32[]{:S(2)}) collective-permute-start(bf16[320,768]{1,0:T(8,128)(2,1)S(1)} %get-tuple-element.92), channel_id=1, source_target_pairs={{0,96},{4,28},{8,104},{12,4},{16,112},{20,12},{24,120},{28,20},{32... | collective-permute-start | bytes 1474568 | tf_op jit(solution)/shard_map/ppermute | solution.py:672
  83.6 10.0 %collective-permute-start.9 = (bf16[320,768]{1,0:T(8,128)(2,1)S(1)}, bf16[320,768]{1,0:T(8,128)(2,1)S(1)}, u32[]{:S(2)}, u32[]{:S(2)}) collective-permute-start(bf16[320,768]{1,0:T(8,128)(2,1)S(1)} %get-tuple-element.86.refs_8_), channel_id=1, source_target_pairs={{0,32},{4,12},{8,40},{12,20},{16,48},{20,28},{24,56},{28,4},{32,64... | collective-permute-start | bytes 1474568 | tf_op jit(solution)/shard_map/ppermute | solution.py:672
  93.6 4.3 %copy-start.1 = (bf16[2560,256]{1,0:T(8,128)(2,1)S(1)}, bf16[2560,256]{1,0:T(8,128)(2,1)}, u32[]{:S(2)}) copy-start(bf16[2560,256]{1,0:T(8,128)(2,1)} %w_bc.3) | copy-start | bytes 3932164
  93.9 15.4 %collective-permute-start.11 = (bf16[640,768]{1,0:T(8,128)(2,1)S(1)}, bf16[640,768]{1,0:T(8,128)(2,1)S(1)}, u32[]{:S(2)}, u32[]{:S(2)}) collective-permute-start(bf16[640,768]{1,0:T(8,128)(2,1)S(1)} %get-tuple-element.94.tie), channel_id=1, source_target_pairs={{0,32},{4,12},{8,40},{12,20},{16,48},{20,28},{24,56},{28,4},{32,64... | collective-permute-start | bytes 2949128 | tf_op jit(solution)/shard_map/ppermute | solution.py:672
  93.9 15.3 %collective-permute-start.12 = (bf16[640,768]{1,0:T(8,128)(2,1)S(1)}, bf16[640,768]{1,0:T(8,128)(2,1)S(1)}, u32[]{:S(2)}, u32[]{:S(2)}) collective-permute-start(bf16[640,768]{1,0:T(8,128)(2,1)S(1)} %get-tuple-element.95), channel_id=1, source_target_pairs={{0,96},{4,28},{8,104},{12,4},{16,112},{20,12},{24,120},{28,20},{32... | collective-permute-start | bytes 2949128 | tf_op jit(solution)/shard_map/ppermute | solution.py:672
  104.2 8.6 %collective-permute-start.17 = (bf16[320,256]{1,0:T(8,128)(2,1)S(1)}, bf16[320,256]{1,0:T(8,128)(2,1)S(1)}, u32[]{:S(2)}, u32[]{:S(2)}) collective-permute-start(bf16[320,256]{1,0:T(8,128)(2,1)S(1)} %get-tuple-element.108), channel_id=1, source_target_pairs={{0,1},{1,2},{2,3},{3,0},{4,5},{5,6},{6,7},{7,4},{8,9},{9,10},{10,1... | collective-permute-start | bytes 491528 | tf_op jit(solution)/shard_map/ppermute | solution.py:676
  105.3 7.6 %collective-permute-start.18 = (bf16[320,256]{1,0:T(8,128)(2,1)S(1)}, bf16[320,256]{1,0:T(8,128)(2,1)S(1)}, u32[]{:S(2)}, u32[]{:S(2)}) collective-permute-start(bf16[320,256]{1,0:T(8,128)(2,1)S(1)} %get-tuple-element.111), channel_id=1, source_target_pairs={{0,3},{1,0},{2,1},{3,2},{4,7},{5,4},{6,5},{7,6},{8,11},{9,8},{10,9... | collective-permute-start | bytes 491528 | tf_op jit(solution)/shard_map/ppermute | solution.py:676
  109.5 10.1 %copy-start.6 = (bf16[1280,256]{1,0:T(8,128)(2,1)S(1)}, bf16[1280,256]{1,0:T(8,128)(2,1)}, u32[]{:S(2)}) copy-start(bf16[1280,256]{1,0:T(8,128)(2,1)} %get-tuple-element.68.dyt) | copy-start | bytes 1966084
  109.5 10.1 %copy-start.8 = (f32[1280,128]{1,0:T(8,128)S(1)}, f32[1280,128]{1,0:T(8,128)}, u32[]{:S(2)}) copy-start(f32[1280,128]{1,0:T(8,128)} %copy-done.7) | copy-start | bytes 1966084
  109.5 10.1 %copy-start.10 = (f32[1280,128]{1,0:T(8,128)S(1)}, f32[1280,128]{1,0:T(8,128)}, u32[]{:S(2)}) copy-start(f32[1280,128]{1,0:T(8,128)} %copy-done.9) | copy-start | bytes 1966084
  109.5 10.1 %copy-start.19 = (f32[20,256]{1,0:T(8,128)S(1)}, f32[20,256]{1,0:T(8,128)}, u32[]{:S(2)}) copy-start(f32[20,256]{1,0:T(8,128)} %get-tuple-element.66.cum) | copy-start | bytes 61444
  109.6 10.1 %copy-start.20 = (f32[20,256]{1,0:T(8,128)S(1)}, f32[20,256]{1,0:T(8,128)}, u32[]{:S(2)}) copy-start(f32[20,256]{1,0:T(8,128)} %get-tuple-element.67.logd) | copy-start | bytes 61444
  109.6 10.1 %copy-start.21 = (f32[20,256]{1,0:T(8,128)S(1)}, f32[20,256]{1,0:T(8,128)}, u32[]{:S(2)}) copy-start(f32[20,256]{1,0:T(8,128)} %get-tuple-element.118.halves) | copy-start | bytes 61444
  109.6 10.1 %copy-start.22 = (f32[20,256]{1,0:T(8,128)S(1)}, f32[20,256]{1,0:T(8,128)}, u32[]{:S(2)}) copy-start(f32[20,256]{1,0:T(8,128)} %get-tuple-element.119.cross) | copy-start | bytes 61444
  109.6 6.7 %collective-permute-start.13 = (bf16[80,768]{1,0:T(8,128)(2,1)S(1)}, bf16[80,768]{1,0:T(8,128)(2,1)S(1)}, u32[]{:S(2)}, u32[]{:S(2)}) collective-permute-start(bf16[80,768]{1,0:T(8,128)(2,1)S(1)} %get-tuple-element.99), channel_id=1, source_target_pairs={{0,8},{4,36},{8,16},{12,44},{16,24},{20,52},{24,0},{28,60},{32,40}... | collective-permute-start | bytes 368648 | tf_op jit(solution)/shard_map/ppermute | solution.py:672
  109.9 6.4 %collective-permute-start.14 = (bf16[80,768]{1,0:T(8,128)(2,1)S(1)}, bf16[80,768]{1,0:T(8,128)(2,1)S(1)}, u32[]{:S(2)}, u32[]{:S(2)}) collective-permute-start(bf16[80,768]{1,0:T(8,128)(2,1)S(1)} %get-tuple-element.102), channel_id=1, source_target_pairs={{0,24},{4,100},{8,0},{12,108},{16,8},{20,116},{24,16},{28,124},{32... | collective-permute-start | bytes 368648 | tf_op jit(solution)/shard_map/ppermute | solution.py:672
  113.0 10.3 %collective-permute-start.19 = (bf16[640,256]{1,0:T(8,128)(2,1)S(1)}, bf16[640,256]{1,0:T(8,128)(2,1)S(1)}, u32[]{:S(2)}, u32[]{:S(2)}) collective-permute-start(bf16[640,256]{1,0:T(8,128)(2,1)S(1)} %get-tuple-element.113), channel_id=1, source_target_pairs={{0,1},{1,2},{2,3},{3,0},{4,5},{5,6},{6,7},{7,4},{8,9},{9,10},{10,1... | collective-permute-start | bytes 983048 | tf_op jit(solution)/shard_map/ppermute | solution.py:676
  114.1 9.2 %collective-permute-start.20 = (bf16[640,256]{1,0:T(8,128)(2,1)S(1)}, bf16[640,256]{1,0:T(8,128)(2,1)S(1)}, u32[]{:S(2)}, u32[]{:S(2)}) collective-permute-start(bf16[640,256]{1,0:T(8,128)(2,1)S(1)} %get-tuple-element.114), channel_id=1, source_target_pairs={{0,3},{1,0},{2,1},{3,2},{4,7},{5,4},{6,5},{7,6},{8,11},{9,8},{10,9... | collective-permute-start | bytes 983048 | tf_op jit(solution)/shard_map/ppermute | solution.py:676
  116.4 7.5 %collective-permute-start.15 = (bf16[160,768]{1,0:T(8,128)(2,1)S(1)}, bf16[160,768]{1,0:T(8,128)(2,1)S(1)}, u32[]{:S(2)}, u32[]{:S(2)}) collective-permute-start(bf16[160,768]{1,0:T(8,128)(2,1)S(1)} %get-tuple-element.104), channel_id=1, source_target_pairs={{0,8},{4,36},{8,16},{12,44},{16,24},{20,52},{24,0},{28,60},{32,40}... | collective-permute-start | bytes 737288 | tf_op jit(solution)/shard_map/ppermute | solution.py:672
  116.4 7.4 %collective-permute-start.16 = (bf16[160,768]{1,0:T(8,128)(2,1)S(1)}, bf16[160,768]{1,0:T(8,128)(2,1)S(1)}, u32[]{:S(2)}, u32[]{:S(2)}) collective-permute-start(bf16[160,768]{1,0:T(8,128)(2,1)S(1)} %get-tuple-element.105), channel_id=1, source_target_pairs={{0,24},{4,100},{8,0},{12,108},{16,8},{20,116},{24,16},{28,124},{32... | collective-permute-start | bytes 737288 | tf_op jit(solution)/shard_map/ppermute | solution.py:672

commit v5 on v4

--- a/solution.py
+++ b/solution.py
@@ -151,8 +151,10 @@
 def early_kernel(
     code, before, normed, w_bc, step, grad_y, conv_w, w_x, *refs
 ):
-    bmat, cmat, cum, logd, dyt, dywt, xgt, xlt, slope, xwt, msg = refs[:11]
-    pulled, turn, ext, pre, own, held, sems = refs[11:]
+    bmat, cmat, cum, logd, dyt_out, dywt_out, xgt_out, xlt_out, slope_out, xwt_out, msg = refs[:11]
+    pulled, turn, ext, pre, own, held, sems = refs[11:18]
+    dyt, dywt, xgt, xlt, slope, xwt, front_sems, out_sems = refs[18:]
+    leaving = []
     copies = [
         pltpu.make_async_copy(w_x.at[:, pl.ds(BLK * i, BLK)], held.at[i], sems.at[i])
         for i in range(NBLK)
@@ -164,6 +166,9 @@
     through = front_part(
         normed, w_bc, code, step, grad_y, bmat, cmat, cum, logd, dyt, dywt, pulled, turn
     )
+    for at, (source, goal) in enumerate(((dyt, dyt_out), (dywt, dywt_out))):
+        leaving.append(pltpu.make_async_copy(source, goal, front_sems.at[at]))
+        leaving[-1].start()
     b_high, b_low = split(bmat[...])
     for i in range(NBLK + 1):
         if i < NBLK:
@@ -193,16 +198,29 @@
         high, low = split(jnp.concatenate(parts, axis=0))
         xwt[cols, :] = high
         own[cols, :] = nn(high, b_high) + (nn(low, b_high) + nn(high, b_low))
+        piece = pl.ds(BLK * block, BLK)
+        pairs = [
+            (one.at[piece, :], goal.at[piece, :])
+            for one, goal in ((xgt, xgt_out), (xlt, xlt_out), (xwt, xwt_out))
+        ]
+        pairs.append((slope.at[:, piece], slope_out.at[:, piece]))
+        for at, (source, goal) in enumerate(pairs):
+            leaving.append(pltpu.make_async_copy(source, goal, out_sems.at[block, at]))
+            leaving[-1].start()
     for k in range(SEQ):
         rows = slice(SLICE * k, SLICE * (k + 1))
         msg[k] = jnp.concatenate([pulled[rows, :], own[rows, :], through], axis=0).astype(BF16)
+    for one in leaving:
+        one.wait()
 
 
 def early(code, before, normed, w_bc, step, grad_y, conv_w, w_x):
     vm = pl.BlockSpec(memory_space=pltpu.VMEM)
+    away = pl.BlockSpec(memory_space=pl.ANY)
     return pl.pallas_call(
         early_kernel,
-        in_specs=[vm] * 7 + [pl.BlockSpec(memory_space=pl.ANY)],
+        in_specs=[vm] * 7 + [away],
+        out_specs=(vm,) * 4 + (away,) * 6 + (vm,),
         out_shape=(
             jax.ShapeDtypeStruct((T, STATE), F32),
             jax.ShapeDtypeStruct((T, STATE), F32),
@@ -224,6 +242,14 @@
             pltpu.VMEM((CH, STATE), F32),
             pltpu.VMEM((NBLK, D, BLK), BF16),
             pltpu.SemaphoreType.DMA((NBLK,)),
+            pltpu.VMEM((CH, T), BF16),
+            pltpu.VMEM((CH, T), BF16),
+            pltpu.VMEM((CH, T), BF16),
+            pltpu.VMEM((CH, T), BF16),
+            pltpu.VMEM((T, CH), F32),
+            pltpu.VMEM((CH, T), BF16),
+            pltpu.SemaphoreType.DMA((2,)),
+            pltpu.SemaphoreType.DMA((NBLK, 4)),
         ],
         compiler_params=params(56),
         cost_estimate=cost(2 * T * D * (CH + 256), 16 * 2**20, T * CH),
@@ -306,13 +332,15 @@
     )(grad_y, dyt, xgt, cum, bmat, cmat, tie)
 
 
-def shared_kernel(back, xwt, dywt, dbc, ds, st, shared):
+def shared_kernel(back, xwt, dywt, dbc, ds, st, shared, ds_wide, st_wide):
     for k in range(SEQ):
         rows = slice(SLICE * k, SLICE * (k + 1))
         both = back[k].astype(F32)
-        ds[rows, :] = both[:SLICE]
-        st[rows, :] = both[SLICE:]
-    for at, (state, tokens) in enumerate(((ds, xwt), (st, dywt))):
+        ds_wide[rows, :] = both[:SLICE]
+        st_wide[rows, :] = both[SLICE:]
+    ds[...] = ds_wide[...].astype(BF16)
+    st[...] = st_wide[...].astype(BF16)
+    for at, (state, tokens) in enumerate(((ds_wide, xwt), (st_wide, dywt))):
         turned = state[...].T.astype(BF16)
         part = nn(turned, tokens[...]) + dbc[STATE * at : STATE * (at + 1), :]
         shared[:, STATE * at : STATE * (at + 1)] = part.T.astype(BF16)
@@ -322,10 +350,11 @@
     return pl.pallas_call(
         shared_kernel,
         out_shape=(
-            jax.ShapeDtypeStruct((CH, STATE), F32),
-            jax.ShapeDtypeStruct((CH, STATE), F32),
+            jax.ShapeDtypeStruct((CH, STATE), BF16),
+            jax.ShapeDtypeStruct((CH, STATE), BF16),
             jax.ShapeDtypeStruct((T, 2 * STATE), BF16),
         ),
+        scratch_shapes=[pltpu.VMEM((CH, STATE), F32), pltpu.VMEM((CH, STATE), F32)],
         compiler_params=params(),
         cost_estimate=cost(4 * CH * T * 128, 4 * 2**20),
     )(back, xwt, dywt, dbc)
@@ -353,8 +382,7 @@
         for one in copies[i]:
             one.wait()
         back_i, dxg_i, dyt_i, xgt_i, xlt_i, slope_i = [buffer.at[i] for buffer in held]
-        d_high, d_low = split(back_i[...])
-        later = nt(d_high, b_high) + (nt(d_low, b_high) + nt(d_high, b_low))
+        later = nt(back_i[...], b_high) + nt(back_i[...], b_low)
         parts = []
         for q in range(BLK // HEAD_DIM):
             index = i * (BLK // HEAD_DIM) + q
@@ -399,7 +427,7 @@
         scratch_shapes=[
             pltpu.VMEM((2, T + 16, BLK), F32),
             pltpu.SemaphoreType.DMA((NBLK, 6)),
-            pltpu.VMEM((NBLK, BLK, STATE), F32),
+            pltpu.VMEM((NBLK, BLK, STATE), BF16),
             pltpu.VMEM((NBLK, BLK, T), F32),
             pltpu.VMEM((NBLK, BLK, T), BF16),
             pltpu.VMEM((NBLK, BLK, T), BF16),
@@ -413,14 +441,16 @@
 
 def step_kernel(fore, back, cmat, dyt, cum, logd, rc, halves, cross, tie, gls):
     del tie
-    before = wide(nt, fore[...], cmat[...])
+    c_high, c_low = split(cmat[...])
+    before = nt(fore[...], c_high) + nt(fore[...], c_low)
     cums = cum[...]
     inner = []
     through = []
     for h in range(HEADS):
         rows = slice(64 * h, 64 * h + 64)
         inner.append(jnp.sum(dyt[rows, :].astype(F32) * before[rows], axis=0, keepdims=True))
-        both = jnp.sum(fore[rows, :] * back[rows, :], axis=0, keepdims=True)
+        both = fore[rows, :].astype(F32) * back[rows, :].astype(F32)
+        both = jnp.sum(both, axis=0, keepdims=True)
         through.append(jnp.sum(both, axis=1, keepdims=True))
     arriving = rc[...] + jnp.exp(cums) * SCALE * jnp.concatenate(inner, axis=0)
     later = jnp.dot(arriving, triangle(False), precision=HIGH, preferred_element_type=F32)
@@ -541,6 +571,22 @@
     )(*[one for triple in triples for one in triple])
 
 
+def pass_kernel(near_up, up, near_down, down, out_up, out_down):
+    size = near_up.shape[0]
+    out_up[...] = (near_up[...] + up[:size, :].astype(F32)).astype(BF16)
+    out_down[...] = (near_down[...] + down[:size, :].astype(F32)).astype(BF16)
+
+
+def pass_on(near_up, up, near_down, down):
+    one = jax.ShapeDtypeStruct(near_up.shape, BF16)
+    return pl.pallas_call(
+        pass_kernel,
+        out_shape=(one, one),
+        compiler_params=params(),
+        cost_estimate=cost(10**6, 2 * 2**20),
+    )(near_up, up, near_down, down)
+
+
 def turn_kernel(here_a, here_b, up, down, far_up, far_down, near_up, near_down, dir_up, dir_down, a, b):
     size = 4 * ROWS
 
@@ -575,7 +621,9 @@
     )(here_a, here_b, up, down)
 
 
-def last_kernel(a, b, up, down, here_u, up_u, down_u, grad_wx, grad_wbc, grad_u):
+def last_kernel(
+    a, b, up, down, here_u, up_u, down_u, near_up, near_down, grad_wx, grad_wbc, grad_u
+):
     norm = (T * SEQ) ** (-0.5)
     first = a[...] + (up[:ROWS, :].astype(F32) + down[ROWS:, :].astype(F32))
     second = b[...] + (down[:ROWS, :].astype(F32) + up[ROWS:, :].astype(F32))
@@ -584,8 +632,8 @@
     grad_wbc[:, :STATE] = first[:, WIDE:] * norm
     grad_wbc[:, STATE:] = second[:, WIDE:] * norm
     size = here_u.shape[0] // 2
-    low = here_u[:size, :] + (up_u[:size, :].astype(F32) + down_u[size:, :].astype(F32))
-    high = here_u[size:, :] + (down_u[:size, :].astype(F32) + up_u[size:, :].astype(F32))
+    low = here_u[:size, :] + (near_up[...].astype(F32) + down_u[size:, :].astype(F32))
+    high = here_u[size:, :] + (near_down[...].astype(F32) + up_u[size:, :].astype(F32))
     grad_u[:size, :] = low.astype(BF16)
     grad_u[size:, :] = high.astype(BF16)
 
@@ -605,7 +653,7 @@
 
 def input_kernel(order, w_x, w_bc, grad, halo, shared, tie, *refs):
     del tie
-    far_up, far_down, near_up, near_down, dir_up, dir_down, here, held, small, sems = refs
+    far_up, far_down, near_up, near_down, here, held, small, sems = refs
     size = D // ZS
     half = size // 2
     copies = []
@@ -620,25 +668,29 @@
     edge = jnp.concatenate([jnp.zeros((8, CH), F32), halo[...]], axis=0)
     last = (grad[T - 16 :, :].astype(F32) + edge).astype(BF16)
     right = jnp.concatenate([grad[: T - 16, :], last], axis=0)
-    outs = ((far_up, far_down), (near_up, dir_up), (dir_down, near_down))
     for at, r in enumerate(turn):
         copies[at].wait()
         part = nt(held[at], right)
-        if r == 0:
+        if r == 2:
+            far_up[:half, :] = part[:half].astype(BF16)
+            far_down[:half, :] = part[half:].astype(BF16)
+        elif r == 0:
             last_copy.wait()
             here[...] = part + nt(small[...], shared[...])
+        elif r == 1:
+            near_up[...] = part[:half]
+            far_up[half:, :] = part[half:].astype(BF16)
         else:
-            low, high = outs[at]
-            low[...] = part[:half].astype(low.dtype)
-            high[...] = part[half:].astype(high.dtype)
+            far_down[half:, :] = part[:half].astype(BF16)
+            near_down[...] = part[half:]
 
 
 def input_part(order, w_x, w_bc, grad, halo, shared, tie):
     rows = D // ZS
     vm = pl.BlockSpec(memory_space=pltpu.VMEM)
     away = pl.BlockSpec(memory_space=pl.ANY)
-    sizes = (rows // 2,) * 6 + (rows,)
-    types = (BF16, BF16, F32, F32, BF16, BF16, F32)
+    sizes = (rows, rows, rows // 2, rows // 2, rows)
+    types = (BF16, BF16, F32, F32, F32)
     return pl.pallas_call(
         input_kernel,
         in_specs=[pl.BlockSpec(memory_space=pltpu.SMEM), away, away, vm, vm, vm, away],
@@ -740,7 +792,7 @@
     )
     up, down = join((near_up, ru, dir_up), (near_down, rd, dir_down))
     ru, rd = move[1](up), move[-1](down)
-    z_far_up, z_far_down, z_up, z_down, z_dir_up, z_dir_down, z_here = input_part(
+    z_far_up, z_far_down, z_up, z_down, z_here = input_part(
         order_z, w_x, w_bc, dpre, halo_mine, shared, up
     )
     gls = step_part(st, ds, cmat, dyt, cum, logd, rc, halves, cross, z_here)
@@ -749,11 +801,13 @@
     )
     ru, rd = turn[1](far_up), turn[-1](far_down)
     zu, zd = head[1](z_far_up), head[-1](z_far_down)
-    z_up, z_down = join((z_up, zu, z_dir_up), (z_down, zd, z_dir_down))
-    zu, zd = head[1](z_up), head[-1](z_down)
+    z_up, z_down = pass_on(z_up, zu, z_down, zd)
+    z_near_up, z_near_down = head[1](z_up), head[-1](z_down)
     up, down = join((near_up, ru, dir_up), (near_down, rd, dir_down))
     ru, rd = turn[1](up), turn[-1](down)
-    grad_wx, grad_wbc, grad_u = last_part(here_a, here_b, ru, rd, z_here, zu, zd)
+    grad_wx, grad_wbc, grad_u = last_part(
+        here_a, here_b, ru, rd, z_here, zu, zd, z_near_up, z_near_down
+    )
     return (grad_u, grad_wx, grad_wbc, gls)
 
 

time: 126 us -> 128 us (1.016)
  waiting for transfers between devices: 17.3 us -> 18.6 us
    ppermute x8, waiting for transfers between devices: 9.78 us -> 12.1 us  [along(): return lambda value: lax.ppermute(value, 'seq', ring(first, by))]
    unnamed x52 -> x56, local copies, waits for them, and re-layouts: 9.22 us -> 9.9 us
    pallas_call x1 -> x2, Pallas kernels: 10.4 us -> 10.6 us  [the longest x1 10.5 us: early(): pl.pallas_call(early_kernel, in_specs=[vm] * 7 + [away], out_specs=(vm,)...]
  transfers between devices with their start and end apart: 22 -> 22, of which waited for: 8 -> 8; matrix products, arithmetic and copies ran while one was open for 1% -> 1% of each run, Pallas kernels for 17% -> 16%
where the time goes in v5:
time: 128 us; the launch traced here: 127 us
  starting transfers between devices  42.8 us (33%)
  Pallas kernels  34.8 us (27%)
  waiting for transfers between devices  18.6 us (15%)
  blocking collectives  17.9 us (14%)
  local copies, waits for them, and re-layouts  12.2 us (10%)
    all_to_all x1, blocking collectives, body(): back = lax.all_to_all(chain(table, recv, rc), 'seq', 0, 0)  17.9 us
    ppermute x8, starting transfers between devices, along(): return lambda value: lax.ppermute(value, 'seq', ring(first, by))  13.4 us
    ppermute x7, starting transfers between devices, along_head(): lax.ppermute(value, 'head', [(i, (i + by) % ZS) for i in range(ZS)])  13.1 us
    ppermute x8, waiting for transfers between devices, along(): return lambda value: lax.ppermute(value, 'seq', ring(first, by))  12.1 us
    all_to_all x1, starting transfers between devices, body(): recv = lax.all_to_all(msg, 'seq', 0, 0)  11.1 us
    pallas_call x1, Pallas kernels, early(): pl.pallas_call(early_kernel, in_specs=[vm] * 7 + [away], out_specs=(vm,)...  10.5 us
    unnamed x56, local copies, waits for them, and re-layouts  9.9 us
    pallas_call x1, Pallas kernels, input_part(): pl.pallas_call(input_kernel, in_specs=[pl.BlockSpec(memory_space=pltpu.SM...  6.31 us
  transfers between devices with their start and end apart: 22, of which 8 were waited for; matrix products, arithmetic and copies ran while one was open for 1% of the time, Pallas kernels for 16%

profile of v5, /device:TPU:0, one launch (start us, length us, event | category | flops | bytes accessed | tf_op | source)
XLA Modules:
  0.0 127.4 jit_solution(5382868696146168426)
XLA Ops:
  0.6 0.9 slice.9
  1.5 1.3 %collective-permute-start = (bf16[16,2560]{1,0:T(8,128)(2,1)S(1)}, bf16[16,2560]{1,0:T(8,128)(2,1)S(1)}, u32[]{:S(2)}, u32[]{:S(2)}) collective-permute-start(bf16[16,2560]{1,0:T(8,128)(2,1)S(1)} %slice.9), channel_id=1, source_target_pairs={{0,4},{4,8},{8,12},{12,16},{16,20},{20,24},{24,28},{28,32},{32,36}... | collective-permute-start | bytes 245768 | tf_op jit(solution)/shard_map/ppermute | solution.py:758
  2.8 0.9 collective-permute-done.before
  4.4 10.5 %shard_map.120 = (f32[256,128]{1,0:T(8,128)}, f32[256,128]{1,0:T(8,128)}, f32[20,256]{1,0:T(8,128)}, f32[20,256]{1,0:T(8,128)}, bf16[1280,256]{1,0:T(8,128)(2,1)...) custom-call(s32[1,20]{1,0:T(1,128)} %bitcast.5, ...), custom_call_target="tpu_custom_call" | custom-call | flops 2013265920 | bytes 16777216 | tf_op jit(solution)/shard_map/pallas_call | solution.py:220
  14.9 11.1 %all-to-all-start = ((bf16[32,96,128]{2,1,0:T(8,128)(2,1)}), bf16[32,96,128]{2,1,0:T(8,128)(2,1)S(1)}, u32[]{:S(2)}, u32[]{:S(2)}) async-start(bf16[32,96,128]{2,1,0:T(8,128)(2,1)} %get-tuple-element.60.tie), calls=%async_computation | async-start | bytes 1572864 | tf_op jit(solution)/shard_map/all_to_all | solution.py:763
  26.0 0.7 fusion.order.table
  26.7 1.1 copy-done.2
  27.9 1.0 shard_map.121
  28.9 0.9 copy-done.25
  29.8 1.1 copy-done.17
  30.9 0.9 copy-done.19
  31.8 0.7 copy-done.20
  32.5 3.5 %shard_map.122 = (f32[1280,256]{1,0:T(8,128)S(1)}, f32[20,256]{1,0:T(8,128)S(1)}, f32[256,256]{1,0:T(8,128)S(1)}) custom-call(bf16[256,1280]{1,0:T(8,128)(2,1)S(1)} %copy-done.17, bf16[1280,256]{1,0:T(8,128)(2,1)S(1)} %copy-done.5, bf16[1280,256]{1,0:T(8,128)(2,1)S(1)} %copy-done.12, f32[20,256]{1,0:T(8,128)S(1)} %copy-done.20, f32[256,128]{1,0:T(8,128)S(1)} %copy-done.19, ...), custom_call_target="tpu_custom_call" | custom-call | flops 1342177280 | bytes 4194304 | tf_op jit(solution)/shard_map/pallas_call | solution.py:311
  36.1 1.1 copy-done.11
  37.2 0.8 copy-done.13
  38.0 1.8 %all-to-all-done.recv = bf16[32,96,128]{2,1,0:T(8,128)(2,1)S(1)} async-done(((bf16[32,96,128]{2,1,0:T(8,128)(2,1)}), bf16[32,96,128]{2,1,0:T(8,128)(2,1)S(1)}, u32[]{:S(2)}, u32[]{:S(2)}) %all-to-all-start) | async-done | bytes 786464 | tf_op jit(solution)/shard_map/all_to_all | solution.py:763
  39.9 1.0 shard_map.123
  40.9 17.9 %all_to_all.10.back = bf16[32,80,128]{2,1,0:T(8,128)(2,1)S(1)} all-to-all(bf16[32,80,128]{2,1,0:T(8,128)(2,1)S(1)} %shard_map.123), channel_id=1, replica_groups=mesh['seq'=32,'head'=4] {'seq'}, dimensions={0} | all-to-all | bytes 1310720 | tf_op jit(solution)/shard_map/all_to_all | solution.py:767
  59.3 0.7 copy-done.7
  60.0 0.7 copy-done.9
  60.7 1.9 %collective-permute-start.5 = (bf16[256,256]{1,0:T(8,128)(2,1)S(1)}, bf16[256,256]{1,0:T(8,128)(2,1)S(1)}, u32[]{:S(2)}, u32[]{:S(2)}) collective-permute-start(bf16[256,256]{1,0:T(8,128)(2,1)S(1)} %get-tuple-element.80), channel_id=1, source_target_pairs={{0,1},{1,2},{2,3},{3,0},{4,5},{5,6},{6,7},{7,4},{8,9},{9,10},{10,1... | collective-permute-start | bytes 393224 | tf_op jit(solution)/shard_map/ppermute | solution.py:728
  62.6 3.6 %collective-permute-start.6 = (bf16[256,256]{1,0:T(8,128)(2,1)S(1)}, bf16[256,256]{1,0:T(8,128)(2,1)S(1)}, u32[]{:S(2)}, u32[]{:S(2)}) collective-permute-start(bf16[256,256]{1,0:T(8,128)(2,1)S(1)} %get-tuple-element.80), channel_id=1, source_target_pairs={{0,2},{1,3},{2,0},{3,1},{4,6},{5,7},{6,4},{7,5},{8,10},{9,11},{10,... | collective-permute-start | bytes 393224 | tf_op jit(solution)/shard_map/ppermute | solution.py:728
  66.2 1.0 collective-permute-start.7
  67.2 5.5 %shard_map.125 = (bf16[256,1280]{1,0:T(8,128)(2,1)}, f32[8,1280]{1,0:T(8,128)}, f32[20,256]{1,0:T(8,128)}, f32[20,256]{1,0:T(8,128)}) custom-call(f32[20]{0:T(128)} %skip.1, f32[256,128]{1,0:T(8,128)} %get-tuple-element.63.bmat, f32[4,1280]{1,0:T(4,128)} %taps.1, f32[20,256]{1,0:T(8,128)} %get-tuple-element.64.cum, f32[20,256]{1,0:T(8,128)} %get-tuple-element.65.logd, ...), custom_call_target="tpu_custom_call" | custom-call | flops 167772160 | bytes 6291456 | tf_op jit(solution)/shard_map/pallas_call | solution.py:418
  72.8 1.3 %collective-permute-start.4 = (f32[8,1280]{1,0:T(8,128)}, f32[8,1280]{1,0:T(8,128)S(1)}, u32[]{:S(2)}, u32[]{:S(2)}) collective-permute-start(f32[8,1280]{1,0:T(8,128)} %get-tuple-element.79), channel_id=1, source_target_pairs={{8,0},{16,8},{24,16},{32,24},{40,32},{48,40},{56,48},{64,56},{72,6... | collective-permute-start | bytes 122888 | tf_op jit(solution)/shard_map/ppermute | solution.py:776
  74.1 1.3 %collective-permute-start.3 = (f32[8,1280]{1,0:T(8,128)}, f32[8,1280]{1,0:T(8,128)S(1)}, u32[]{:S(2)}, u32[]{:S(2)}) collective-permute-start(f32[8,1280]{1,0:T(8,128)} %get-tuple-element.79), channel_id=1, source_target_pairs={{4,0},{8,4},{12,8},{16,12},{20,16},{24,20},{28,24},{32,28},{36,32}... | collective-permute-start | bytes 122888 | tf_op jit(solution)/shard_map/ppermute | solution.py:775
  75.4 1.2 collective-permute-start.2
  76.8 2.1 %collective-permute-done.4 = f32[8,1280]{1,0:T(8,128)S(1)} collective-permute-done((f32[8,1280]{1,0:T(8,128)}, f32[8,1280]{1,0:T(8,128)S(1)}, u32[]{:S(2)}, u32[]{:S(2)}) %collective-permute-start.4) | collective-permute-done | bytes 40992 | tf_op jit(solution)/shard_map/ppermute | solution.py:776
  79.0 1.1 copy-done.3
  80.1 0.8 shard_map.126
  80.9 3.2 %collective-permute-start.10 = (bf16[320,768]{1,0:T(8,128)(2,1)S(1)}, bf16[320,768]{1,0:T(8,128)(2,1)S(1)}, u32[]{:S(2)}, u32[]{:S(2)}) collective-permute-start(bf16[320,768]{1,0:T(8,128)(2,1)S(1)} %get-tuple-element.90), channel_id=1, source_target_pairs={{0,96},{4,28},{8,104},{12,4},{16,112},{20,12},{24,120},{28,20},{32... | collective-permute-start | bytes 1474568 | tf_op jit(solution)/shard_map/ppermute | solution.py:724
  84.3 2.3 %shard_map.127 = (f32[320,768]{1,0:T(8,128)S(1)}, f32[320,768]{1,0:T(8,128)S(1)}, bf16[320,768]{1,0:T(8,128)(2,1)S(1)}, bf16[320,768]{1,0:T(8,128)(2,1)S(1)}, f3...) custom-call(bf16[1280,256]{1,0:T(8,128)(2,1)S(1)} %copy-done.14, bf16[1280,256]{1,0:T(8,128)(2,1)S(1)} %collective-permute-done.1.refs_1_, ...), custom_call_target="tpu_custom_call" | custom-call | flops 1509949440 | bytes 9437184 | tf_op jit(solution)/shard_map/pallas_call | solution.py:543
  86.6 4.5 %collective-permute-done.10.refs_4_ = bf16[320,768]{1,0:T(8,128)(2,1)S(1)} collective-permute-done((bf16[320,768]{1,0:T(8,128)(2,1)S(1)}, bf16[320,768]{1,0:T(8,128)(2,1)S(1)}, u32[]{:S(2)}, u32[]{:S(2)}) %collective-permute-start.10) | collective-permute-done | bytes 491552 | tf_op jit(solution)/shard_map/ppermute | solution.py:724
  91.0 3.1 %collective-permute-done.9.refs_1_ = bf16[320,768]{1,0:T(8,128)(2,1)S(1)} collective-permute-done((bf16[320,768]{1,0:T(8,128)(2,1)S(1)}, bf16[320,768]{1,0:T(8,128)(2,1)S(1)}, u32[]{:S(2)}, u32[]{:S(2)}) %collective-permute-start.9) | collective-permute-done | bytes 491552 | tf_op jit(solution)/shard_map/ppermute | solution.py:724
  94.5 3.2 %collective-permute-start.12 = (bf16[640,768]{1,0:T(8,128)(2,1)S(1)}, bf16[640,768]{1,0:T(8,128)(2,1)S(1)}, u32[]{:S(2)}, u32[]{:S(2)}) collective-permute-start(bf16[640,768]{1,0:T(8,128)(2,1)S(1)} %get-tuple-element.93), channel_id=1, source_target_pairs={{0,96},{4,28},{8,104},{12,4},{16,112},{20,12},{24,120},{28,20},{32... | collective-permute-start | bytes 2949128 | tf_op jit(solution)/shard_map/ppermute | solution.py:724
  97.7 0.7 constant_dynamic-slice_fusion
  98.4 6.3 %shard_map.131 = (bf16[640,256]{1,0:T(8,128)(2,1)S(1)}, bf16[640,256]{1,0:T(8,128)(2,1)S(1)}, f32[320,256]{1,0:T(8,128)S(1)}, f32[320,256]{1,0:T(8,128)S(1)}, f32[640,256]{1,0:T(8,128)S(1)}) custom-call(s32[4]{0:T(128)S(1)} %slice_bitcast_fusion.order, bf16[2560,1280]{1,0:T(8,128)(2,1)} %w_x.3, bf16[2560,256]{1,0:T(8,128)(2,1)S(1)} %copy-done.1, ...), custom_call_target="tpu_custom_call" | custom-call | flops 1761607680 | bytes 10485760 | tf_op jit(solution)/shard_map/pallas_call | solution.py:694
  104.8 1.1 collective-permute-start.17
  105.8 2.2 %collective-permute-start.18 = (bf16[640,256]{1,0:T(8,128)(2,1)S(1)}, bf16[640,256]{1,0:T(8,128)(2,1)S(1)}, u32[]{:S(2)}, u32[]{:S(2)}) collective-permute-start(bf16[640,256]{1,0:T(8,128)(2,1)S(1)} %get-tuple-element.106), channel_id=1, source_target_pairs={{0,3},{1,0},{2,1},{3,2},{4,7},{5,4},{6,5},{7,6},{8,11},{9,8},{10,9... | collective-permute-start | bytes 983048 | tf_op jit(solution)/shard_map/ppermute | solution.py:728
  108.1 1.7 %collective-permute-done.11.up = bf16[640,768]{1,0:T(8,128)(2,1)S(1)} collective-permute-done((bf16[640,768]{1,0:T(8,128)(2,1)S(1)}, bf16[640,768]{1,0:T(8,128)(2,1)S(1)}, u32[]{:S(2)}, u32[]{:S(2)}) %collective-permute-start.11) | collective-permute-done | bytes 983072 | tf_op jit(solution)/shard_map/ppermute | solution.py:724
  110.4 3.0 %collective-permute-start.14 = (bf16[80,768]{1,0:T(8,128)(2,1)S(1)}, bf16[80,768]{1,0:T(8,128)(2,1)S(1)}, u32[]{:S(2)}, u32[]{:S(2)}) collective-permute-start(bf16[80,768]{1,0:T(8,128)(2,1)S(1)} %get-tuple-element.100), channel_id=1, source_target_pairs={{0,24},{4,100},{8,0},{12,108},{16,8},{20,116},{24,16},{28,124},{32... | collective-permute-start | bytes 368648 | tf_op jit(solution)/shard_map/ppermute | solution.py:724
  113.4 2.9 %collective-permute-done.13.refs_1_ = bf16[80,768]{1,0:T(8,128)(2,1)S(1)} collective-permute-done((bf16[80,768]{1,0:T(8,128)(2,1)S(1)}, bf16[80,768]{1,0:T(8,128)(2,1)S(1)}, u32[]{:S(2)}, u32[]{:S(2)}) %collective-permute-start.13) | collective-permute-done | bytes 122912 | tf_op jit(solution)/shard_map/ppermute | solution.py:724
  116.4 3.3 %collective-permute-start.16 = (bf16[160,768]{1,0:T(8,128)(2,1)S(1)}, bf16[160,768]{1,0:T(8,128)(2,1)S(1)}, u32[]{:S(2)}, u32[]{:S(2)}) collective-permute-start(bf16[160,768]{1,0:T(8,128)(2,1)S(1)} %get-tuple-element.103), channel_id=1, source_target_pairs={{0,24},{4,100},{8,0},{12,108},{16,8},{20,116},{24,16},{28,124},{32... | collective-permute-start | bytes 737288 | tf_op jit(solution)/shard_map/ppermute | solution.py:724
  119.8 1.1 collective-permute-start.19
  120.9 2.2 %collective-permute-start.20 = (bf16[320,256]{1,0:T(8,128)(2,1)S(1)}, bf16[320,256]{1,0:T(8,128)(2,1)S(1)}, u32[]{:S(2)}, u32[]{:S(2)}) collective-permute-start(bf16[320,256]{1,0:T(8,128)(2,1)S(1)} %get-tuple-element.110), channel_id=1, source_target_pairs={{0,3},{1,0},{2,1},{3,2},{4,7},{5,4},{6,5},{7,6},{8,11},{9,8},{10,9... | collective-permute-start | bytes 491528 | tf_op jit(solution)/shard_map/ppermute | solution.py:728
  123.1 1.6 %shard_map.134 = f32[20,256]{1,0:T(8,128)} custom-call(bf16[1280,128]{1,0:T(8,128)(2,1)S(1)} %copy-done.10, bf16[1280,128]{1,0:T(8,128)(2,1)S(1)} %copy-done.8, f32[256,128]{1,0:T(8,128)S(1)} %copy-done.18, bf16[1280,256]{1,0:T(8,128)(2,1)S(1)} %copy-done.6, f32[20,256]{1,0:T(8,128)S(1)} %copy-done.21, f32[20,256]{1,0:T(8,128)S(1)} %copy-done.22, ...), custom_call_target="tpu_custom_call" | custom-call | flops 167772160 | bytes 4194304 | tf_op jit(solution)/shard_map/pallas_call | solution.py:467
  124.8 1.6 %collective-permute-done.19.near_up = bf16[320,256]{1,0:T(8,128)(2,1)S(1)} collective-permute-done((bf16[320,256]{1,0:T(8,128)(2,1)S(1)}, bf16[320,256]{1,0:T(8,128)(2,1)S(1)}, u32[]{:S(2)}, u32[]{:S(2)}) %collective-permute-start.19) | collective-permute-done | bytes 163872 | tf_op jit(solution)/shard_map/ppermute | solution.py:728
  126.4 1.0 shard_map.133
  (74 shorter events, 2.7 us)
Async XLA Ops:
  1.5 2.2 %collective-permute-start = (bf16[16,2560]{1,0:T(8,128)(2,1)S(1)}, bf16[16,2560]{1,0:T(8,128)(2,1)S(1)}, u32[]{:S(2)}, u32[]{:S(2)}) collective-permute-start(bf16[16,2560]{1,0:T(8,128)(2,1)S(1)} %slice.9), channel_id=1, source_target_pairs={{0,4},{4,8},{8,12},{12,16},{16,20},{20,24},{24,28},{28,32},{32,36}... | collective-permute-start | bytes 245768 | tf_op jit(solution)/shard_map/ppermute | solution.py:758
  14.9 11.8 %copy-start = (bf16[256,2560]{1,0:T(8,128)(2,1)S(1)}, bf16[256,2560]{1,0:T(8,128)(2,1)}, u32[]{:S(2)}) copy-start(bf16[256,2560]{1,0:T(8,128)(2,1)} %normed.3) | copy-start | bytes 3932164
  14.9 14.9 %copy-start.18 = (f32[256,128]{1,0:T(8,128)S(1)}, f32[256,128]{1,0:T(8,128)}, u32[]{:S(2)}) copy-start(f32[256,128]{1,0:T(8,128)} %get-tuple-element.68.cmat) | copy-start | bytes 393220
  14.9 25.0 %all-to-all-start = ((bf16[32,96,128]{2,1,0:T(8,128)(2,1)}), bf16[32,96,128]{2,1,0:T(8,128)(2,1)S(1)}, u32[]{:S(2)}, u32[]{:S(2)}) async-start(bf16[32,96,128]{2,1,0:T(8,128)(2,1)} %get-tuple-element.60.tie), calls=%async_computation | async-start | bytes 1572864 | tf_op jit(solution)/shard_map/all_to_all | solution.py:763
  26.7 1.1 copy-start.2
  27.8 1.9 %copy-start.5 = (bf16[1280,256]{1,0:T(8,128)(2,1)S(1)}, bf16[1280,256]{1,0:T(8,128)(2,1)}, u32[]{:S(2)}) copy-start(bf16[1280,256]{1,0:T(8,128)(2,1)} %get-tuple-element.66.dyt) | copy-start | bytes 1966084
  27.8 1.9 %copy-start.12 = (bf16[1280,256]{1,0:T(8,128)(2,1)S(1)}, bf16[1280,256]{1,0:T(8,128)(2,1)}, u32[]{:S(2)}) copy-start(bf16[1280,256]{1,0:T(8,128)(2,1)} %get-tuple-element.67.xgt) | copy-start | bytes 1966084
  28.9 0.9 copy-start.25
  29.8 1.1 copy-start.17
  30.9 0.9 copy-start.19
  31.8 0.7 copy-start.20
  36.1 1.1 copy-start.11
  37.2 0.8 copy-start.13
  39.9 18.9 %copy-start.15 = (bf16[1280,256]{1,0:T(8,128)(2,1)S(1)}, bf16[1280,256]{1,0:T(8,128)(2,1)}, u32[]{:S(2)}) copy-start(bf16[1280,256]{1,0:T(8,128)(2,1)} %get-tuple-element.71.dywt) | copy-start | bytes 1966084
  39.9 18.9 %copy-start.16 = (bf16[1280,256]{1,0:T(8,128)(2,1)S(1)}, bf16[1280,256]{1,0:T(8,128)(2,1)}, u32[]{:S(2)}) copy-start(bf16[1280,256]{1,0:T(8,128)(2,1)} %get-tuple-element.70.xwt) | copy-start | bytes 1966084
  58.8 8.5 %copy-start.26 = (bf16[1280,256]{1,0:T(8,128)(2,1)S(1)}, bf16[1280,256]{1,0:T(8,128)(2,1)}, u32[]{:S(2)}) copy-start(bf16[1280,256]{1,0:T(8,128)(2,1)} %copy-done.25) | copy-start | bytes 1966084
  59.3 0.7 copy-start.7
  60.7 13.4 %collective-permute-start.5 = (bf16[256,256]{1,0:T(8,128)(2,1)S(1)}, bf16[256,256]{1,0:T(8,128)(2,1)S(1)}, u32[]{:S(2)}, u32[]{:S(2)}) collective-permute-start(bf16[256,256]{1,0:T(8,128)(2,1)S(1)} %get-tuple-element.80), channel_id=1, source_target_pairs={{0,1},{1,2},{2,3},{3,0},{4,5},{5,6},{6,7},{7,4},{8,9},{9,10},{10,1... | collective-permute-start | bytes 393224 | tf_op jit(solution)/shard_map/ppermute | solution.py:728
  62.6 12.8 %collective-permute-start.6 = (bf16[256,256]{1,0:T(8,128)(2,1)S(1)}, bf16[256,256]{1,0:T(8,128)(2,1)S(1)}, u32[]{:S(2)}, u32[]{:S(2)}) collective-permute-start(bf16[256,256]{1,0:T(8,128)(2,1)S(1)} %get-tuple-element.80), channel_id=1, source_target_pairs={{0,2},{1,3},{2,0},{3,1},{4,6},{5,7},{6,4},{7,5},{8,10},{9,11},{10,... | collective-permute-start | bytes 393224 | tf_op jit(solution)/shard_map/ppermute | solution.py:728
  66.2 10.4 %collective-permute-start.7 = (bf16[256,256]{1,0:T(8,128)(2,1)S(1)}, bf16[256,256]{1,0:T(8,128)(2,1)S(1)}, u32[]{:S(2)}, u32[]{:S(2)}) collective-permute-start(bf16[256,256]{1,0:T(8,128)(2,1)S(1)} %get-tuple-element.80), channel_id=1, source_target_pairs={{0,3},{1,0},{2,1},{3,2},{4,7},{5,4},{6,5},{7,6},{8,11},{9,8},{10,9... | collective-permute-start | bytes 393224 | tf_op jit(solution)/shard_map/ppermute | solution.py:728
  67.2 11.7 %collective-permute-start.1 = (bf16[1280,256]{1,0:T(8,128)(2,1)S(1)}, bf16[1280,256]{1,0:T(8,128)(2,1)S(1)}, u32[]{:S(2)}, u32[]{:S(2)}) collective-permute-start(bf16[1280,256]{1,0:T(8,128)(2,1)S(1)} %copy-done.26), channel_id=1, source_target_pairs={{0,4},{4,0},{8,12},{12,8},{16,20},{20,16},{24,28},{28,24},{32,36},... | collective-permute-start | bytes 1966088 | tf_op jit(solution)/shard_map/ppermute | solution.py:765
  67.2 11.7 %copy-start.14 = (bf16[1280,256]{1,0:T(8,128)(2,1)S(1)}, bf16[1280,256]{1,0:T(8,128)(2,1)}, u32[]{:S(2)}) copy-start(bf16[1280,256]{1,0:T(8,128)(2,1)} %copy-done.13) | copy-start | bytes 1966084
  72.8 6.1 %collective-permute-start.4 = (f32[8,1280]{1,0:T(8,128)}, f32[8,1280]{1,0:T(8,128)S(1)}, u32[]{:S(2)}, u32[]{:S(2)}) collective-permute-start(f32[8,1280]{1,0:T(8,128)} %get-tuple-element.79), channel_id=1, source_target_pairs={{8,0},{16,8},{24,16},{32,24},{40,32},{48,40},{56,48},{64,56},{72,6... | collective-permute-start | bytes 122888 | tf_op jit(solution)/shard_map/ppermute | solution.py:776
  74.1 4.8 %collective-permute-start.3 = (f32[8,1280]{1,0:T(8,128)}, f32[8,1280]{1,0:T(8,128)S(1)}, u32[]{:S(2)}, u32[]{:S(2)}) collective-permute-start(f32[8,1280]{1,0:T(8,128)} %get-tuple-element.79), channel_id=1, source_target_pairs={{4,0},{8,4},{12,8},{16,12},{20,16},{24,20},{28,24},{32,28},{36,32}... | collective-permute-start | bytes 122888 | tf_op jit(solution)/shard_map/ppermute | solution.py:775
  75.4 3.5 %collective-permute-start.2 = (bf16[256,1280]{1,0:T(8,128)(2,1)}, bf16[256,1280]{1,0:T(8,128)(2,1)S(1)}, u32[]{:S(2)}, u32[]{:S(2)}) collective-permute-start(bf16[256,1280]{1,0:T(8,128)(2,1)} %get-tuple-element.78.refs_2_.grad), channel_id=1, source_target_pairs={{0,4},{4,0},{8,12},{12,8},{16,20},{20,16},{24,28},{28,24},{32,36},... | collective-permute-start | bytes 1966088 | tf_op jit(solution)/shard_map/ppermute | solution.py:774
  76.7 2.2 %collective-permute-start.8 = (bf16[256,256]{1,0:T(8,128)(2,1)S(1)}, bf16[256,256]{1,0:T(8,128)(2,1)S(1)}, u32[]{:S(2)}, u32[]{:S(2)}) collective-permute-start(bf16[256,256]{1,0:T(8,128)(2,1)S(1)} %add_convert_fusion.refs_6_.shared), channel_id=1, source_target_pairs={{0,4},{4,0},{8,12},{12,8},{16,20},{20,16},{24,28},{28,24},{32,36},... | collective-permute-start | bytes 393224 | tf_op jit(solution)/shard_map/ppermute | solution.py:782
  79.0 1.1 copy-start.3
  80.1 4.3 %copy-start.4 = (bf16[256,1280]{1,0:T(8,128)(2,1)S(1)}, bf16[256,1280]{1,0:T(8,128)(2,1)}, u32[]{:S(2)}) copy-start(bf16[256,1280]{1,0:T(8,128)(2,1)} %get-tuple-element.78.refs_2_.grad) | copy-start | bytes 1966084
  80.9 10.1 %collective-permute-start.10 = (bf16[320,768]{1,0:T(8,128)(2,1)S(1)}, bf16[320,768]{1,0:T(8,128)(2,1)S(1)}, u32[]{:S(2)}, u32[]{:S(2)}) collective-permute-start(bf16[320,768]{1,0:T(8,128)(2,1)S(1)} %get-tuple-element.90), channel_id=1, source_target_pairs={{0,96},{4,28},{8,104},{12,4},{16,112},{20,12},{24,120},{28,20},{32... | collective-permute-start | bytes 1474568 | tf_op jit(solution)/shard_map/ppermute | solution.py:724
  84.1 10.0 %collective-permute-start.9 = (bf16[320,768]{1,0:T(8,128)(2,1)S(1)}, bf16[320,768]{1,0:T(8,128)(2,1)S(1)}, u32[]{:S(2)}, u32[]{:S(2)}) collective-permute-start(bf16[320,768]{1,0:T(8,128)(2,1)S(1)} %get-tuple-element.84.refs_8_), channel_id=1, source_target_pairs={{0,32},{4,12},{8,40},{12,20},{16,48},{20,28},{24,56},{28,4},{32,64... | collective-permute-start | bytes 1474568 | tf_op jit(solution)/shard_map/ppermute | solution.py:724
  94.2 4.3 %copy-start.1 = (bf16[2560,256]{1,0:T(8,128)(2,1)S(1)}, bf16[2560,256]{1,0:T(8,128)(2,1)}, u32[]{:S(2)}) copy-start(bf16[2560,256]{1,0:T(8,128)(2,1)} %w_bc.3) | copy-start | bytes 3932164
  94.4 15.4 %collective-permute-start.11 = (bf16[640,768]{1,0:T(8,128)(2,1)S(1)}, bf16[640,768]{1,0:T(8,128)(2,1)S(1)}, u32[]{:S(2)}, u32[]{:S(2)}) collective-permute-start(bf16[640,768]{1,0:T(8,128)(2,1)S(1)} %get-tuple-element.92.tie), channel_id=1, source_target_pairs={{0,32},{4,12},{8,40},{12,20},{16,48},{20,28},{24,56},{28,4},{32,64... | collective-permute-start | bytes 2949128 | tf_op jit(solution)/shard_map/ppermute | solution.py:724
  94.5 15.3 %collective-permute-start.12 = (bf16[640,768]{1,0:T(8,128)(2,1)S(1)}, bf16[640,768]{1,0:T(8,128)(2,1)S(1)}, u32[]{:S(2)}, u32[]{:S(2)}) collective-permute-start(bf16[640,768]{1,0:T(8,128)(2,1)S(1)} %get-tuple-element.93), channel_id=1, source_target_pairs={{0,96},{4,28},{8,104},{12,4},{16,112},{20,12},{24,120},{28,20},{32... | collective-permute-start | bytes 2949128 | tf_op jit(solution)/shard_map/ppermute | solution.py:724
  104.8 15.0 %collective-permute-start.17 = (bf16[640,256]{1,0:T(8,128)(2,1)S(1)}, bf16[640,256]{1,0:T(8,128)(2,1)S(1)}, u32[]{:S(2)}, u32[]{:S(2)}) collective-permute-start(bf16[640,256]{1,0:T(8,128)(2,1)S(1)} %get-tuple-element.105), channel_id=1, source_target_pairs={{0,1},{1,2},{2,3},{3,0},{4,5},{5,6},{6,7},{7,4},{8,9},{9,10},{10,1... | collective-permute-start | bytes 983048 | tf_op jit(solution)/shard_map/ppermute | solution.py:728
  105.8 13.9 %collective-permute-start.18 = (bf16[640,256]{1,0:T(8,128)(2,1)S(1)}, bf16[640,256]{1,0:T(8,128)(2,1)S(1)}, u32[]{:S(2)}, u32[]{:S(2)}) collective-permute-start(bf16[640,256]{1,0:T(8,128)(2,1)S(1)} %get-tuple-element.106), channel_id=1, source_target_pairs={{0,3},{1,0},{2,1},{3,2},{4,7},{5,4},{6,5},{7,6},{8,11},{9,8},{10,9... | collective-permute-start | bytes 983048 | tf_op jit(solution)/shard_map/ppermute | solution.py:728
  110.0 13.1 %copy-start.6 = (bf16[1280,256]{1,0:T(8,128)(2,1)S(1)}, bf16[1280,256]{1,0:T(8,128)(2,1)}, u32[]{:S(2)}) copy-start(bf16[1280,256]{1,0:T(8,128)(2,1)} %get-tuple-element.66.dyt) | copy-start | bytes 1966084
  110.0 13.1 %copy-start.8 = (bf16[1280,128]{1,0:T(8,128)(2,1)S(1)}, bf16[1280,128]{1,0:T(8,128)(2,1)}, u32[]{:S(2)}) copy-start(bf16[1280,128]{1,0:T(8,128)(2,1)} %copy-done.7) | copy-start | bytes 983044
  110.1 13.0 %copy-start.10 = (bf16[1280,128]{1,0:T(8,128)(2,1)S(1)}, bf16[1280,128]{1,0:T(8,128)(2,1)}, u32[]{:S(2)}) copy-start(bf16[1280,128]{1,0:T(8,128)(2,1)} %copy-done.9) | copy-start | bytes 983044
  110.1 13.0 %copy-start.21 = (f32[20,256]{1,0:T(8,128)S(1)}, f32[20,256]{1,0:T(8,128)}, u32[]{:S(2)}) copy-start(f32[20,256]{1,0:T(8,128)} %get-tuple-element.64.cum) | copy-start | bytes 61444
  110.1 13.0 %copy-start.22 = (f32[20,256]{1,0:T(8,128)S(1)}, f32[20,256]{1,0:T(8,128)}, u32[]{:S(2)}) copy-start(f32[20,256]{1,0:T(8,128)} %get-tuple-element.65.logd) | copy-start | bytes 61444
  110.1 13.0 %copy-start.23 = (f32[20,256]{1,0:T(8,128)S(1)}, f32[20,256]{1,0:T(8,128)}, u32[]{:S(2)}) copy-start(f32[20,256]{1,0:T(8,128)} %get-tuple-element.114.halves) | copy-start | bytes 61444
  110.1 13.0 %copy-start.24 = (f32[20,256]{1,0:T(8,128)S(1)}, f32[20,256]{1,0:T(8,128)}, u32[]{:S(2)}) copy-start(f32[20,256]{1,0:T(8,128)} %get-tuple-element.115.cross) | copy-start | bytes 61444
  110.1 6.2 %collective-permute-start.13 = (bf16[80,768]{1,0:T(8,128)(2,1)S(1)}, bf16[80,768]{1,0:T(8,128)(2,1)S(1)}, u32[]{:S(2)}, u32[]{:S(2)}) collective-permute-start(bf16[80,768]{1,0:T(8,128)(2,1)S(1)} %get-tuple-element.97), channel_id=1, source_target_pairs={{0,8},{4,36},{8,16},{12,44},{16,24},{20,52},{24,0},{28,60},{32,40}... | collective-permute-start | bytes 368648 | tf_op jit(solution)/shard_map/ppermute | solution.py:724
  110.4 5.9 %collective-permute-start.14 = (bf16[80,768]{1,0:T(8,128)(2,1)S(1)}, bf16[80,768]{1,0:T(8,128)(2,1)S(1)}, u32[]{:S(2)}, u32[]{:S(2)}) collective-permute-start(bf16[80,768]{1,0:T(8,128)(2,1)S(1)} %get-tuple-element.100), channel_id=1, source_target_pairs={{0,24},{4,100},{8,0},{12,108},{16,8},{20,116},{24,16},{28,124},{32... | collective-permute-start | bytes 368648 | tf_op jit(solution)/shard_map/ppermute | solution.py:724
  116.3 10.1 %collective-permute-start.15 = (bf16[160,768]{1,0:T(8,128)(2,1)S(1)}, bf16[160,768]{1,0:T(8,128)(2,1)S(1)}, u32[]{:S(2)}, u32[]{:S(2)}) collective-permute-start(bf16[160,768]{1,0:T(8,128)(2,1)S(1)} %get-tuple-element.102), channel_id=1, source_target_pairs={{0,8},{4,36},{8,16},{12,44},{16,24},{20,52},{24,0},{28,60},{32,40}... | collective-permute-start | bytes 737288 | tf_op jit(solution)/shard_map/ppermute | solution.py:724
  116.4 10.0 %collective-permute-start.16 = (bf16[160,768]{1,0:T(8,128)(2,1)S(1)}, bf16[160,768]{1,0:T(8,128)(2,1)S(1)}, u32[]{:S(2)}, u32[]{:S(2)}) collective-permute-start(bf16[160,768]{1,0:T(8,128)(2,1)S(1)} %get-tuple-element.103), channel_id=1, source_target_pairs={{0,24},{4,100},{8,0},{12,108},{16,8},{20,116},{24,16},{28,124},{32... | collective-permute-start | bytes 737288 | tf_op jit(solution)/shard_map/ppermute | solution.py:724
  119.8 6.6 %collective-permute-start.19 = (bf16[320,256]{1,0:T(8,128)(2,1)S(1)}, bf16[320,256]{1,0:T(8,128)(2,1)S(1)}, u32[]{:S(2)}, u32[]{:S(2)}) collective-permute-start(bf16[320,256]{1,0:T(8,128)(2,1)S(1)} %get-tuple-element.109), channel_id=1, source_target_pairs={{0,1},{1,2},{2,3},{3,0},{4,5},{5,6},{6,7},{7,4},{8,9},{9,10},{10,1... | collective-permute-start | bytes 491528 | tf_op jit(solution)/shard_map/ppermute | solution.py:728
  120.9 5.5 %collective-permute-start.20 = (bf16[320,256]{1,0:T(8,128)(2,1)S(1)}, bf16[320,256]{1,0:T(8,128)(2,1)S(1)}, u32[]{:S(2)}, u32[]{:S(2)}) collective-permute-start(bf16[320,256]{1,0:T(8,128)(2,1)S(1)} %get-tuple-element.110), channel_id=1, source_target_pairs={{0,3},{1,0},{2,1},{3,2},{4,7},{5,4},{6,5},{7,6},{8,11},{9,8},{10,9... | collective-permute-start | bytes 491528 | tf_op jit(solution)/shard_map/ppermute | solution.py:728
  (2 other events, 1.4 us)

commit v6 on v4

--- a/solution.py
+++ b/solution.py
@@ -306,13 +306,15 @@
     )(grad_y, dyt, xgt, cum, bmat, cmat, tie)
 
 
-def shared_kernel(back, xwt, dywt, dbc, ds, st, shared):
+def shared_kernel(back, xwt, dywt, dbc, ds, st, shared, ds_wide, st_wide):
     for k in range(SEQ):
         rows = slice(SLICE * k, SLICE * (k + 1))
         both = back[k].astype(F32)
-        ds[rows, :] = both[:SLICE]
-        st[rows, :] = both[SLICE:]
-    for at, (state, tokens) in enumerate(((ds, xwt), (st, dywt))):
+        ds_wide[rows, :] = both[:SLICE]
+        st_wide[rows, :] = both[SLICE:]
+    ds[...] = ds_wide[...].astype(BF16)
+    st[...] = st_wide[...].astype(BF16)
+    for at, (state, tokens) in enumerate(((ds_wide, xwt), (st_wide, dywt))):
         turned = state[...].T.astype(BF16)
         part = nn(turned, tokens[...]) + dbc[STATE * at : STATE * (at + 1), :]
         shared[:, STATE * at : STATE * (at + 1)] = part.T.astype(BF16)
@@ -322,10 +324,11 @@
     return pl.pallas_call(
         shared_kernel,
         out_shape=(
-            jax.ShapeDtypeStruct((CH, STATE), F32),
-            jax.ShapeDtypeStruct((CH, STATE), F32),
+            jax.ShapeDtypeStruct((CH, STATE), BF16),
+            jax.ShapeDtypeStruct((CH, STATE), BF16),
             jax.ShapeDtypeStruct((T, 2 * STATE), BF16),
         ),
+        scratch_shapes=[pltpu.VMEM((CH, STATE), F32), pltpu.VMEM((CH, STATE), F32)],
         compiler_params=params(),
         cost_estimate=cost(4 * CH * T * 128, 4 * 2**20),
     )(back, xwt, dywt, dbc)
@@ -353,8 +356,7 @@
         for one in copies[i]:
             one.wait()
         back_i, dxg_i, dyt_i, xgt_i, xlt_i, slope_i = [buffer.at[i] for buffer in held]
-        d_high, d_low = split(back_i[...])
-        later = nt(d_high, b_high) + (nt(d_low, b_high) + nt(d_high, b_low))
+        later = nt(back_i[...], b_high) + nt(back_i[...], b_low)
         parts = []
         for q in range(BLK // HEAD_DIM):
             index = i * (BLK // HEAD_DIM) + q
@@ -399,7 +401,7 @@
         scratch_shapes=[
             pltpu.VMEM((2, T + 16, BLK), F32),
             pltpu.SemaphoreType.DMA((NBLK, 6)),
-            pltpu.VMEM((NBLK, BLK, STATE), F32),
+            pltpu.VMEM((NBLK, BLK, STATE), BF16),
             pltpu.VMEM((NBLK, BLK, T), F32),
             pltpu.VMEM((NBLK, BLK, T), BF16),
             pltpu.VMEM((NBLK, BLK, T), BF16),
@@ -413,14 +415,16 @@
 
 def step_kernel(fore, back, cmat, dyt, cum, logd, rc, halves, cross, tie, gls):
     del tie
-    before = wide(nt, fore[...], cmat[...])
+    c_high, c_low = split(cmat[...])
+    before = nt(fore[...], c_high) + nt(fore[...], c_low)
     cums = cum[...]
     inner = []
     through = []
     for h in range(HEADS):
         rows = slice(64 * h, 64 * h + 64)
         inner.append(jnp.sum(dyt[rows, :].astype(F32) * before[rows], axis=0, keepdims=True))
-        both = jnp.sum(fore[rows, :] * back[rows, :], axis=0, keepdims=True)
+        both = fore[rows, :].astype(F32) * back[rows, :].astype(F32)
+        both = jnp.sum(both, axis=0, keepdims=True)
         through.append(jnp.sum(both, axis=1, keepdims=True))
     arriving = rc[...] + jnp.exp(cums) * SCALE * jnp.concatenate(inner, axis=0)
     later = jnp.dot(arriving, triangle(False), precision=HIGH, preferred_element_type=F32)

time: 126 us -> 127 us (level)
    unnamed x52 -> x56, local copies, waits for them, and re-layouts: 9.22 us -> 9.9 us
where the time goes in v6:
time: 127 us; the launch traced here: 125 us
  starting transfers between devices  42.7 us (34%)
  Pallas kernels  34.7 us (27%)
  blocking collectives  17.9 us (14%)
  waiting for transfers between devices  16.6 us (13%)
  local copies, waits for them, and re-layouts  12.2 us (10%)
    all_to_all x1, blocking collectives, body(): back = lax.all_to_all(chain(table, recv, rc), 'seq', 0, 0)  17.9 us
    ppermute x8, starting transfers between devices, along(): return lambda value: lax.ppermute(value, 'seq', ring(first, by))  13.3 us
    ppermute x7, starting transfers between devices, along_head(): lax.ppermute(value, 'head', [(i, (i + by) % ZS) for i in range(ZS)])  13.1 us
    all_to_all x1, starting transfers between devices, body(): recv = lax.all_to_all(msg, 'seq', 0, 0)  11.1 us
    pallas_call x1, Pallas kernels, early(): pl.pallas_call(early_kernel, in_specs=[vm] * 7 + [pl.BlockSpec(memory_spa...  10.4 us
    unnamed x56, local copies, waits for them, and re-layouts  9.9 us
    ppermute x8, waiting for transfers between devices, along(): return lambda value: lax.ppermute(value, 'seq', ring(first, by))  9.77 us
    pallas_call x1, Pallas kernels, input_part(): pl.pallas_call(input_kernel, in_specs=[pl.BlockSpec(memory_space=pltpu.SM...  6.31 us
  transfers between devices with their start and end apart: 22, of which 8 were waited for; matrix products, arithmetic and copies ran while one was open for 1% of the time, Pallas kernels for 17%

profile of v6, /device:TPU:0, one launch (start us, length us, event | category | flops | bytes accessed | tf_op | source)
XLA Modules:
  0.0 125.2 jit_solution(2549532095164948950)
XLA Ops:
  0.6 0.9 slice.9
  1.5 1.3 %collective-permute-start = (bf16[16,2560]{1,0:T(8,128)(2,1)S(1)}, bf16[16,2560]{1,0:T(8,128)(2,1)S(1)}, u32[]{:S(2)}, u32[]{:S(2)}) collective-permute-start(bf16[16,2560]{1,0:T(8,128)(2,1)S(1)} %slice.9), channel_id=1, source_target_pairs={{0,4},{4,8},{8,12},{12,16},{16,20},{20,24},{24,28},{28,32},{32,36}... | collective-permute-start | bytes 245768 | tf_op jit(solution)/shard_map/ppermute | solution.py:710
  2.8 0.9 collective-permute-done.before
  3.7 0.6 copy-done.27
  4.4 10.4 %shard_map.120 = (f32[256,128]{1,0:T(8,128)}, f32[256,128]{1,0:T(8,128)}, f32[20,256]{1,0:T(8,128)}, f32[20,256]{1,0:T(8,128)}, bf16[1280,256]{1,0:T(8,128)(2,1)...) custom-call(s32[1,20]{1,0:T(1,128)} %bitcast.5, ...), custom_call_target="tpu_custom_call" | custom-call | flops 2013265920 | bytes 16777216 | tf_op jit(solution)/shard_map/pallas_call | solution.py:203
  14.8 11.1 %all-to-all-start = ((bf16[32,96,128]{2,1,0:T(8,128)(2,1)}), bf16[32,96,128]{2,1,0:T(8,128)(2,1)S(1)}, u32[]{:S(2)}, u32[]{:S(2)}) async-start(bf16[32,96,128]{2,1,0:T(8,128)(2,1)} %get-tuple-element.62.tie), calls=%async_computation | async-start | bytes 1572864 | tf_op jit(solution)/shard_map/all_to_all | solution.py:715
  25.9 0.7 fusion.order.table
  26.6 1.1 copy-done.2
  27.7 1.0 shard_map.121
  28.8 0.9 copy-done.25
  29.7 1.1 copy-done.17
  30.8 0.9 copy-done.19
  31.7 0.7 copy-done.20
  32.4 3.5 %shard_map.122 = (f32[1280,256]{1,0:T(8,128)S(1)}, f32[20,256]{1,0:T(8,128)S(1)}, f32[256,256]{1,0:T(8,128)S(1)}) custom-call(bf16[256,1280]{1,0:T(8,128)(2,1)S(1)} %copy-done.17, bf16[1280,256]{1,0:T(8,128)(2,1)S(1)} %copy-done.5, bf16[1280,256]{1,0:T(8,128)(2,1)S(1)} %copy-done.12, f32[20,256]{1,0:T(8,128)S(1)} %copy-done.20, f32[256,128]{1,0:T(8,128)S(1)} %copy-done.19, ...), custom_call_target="tpu_custom_call" | custom-call | flops 1342177280 | bytes 4194304 | tf_op jit(solution)/shard_map/pallas_call | solution.py:285
  36.0 1.1 copy-done.11
  37.0 0.8 copy-done.13
  37.9 1.8 %all-to-all-done.recv = bf16[32,96,128]{2,1,0:T(8,128)(2,1)S(1)} async-done(((bf16[32,96,128]{2,1,0:T(8,128)(2,1)}), bf16[32,96,128]{2,1,0:T(8,128)(2,1)S(1)}, u32[]{:S(2)}, u32[]{:S(2)}) %all-to-all-start) | async-done | bytes 786464 | tf_op jit(solution)/shard_map/all_to_all | solution.py:715
  39.7 1.0 shard_map.123
  40.8 17.9 %all_to_all.10.back = bf16[32,80,128]{2,1,0:T(8,128)(2,1)S(1)} all-to-all(bf16[32,80,128]{2,1,0:T(8,128)(2,1)S(1)} %shard_map.123), channel_id=1, replica_groups=mesh['seq'=32,'head'=4] {'seq'}, dimensions={0} | all-to-all | bytes 1310720 | tf_op jit(solution)/shard_map/all_to_all | solution.py:719
  59.2 0.7 copy-done.7
  59.9 0.7 copy-done.9
  60.6 1.9 %collective-permute-start.5 = (bf16[256,256]{1,0:T(8,128)(2,1)S(1)}, bf16[256,256]{1,0:T(8,128)(2,1)S(1)}, u32[]{:S(2)}, u32[]{:S(2)}) collective-permute-start(bf16[256,256]{1,0:T(8,128)(2,1)S(1)} %get-tuple-element.82), channel_id=1, source_target_pairs={{0,1},{1,2},{2,3},{3,0},{4,5},{5,6},{6,7},{7,4},{8,9},{9,10},{10,1... | collective-permute-start | bytes 393224 | tf_op jit(solution)/shard_map/ppermute | solution.py:680
  62.5 3.6 %collective-permute-start.6 = (bf16[256,256]{1,0:T(8,128)(2,1)S(1)}, bf16[256,256]{1,0:T(8,128)(2,1)S(1)}, u32[]{:S(2)}, u32[]{:S(2)}) collective-permute-start(bf16[256,256]{1,0:T(8,128)(2,1)S(1)} %get-tuple-element.82), channel_id=1, source_target_pairs={{0,2},{1,3},{2,0},{3,1},{4,6},{5,7},{6,4},{7,5},{8,10},{9,11},{10,... | collective-permute-start | bytes 393224 | tf_op jit(solution)/shard_map/ppermute | solution.py:680
  66.1 1.0 collective-permute-start.7
  67.1 5.5 %shard_map.125 = (bf16[256,1280]{1,0:T(8,128)(2,1)}, f32[8,1280]{1,0:T(8,128)}, f32[20,256]{1,0:T(8,128)}, f32[20,256]{1,0:T(8,128)}) custom-call(f32[20]{0:T(128)} %skip.1, f32[256,128]{1,0:T(8,128)} %get-tuple-element.65.bmat, f32[4,1280]{1,0:T(4,128)} %taps.1, f32[20,256]{1,0:T(8,128)} %get-tuple-element.66.cum, f32[20,256]{1,0:T(8,128)} %get-tuple-element.67.logd, ...), custom_call_target="tpu_custom_call" | custom-call | flops 167772160 | bytes 6291456 | tf_op jit(solution)/shard_map/pallas_call | solution.py:392
  72.7 1.3 %collective-permute-start.4 = (f32[8,1280]{1,0:T(8,128)}, f32[8,1280]{1,0:T(8,128)S(1)}, u32[]{:S(2)}, u32[]{:S(2)}) collective-permute-start(f32[8,1280]{1,0:T(8,128)} %get-tuple-element.81), channel_id=1, source_target_pairs={{8,0},{16,8},{24,16},{32,24},{40,32},{48,40},{56,48},{64,56},{72,6... | collective-permute-start | bytes 122888 | tf_op jit(solution)/shard_map/ppermute | solution.py:728
  74.0 1.3 %collective-permute-start.3 = (f32[8,1280]{1,0:T(8,128)}, f32[8,1280]{1,0:T(8,128)S(1)}, u32[]{:S(2)}, u32[]{:S(2)}) collective-permute-start(f32[8,1280]{1,0:T(8,128)} %get-tuple-element.81), channel_id=1, source_target_pairs={{4,0},{8,4},{12,8},{16,12},{20,16},{24,20},{28,24},{32,28},{36,32}... | collective-permute-start | bytes 122888 | tf_op jit(solution)/shard_map/ppermute | solution.py:727
  75.3 1.2 collective-permute-start.2
  76.7 2.1 %collective-permute-done.4 = f32[8,1280]{1,0:T(8,128)S(1)} collective-permute-done((f32[8,1280]{1,0:T(8,128)}, f32[8,1280]{1,0:T(8,128)S(1)}, u32[]{:S(2)}, u32[]{:S(2)}) %collective-permute-start.4) | collective-permute-done | bytes 40992 | tf_op jit(solution)/shard_map/ppermute | solution.py:728
  78.9 1.1 copy-done.3
  79.9 0.8 shard_map.126
  80.8 3.2 %collective-permute-start.10 = (bf16[320,768]{1,0:T(8,128)(2,1)S(1)}, bf16[320,768]{1,0:T(8,128)(2,1)S(1)}, u32[]{:S(2)}, u32[]{:S(2)}) collective-permute-start(bf16[320,768]{1,0:T(8,128)(2,1)S(1)} %get-tuple-element.92), channel_id=1, source_target_pairs={{0,96},{4,28},{8,104},{12,4},{16,112},{20,12},{24,120},{28,20},{32... | collective-permute-start | bytes 1474568 | tf_op jit(solution)/shard_map/ppermute | solution.py:676
  84.2 2.3 %shard_map.127 = (f32[320,768]{1,0:T(8,128)S(1)}, f32[320,768]{1,0:T(8,128)S(1)}, bf16[320,768]{1,0:T(8,128)(2,1)S(1)}, bf16[320,768]{1,0:T(8,128)(2,1)S(1)}, f3...) custom-call(bf16[1280,256]{1,0:T(8,128)(2,1)S(1)} %copy-done.14, bf16[1280,256]{1,0:T(8,128)(2,1)S(1)} %collective-permute-done.1.refs_1_, ...), custom_call_target="tpu_custom_call" | custom-call | flops 1509949440 | bytes 9437184 | tf_op jit(solution)/shard_map/pallas_call | solution.py:517
  86.5 4.5 %collective-permute-done.10.refs_4_ = bf16[320,768]{1,0:T(8,128)(2,1)S(1)} collective-permute-done((bf16[320,768]{1,0:T(8,128)(2,1)S(1)}, bf16[320,768]{1,0:T(8,128)(2,1)S(1)}, u32[]{:S(2)}, u32[]{:S(2)}) %collective-permute-start.10) | collective-permute-done | bytes 491552 | tf_op jit(solution)/shard_map/ppermute | solution.py:676
  90.9 3.1 %collective-permute-done.9.refs_1_ = bf16[320,768]{1,0:T(8,128)(2,1)S(1)} collective-permute-done((bf16[320,768]{1,0:T(8,128)(2,1)S(1)}, bf16[320,768]{1,0:T(8,128)(2,1)S(1)}, u32[]{:S(2)}, u32[]{:S(2)}) %collective-permute-start.9) | collective-permute-done | bytes 491552 | tf_op jit(solution)/shard_map/ppermute | solution.py:676
  94.3 3.2 %collective-permute-start.12 = (bf16[640,768]{1,0:T(8,128)(2,1)S(1)}, bf16[640,768]{1,0:T(8,128)(2,1)S(1)}, u32[]{:S(2)}, u32[]{:S(2)}) collective-permute-start(bf16[640,768]{1,0:T(8,128)(2,1)S(1)} %get-tuple-element.95), channel_id=1, source_target_pairs={{0,96},{4,28},{8,104},{12,4},{16,112},{20,12},{24,120},{28,20},{32... | collective-permute-start | bytes 2949128 | tf_op jit(solution)/shard_map/ppermute | solution.py:676
  97.6 0.7 constant_dynamic-slice_fusion
  98.3 6.3 %shard_map.131 = (bf16[320,256]{1,0:T(8,128)(2,1)S(1)}, bf16[320,256]{1,0:T(8,128)(2,1)S(1)}, f32[320,256]{1,0:T(8,128)S(1)}, f32[320,256]{1,0:T(8,128)S(1)}, bf...) custom-call(s32[4]{0:T(128)S(1)} %slice_bitcast_fusion.order, ...), custom_call_target="tpu_custom_call" | custom-call | flops 1761607680 | bytes 10485760 | tf_op jit(solution)/shard_map/pallas_call | solution.py:646
  104.6 1.1 collective-permute-start.17
  105.7 2.2 %collective-permute-start.18 = (bf16[320,256]{1,0:T(8,128)(2,1)S(1)}, bf16[320,256]{1,0:T(8,128)(2,1)S(1)}, u32[]{:S(2)}, u32[]{:S(2)}) collective-permute-start(bf16[320,256]{1,0:T(8,128)(2,1)S(1)} %get-tuple-element.111), channel_id=1, source_target_pairs={{0,3},{1,0},{2,1},{3,2},{4,7},{5,4},{6,5},{7,6},{8,11},{9,8},{10,9... | collective-permute-start | bytes 491528 | tf_op jit(solution)/shard_map/ppermute | solution.py:680
  107.9 1.7 %collective-permute-done.11.up = bf16[640,768]{1,0:T(8,128)(2,1)S(1)} collective-permute-done((bf16[640,768]{1,0:T(8,128)(2,1)S(1)}, bf16[640,768]{1,0:T(8,128)(2,1)S(1)}, u32[]{:S(2)}, u32[]{:S(2)}) %collective-permute-start.11) | collective-permute-done | bytes 983072 | tf_op jit(solution)/shard_map/ppermute | solution.py:676
  110.3 3.0 %collective-permute-start.14 = (bf16[80,768]{1,0:T(8,128)(2,1)S(1)}, bf16[80,768]{1,0:T(8,128)(2,1)S(1)}, u32[]{:S(2)}, u32[]{:S(2)}) collective-permute-start(bf16[80,768]{1,0:T(8,128)(2,1)S(1)} %get-tuple-element.102), channel_id=1, source_target_pairs={{0,24},{4,100},{8,0},{12,108},{16,8},{20,116},{24,16},{28,124},{32... | collective-permute-start | bytes 368648 | tf_op jit(solution)/shard_map/ppermute | solution.py:676
  113.4 1.1 collective-permute-start.19
  114.5 2.2 %collective-permute-start.20 = (bf16[640,256]{1,0:T(8,128)(2,1)S(1)}, bf16[640,256]{1,0:T(8,128)(2,1)S(1)}, u32[]{:S(2)}, u32[]{:S(2)}) collective-permute-start(bf16[640,256]{1,0:T(8,128)(2,1)S(1)} %get-tuple-element.114), channel_id=1, source_target_pairs={{0,3},{1,0},{2,1},{3,2},{4,7},{5,4},{6,5},{7,6},{8,11},{9,8},{10,9... | collective-permute-start | bytes 983048 | tf_op jit(solution)/shard_map/ppermute | solution.py:680
  116.8 3.2 %collective-permute-start.16 = (bf16[160,768]{1,0:T(8,128)(2,1)S(1)}, bf16[160,768]{1,0:T(8,128)(2,1)S(1)}, u32[]{:S(2)}, u32[]{:S(2)}) collective-permute-start(bf16[160,768]{1,0:T(8,128)(2,1)S(1)} %get-tuple-element.105), channel_id=1, source_target_pairs={{0,24},{4,100},{8,0},{12,108},{16,8},{20,116},{24,16},{28,124},{32... | collective-permute-start | bytes 737288 | tf_op jit(solution)/shard_map/ppermute | solution.py:676
  120.1 1.6 %shard_map.134 = f32[20,256]{1,0:T(8,128)} custom-call(bf16[1280,128]{1,0:T(8,128)(2,1)S(1)} %copy-done.10, bf16[1280,128]{1,0:T(8,128)(2,1)S(1)} %copy-done.8, f32[256,128]{1,0:T(8,128)S(1)} %copy-done.18, bf16[1280,256]{1,0:T(8,128)(2,1)S(1)} %copy-done.6, f32[20,256]{1,0:T(8,128)S(1)} %copy-done.21, f32[20,256]{1,0:T(8,128)S(1)} %copy-done.22, ...), custom_call_target="tpu_custom_call" | custom-call | flops 167772160 | bytes 4194304 | tf_op jit(solution)/shard_map/pallas_call | solution.py:441
  121.7 2.0 %collective-permute-done.19.up_u = bf16[640,256]{1,0:T(8,128)(2,1)S(1)} collective-permute-done((bf16[640,256]{1,0:T(8,128)(2,1)S(1)}, bf16[640,256]{1,0:T(8,128)(2,1)S(1)}, u32[]{:S(2)}, u32[]{:S(2)}) %collective-permute-start.19) | collective-permute-done | bytes 327712 | tf_op jit(solution)/shard_map/ppermute | solution.py:680
  124.2 1.0 shard_map.133
  (74 shorter events, 2.6 us)
Async XLA Ops:
  1.5 2.2 %collective-permute-start = (bf16[16,2560]{1,0:T(8,128)(2,1)S(1)}, bf16[16,2560]{1,0:T(8,128)(2,1)S(1)}, u32[]{:S(2)}, u32[]{:S(2)}) collective-permute-start(bf16[16,2560]{1,0:T(8,128)(2,1)S(1)} %slice.9), channel_id=1, source_target_pairs={{0,4},{4,8},{8,12},{12,16},{16,20},{20,24},{24,28},{28,32},{32,36}... | collective-permute-start | bytes 245768 | tf_op jit(solution)/shard_map/ppermute | solution.py:710
  14.8 11.8 %copy-start = (bf16[256,2560]{1,0:T(8,128)(2,1)S(1)}, bf16[256,2560]{1,0:T(8,128)(2,1)}, u32[]{:S(2)}) copy-start(bf16[256,2560]{1,0:T(8,128)(2,1)} %normed.3) | copy-start | bytes 3932164
  14.8 14.9 %copy-start.18 = (f32[256,128]{1,0:T(8,128)S(1)}, f32[256,128]{1,0:T(8,128)}, u32[]{:S(2)}) copy-start(f32[256,128]{1,0:T(8,128)} %get-tuple-element.70.cmat) | copy-start | bytes 393220
  14.8 25.0 %all-to-all-start = ((bf16[32,96,128]{2,1,0:T(8,128)(2,1)}), bf16[32,96,128]{2,1,0:T(8,128)(2,1)S(1)}, u32[]{:S(2)}, u32[]{:S(2)}) async-start(bf16[32,96,128]{2,1,0:T(8,128)(2,1)} %get-tuple-element.62.tie), calls=%async_computation | async-start | bytes 1572864 | tf_op jit(solution)/shard_map/all_to_all | solution.py:715
  26.6 1.1 copy-start.2
  27.7 1.9 %copy-start.5 = (bf16[1280,256]{1,0:T(8,128)(2,1)S(1)}, bf16[1280,256]{1,0:T(8,128)(2,1)}, u32[]{:S(2)}) copy-start(bf16[1280,256]{1,0:T(8,128)(2,1)} %get-tuple-element.68.dyt) | copy-start | bytes 1966084
  27.7 1.9 %copy-start.12 = (bf16[1280,256]{1,0:T(8,128)(2,1)S(1)}, bf16[1280,256]{1,0:T(8,128)(2,1)}, u32[]{:S(2)}) copy-start(bf16[1280,256]{1,0:T(8,128)(2,1)} %get-tuple-element.69.xgt) | copy-start | bytes 1966084
  28.8 0.9 copy-start.25
  29.7 1.1 copy-start.17
  30.8 0.9 copy-start.19
  31.7 0.7 copy-start.20
  36.0 1.1 copy-start.11
  37.0 0.8 copy-start.13
  39.7 18.9 %copy-start.15 = (bf16[1280,256]{1,0:T(8,128)(2,1)S(1)}, bf16[1280,256]{1,0:T(8,128)(2,1)}, u32[]{:S(2)}) copy-start(bf16[1280,256]{1,0:T(8,128)(2,1)} %get-tuple-element.73.dywt) | copy-start | bytes 1966084
  39.7 18.9 %copy-start.16 = (bf16[1280,256]{1,0:T(8,128)(2,1)S(1)}, bf16[1280,256]{1,0:T(8,128)(2,1)}, u32[]{:S(2)}) copy-start(bf16[1280,256]{1,0:T(8,128)(2,1)} %get-tuple-element.72.xwt) | copy-start | bytes 1966084
  58.7 8.5 %copy-start.26 = (bf16[1280,256]{1,0:T(8,128)(2,1)S(1)}, bf16[1280,256]{1,0:T(8,128)(2,1)}, u32[]{:S(2)}) copy-start(bf16[1280,256]{1,0:T(8,128)(2,1)} %copy-done.25) | copy-start | bytes 1966084
  59.1 0.7 copy-start.7
  60.6 13.4 %collective-permute-start.5 = (bf16[256,256]{1,0:T(8,128)(2,1)S(1)}, bf16[256,256]{1,0:T(8,128)(2,1)S(1)}, u32[]{:S(2)}, u32[]{:S(2)}) collective-permute-start(bf16[256,256]{1,0:T(8,128)(2,1)S(1)} %get-tuple-element.82), channel_id=1, source_target_pairs={{0,1},{1,2},{2,3},{3,0},{4,5},{5,6},{6,7},{7,4},{8,9},{9,10},{10,1... | collective-permute-start | bytes 393224 | tf_op jit(solution)/shard_map/ppermute | solution.py:680
  62.5 12.8 %collective-permute-start.6 = (bf16[256,256]{1,0:T(8,128)(2,1)S(1)}, bf16[256,256]{1,0:T(8,128)(2,1)S(1)}, u32[]{:S(2)}, u32[]{:S(2)}) collective-permute-start(bf16[256,256]{1,0:T(8,128)(2,1)S(1)} %get-tuple-element.82), channel_id=1, source_target_pairs={{0,2},{1,3},{2,0},{3,1},{4,6},{5,7},{6,4},{7,5},{8,10},{9,11},{10,... | collective-permute-start | bytes 393224 | tf_op jit(solution)/shard_map/ppermute | solution.py:680
  66.1 10.4 %collective-permute-start.7 = (bf16[256,256]{1,0:T(8,128)(2,1)S(1)}, bf16[256,256]{1,0:T(8,128)(2,1)S(1)}, u32[]{:S(2)}, u32[]{:S(2)}) collective-permute-start(bf16[256,256]{1,0:T(8,128)(2,1)S(1)} %get-tuple-element.82), channel_id=1, source_target_pairs={{0,3},{1,0},{2,1},{3,2},{4,7},{5,4},{6,5},{7,6},{8,11},{9,8},{10,9... | collective-permute-start | bytes 393224 | tf_op jit(solution)/shard_map/ppermute | solution.py:680
  67.1 11.7 %collective-permute-start.1 = (bf16[1280,256]{1,0:T(8,128)(2,1)S(1)}, bf16[1280,256]{1,0:T(8,128)(2,1)S(1)}, u32[]{:S(2)}, u32[]{:S(2)}) collective-permute-start(bf16[1280,256]{1,0:T(8,128)(2,1)S(1)} %copy-done.26), channel_id=1, source_target_pairs={{0,4},{4,0},{8,12},{12,8},{16,20},{20,16},{24,28},{28,24},{32,36},... | collective-permute-start | bytes 1966088 | tf_op jit(solution)/shard_map/ppermute | solution.py:717
  67.1 11.7 %copy-start.14 = (bf16[1280,256]{1,0:T(8,128)(2,1)S(1)}, bf16[1280,256]{1,0:T(8,128)(2,1)}, u32[]{:S(2)}) copy-start(bf16[1280,256]{1,0:T(8,128)(2,1)} %copy-done.13) | copy-start | bytes 1966084
  72.7 6.1 %collective-permute-start.4 = (f32[8,1280]{1,0:T(8,128)}, f32[8,1280]{1,0:T(8,128)S(1)}, u32[]{:S(2)}, u32[]{:S(2)}) collective-permute-start(f32[8,1280]{1,0:T(8,128)} %get-tuple-element.81), channel_id=1, source_target_pairs={{8,0},{16,8},{24,16},{32,24},{40,32},{48,40},{56,48},{64,56},{72,6... | collective-permute-start | bytes 122888 | tf_op jit(solution)/shard_map/ppermute | solution.py:728
  74.0 4.8 %collective-permute-start.3 = (f32[8,1280]{1,0:T(8,128)}, f32[8,1280]{1,0:T(8,128)S(1)}, u32[]{:S(2)}, u32[]{:S(2)}) collective-permute-start(f32[8,1280]{1,0:T(8,128)} %get-tuple-element.81), channel_id=1, source_target_pairs={{4,0},{8,4},{12,8},{16,12},{20,16},{24,20},{28,24},{32,28},{36,32}... | collective-permute-start | bytes 122888 | tf_op jit(solution)/shard_map/ppermute | solution.py:727
  75.3 3.5 %collective-permute-start.2 = (bf16[256,1280]{1,0:T(8,128)(2,1)}, bf16[256,1280]{1,0:T(8,128)(2,1)S(1)}, u32[]{:S(2)}, u32[]{:S(2)}) collective-permute-start(bf16[256,1280]{1,0:T(8,128)(2,1)} %get-tuple-element.80.refs_2_.grad), channel_id=1, source_target_pairs={{0,4},{4,0},{8,12},{12,8},{16,20},{20,16},{24,28},{28,24},{32,36},... | collective-permute-start | bytes 1966088 | tf_op jit(solution)/shard_map/ppermute | solution.py:726
  76.6 2.2 %collective-permute-start.8 = (bf16[256,256]{1,0:T(8,128)(2,1)S(1)}, bf16[256,256]{1,0:T(8,128)(2,1)S(1)}, u32[]{:S(2)}, u32[]{:S(2)}) collective-permute-start(bf16[256,256]{1,0:T(8,128)(2,1)S(1)} %add_convert_fusion.refs_6_.shared), channel_id=1, source_target_pairs={{0,4},{4,0},{8,12},{12,8},{16,20},{20,16},{24,28},{28,24},{32,36},... | collective-permute-start | bytes 393224 | tf_op jit(solution)/shard_map/ppermute | solution.py:734
  78.9 1.1 copy-start.3
  79.9 4.3 %copy-start.4 = (bf16[256,1280]{1,0:T(8,128)(2,1)S(1)}, bf16[256,1280]{1,0:T(8,128)(2,1)}, u32[]{:S(2)}) copy-start(bf16[256,1280]{1,0:T(8,128)(2,1)} %get-tuple-element.80.refs_2_.grad) | copy-start | bytes 1966084
  80.8 10.1 %collective-permute-start.10 = (bf16[320,768]{1,0:T(8,128)(2,1)S(1)}, bf16[320,768]{1,0:T(8,128)(2,1)S(1)}, u32[]{:S(2)}, u32[]{:S(2)}) collective-permute-start(bf16[320,768]{1,0:T(8,128)(2,1)S(1)} %get-tuple-element.92), channel_id=1, source_target_pairs={{0,96},{4,28},{8,104},{12,4},{16,112},{20,12},{24,120},{28,20},{32... | collective-permute-start | bytes 1474568 | tf_op jit(solution)/shard_map/ppermute | solution.py:676
  84.0 10.0 %collective-permute-start.9 = (bf16[320,768]{1,0:T(8,128)(2,1)S(1)}, bf16[320,768]{1,0:T(8,128)(2,1)S(1)}, u32[]{:S(2)}, u32[]{:S(2)}) collective-permute-start(bf16[320,768]{1,0:T(8,128)(2,1)S(1)} %get-tuple-element.86.refs_8_), channel_id=1, source_target_pairs={{0,32},{4,12},{8,40},{12,20},{16,48},{20,28},{24,56},{28,4},{32,64... | collective-permute-start | bytes 1474568 | tf_op jit(solution)/shard_map/ppermute | solution.py:676
  94.0 4.3 %copy-start.1 = (bf16[2560,256]{1,0:T(8,128)(2,1)S(1)}, bf16[2560,256]{1,0:T(8,128)(2,1)}, u32[]{:S(2)}) copy-start(bf16[2560,256]{1,0:T(8,128)(2,1)} %w_bc.3) | copy-start | bytes 3932164
  94.3 15.4 %collective-permute-start.11 = (bf16[640,768]{1,0:T(8,128)(2,1)S(1)}, bf16[640,768]{1,0:T(8,128)(2,1)S(1)}, u32[]{:S(2)}, u32[]{:S(2)}) collective-permute-start(bf16[640,768]{1,0:T(8,128)(2,1)S(1)} %get-tuple-element.94.tie), channel_id=1, source_target_pairs={{0,32},{4,12},{8,40},{12,20},{16,48},{20,28},{24,56},{28,4},{32,64... | collective-permute-start | bytes 2949128 | tf_op jit(solution)/shard_map/ppermute | solution.py:676
  94.3 15.3 %collective-permute-start.12 = (bf16[640,768]{1,0:T(8,128)(2,1)S(1)}, bf16[640,768]{1,0:T(8,128)(2,1)S(1)}, u32[]{:S(2)}, u32[]{:S(2)}) collective-permute-start(bf16[640,768]{1,0:T(8,128)(2,1)S(1)} %get-tuple-element.95), channel_id=1, source_target_pairs={{0,96},{4,28},{8,104},{12,4},{16,112},{20,12},{24,120},{28,20},{32... | collective-permute-start | bytes 2949128 | tf_op jit(solution)/shard_map/ppermute | solution.py:676
  104.6 8.7 %collective-permute-start.17 = (bf16[320,256]{1,0:T(8,128)(2,1)S(1)}, bf16[320,256]{1,0:T(8,128)(2,1)S(1)}, u32[]{:S(2)}, u32[]{:S(2)}) collective-permute-start(bf16[320,256]{1,0:T(8,128)(2,1)S(1)} %get-tuple-element.108), channel_id=1, source_target_pairs={{0,1},{1,2},{2,3},{3,0},{4,5},{5,6},{6,7},{7,4},{8,9},{9,10},{10,1... | collective-permute-start | bytes 491528 | tf_op jit(solution)/shard_map/ppermute | solution.py:680
  105.7 7.6 %collective-permute-start.18 = (bf16[320,256]{1,0:T(8,128)(2,1)S(1)}, bf16[320,256]{1,0:T(8,128)(2,1)S(1)}, u32[]{:S(2)}, u32[]{:S(2)}) collective-permute-start(bf16[320,256]{1,0:T(8,128)(2,1)S(1)} %get-tuple-element.111), channel_id=1, source_target_pairs={{0,3},{1,0},{2,1},{3,2},{4,7},{5,4},{6,5},{7,6},{8,11},{9,8},{10,9... | collective-permute-start | bytes 491528 | tf_op jit(solution)/shard_map/ppermute | solution.py:680
  109.9 10.1 %copy-start.6 = (bf16[1280,256]{1,0:T(8,128)(2,1)S(1)}, bf16[1280,256]{1,0:T(8,128)(2,1)}, u32[]{:S(2)}) copy-start(bf16[1280,256]{1,0:T(8,128)(2,1)} %get-tuple-element.68.dyt) | copy-start | bytes 1966084
  109.9 10.1 %copy-start.8 = (bf16[1280,128]{1,0:T(8,128)(2,1)S(1)}, bf16[1280,128]{1,0:T(8,128)(2,1)}, u32[]{:S(2)}) copy-start(bf16[1280,128]{1,0:T(8,128)(2,1)} %copy-done.7) | copy-start | bytes 983044
  109.9 10.1 %copy-start.10 = (bf16[1280,128]{1,0:T(8,128)(2,1)S(1)}, bf16[1280,128]{1,0:T(8,128)(2,1)}, u32[]{:S(2)}) copy-start(bf16[1280,128]{1,0:T(8,128)(2,1)} %copy-done.9) | copy-start | bytes 983044
  109.9 10.1 %copy-start.21 = (f32[20,256]{1,0:T(8,128)S(1)}, f32[20,256]{1,0:T(8,128)}, u32[]{:S(2)}) copy-start(f32[20,256]{1,0:T(8,128)} %get-tuple-element.66.cum) | copy-start | bytes 61444
  110.0 10.1 %copy-start.22 = (f32[20,256]{1,0:T(8,128)S(1)}, f32[20,256]{1,0:T(8,128)}, u32[]{:S(2)}) copy-start(f32[20,256]{1,0:T(8,128)} %get-tuple-element.67.logd) | copy-start | bytes 61444
  110.0 10.1 %copy-start.23 = (f32[20,256]{1,0:T(8,128)S(1)}, f32[20,256]{1,0:T(8,128)}, u32[]{:S(2)}) copy-start(f32[20,256]{1,0:T(8,128)} %get-tuple-element.118.halves) | copy-start | bytes 61444
  110.0 10.1 %copy-start.24 = (f32[20,256]{1,0:T(8,128)S(1)}, f32[20,256]{1,0:T(8,128)}, u32[]{:S(2)}) copy-start(f32[20,256]{1,0:T(8,128)} %get-tuple-element.119.cross) | copy-start | bytes 61444
  110.0 6.7 %collective-permute-start.13 = (bf16[80,768]{1,0:T(8,128)(2,1)S(1)}, bf16[80,768]{1,0:T(8,128)(2,1)S(1)}, u32[]{:S(2)}, u32[]{:S(2)}) collective-permute-start(bf16[80,768]{1,0:T(8,128)(2,1)S(1)} %get-tuple-element.99), channel_id=1, source_target_pairs={{0,8},{4,36},{8,16},{12,44},{16,24},{20,52},{24,0},{28,60},{32,40}... | collective-permute-start | bytes 368648 | tf_op jit(solution)/shard_map/ppermute | solution.py:676
  110.3 6.4 %collective-permute-start.14 = (bf16[80,768]{1,0:T(8,128)(2,1)S(1)}, bf16[80,768]{1,0:T(8,128)(2,1)S(1)}, u32[]{:S(2)}, u32[]{:S(2)}) collective-permute-start(bf16[80,768]{1,0:T(8,128)(2,1)S(1)} %get-tuple-element.102), channel_id=1, source_target_pairs={{0,24},{4,100},{8,0},{12,108},{16,8},{20,116},{24,16},{28,124},{32... | collective-permute-start | bytes 368648 | tf_op jit(solution)/shard_map/ppermute | solution.py:676
  113.4 10.3 %collective-permute-start.19 = (bf16[640,256]{1,0:T(8,128)(2,1)S(1)}, bf16[640,256]{1,0:T(8,128)(2,1)S(1)}, u32[]{:S(2)}, u32[]{:S(2)}) collective-permute-start(bf16[640,256]{1,0:T(8,128)(2,1)S(1)} %get-tuple-element.113), channel_id=1, source_target_pairs={{0,1},{1,2},{2,3},{3,0},{4,5},{5,6},{6,7},{7,4},{8,9},{9,10},{10,1... | collective-permute-start | bytes 983048 | tf_op jit(solution)/shard_map/ppermute | solution.py:680
  114.5 9.2 %collective-permute-start.20 = (bf16[640,256]{1,0:T(8,128)(2,1)S(1)}, bf16[640,256]{1,0:T(8,128)(2,1)S(1)}, u32[]{:S(2)}, u32[]{:S(2)}) collective-permute-start(bf16[640,256]{1,0:T(8,128)(2,1)S(1)} %get-tuple-element.114), channel_id=1, source_target_pairs={{0,3},{1,0},{2,1},{3,2},{4,7},{5,4},{6,5},{7,6},{8,11},{9,8},{10,9... | collective-permute-start | bytes 983048 | tf_op jit(solution)/shard_map/ppermute | solution.py:680
  116.7 7.5 %collective-permute-start.15 = (bf16[160,768]{1,0:T(8,128)(2,1)S(1)}, bf16[160,768]{1,0:T(8,128)(2,1)S(1)}, u32[]{:S(2)}, u32[]{:S(2)}) collective-permute-start(bf16[160,768]{1,0:T(8,128)(2,1)S(1)} %get-tuple-element.104), channel_id=1, source_target_pairs={{0,8},{4,36},{8,16},{12,44},{16,24},{20,52},{24,0},{28,60},{32,40}... | collective-permute-start | bytes 737288 | tf_op jit(solution)/shard_map/ppermute | solution.py:676
  116.8 7.4 %collective-permute-start.16 = (bf16[160,768]{1,0:T(8,128)(2,1)S(1)}, bf16[160,768]{1,0:T(8,128)(2,1)S(1)}, u32[]{:S(2)}, u32[]{:S(2)}) collective-permute-start(bf16[160,768]{1,0:T(8,128)(2,1)S(1)} %get-tuple-element.105), channel_id=1, source_target_pairs={{0,24},{4,100},{8,0},{12,108},{16,8},{20,116},{24,16},{28,124},{32... | collective-permute-start | bytes 737288 | tf_op jit(solution)/shard_map/ppermute | solution.py:676
  (2 other events, 1.4 us)
